TPU v7x, 32 devices: a whole 2x2x4 slice. The times are simulated.
32 devices in a mesh: seq: 16 (over z, y, x), head: 2 (over core).
Axes of the slice: x: 2, y: 2, z: 4, core: 2. Of those that a mesh axis runs over, the one named last changes fastest.
Arguments:
- queries: bfloat16 [2048, 4096], P('seq', 'head'), may hold values from -0.71875 to 0.71875
- key_rows: bfloat16 [2048, 4096], P('seq', 'head'), may hold values from -0.71875 to 0.71875
- value_rows: bfloat16 [2048, 4096], P('seq', 'head'), may hold values from -0.71875 to 0.71875
- segment_ids: int32 [2048], P('seq'), may hold values from 0 to 7, never falling along the last dimension, each value on 1 to 512 neighbouring positions
- decay_span: float32 [32], P('head'), may hold values from 30 to 20480, as said below
- norm_gain: float32 [4096], P('head'), may hold values from 0.5 to 1.5
- out_grad: bfloat16 [2048, 4096], P('seq', 'head'), may hold values from -0.71875 to 0.71875
Outputs:
- query_grad: bfloat16 [2048, 4096], P('seq', 'head')
- key_grad: bfloat16 [2048, 4096], P('seq', 'head')
- value_grad: bfloat16 [2048, 4096], P('seq', 'head')
- gain_grad: float32 [4096], P('head')
Inputs may be any that keep to these rules, and one draw needn't show every extreme that they name: segment_ids never falls along the segment; every document of the 8 has a token and the longest has 512. The decay per token of head h is exp(-1 / decay_span[h]).
All inputs are finite; a program needn't handle non-finite values.
Results may differ from a plain program's by a relative error of at most 0.0012.
Values sent between devices are 32-bit elements; how exact they have to be, the bound alone decides.
No kernel may reach another device: no remote copies, remote signals or barrier semaphores. Data moves between devices by JAX's collectives and lax.ppermute only.
A program may use at most 64 MiB of HBM per device.

v0:
```python
import jax
import jax.numpy as jnp
from jax import lax
from jax.sharding import PartitionSpec as P

HEADS = 32
HEAD_DIM = 128


exact = lax.Precision.HIGHEST


def shifted(array, axis, by):
    devices = lax.axis_size(axis)
    pairs = [(i, i + by) for i in range(devices) if 0 <= i + by < devices]
    return lax.ppermute(array, axis, pairs)


def combine_forward(earlier, later):
    state_early, decay_early, first_early, last_early = earlier
    state_late, decay_late, first_late, last_late = later
    passes = jnp.logical_or(
        jnp.logical_and(first_late == last_late, first_late == last_early), first_late < 0
    )
    factor = jnp.where(passes, decay_late, 0.0)
    return (
        state_late + factor[:, None, None] * state_early,
        decay_early * decay_late,
        jnp.where(first_early < 0, first_late, first_early),
        jnp.where(last_late < 0, last_early, last_late),
    )


def combine_backward(earlier, later):
    state_high, decay_high, first_high, last_high = earlier
    state_low, decay_low, first_low, last_low = later
    passes = jnp.logical_or(
        jnp.logical_and(first_low == last_low, last_low == first_high), first_low < 0
    )
    factor = jnp.where(passes, decay_low, 0.0)
    return (
        state_low + factor[:, None, None] * state_high,
        decay_high * decay_low,
        jnp.where(first_low < 0, first_high, first_low),
        jnp.where(last_high < 0, last_low, last_high),
    )


def select_tree(condition, left_tree, right_tree):
    return jax.tree.map(
        lambda left_leaf, right_leaf: jnp.where(condition, left_leaf, right_leaf),
        left_tree,
        right_tree,
    )


def doubling_prefix(summary, identity, backward):
    members = lax.axis_size("seq")
    position = lax.axis_index("seq")
    distances = [1]
    reach = 1
    while reach < members:
        distances.append(reach)
        reach = reach * 2
    result = summary
    for rounds, distance in enumerate(distances):
        if backward:
            incoming = shifted(result, "seq", -distance)
            valid = position + distance <= members - 1
        else:
            incoming = shifted(result, "seq", distance)
            valid = position >= distance
        if rounds == 0:
            result = select_tree(valid, incoming, identity)
        else:
            merged = (
                combine_backward(incoming, result)
                if backward
                else combine_forward(incoming, result)
            )
            result = select_tree(valid, merged, result)
    return result


def local(queries, key_rows, value_rows, segment_ids, decay_span, norm_gain, out_grad):
    tok_rows = queries.shape[0]
    heads_here = decay_span.shape[0]
    all_features = HEADS * HEAD_DIM
    block_rows = min(tok_rows, 512)
    block_count = tok_rows // block_rows
    seg_float = segment_ids.astype(jnp.float32)
    positions = jnp.arange(tok_rows, dtype=jnp.float32)
    first_seg = seg_float[0]
    last_seg = seg_float[-1]
    query_full = queries.reshape(tok_rows, heads_here, HEAD_DIM).astype(jnp.float32)
    key_full = key_rows.reshape(tok_rows, heads_here, HEAD_DIM).astype(jnp.float32)
    value_full = value_rows.reshape(tok_rows, heads_here, HEAD_DIM).astype(jnp.float32)
    shard_decay = jnp.exp(-tok_rows / decay_span)
    tail_on = jnp.where(
        (seg_float == last_seg)[:, None],
        jnp.exp(-(tok_rows - 1.0 - positions)[:, None] / decay_span[None, :]),
        0.0,
    )
    local_state = jnp.einsum(
        "thi,thj->hij", key_full * tail_on[:, :, None], value_full, precision=exact
    )
    summary = (local_state, shard_decay, first_seg, last_seg)
    identity = (
        jnp.zeros_like(local_state),
        jnp.ones_like(decay_span),
        jnp.float32(-1.0),
        jnp.float32(-1.0),
    )
    prefix = doubling_prefix(summary, identity, False)
    state_in = prefix[0]
    prev_seg = prefix[3]
    offsets = jnp.arange(block_rows, dtype=jnp.float32)
    offset_gap = offsets[:, None] - offsets[None, :]
    causal = offset_gap >= 0
    decay_tile = jnp.where(
        causal[None], jnp.exp(-jnp.maximum(offset_gap, 0.0)[None] / decay_span[:, None, None]), 0.0
    )
    into_weight = jnp.exp(-(offsets + 1.0)[:, None] / decay_span[None, :])
    tail_weight = jnp.exp(-(block_rows - 1.0 - offsets)[:, None] / decay_span[None, :])
    start_weight = jnp.exp(-offsets[:, None] / decay_span[None, :])
    next_weight = jnp.exp(-(block_rows - offsets)[:, None] / decay_span[None, :])
    whole_weight = jnp.exp(-block_rows / decay_span)
    query_blocks = query_full.reshape(block_count, block_rows, heads_here, HEAD_DIM)
    key_blocks = key_full.reshape(block_count, block_rows, heads_here, HEAD_DIM)
    value_blocks = value_full.reshape(block_count, block_rows, heads_here, HEAD_DIM)
    grad_blocks = out_grad.reshape(block_count, block_rows, heads_here * HEAD_DIM)
    seg_blocks = seg_float.reshape(block_count, block_rows)

    def forward_step(carry, inputs):
        state_now, carry_seg, gain_acc = carry
        query_blk, key_blk, value_blk, dy_blk, seg_blk = inputs
        dy_full = dy_blk.astype(jnp.float32)
        same_doc = (seg_blk[:, None] == seg_blk[None, :]).astype(jnp.float32)
        weights = decay_tile * same_doc[None]
        scores = jnp.einsum("thd,shd->hts", query_blk, key_blk, precision=exact) * weights
        inter_on = jnp.where((seg_blk == carry_seg)[:, None], into_weight, 0.0)
        attended = jnp.einsum("hts,shd->thd", scores, value_blk, precision=exact)
        attended = attended + inter_on[:, :, None] * jnp.einsum(
            "thi,hij->thj", query_blk, state_now, precision=exact
        )
        flat_out = attended.reshape(block_rows, heads_here * HEAD_DIM)
        square_part = jnp.sum(flat_out * flat_out, axis=1)
        cross_part = jnp.sum(dy_full * norm_gain[None, :] * flat_out, axis=1)
        square_total, cross_total = lax.psum((square_part, cross_part), "head")
        inv_scale = lax.rsqrt(square_total / all_features + 1e-06)
        out_back = (
            norm_gain[None, :] * dy_full * inv_scale[:, None]
            - flat_out * (inv_scale * inv_scale * inv_scale * cross_total / all_features)[:, None]
        )
        gain_acc = gain_acc + jnp.sum(dy_full * flat_out * inv_scale[:, None], axis=0)
        back_heads = out_back.reshape(block_rows, heads_here, HEAD_DIM)
        grad_scores = jnp.einsum("thd,shd->hts", back_heads, value_blk, precision=exact) * weights
        query_part = jnp.einsum("hts,shd->thd", grad_scores, key_blk, precision=exact)
        query_part = query_part + inter_on[:, :, None] * jnp.einsum(
            "thj,hij->thi", back_heads, state_now, precision=exact
        )
        tail_blk = jnp.where((seg_blk == seg_blk[-1])[:, None], tail_weight, 0.0)
        passes = jnp.logical_and(seg_blk[0] == seg_blk[-1], seg_blk[0] == carry_seg)
        factor = jnp.where(passes, whole_weight, 0.0)
        new_state = (
            jnp.einsum("thi,thj->hij", key_blk * tail_blk[:, :, None], value_blk, precision=exact)
            + factor[:, None, None] * state_now
        )
        outputs = (
            back_heads,
            query_part.reshape(block_rows, heads_here * HEAD_DIM).astype(jnp.bfloat16),
        )
        return ((new_state, seg_blk[-1], gain_acc), outputs)

    start_carry = (state_in, prev_seg, jnp.zeros((heads_here * HEAD_DIM,), jnp.float32))
    forward_carry, forward_out = lax.scan(
        forward_step, start_carry, (query_blocks, key_blocks, value_blocks, grad_blocks, seg_blocks)
    )
    back_blocks = forward_out[0]
    query_grad = forward_out[1].reshape(tok_rows, heads_here * HEAD_DIM)
    gain_local = forward_carry[2]
    back_all = back_blocks.reshape(tok_rows, heads_here, HEAD_DIM)
    start_on = jnp.where(
        (seg_float == first_seg)[:, None], jnp.exp(-positions[:, None] / decay_span[None, :]), 0.0
    )
    local_grad = jnp.einsum(
        "thi,thj->hij", query_full * start_on[:, :, None], back_all, precision=exact
    )
    back_summary = (local_grad, shard_decay, first_seg, last_seg)
    suffix = doubling_prefix(back_summary, identity, True)
    grad_in = suffix[0]
    next_seg = suffix[2]

    def backward_step(carry, inputs):
        grad_state, carry_seg = carry
        query_blk, key_blk, value_blk, back_heads, seg_blk = inputs[:5]
        same_doc = (seg_blk[:, None] == seg_blk[None, :]).astype(jnp.float32)
        weights = decay_tile * same_doc[None]
        scores = jnp.einsum("thd,shd->hts", query_blk, key_blk, precision=exact) * weights
        grad_scores = jnp.einsum("thd,shd->hts", back_heads, value_blk, precision=exact) * weights
        key_part = jnp.einsum("hts,thd->shd", grad_scores, query_blk, precision=exact)
        value_part = jnp.einsum("hts,thd->shd", scores, back_heads, precision=exact)
        back_on = jnp.where((seg_blk == carry_seg)[:, None], next_weight, 0.0)
        key_part = key_part + back_on[:, :, None] * jnp.einsum(
            "hij,shj->shi", grad_state, value_blk, precision=exact
        )
        value_part = value_part + back_on[:, :, None] * jnp.einsum(
            "hij,shi->shj", grad_state, key_blk, precision=exact
        )
        start_blk = jnp.where((seg_blk == seg_blk[0])[:, None], start_weight, 0.0)
        passes = jnp.logical_and(seg_blk[0] == seg_blk[-1], seg_blk[-1] == carry_seg)
        factor = jnp.where(passes, whole_weight, 0.0)
        new_state = (
            jnp.einsum(
                "thi,thj->hij", query_blk * start_blk[:, :, None], back_heads, precision=exact
            )
            + factor[:, None, None] * grad_state
        )
        return (
            (new_state, seg_blk[0]),
            (
                key_part.reshape(block_rows, heads_here * HEAD_DIM).astype(jnp.bfloat16),
                value_part.reshape(block_rows, heads_here * HEAD_DIM).astype(jnp.bfloat16),
            ),
        )

    backward_inputs = (query_blocks, key_blocks, value_blocks, back_blocks, seg_blocks)
    _, (key_grad, value_grad) = lax.scan(
        backward_step, (grad_in, next_seg), backward_inputs, reverse=True
    )
    gain_grad = lax.psum(gain_local, "seq")
    return (
        query_grad,
        key_grad.reshape(tok_rows, heads_here * HEAD_DIM),
        value_grad.reshape(tok_rows, heads_here * HEAD_DIM),
        gain_grad,
    )


def solution(mesh):
    in_specs = (
        P("seq", "head"),
        P("seq", "head"),
        P("seq", "head"),
        P("seq"),
        P("head"),
        P("head"),
        P("seq", "head"),
    )
    out_specs = (P("seq", "head"), P("seq", "head"), P("seq", "head"), P("head"))
    return jax.shard_map(local, mesh=mesh, in_specs=in_specs, out_specs=out_specs, check_vma=False)
```

profile of v0, /device:TPU:16, one launch (start us, length us, event | category | flops | bytes accessed | tf_op | source)
XLA Modules:
  0.0 441.8 jit_solution(4344961286656516120)
XLA Ops:
  1.9 4.2 collective-permute-start.18
  10.5 7.0 %collective-permute-start.19 = (f32[]{:T(128)}, f32[]{:T(128)}, u32[]{:S(2)}, u32[]{:S(2)}) collective-permute-start(f32[]{:T(128)} %select_n.341), channel_id=1, source_target_pairs={{2,0},{4,2},{6,4},{8,6},{10,8},{12,10},{14,12},{16,14},{18,16},{20... | collective-permute-start | bytes 20 | tf_op jit(solution)/shard_map/ppermute | solution.py:16
  18.1 3.2 collective-permute-start.1
  21.9 3.8 collective-permute-start.20
  26.3 4.7 %collective-permute-start.2 = (f32[]{:T(128)}, f32[]{:T(128)}, u32[]{:S(2)}, u32[]{:S(2)}) collective-permute-start(f32[]{:T(128)} %select_n.301), channel_id=1, source_target_pairs={{0,4},{2,6},{4,8},{6,10},{8,12},{10,14},{12,16},{14,18},{16,20},{1... | collective-permute-start | bytes 20 | tf_op jit(solution)/shard_map/ppermute | solution.py:16
  31.5 3.6 collective-permute-start.21
  35.8 4.8 %collective-permute-start.3 = (f32[]{:T(128)}, f32[]{:T(128)}, u32[]{:S(2)}, u32[]{:S(2)}) collective-permute-start(f32[]{:T(128)} %select_n.303), channel_id=1, source_target_pairs={{0,8},{2,10},{4,12},{6,14},{8,16},{10,18},{12,20},{14,22},{16,24},... | collective-permute-start | bytes 20 | tf_op jit(solution)/shard_map/ppermute | solution.py:16
  41.2 3.1 collective-permute-start.22
  47.0 4.3 collective-permute-done.4
  55.4 4.8 %collective-permute-start.5 = (f32[16,128,128]{2,1,0:T(8,128)S(1)}, f32[16,128,128]{2,1,0:T(8,128)S(1)}, u32[]{:S(2)}, u32[]{:S(2)}) collective-permute-start(f32[16,128,128]{2,1,0:T(8,128)S(1)} %fusion.16), channel_id=1, source_target_pairs={{0,2},{2,4},{4,6},{6,8},{8,10},{10,12},{12,14},{14,16},{16,18},{18... | collective-permute-start | bytes 3145736 | tf_op jit(solution)/shard_map/ppermute | solution.py:16
  60.2 19.9 %collective-permute-done.5 = f32[16,128,128]{2,1,0:T(8,128)S(1)} collective-permute-done((f32[16,128,128]{2,1,0:T(8,128)S(1)}, f32[16,128,128]{2,1,0:T(8,128)S(1)}, u32[]{:S(2)}, u32[]{:S(2)}) %collective-permute-start.5) | collective-permute-done | bytes 1048608 | tf_op jit(solution)/shard_map/ppermute | solution.py:16
  80.2 2.3 collective-permute-start.8
  82.5 4.8 %collective-permute-start.6 = (f32[]{:T(128)}, f32[]{:T(128)}, u32[]{:S(2)}, u32[]{:S(2)}) collective-permute-start(f32[]{:T(128)} %bitcast.4), channel_id=1, source_target_pairs={{0,2},{2,4},{4,6},{6,8},{8,10},{10,12},{12,14},{14,16},{16,18},{18... | collective-permute-start | bytes 20 | tf_op jit(solution)/shard_map/ppermute | solution.py:16
  87.4 4.4 collective-permute-start.7
  91.8 10.9 %collective-permute-done.6 = f32[]{:T(128)} collective-permute-done((f32[]{:T(128)}, f32[]{:T(128)}, u32[]{:S(2)}, u32[]{:S(2)}) %collective-permute-start.6) | collective-permute-done | bytes 36 | tf_op jit(solution)/shard_map/ppermute | solution.py:16
  107.3 3.6 collective-permute-start.9
  110.9 12.4 %collective-permute-done.9 = f32[]{:T(128)} collective-permute-done((f32[]{:T(128)}, f32[]{:T(128)}, u32[]{:S(2)}, u32[]{:S(2)}) %collective-permute-start.9) | collective-permute-done | bytes 36 | tf_op jit(solution)/shard_map/ppermute | solution.py:16
  127.2 5.4 %collective-permute-done.10 = f32[16]{0:T(128)S(1)} collective-permute-done((f32[16]{0:T(128)S(1)}, f32[16]{0:T(128)S(1)}, u32[]{:S(2)}, u32[]{:S(2)}) %collective-permute-start.10) | collective-permute-done | bytes 96 | tf_op jit(solution)/shard_map/ppermute | solution.py:16
  135.0 3.1 collective-permute-start.14
  138.2 3.2 collective-permute-start.12
  141.4 6.7 %collective-permute-done.12 = f32[]{:T(128)} collective-permute-done((f32[]{:T(128)}, f32[]{:T(128)}, u32[]{:S(2)}, u32[]{:S(2)}) %collective-permute-start.12) | collective-permute-done | bytes 36 | tf_op jit(solution)/shard_map/ppermute | solution.py:16
  151.9 10.0 %collective-permute-done.13 = f32[16]{0:T(128)S(1)} collective-permute-done((f32[16]{0:T(128)S(1)}, f32[16]{0:T(128)S(1)}, u32[]{:S(2)}, u32[]{:S(2)}) %collective-permute-start.13) | collective-permute-done | bytes 96 | tf_op jit(solution)/shard_map/ppermute | solution.py:16
  161.9 4.0 collective-permute-done.14
  172.9 2.2 convolution_bitcast_fusion.7
  175.1 3.2 collective-permute-start.15
  178.3 19.3 %collective-permute-done.15 = f32[]{:T(128)} collective-permute-done((f32[]{:T(128)}, f32[]{:T(128)}, u32[]{:S(2)}, u32[]{:S(2)}) %collective-permute-start.15) | collective-permute-done | bytes 36 | tf_op jit(solution)/shard_map/ppermute | solution.py:16
  201.4 3.5 collective-permute-done.16
  204.9 3.0 multiply_reduce_fusion.2
  207.9 2.5 psum.23
  211.0 2.5 psum.24
  215.1 2.3 fusion.13
  219.4 25.2 %collective-permute-done.23 = f32[16,128,128]{2,1,0:T(8,128)S(1)} collective-permute-done((f32[16,128,128]{2,1,0:T(8,128)S(1)}, f32[16,128,128]{2,1,0:T(8,128)S(1)}, u32[]{:S(2)}, u32[]{:S(2)}) %collective-permute-start.23) | collective-permute-done | bytes 1048608 | tf_op jit(solution)/shard_map/ppermute | solution.py:16
  245.7 3.8 collective-permute-start.26
  251.5 4.7 %collective-permute-start.25 = (f32[16]{0:T(128)S(1)}, f32[16]{0:T(128)S(1)}, u32[]{:S(2)}, u32[]{:S(2)}) collective-permute-start(f32[16]{0:T(128)S(1)} %divide_exponential_fusion.5), channel_id=1, source_target_pairs={{2,0},{4,2},{6,4},{8,6},{10,8},{12,10},{14,12},{16,14},{18,16},{20... | collective-permute-start | bytes 200 | tf_op jit(solution)/shard_map/ppermute | solution.py:16
  256.2 17.0 %collective-permute-done.24 = f32[]{:T(128)} collective-permute-done((f32[]{:T(128)}, f32[]{:T(128)}, u32[]{:S(2)}, u32[]{:S(2)}) %collective-permute-start.24) | collective-permute-done | bytes 36 | tf_op jit(solution)/shard_map/ppermute | solution.py:16
  274.5 2.4 add_select_fusion.3
  278.8 21.9 %collective-permute-start.27 = (f32[]{:T(128)}, f32[]{:T(128)}, u32[]{:S(2)}, u32[]{:S(2)}) collective-permute-start(f32[]{:T(128)} %select_n.357), channel_id=1, source_target_pairs={{2,0},{4,2},{6,4},{8,6},{10,8},{12,10},{14,12},{16,14},{18,16},{20... | collective-permute-start | bytes 20 | tf_op jit(solution)/shard_map/ppermute | solution.py:16
  302.5 6.0 %collective-permute-start.28 = (f32[16]{0:T(128)S(1)}, f32[16]{0:T(128)S(1)}, u32[]{:S(2)}, u32[]{:S(2)}) collective-permute-start(f32[16]{0:T(128)S(1)} %get-tuple-element.77), channel_id=1, source_target_pairs={{2,0},{4,2},{6,4},{8,6},{10,8},{12,10},{14,12},{16,14},{18,16},{20... | collective-permute-start | bytes 200 | tf_op jit(solution)/shard_map/ppermute | solution.py:16
  314.5 20.0 %collective-permute-start.30 = (f32[]{:T(128)}, f32[]{:T(128)}, u32[]{:S(2)}, u32[]{:S(2)}) collective-permute-start(f32[]{:T(128)} %select_n.364), channel_id=1, source_target_pairs={{4,0},{6,2},{8,4},{10,6},{12,8},{14,10},{16,12},{18,14},{20,16},{2... | collective-permute-start | bytes 20 | tf_op jit(solution)/shard_map/ppermute | solution.py:16
  335.6 3.3 collective-permute-start.33
  343.1 5.3 %collective-permute-start.31 = (f32[16]{0:T(128)S(1)}, f32[16]{0:T(128)S(1)}, u32[]{:S(2)}, u32[]{:S(2)}) collective-permute-start(f32[16]{0:T(128)S(1)} %get-tuple-element.75), channel_id=1, source_target_pairs={{4,0},{6,2},{8,4},{10,6},{12,8},{14,10},{16,12},{18,14},{20,16},{2... | collective-permute-start | bytes 200 | tf_op jit(solution)/shard_map/ppermute | solution.py:16
  350.2 2.4 collective-permute-start.34
  352.6 3.0 collective-permute-done.34
  359.0 2.8 collective-permute-start.35
  363.1 3.4 fusion.10
  368.5 58.5 %psum.25 = f32[2048]{0:T(1024)} all-reduce(f32[2048]{0:T(1024)S(1)} %bitcast.109), channel_id=1, replica_groups=mesh['seq'=16,'head'=2] {'seq'}, use_global_device_ids=true, to_apply=%region_5.6 | all-reduce | flops 2048 | bytes 16384 | tf_op jit(solution)/shard_map/psum | solution.py:231
  431.2 3.3 fusion.8
  436.6 3.1 fusion.9
  (111 shorter events, 61.5 us)
Async XLA Ops:
  0.6 54.0 %copy-start = (bf16[128,2048]{1,0:T(8,128)(2,1)S(1)}, bf16[128,2048]{1,0:T(8,128)(2,1)}, u32[]{:S(2)}) copy-start(bf16[128,2048]{1,0:T(8,128)(2,1)} %param.9) | copy-start | bytes 1572868
  1.9 7.9 %collective-permute-start.18 = (f32[]{:T(128)}, f32[]{:T(128)}, u32[]{:S(2)}, u32[]{:S(2)}) collective-permute-start(f32[]{:T(128)} %bitcast.4), channel_id=1, source_target_pairs={{2,0},{4,2},{6,4},{8,6},{10,8},{12,10},{14,12},{16,14},{18,16},{20... | collective-permute-start | bytes 20 | tf_op jit(solution)/shard_map/ppermute | solution.py:16
  6.2 11.3 %collective-permute-start = (f32[]{:T(128)}, f32[]{:T(128)}, u32[]{:S(2)}, u32[]{:S(2)}) collective-permute-start(f32[]{:T(128)} %bitcast.3), channel_id=1, source_target_pairs={{0,2},{2,4},{4,6},{6,8},{8,10},{10,12},{12,14},{14,16},{16,18},{18... | collective-permute-start | bytes 20 | tf_op jit(solution)/shard_map/ppermute | solution.py:16
  9.8 45.6 %copy-start.4 = (bf16[128,16,128]{0,2,1:T(8,128)(2,1)}, bf16[128,16,128]{0,2,1:T(8,128)(2,1)S(1)}, u32[]{:S(2)}) copy-start(bf16[128,16,128]{0,2,1:T(8,128)(2,1)S(1)} %copy.15) | copy-start | bytes 1572868
  10.5 10.8 %collective-permute-start.19 = (f32[]{:T(128)}, f32[]{:T(128)}, u32[]{:S(2)}, u32[]{:S(2)}) collective-permute-start(f32[]{:T(128)} %select_n.341), channel_id=1, source_target_pairs={{2,0},{4,2},{6,4},{8,6},{10,8},{12,10},{14,12},{16,14},{18,16},{20... | collective-permute-start | bytes 20 | tf_op jit(solution)/shard_map/ppermute | solution.py:16
  18.1 7.5 %collective-permute-start.1 = (f32[]{:T(128)}, f32[]{:T(128)}, u32[]{:S(2)}, u32[]{:S(2)}) collective-permute-start(f32[]{:T(128)} %select_n.299), channel_id=1, source_target_pairs={{0,2},{2,4},{4,6},{6,8},{8,10},{10,12},{12,14},{14,16},{16,18},{18... | collective-permute-start | bytes 20 | tf_op jit(solution)/shard_map/ppermute | solution.py:16
  21.9 9.1 %collective-permute-start.20 = (f32[]{:T(128)}, f32[]{:T(128)}, u32[]{:S(2)}, u32[]{:S(2)}) collective-permute-start(f32[]{:T(128)} %select_n.343), channel_id=1, source_target_pairs={{4,0},{6,2},{8,4},{10,6},{12,8},{14,10},{16,12},{18,14},{20,16},{2... | collective-permute-start | bytes 20 | tf_op jit(solution)/shard_map/ppermute | solution.py:16
  26.3 8.9 %collective-permute-start.2 = (f32[]{:T(128)}, f32[]{:T(128)}, u32[]{:S(2)}, u32[]{:S(2)}) collective-permute-start(f32[]{:T(128)} %select_n.301), channel_id=1, source_target_pairs={{0,4},{2,6},{4,8},{6,10},{8,12},{10,14},{12,16},{14,18},{16,20},{1... | collective-permute-start | bytes 20 | tf_op jit(solution)/shard_map/ppermute | solution.py:16
  31.5 9.1 %collective-permute-start.21 = (f32[]{:T(128)}, f32[]{:T(128)}, u32[]{:S(2)}, u32[]{:S(2)}) collective-permute-start(f32[]{:T(128)} %select_n.345), channel_id=1, source_target_pairs={{8,0},{10,2},{12,4},{14,6},{16,8},{18,10},{20,12},{22,14},{24,16},... | collective-permute-start | bytes 20 | tf_op jit(solution)/shard_map/ppermute | solution.py:16
  35.8 8.6 %collective-permute-start.3 = (f32[]{:T(128)}, f32[]{:T(128)}, u32[]{:S(2)}, u32[]{:S(2)}) collective-permute-start(f32[]{:T(128)} %select_n.303), channel_id=1, source_target_pairs={{0,8},{2,10},{4,12},{6,14},{8,16},{10,18},{12,20},{14,22},{16,24},... | collective-permute-start | bytes 20 | tf_op jit(solution)/shard_map/ppermute | solution.py:16
  41.2 5.0 %collective-permute-start.22 = (f32[]{:T(128)}, f32[]{:T(128)}, u32[]{:S(2)}, u32[]{:S(2)}) collective-permute-start(f32[]{:T(128)} %select_n.347), channel_id=1, source_target_pairs={{16,0},{18,2},{20,4},{22,6},{24,8},{26,10},{28,12},{30,14},{17,1},... | collective-permute-start | bytes 20 | tf_op jit(solution)/shard_map/ppermute | solution.py:16
  45.0 6.3 %collective-permute-start.4 = (f32[]{:T(128)}, f32[]{:T(128)}, u32[]{:S(2)}, u32[]{:S(2)}) collective-permute-start(f32[]{:T(128)} %select_n.305), channel_id=1, source_target_pairs={{0,16},{2,18},{4,20},{6,22},{8,24},{10,26},{12,28},{14,30},{1,17},... | collective-permute-start | bytes 20 | tf_op jit(solution)/shard_map/ppermute | solution.py:16
  55.4 24.8 %collective-permute-start.5 = (f32[16,128,128]{2,1,0:T(8,128)S(1)}, f32[16,128,128]{2,1,0:T(8,128)S(1)}, u32[]{:S(2)}, u32[]{:S(2)}) collective-permute-start(f32[16,128,128]{2,1,0:T(8,128)S(1)} %fusion.16), channel_id=1, source_target_pairs={{0,2},{2,4},{4,6},{6,8},{8,10},{10,12},{12,14},{14,16},{16,18},{18... | collective-permute-start | bytes 3145736 | tf_op jit(solution)/shard_map/ppermute | solution.py:16
  80.2 23.7 %collective-permute-start.8 = (f32[16,128,128]{2,1,0:T(8,128)S(1)}, f32[16,128,128]{2,1,0:T(8,128)}, u32[]{:S(2)}, u32[]{:S(2)}) collective-permute-start(f32[16,128,128]{2,1,0:T(8,128)S(1)} %broadcast_select_fusion.1), channel_id=1, source_target_pairs={{0,2},{2,4},{4,6},{6,8},{8,10},{10,12},{12,14},{14,16},{16,18},{18... | collective-permute-start | bytes 3145736 | tf_op jit(solution)/shard_map/ppermute | solution.py:16
  82.5 20.1 %collective-permute-start.6 = (f32[]{:T(128)}, f32[]{:T(128)}, u32[]{:S(2)}, u32[]{:S(2)}) collective-permute-start(f32[]{:T(128)} %bitcast.4), channel_id=1, source_target_pairs={{0,2},{2,4},{4,6},{6,8},{8,10},{10,12},{12,14},{14,16},{16,18},{18... | collective-permute-start | bytes 20 | tf_op jit(solution)/shard_map/ppermute | solution.py:16
  87.4 16.6 %collective-permute-start.7 = (f32[16]{0:T(128)S(1)}, f32[16]{0:T(128)S(1)}, u32[]{:S(2)}, u32[]{:S(2)}) collective-permute-start(f32[16]{0:T(128)S(1)} %divide_exponential_fusion.5), channel_id=1, source_target_pairs={{0,2},{2,4},{4,6},{6,8},{8,10},{10,12},{12,14},{14,16},{16,18},{18... | collective-permute-start | bytes 200 | tf_op jit(solution)/shard_map/ppermute | solution.py:16
  105.4 27.2 %collective-permute-start.11 = (f32[16,128,128]{2,1,0:T(8,128)S(1)}, f32[16,128,128]{2,1,0:T(8,128)S(1)}, u32[]{:S(2)}, u32[]{:S(2)}) collective-permute-start(f32[16,128,128]{2,1,0:T(8,128)S(1)} %add_select_fusion.7), channel_id=1, source_target_pairs={{0,4},{2,6},{4,8},{6,10},{8,12},{10,14},{12,16},{14,18},{16,20},{1... | collective-permute-start | bytes 3145736 | tf_op jit(solution)/shard_map/ppermute | solution.py:16
  107.3 16.0 %collective-permute-start.9 = (f32[]{:T(128)}, f32[]{:T(128)}, u32[]{:S(2)}, u32[]{:S(2)}) collective-permute-start(f32[]{:T(128)} %select_n.315), channel_id=1, source_target_pairs={{0,2},{2,4},{4,6},{6,8},{8,10},{10,12},{12,14},{14,16},{16,18},{18... | collective-permute-start | bytes 20 | tf_op jit(solution)/shard_map/ppermute | solution.py:16
  125.3 7.3 %collective-permute-start.10 = (f32[16]{0:T(128)S(1)}, f32[16]{0:T(128)S(1)}, u32[]{:S(2)}, u32[]{:S(2)}) collective-permute-start(f32[16]{0:T(128)S(1)} %get-tuple-element.97), channel_id=1, source_target_pairs={{0,2},{2,4},{4,6},{6,8},{8,10},{10,12},{12,14},{14,16},{16,18},{18... | collective-permute-start | bytes 200 | tf_op jit(solution)/shard_map/ppermute | solution.py:16
  135.0 30.9 %copy-start.10 = (f32[16,128,128]{2,1,0:T(8,128)}, f32[16,128,128]{2,1,0:T(8,128)S(1)}, u32[]{:S(2)}) copy-start(f32[16,128,128]{2,1,0:T(8,128)S(1)} %add_select_fusion.6) | copy-start | bytes 3145732
  135.0 30.9 %collective-permute-start.14 = (f32[16,128,128]{2,1,0:T(8,128)S(1)}, f32[16,128,128]{2,1,0:T(8,128)S(1)}, u32[]{:S(2)}, u32[]{:S(2)}) collective-permute-start(f32[16,128,128]{2,1,0:T(8,128)S(1)} %add_select_fusion.6), channel_id=1, source_target_pairs={{0,8},{2,10},{4,12},{6,14},{8,16},{10,18},{12,20},{14,22},{16,24},... | collective-permute-start | bytes 3145736 | tf_op jit(solution)/shard_map/ppermute | solution.py:16
  138.2 9.9 %collective-permute-start.12 = (f32[]{:T(128)}, f32[]{:T(128)}, u32[]{:S(2)}, u32[]{:S(2)}) collective-permute-start(f32[]{:T(128)} %select_n.322), channel_id=1, source_target_pairs={{0,4},{2,6},{4,8},{6,10},{8,12},{10,14},{12,16},{14,18},{16,20},{1... | collective-permute-start | bytes 20 | tf_op jit(solution)/shard_map/ppermute | solution.py:16
  150.0 11.9 %collective-permute-start.13 = (f32[16]{0:T(128)S(1)}, f32[16]{0:T(128)S(1)}, u32[]{:S(2)}, u32[]{:S(2)}) collective-permute-start(f32[16]{0:T(128)S(1)} %get-tuple-element.95), channel_id=1, source_target_pairs={{0,4},{2,6},{4,8},{6,10},{8,12},{10,14},{12,16},{14,18},{16,20},{1... | collective-permute-start | bytes 200 | tf_op jit(solution)/shard_map/ppermute | solution.py:16
  167.3 3.9 copy-start.2
  167.3 37.6 %collective-permute-start.17 = (f32[16,128,128]{2,1,0:T(8,128)S(1)}, f32[16,128,128]{2,1,0:T(8,128)}, u32[]{:S(2)}, u32[]{:S(2)}) collective-permute-start(f32[16,128,128]{2,1,0:T(8,128)S(1)} %add_select_fusion.5), channel_id=1, source_target_pairs={{0,16},{2,18},{4,20},{6,22},{8,24},{10,26},{12,28},{14,30},{1,17},... | collective-permute-start | bytes 3145736 | tf_op jit(solution)/shard_map/ppermute | solution.py:16
  172.9 2.2 copy-start.7
  175.1 22.5 %collective-permute-start.15 = (f32[]{:T(128)}, f32[]{:T(128)}, u32[]{:S(2)}, u32[]{:S(2)}) collective-permute-start(f32[]{:T(128)} %select_n.328), channel_id=1, source_target_pairs={{0,8},{2,10},{4,12},{6,14},{8,16},{10,18},{12,20},{14,22},{16,24},... | collective-permute-start | bytes 20 | tf_op jit(solution)/shard_map/ppermute | solution.py:16
  199.5 5.4 %collective-permute-start.16 = (f32[16]{0:T(128)S(1)}, f32[16]{0:T(128)S(1)}, u32[]{:S(2)}, u32[]{:S(2)}) collective-permute-start(f32[16]{0:T(128)S(1)} %get-tuple-element.93), channel_id=1, source_target_pairs={{0,8},{2,10},{4,12},{6,14},{8,16},{10,18},{12,20},{14,22},{16,24},... | collective-permute-start | bytes 200 | tf_op jit(solution)/shard_map/ppermute | solution.py:16
  207.9 3.1 copy-start.1
  207.9 2.5 copy-start.15
  217.3 27.3 %collective-permute-start.23 = (f32[16,128,128]{2,1,0:T(8,128)S(1)}, f32[16,128,128]{2,1,0:T(8,128)S(1)}, u32[]{:S(2)}, u32[]{:S(2)}) collective-permute-start(f32[16,128,128]{2,1,0:T(8,128)S(1)} %fusion.13), channel_id=1, source_target_pairs={{2,0},{4,2},{6,4},{8,6},{10,8},{12,10},{14,12},{16,14},{18,16},{20... | collective-permute-start | bytes 3145736 | tf_op jit(solution)/shard_map/ppermute | solution.py:16
  245.7 28.8 %collective-permute-start.26 = (f32[16,128,128]{2,1,0:T(8,128)}, f32[16,128,128]{2,1,0:T(8,128)}, u32[]{:S(2)}, u32[]{:S(2)}) collective-permute-start(f32[16,128,128]{2,1,0:T(8,128)} %broadcast_select_fusion), channel_id=1, source_target_pairs={{2,0},{4,2},{6,4},{8,6},{10,8},{12,10},{14,12},{16,14},{18,16},{20... | collective-permute-start | bytes 3145736 | tf_op jit(solution)/shard_map/ppermute | solution.py:16
  249.5 23.7 %collective-permute-start.24 = (f32[]{:T(128)}, f32[]{:T(128)}, u32[]{:S(2)}, u32[]{:S(2)}) collective-permute-start(f32[]{:T(128)} %bitcast.3), channel_id=1, source_target_pairs={{2,0},{4,2},{6,4},{8,6},{10,8},{12,10},{14,12},{16,14},{18,16},{20... | collective-permute-start | bytes 20 | tf_op jit(solution)/shard_map/ppermute | solution.py:16
  251.5 23.0 %collective-permute-start.25 = (f32[16]{0:T(128)S(1)}, f32[16]{0:T(128)S(1)}, u32[]{:S(2)}, u32[]{:S(2)}) collective-permute-start(f32[16]{0:T(128)S(1)} %divide_exponential_fusion.5), channel_id=1, source_target_pairs={{2,0},{4,2},{6,4},{8,6},{10,8},{12,10},{14,12},{16,14},{18,16},{20... | collective-permute-start | bytes 200 | tf_op jit(solution)/shard_map/ppermute | solution.py:16
  276.9 32.9 %collective-permute-start.29 = (f32[16,128,128]{2,1,0:T(8,128)}, f32[16,128,128]{2,1,0:T(8,128)S(1)}, u32[]{:S(2)}, u32[]{:S(2)}) collective-permute-start(f32[16,128,128]{2,1,0:T(8,128)} %add_select_fusion.3), channel_id=1, source_target_pairs={{4,0},{6,2},{8,4},{10,6},{12,8},{14,10},{16,12},{18,14},{20,16},{2... | collective-permute-start | bytes 3145736 | tf_op jit(solution)/shard_map/ppermute | solution.py:16
  278.8 21.9 %collective-permute-start.27 = (f32[]{:T(128)}, f32[]{:T(128)}, u32[]{:S(2)}, u32[]{:S(2)}) collective-permute-start(f32[]{:T(128)} %select_n.357), channel_id=1, source_target_pairs={{2,0},{4,2},{6,4},{8,6},{10,8},{12,10},{14,12},{16,14},{18,16},{20... | collective-permute-start | bytes 20 | tf_op jit(solution)/shard_map/ppermute | solution.py:16
  302.5 7.3 %collective-permute-start.28 = (f32[16]{0:T(128)S(1)}, f32[16]{0:T(128)S(1)}, u32[]{:S(2)}, u32[]{:S(2)}) collective-permute-start(f32[16]{0:T(128)S(1)} %get-tuple-element.77), channel_id=1, source_target_pairs={{2,0},{4,2},{6,4},{8,6},{10,8},{12,10},{14,12},{16,14},{18,16},{20... | collective-permute-start | bytes 200 | tf_op jit(solution)/shard_map/ppermute | solution.py:16
  312.5 44.3 %copy-start.9 = (f32[16,128,128]{2,1,0:T(8,128)}, f32[16,128,128]{2,1,0:T(8,128)S(1)}, u32[]{:S(2)}) copy-start(f32[16,128,128]{2,1,0:T(8,128)S(1)} %add_select_fusion.2) | copy-start | bytes 3145732
  312.5 44.3 %collective-permute-start.32 = (f32[16,128,128]{2,1,0:T(8,128)S(1)}, f32[16,128,128]{2,1,0:T(8,128)}, u32[]{:S(2)}, u32[]{:S(2)}) collective-permute-start(f32[16,128,128]{2,1,0:T(8,128)S(1)} %add_select_fusion.2), channel_id=1, source_target_pairs={{8,0},{10,2},{12,4},{14,6},{16,8},{18,10},{20,12},{22,14},{24,16},... | collective-permute-start | bytes 3145736 | tf_op jit(solution)/shard_map/ppermute | solution.py:16
  314.5 20.0 %collective-permute-start.30 = (f32[]{:T(128)}, f32[]{:T(128)}, u32[]{:S(2)}, u32[]{:S(2)}) collective-permute-start(f32[]{:T(128)} %select_n.364), channel_id=1, source_target_pairs={{4,0},{6,2},{8,4},{10,6},{12,8},{14,10},{16,12},{18,14},{20,16},{2... | collective-permute-start | bytes 20 | tf_op jit(solution)/shard_map/ppermute | solution.py:16
  335.6 5.5 %collective-permute-start.33 = (f32[]{:T(128)}, f32[]{:T(128)}, u32[]{:S(2)}, u32[]{:S(2)}) collective-permute-start(f32[]{:T(128)} %select_n.370), channel_id=1, source_target_pairs={{8,0},{10,2},{12,4},{14,6},{16,8},{18,10},{20,12},{22,14},{24,16},... | collective-permute-start | bytes 20 | tf_op jit(solution)/shard_map/ppermute | solution.py:16
  343.1 7.1 %collective-permute-start.31 = (f32[16]{0:T(128)S(1)}, f32[16]{0:T(128)S(1)}, u32[]{:S(2)}, u32[]{:S(2)}) collective-permute-start(f32[16]{0:T(128)S(1)} %get-tuple-element.75), channel_id=1, source_target_pairs={{4,0},{6,2},{8,4},{10,6},{12,8},{14,10},{16,12},{18,14},{20,16},{2... | collective-permute-start | bytes 200 | tf_op jit(solution)/shard_map/ppermute | solution.py:16
  350.2 5.4 %collective-permute-start.34 = (f32[16]{0:T(128)S(1)}, f32[16]{0:T(128)S(1)}, u32[]{:S(2)}, u32[]{:S(2)}) collective-permute-start(f32[16]{0:T(128)S(1)} %get-tuple-element.73), channel_id=1, source_target_pairs={{8,0},{10,2},{12,4},{14,6},{16,8},{18,10},{20,12},{22,14},{24,16},... | collective-permute-start | bytes 200 | tf_op jit(solution)/shard_map/ppermute | solution.py:16
  356.8 5.0 %copy-start.11 = (f32[16,128,128]{2,1,0:T(8,128)}, f32[16,128,128]{2,1,0:T(8,128)S(1)}, u32[]{:S(2)}) copy-start(f32[16,128,128]{2,1,0:T(8,128)S(1)} %convolution_multiply_fusion) | copy-start | bytes 3145732
  356.9 5.0 %copy-start.5 = (bf16[128,16,128]{0,2,1:T(8,128)(2,1)S(1)}, bf16[128,16,128]{0,2,1:T(8,128)(2,1)}, u32[]{:S(2)}) copy-start(bf16[128,16,128]{0,2,1:T(8,128)(2,1)} %copy-done.4) | copy-start | bytes 1572868
  359.0 4.1 copy-start.3
  359.0 72.2 %collective-permute-start.35 = (f32[16,128,128]{2,1,0:T(8,128)S(1)}, f32[16,128,128]{2,1,0:T(8,128)}, u32[]{:S(2)}, u32[]{:S(2)}) collective-permute-start(f32[16,128,128]{2,1,0:T(8,128)S(1)} %add_select_fusion.1), channel_id=1, source_target_pairs={{16,0},{18,2},{20,4},{22,6},{24,8},{26,10},{28,12},{30,14},{17,1},... | collective-permute-start | bytes 3145736 | tf_op jit(solution)/shard_map/ppermute | solution.py:16
  431.2 5.4 %copy-start.12 = (bf16[128,2048]{1,0:T(8,128)(2,1)S(1)}, bf16[128,2048]{1,0:T(8,128)(2,1)}, u32[]{:S(2)}) copy-start(bf16[128,2048]{1,0:T(8,128)(2,1)} %param.8) | copy-start | bytes 1572868
  (6 other events, 7.4 us)
where the time goes:
time: 444 us; the launch traced here: 442 us
  starting transfers between devices  154 us (35%)
  waiting for transfers between devices  146 us (33%)
  blocking collectives  63.4 us (14%)
  matrix products  26 us (6%)
  between operations  21.5 us (5%)
  other arithmetic  16.2 us (4%)
  local copies, waits for them, and re-layouts  14.3 us (3%)
    ppermute x36, starting transfers between devices, shifted(): return lax.ppermute(array, axis, pairs)  154 us
    ppermute x36, waiting for transfers between devices, shifted(): return lax.ppermute(array, axis, pairs)  146 us
    psum x1, blocking collectives, local(): gain_grad = lax.psum(gain_local, 'seq')  58.5 us
    select_n x8, other arithmetic, select_tree(): jnp.where(condition, left_leaf, right_leaf)  11.7 us
    unnamed x40, local copies, waits for them, and re-layouts  10.7 us
  transfers between devices with their start and end apart: 36, of which 16 were waited for; matrix products, arithmetic and copies ran while one was open for 5% of the time, Pallas kernels for 0%

commit v1 on v0

v1 whole, which is shorter than its diff:
```python
import jax
import jax.numpy as jnp
from jax import lax
from jax.experimental import pallas as pl
from jax.experimental.pallas import tpu as pltpu
from jax.sharding import PartitionSpec as P

GROUP = 4
INFO = 8
FAR = 1e9
f32 = jnp.float32
bf16 = jnp.bfloat16


def dot(a, b, over_a=1, over_b=0):
    return lax.dot_general(a, b, (((over_a,), (over_b,)), ((), ())), preferred_element_type=f32)


def halves(x):
    high = x.astype(bf16)
    return high, (x - high.astype(f32)).astype(bf16)


def decay(steps, span):
    return jnp.exp(-steps / span)


class Sizes:
    def __init__(self, queries, decay_span):
        self.rows = queries.shape[0]
        self.heads = decay_span.shape[0]
        self.dim = queries.shape[1] // self.heads
        self.per = self.heads // GROUP
        self.wide = self.per * self.dim
        self.state = self.per * self.dim
        self.pad = -(-self.per // 8) * 8


def markers(seg_ref, size):
    row = seg_ref[...].astype(f32) + 1.0
    return row, jnp.broadcast_to(row, (size.dim, size.rows)).T


def position(size):
    return lax.broadcasted_iota(jnp.int32, (size.rows, size.dim), 0).astype(f32)


def pair_weight(row, size):
    shape = (size.rows, size.rows)
    here = jnp.broadcast_to(row, shape)
    at = lax.broadcasted_iota(jnp.int32, shape, 0)
    by = lax.broadcasted_iota(jnp.int32, shape, 1)
    live = jnp.logical_and(at >= by, here == here.T)
    return jnp.maximum(at - by, 0).astype(f32), live


def info_rows(first_row, second_row, dim):
    index = lax.broadcasted_iota(jnp.int32, (INFO, dim), 0)
    return jnp.where(index == 0, first_row, jnp.where(index == 1, second_row, 0.0))


def span_at(spans, group, size, h):
    return jnp.full((1, size.dim), spans[group * size.per + h], f32)


def call(body, size, name, groups, spans, seg, inputs, outputs, flops, moved):
    def spec(array, chunk):
        if chunk is None:
            return pl.BlockSpec(array.shape, lambda i, g: (0,) * len(array.shape))
        return pl.BlockSpec((array.shape[0], size.wide), lambda i, g: (0, g[chunk]))

    def whole(shape):
        return pl.BlockSpec(shape, lambda i, g: (0,) * len(shape))

    in_specs = [pl.BlockSpec(memory_space=pltpu.SMEM), whole(seg.shape)]
    in_specs += [spec(array, chunk) for array, chunk in inputs]
    return pl.pallas_call(
        body,
        grid_spec=pltpu.PrefetchScalarGridSpec(
            num_scalar_prefetch=1,
            grid=(1,),
            in_specs=in_specs,
            out_specs=[whole(o.shape) for o in outputs],
        ),
        out_shape=outputs,
        compiler_params=pltpu.CompilerParams(vmem_limit_bytes=40 * 1024 * 1024),
        cost_estimate=pl.CostEstimate(flops=flops, bytes_accessed=moved, transcendentals=0),
        name=name,
    )(groups, spans, seg, *[array for array, _ in inputs])


def key_value_states(size, chunks, groups, spans, seg, key_rows, value_rows):
    n = len(chunks)

    def body(g_ref, spans, seg_ref, *refs):
        ins, outs = refs[: 2 * n], refs[2 * n :]
        row, mark = markers(seg_ref, size)
        last, first = mark[size.rows - 1 :, :], mark[:1, :]
        ahead = (size.rows - 1.0) - position(size)
        for c, chunk in enumerate(chunks):
            for h in range(size.per):
                cols = slice(h * size.dim, (h + 1) * size.dim)
                span = span_at(spans, g_ref[chunk], size, h)
                weight = jnp.where(mark == last, decay(ahead, span), 0.0)
                key = ins[2 * c][:, cols]
                high, low = halves(ins[2 * c + 1][:, cols].astype(f32) * weight)
                outs[c][cols, :] = dot(
                    jnp.concatenate([key, key], 0), jnp.concatenate([high, low], 0), 0, 0
                )
            outs[c][size.state :, :] = info_rows(last, first, size.dim)

    inputs = []
    for chunk in chunks:
        inputs += [(key_rows, chunk), (value_rows, chunk)]
    shape = jax.ShapeDtypeStruct((size.state + INFO, size.dim), f32)
    cost = n * size.per * 4 * size.rows * size.dim * size.dim
    return call(
        body, size, "states", groups, spans, seg, inputs, [shape] * n, cost, n * size.wide * 1024
    )


def local_attended(size, chunks, groups, spans, seg, queries, key_rows, value_rows):
    n = len(chunks)

    def body(g_ref, spans, seg_ref, *refs):
        ins, outs = refs[: 3 * n], refs[3 * n :]
        row, _ = markers(seg_ref, size)
        gap, live = pair_weight(row, size)
        for c, chunk in enumerate(chunks):
            for h in range(size.per):
                cols = slice(h * size.dim, (h + 1) * size.dim)
                span = spans[g_ref[chunk] * size.per + h]
                weight = jnp.where(live, decay(gap, jnp.full((1, size.rows), span, f32)), 0.0)
                query, key, value = (ins[3 * c + i][:, cols] for i in range(3))
                high, low = halves(dot(query, key, 1, 1) * weight)
                outs[c][:, cols] = dot(
                    jnp.concatenate([high, low], 1), jnp.concatenate([value, value], 0)
                )

    inputs = []
    for chunk in chunks:
        inputs += [(queries, chunk), (key_rows, chunk), (value_rows, chunk)]
    shape = jax.ShapeDtypeStruct((size.rows, size.wide), f32)
    cost = n * size.per * 6 * size.rows * size.dim * size.dim
    return call(
        body, size, "local", groups, spans, seg, inputs, [shape] * n, cost, n * size.wide * 1024
    )


def places(g_ref, backward):
    if backward:
        return [GROUP - 1 - g_ref[k] for k in range(GROUP)]
    return [g_ref[k] for k in range(GROUP)]


def group_total(size, backward, groups, spans, seg, parts):
    mark_row = size.state + (1 if backward else 0)

    def body(g_ref, spans, seg_ref, *refs):
        ins, out = refs[:GROUP], refs[GROUP]
        place = places(g_ref, backward)
        marks = [ref[mark_row : mark_row + 1, :] for ref in ins]
        end = marks[0]
        for mark in marks[1:]:
            end = jnp.minimum(end, mark) if backward else jnp.maximum(end, mark)
        for h in range(size.per):
            cols = slice(h * size.dim, (h + 1) * size.dim)
            span = span_at(spans, g_ref[0], size, h)
            total = None
            for k in range(GROUP):
                steps = ((GROUP - 1 - place[k]) * size.rows).astype(f32)
                factor = jnp.where(marks[k] == end, decay(steps, span), 0.0)
                term = factor * ins[k][cols, :]
                total = term if total is None else total + term
            out[cols, :] = total
        out[size.state :, :] = info_rows(end, end, size.dim)

    shape = jax.ShapeDtypeStruct((size.state + INFO, size.dim), f32)
    return call(
        body, size, "total", groups, spans, seg, [(p, None) for p in parts], [shape],
        size.state * size.dim * 8, size.state * size.dim * 20,
    )[0]


def group_prefixes(size, backward, groups, spans, seg, parts, entering, riders=()):
    mark_row = size.state + (1 if backward else 0)
    extra = sum(r.shape[0] for r in riders)

    def body(g_ref, spans, seg_ref, *refs):
        ins, enter = refs[:GROUP], refs[GROUP]
        rides, outs = refs[GROUP + 1 : GROUP + 1 + len(riders)], refs[GROUP + 1 + len(riders) :]
        place = places(g_ref, backward)
        marks = [ref[mark_row : mark_row + 1, :] for ref in ins]
        outer = enter[size.state : size.state + 1, :]
        if backward:
            outer = jnp.where(outer == 0.0, FAR, outer)
        carry = []
        for to in range(GROUP):
            now = outer
            for k in range(GROUP):
                if backward:
                    now = jnp.where(place[k] < place[to], jnp.minimum(now, marks[k]), now)
                else:
                    now = jnp.where(place[k] < place[to], jnp.maximum(now, marks[k]), now)
            carry.append(now)
            outs[to][size.state : size.state + INFO, :] = info_rows(now, now, size.dim)
            at = size.state + INFO
            for ride in rides:
                outs[to][at : at + ride.shape[0], :] = ride[...]
                at += ride.shape[0]
        for h in range(size.per):
            cols = slice(h * size.dim, (h + 1) * size.dim)
            span = span_at(spans, g_ref[0], size, h)
            for to in range(GROUP):
                steps = (place[to] * size.rows).astype(f32)
                total = jnp.where(outer == carry[to], decay(steps, span), 0.0) * enter[cols, :]
                for k in range(GROUP):
                    gap = place[to] - 1 - place[k]
                    steps = (jnp.maximum(gap, 0) * size.rows).astype(f32)
                    live = jnp.logical_and(marks[k] == carry[to], gap >= 0)
                    total += jnp.where(live, decay(steps, span), 0.0) * ins[k][cols, :]
                outs[to][cols, :] = total

    shape = jax.ShapeDtypeStruct((size.state + INFO + extra, size.dim), f32)
    inputs = [(p, None) for p in parts] + [(entering, None)] + [(r, None) for r in riders]
    return call(
        body, size, "prefixes", groups, spans, seg, inputs, [shape] * GROUP,
        size.state * size.dim * 40, size.state * size.dim * 36,
    )


def whole_attended(size, groups, spans, seg, queries, out_grad, gain, local, entering):
    chunks = range(GROUP)

    def body(g_ref, spans, seg_ref, *refs):
        ins, outs = refs[: 5 * GROUP], refs[5 * GROUP :]
        _, mark = markers(seg_ref, size)
        behind = position(size) + 1.0
        square = jnp.zeros((size.rows, size.dim), f32)
        cross = jnp.zeros((size.rows, size.dim), f32)
        for c, chunk in enumerate(chunks):
            query_ref, grad_ref, gain_ref, local_ref, state_ref = ins[5 * c : 5 * c + 5]
            live = mark == state_ref[size.state : size.state + 1, :]
            for h in range(size.per):
                cols = slice(h * size.dim, (h + 1) * size.dim)
                span = span_at(spans, g_ref[chunk], size, h)
                weight = jnp.where(live, decay(behind, span), 0.0)
                query = query_ref[:, cols]
                high, low = halves(state_ref[cols, :])
                inter = dot(jnp.concatenate([query, query], 1), jnp.concatenate([high, low], 0))
                out = local_ref[:, cols] + weight * inter
                outs[c][:, cols] = out
                square += out * out
                cross += grad_ref[:, cols].astype(f32) * gain_ref[:, cols] * out
        square = jnp.sum(square.T, axis=0, keepdims=True)
        cross = jnp.sum(cross.T, axis=0, keepdims=True)
        index = lax.broadcasted_iota(jnp.int32, (8, size.rows), 0)
        outs[GROUP][...] = jnp.where(index == 0, square, jnp.where(index == 1, cross, 0.0))

    inputs = []
    for c in chunks:
        inputs += [(queries, c), (out_grad, c), (gain, c), (local[c], None), (entering[c], None)]
    shapes = [jax.ShapeDtypeStruct((size.rows, size.wide), f32)] * GROUP
    shapes.append(jax.ShapeDtypeStruct((8, size.rows), f32))
    return call(
        body, size, "attended", groups, spans, seg, inputs, shapes,
        size.heads * 4 * size.rows * size.dim * size.dim, size.heads * size.dim * size.rows * 16,
    )


def output_grad_states(size, chunks, features, groups, spans, seg, queries, out_grad, gain, attended, sums, before=()):
    n = len(chunks)

    def body(g_ref, spans, seg_ref, *refs):
        sums_ref, ins = refs[0], refs[1 : 1 + 4 * n]
        earlier = refs[1 + 4 * n : 1 + 4 * n + len(before)]
        outs = refs[1 + 4 * n + len(before) :]
        row, mark = markers(seg_ref, size)
        last, first = mark[size.rows - 1 :, :], mark[:1, :]
        wide = (size.dim, size.rows)
        square = jnp.broadcast_to(sums_ref[0:1, :], wide).T
        cross = jnp.broadcast_to(sums_ref[1:2, :], wide).T
        inv = lax.rsqrt(square / features + 1e-06)
        pull = inv * inv * inv * cross / features
        gone = position(size)
        for c, chunk in enumerate(chunks):
            query_ref, grad_ref, gain_ref, att_ref = ins[4 * c : 4 * c + 4]
            back_ref, state_ref = outs[2 * c : 2 * c + 2]
            rows = []
            for h in range(size.per):
                cols = slice(h * size.dim, (h + 1) * size.dim)
                span = span_at(spans, g_ref[chunk], size, h)
                weight = jnp.where(mark == first, decay(gone, span), 0.0)
                grad = grad_ref[:, cols].astype(f32) * inv
                att = att_ref[:, cols]
                back = gain_ref[:, cols] * grad - att * pull
                back_ref[:, cols] = back
                rows.append(jnp.sum(grad * att, axis=0, keepdims=True))
                query = query_ref[:, cols]
                high, low = halves(back * weight)
                state_ref[cols, :] = dot(
                    jnp.concatenate([query, query], 0), jnp.concatenate([high, low], 0), 0, 0
                )
            state_ref[size.state :, :] = info_rows(last, first, size.dim)
            index = lax.broadcasted_iota(jnp.int32, (size.pad, size.dim), 0)
            gains = jnp.zeros((size.pad, size.dim), f32)
            for h, row in enumerate(rows):
                gains = jnp.where(index == h, row, gains)
            at = chunk * size.pad if before else c * size.pad
            outs[2 * n][at : at + size.pad, :] = gains
        for ref, (k, _) in zip(earlier, before):
            outs[2 * n][k * size.pad : (k + 1) * size.pad, :] = ref[...]

    inputs = [(sums, None)]
    for chunk in chunks:
        inputs += [(queries, chunk), (out_grad, chunk), (gain, chunk), (attended[chunk], None)]
    inputs += [(rows, None) for _, rows in before]
    shapes = []
    for _ in chunks:
        shapes.append(jax.ShapeDtypeStruct((size.rows, size.wide), f32))
        shapes.append(jax.ShapeDtypeStruct((size.state + INFO, size.dim), f32))
    held = GROUP if before else n
    shapes.append(jax.ShapeDtypeStruct((held * size.pad, size.dim), f32))
    outs = call(
        body, size, "back", groups, spans, seg, inputs, shapes,
        n * size.per * 4 * size.rows * size.dim * size.dim, n * size.wide * size.rows * 16,
    )
    return outs[0 : 2 * n : 2], outs[1 : 2 * n : 2], outs[2 * n]


def local_gradients(size, groups, spans, seg, queries, key_rows, value_rows, back, entering):
    def body(g_ref, spans, seg_ref, *refs):
        ins, outs = refs[: 5 * GROUP], refs[5 * GROUP :]
        row, mark = markers(seg_ref, size)
        gap, pairs = pair_weight(row, size)
        behind = position(size) + 1.0
        for c in range(GROUP):
            query_ref, key_ref, value_ref, back_ref, state_ref = ins[5 * c : 5 * c + 5]
            live = mark == state_ref[size.state : size.state + 1, :]
            for h in range(size.per):
                cols = slice(h * size.dim, (h + 1) * size.dim)
                span = spans[g_ref[c] * size.per + h]
                weight = jnp.where(pairs, decay(gap, jnp.full((1, size.rows), span, f32)), 0.0)
                query, key, value = query_ref[:, cols], key_ref[:, cols], value_ref[:, cols]
                high, low = halves(back_ref[:, cols])
                grads = dot(
                    jnp.concatenate([high, low], 1), jnp.concatenate([value, value], 1), 1, 1
                )
                grads_high, grads_low = halves(grads * weight)
                part = dot(
                    jnp.concatenate([grads_high, grads_low], 1), jnp.concatenate([key, key], 0)
                )
                state_high, state_low = halves(state_ref[cols, :])
                inter = dot(
                    jnp.concatenate([high, high, low], 1),
                    jnp.concatenate([state_high, state_low, state_high], 1),
                    1, 1,
                )
                into = jnp.where(live, decay(behind, jnp.full((1, size.dim), span, f32)), 0.0)
                start = pl.multiple_of(g_ref[c] * size.wide + h * size.dim, size.dim)
                outs[0][:, pl.ds(start, size.dim)] = (part + into * inter).astype(bf16)
                outs[1 + 2 * c][:, cols] = dot(
                    jnp.concatenate([grads_high, grads_low], 0),
                    jnp.concatenate([query, query], 0),
                    0, 0,
                )
                score_high, score_low = halves(dot(query, key, 1, 1) * weight)
                outs[2 + 2 * c][:, cols] = dot(
                    jnp.concatenate([score_high, score_high, score_low], 0),
                    jnp.concatenate([high, low, high], 0),
                    0, 0,
                )

    inputs = []
    for c in range(GROUP):
        inputs += [(queries, c), (key_rows, c), (value_rows, c), (back[c], None), (entering[c], None)]
    shapes = [jax.ShapeDtypeStruct((size.rows, size.heads * size.dim), bf16)]
    shapes += [jax.ShapeDtypeStruct((size.rows, size.wide), f32)] * (2 * GROUP)
    outs = call(
        body, size, "gradients", groups, spans, seg, inputs, shapes,
        size.heads * 26 * size.rows * size.dim * size.dim, size.heads * size.dim * size.rows * 24,
    )
    return outs[0], outs[1::2], outs[2::2]


def final_gradients(size, groups, spans, seg, key_rows, value_rows, local_key, local_value, entering):
    def body(g_ref, spans, seg_ref, *refs):
        ins, outs = refs[: 5 * GROUP], refs[5 * GROUP :]
        _, mark = markers(seg_ref, size)
        left = size.rows - position(size)
        for c in range(GROUP):
            key_ref, value_ref, local_key_ref, local_value_ref, state_ref = ins[5 * c : 5 * c + 5]
            live = mark == state_ref[size.state : size.state + 1, :]
            for h in range(size.per):
                cols = slice(h * size.dim, (h + 1) * size.dim)
                span = span_at(spans, g_ref[c], size, h)
                weight = jnp.where(live, decay(left, span), 0.0)
                key, value = key_ref[:, cols], value_ref[:, cols]
                high, low = halves(state_ref[cols, :])
                keys = dot(
                    jnp.concatenate([value, value], 1), jnp.concatenate([high, low], 1), 1, 1
                )
                values = dot(jnp.concatenate([key, key], 1), jnp.concatenate([high, low], 0))
                start = pl.multiple_of(g_ref[c] * size.wide + h * size.dim, size.dim)
                here = pl.ds(start, size.dim)
                outs[0][:, here] = (local_key_ref[:, cols] + weight * keys).astype(bf16)
                outs[1][:, here] = (local_value_ref[:, cols] + weight * values).astype(bf16)
                total = None
                for k in range(GROUP):
                    at = size.state + INFO + (k ^ c) * size.pad + h
                    row = ins[5 * k + 4][at : at + 1, :]
                    total = row if total is None else total + row
                outs[2][:, here] = total

    inputs = []
    for c in range(GROUP):
        inputs += [
            (key_rows, c), (value_rows, c), (local_key[c], None), (local_value[c], None),
            (entering[c], None),
        ]
    features = size.heads * size.dim
    shapes = [jax.ShapeDtypeStruct((size.rows, features), bf16)] * 2
    shapes.append(jax.ShapeDtypeStruct((1, features), f32))
    return call(
        body, size, "final", groups, spans, seg, inputs, shapes,
        size.heads * 8 * size.rows * size.dim * size.dim, features * size.rows * 24,
    )


def swap(array, distance):
    members = lax.axis_size("seq")
    return lax.ppermute(array, "seq", [(i, i ^ distance) for i in range(members)])


def shifted(array, by):
    members = lax.axis_size("seq")
    pairs = [(i, i + by) for i in range(members) if 0 <= i + by < members]
    return lax.ppermute(array, "seq", pairs)


def from_other_groups(size, backward, spans, me, total):
    members = lax.axis_size("seq")
    span_tokens = GROUP * size.rows
    longest = members * size.rows // 4
    needed = max(longest - 2, 0) // span_tokens + 1
    way = -GROUP if backward else GROUP
    result = shifted(total, way)
    reach = 1
    mine = lax.dynamic_slice(spans, (me * size.per,), (size.per,))
    while reach < needed:
        incoming = shifted(result, way * reach)
        passes = incoming[size.state, 0] == result[size.state, 0]
        factor = jnp.where(passes, jnp.exp(-(reach * span_tokens) / mine), 0.0)
        factor = jnp.repeat(factor, size.dim)[:, None]
        result = result.at[: size.state].add(factor * incoming[: size.state])
        reach *= 2
    return result


def travel(size, backward, groups, spans, seg, me, states, riders=lambda: ()):
    parts = [states[0]] + [swap(states[k], k) for k in range(1, GROUP)]
    total = group_total(size, backward, groups, spans, seg, parts)
    entering = from_other_groups(size, backward, spans, me, total)
    outs = group_prefixes(size, backward, groups, spans, seg, parts, entering, riders())
    return [outs[0]] + [swap(outs[k], k) for k in range(1, GROUP)]


def local(queries, key_rows, value_rows, segment_ids, decay_span, norm_gain, out_grad):
    size = Sizes(queries, decay_span)
    features = size.heads * size.dim * lax.axis_size("head")
    members = lax.axis_size("seq")
    me = lax.rem(lax.axis_index("seq"), GROUP)
    groups = jnp.bitwise_xor(jnp.arange(GROUP, dtype=jnp.int32), me.astype(jnp.int32))
    seg = segment_ids.reshape(1, size.rows)
    gain = norm_gain.reshape(1, size.heads * size.dim)
    common = (groups, decay_span, seg)

    states = {}
    for chunk in (3, 1, 2, 0):
        states[chunk] = key_value_states(size, (chunk,), *common, key_rows, value_rows)[0]
    nearby = local_attended(size, range(GROUP), *common, queries, key_rows, value_rows)
    entering = travel(size, False, *common, me, states)

    outs = whole_attended(size, *common, queries, out_grad, gain, nearby, entering)
    attended, sums = outs[:GROUP], lax.psum(outs[GROUP], "head")

    back, grad_states, rows = {}, {}, {}
    for chunk in (3, 1, 2):
        b, s, r = output_grad_states(
            size, (chunk,), features, *common, queries, out_grad, gain, attended, sums
        )
        back[chunk], grad_states[chunk], rows[chunk] = b[0], s[0], r
    before = [(k, rows[k]) for k in (3, 1, 2)]
    b, s, gains = output_grad_states(
        size, (0,), features, *common, queries, out_grad, gain, attended, sums, before
    )
    back[0], grad_states[0] = b[0], s[0]

    distance = GROUP
    while distance < members:
        gains = gains + swap(gains, distance)
        distance *= 2

    leaving = travel(size, True, *common, me, grad_states, lambda: (gains,))
    query_grad, local_key, local_value = local_gradients(
        size, *common, queries, key_rows, value_rows, back, entering
    )
    key_grad, value_grad, gain_grad = final_gradients(
        size, *common, key_rows, value_rows, local_key, local_value, leaving
    )
    return query_grad, key_grad, value_grad, gain_grad.reshape(size.heads * size.dim)


def solution(mesh):
    rows = P("seq", "head")
    in_specs = (rows, rows, rows, P("seq"), P("head"), P("head"), rows)
    return jax.shard_map(
        local, mesh=mesh, in_specs=in_specs, out_specs=(rows, rows, rows, P("head")), check_vma=False
    )
```

time: 444 us -> 108 us (0.24)
  the two profiles are of different devices: /device:TPU:16 before, /device:TPU:0 now
where the time goes in v1:
time: 108 us; the launch traced here: 107 us
  waiting for transfers between devices  38.3 us (35%)
  Pallas kernels  33.3 us (31%)
  starting transfers between devices  26.5 us (25%)
  local copies, waits for them, and re-layouts  5.83 us (5%)
  blocking collectives  2.44 us (2%)
    ppermute x14, waiting for transfers between devices, swap(): lax.ppermute(array, 'seq', [(i, i ^ distance) for i in range(members)])  33.9 us
    pallas_call x16, Pallas kernels, call(): pl.pallas_call(body, grid_spec=pltpu.PrefetchScalarGridSpec(num_scalar_pr...  33.3 us
    ppermute x14, starting transfers between devices, swap(): lax.ppermute(array, 'seq', [(i, i ^ distance) for i in range(members)])  21.4 us
    unnamed x30, local copies, waits for them, and re-layouts  5.83 us
    ppermute x2, starting transfers between devices, shifted(): return lax.ppermute(array, 'seq', pairs)  5.1 us
    ppermute x2, waiting for transfers between devices, shifted(): return lax.ppermute(array, 'seq', pairs)  4.43 us
    psum x1, blocking collectives, local(): attended, sums = (outs[:GROUP], lax.psum(outs[GROUP], 'head'))  2.44 us
  transfers between devices with their start and end apart: 16, of which 11 were waited for; matrix products, arithmetic and copies ran while one was open for 0% of the time, Pallas kernels for 16%

profile of v1, /device:TPU:0, one launch (start us, length us, event | category | flops | bytes accessed | tf_op | source)
XLA Modules:
  0.0 107.2 jit_solution(12943977954944029212)
XLA Ops:
  0.7 0.6 copy-done.13
  1.3 1.0 copy-done
  2.4 1.0 copy-done.2
  3.4 1.4 %states.5 = f32[520,128]{1,0:T(8,128)S(1)} custom-call(s32[4]{0:T(128)S(1)} %iota_xor_fusion.g_ref, f32[16]{0:T(128)S(1)} %copy-done.13, s32[1,128]{1,0:T(1,128)S(1)} %bitcast.11, bf16[128,2048]{1,0:T(8,128)(2,1)S(1)} %copy-done, bf16[128,2048]{1,0:T(8,128)(2,1)S(1)} %copy-done.2), custom_call_target="tpu_custom_call" | custom-call | flops 33554432 | bytes 524288 | tf_op jit(solution)/shard_map/states/pallas_call | solution.py:77
  4.8 3.0 %collective-permute-start = (f32[520,128]{1,0:T(8,128)S(1)}, f32[520,128]{1,0:T(8,128)S(1)}, u32[]{:S(2)}, u32[]{:S(2)}) collective-permute-start(f32[520,128]{1,0:T(8,128)S(1)} %states.5), channel_id=1, source_target_pairs={{0,2},{2,0},{4,6},{6,4},{8,10},{10,8},{12,14},{14,12},{16,18},{18,... | collective-permute-start | bytes 798728 | tf_op jit(solution)/shard_map/ppermute | solution.py:432
  7.8 1.4 %states.6 = f32[520,128]{1,0:T(8,128)S(1)} custom-call(s32[4]{0:T(128)S(1)} %iota_xor_fusion.g_ref, f32[16]{0:T(128)S(1)} %copy-done.13, s32[1,128]{1,0:T(1,128)S(1)} %bitcast.12, bf16[128,2048]{1,0:T(8,128)(2,1)S(1)} %copy-done, bf16[128,2048]{1,0:T(8,128)(2,1)S(1)} %copy-done.2), custom_call_target="tpu_custom_call" | custom-call | flops 33554432 | bytes 524288 | tf_op jit(solution)/shard_map/states/pallas_call | solution.py:77
  9.2 1.6 %collective-permute-start.1 = (f32[520,128]{1,0:T(8,128)S(1)}, f32[520,128]{1,0:T(8,128)S(1)}, u32[]{:S(2)}, u32[]{:S(2)}) collective-permute-start(f32[520,128]{1,0:T(8,128)S(1)} %states.6), channel_id=1, source_target_pairs={{0,4},{2,6},{4,0},{6,2},{8,12},{10,14},{12,8},{14,10},{16,20},{18,... | collective-permute-start | bytes 798728 | tf_op jit(solution)/shard_map/ppermute | solution.py:432
  10.8 1.4 %states.7 = f32[520,128]{1,0:T(8,128)S(1)} custom-call(s32[4]{0:T(128)S(1)} %iota_xor_fusion.g_ref, f32[16]{0:T(128)S(1)} %copy-done.13, s32[1,128]{1,0:T(1,128)S(1)} %bitcast.13, bf16[128,2048]{1,0:T(8,128)(2,1)S(1)} %copy-done, bf16[128,2048]{1,0:T(8,128)(2,1)S(1)} %copy-done.2), custom_call_target="tpu_custom_call" | custom-call | flops 33554432 | bytes 524288 | tf_op jit(solution)/shard_map/states/pallas_call | solution.py:77
  12.3 1.4 %states.4.refs_0_ = f32[520,128]{1,0:T(8,128)S(1)} custom-call(s32[4]{0:T(128)S(1)} %iota_xor_fusion.g_ref, f32[16]{0:T(128)S(1)} %copy-done.13, s32[1,128]{1,0:T(1,128)S(1)} %bitcast.14, bf16[128,2048]{1,0:T(8,128)(2,1)S(1)} %copy-done, bf16[128,2048]{1,0:T(8,128)(2,1)S(1)} %copy-done.2), custom_call_target="tpu_custom_call" | custom-call | flops 33554432 | bytes 524288 | tf_op jit(solution)/shard_map/states/pallas_call | solution.py:77
  13.8 0.9 collective-permute-done.refs_1_
  14.6 8.2 %collective-permute-done.1.refs_2_ = f32[520,128]{1,0:T(8,128)S(1)} collective-permute-done((f32[520,128]{1,0:T(8,128)S(1)}, f32[520,128]{1,0:T(8,128)S(1)}, u32[]{:S(2)}, u32[]{:S(2)}) %collective-permute-start.1) | collective-permute-done | bytes 266272 | tf_op jit(solution)/shard_map/ppermute | solution.py:432
  22.9 1.2 %total.2 = f32[520,128]{1,0:T(8,128)S(1)} custom-call(s32[4]{0:T(128)S(1)} %iota_xor_fusion.g_ref, f32[16]{0:T(128)S(1)} %copy-done.13, s32[1,128]{1,0:T(1,128)S(1)} %bitcast.15, f32[520,128]{1,0:T(8,128)S(1)} %states.4.refs_0_, f32[520,128]{1,0:T(8,128)S(1)} %collective-permute-done.refs_1_, f32[520,128]{1,0:T(8,128)S(1)} %collective-permute-done.1.refs_2_, ...), custom_call_target="tpu_custom_call" | custom-call | flops 524288 | bytes 1310720 | tf_op jit(solution)/shard_map/total/pallas_call | solution.py:77
  24.1 3.6 %collective-permute-start.3 = (f32[520,128]{1,0:T(8,128)S(1)}, f32[520,128]{1,0:T(8,128)S(1)}, u32[]{:S(2)}, u32[]{:S(2)}) collective-permute-start(f32[520,128]{1,0:T(8,128)S(1)} %total.2), channel_id=1, source_target_pairs={{0,8},{2,10},{4,12},{6,14},{8,16},{10,18},{12,20},{14,22},{16,24},... | collective-permute-start | bytes 798728 | tf_op jit(solution)/shard_map/ppermute | solution.py:438
  27.7 4.4 %collective-permute-done.3.refs_4_ = f32[520,128]{1,0:T(8,128)S(1)} collective-permute-done((f32[520,128]{1,0:T(8,128)S(1)}, f32[520,128]{1,0:T(8,128)S(1)}, u32[]{:S(2)}, u32[]{:S(2)}) %collective-permute-start.3) | collective-permute-done | bytes 266272 | tf_op jit(solution)/shard_map/ppermute | solution.py:438
  32.2 1.6 %prefixes.2 = (f32[520,128]{1,0:T(8,128)S(1)}, f32[520,128]{1,0:T(8,128)S(1)}, f32[520,128]{1,0:T(8,128)S(1)}, f32[520,128]{1,0:T(8,128)S(1)}) custom-call(s32[4]{0:T(128)S(1)} %iota_xor_fusion.g_ref, f32[16]{0:T(128)S(1)} %copy-done.13, s32[1,128]{1,0:T(1,128)S(1)} %bitcast.16, f32[520,128]{1,0:T(8,128)S(1)} %states.4.refs_0_, ...), custom_call_target="tpu_custom_call" | custom-call | flops 2621440 | bytes 2359296 | tf_op jit(solution)/shard_map/prefixes/pallas_call | solution.py:77
  33.9 1.9 %collective-permute-start.5 = (f32[520,128]{1,0:T(8,128)S(1)}, f32[520,128]{1,0:T(8,128)S(1)}, u32[]{:S(2)}, u32[]{:S(2)}) collective-permute-start(f32[520,128]{1,0:T(8,128)S(1)} %get-tuple-element.50), channel_id=1, source_target_pairs={{0,4},{2,6},{4,0},{6,2},{8,12},{10,14},{12,8},{14,10},{16,20},{18,... | collective-permute-start | bytes 798728 | tf_op jit(solution)/shard_map/ppermute | solution.py:432
  35.8 1.4 %collective-permute-start.6 = (f32[520,128]{1,0:T(8,128)S(1)}, f32[520,128]{1,0:T(8,128)S(1)}, u32[]{:S(2)}, u32[]{:S(2)}) collective-permute-start(f32[520,128]{1,0:T(8,128)S(1)} %get-tuple-element.52), channel_id=1, source_target_pairs={{0,6},{2,4},{4,2},{6,0},{8,14},{10,12},{12,10},{14,8},{16,22},{18,... | collective-permute-start | bytes 798728 | tf_op jit(solution)/shard_map/ppermute | solution.py:432
  37.3 3.7 %local.1 = (f32[128,512]{1,0:T(8,128)S(1)}, f32[128,512]{1,0:T(8,128)S(1)}, f32[128,512]{1,0:T(8,128)S(1)}, f32[128,512]{1,0:T(8,128)S(1)}) custom-call(s32[4]{0:T(128)S(1)} %iota_xor_fusion.g_ref, f32[16]{0:T(128)S(1)} %copy-done.13, s32[1,128]{1,0:T(1,128)S(1)} %bitcast.17, bf16[128,2048]{1,0:T(8,128)(2,1)S(1)} %copy-done.4, ...), custom_call_target="tpu_custom_call" | custom-call | flops 201326592 | bytes 2097152 | tf_op jit(solution)/shard_map/local/pallas_call | solution.py:77
  41.0 1.6 %collective-permute-done.4.refs_9_ = f32[520,128]{1,0:T(8,128)S(1)} collective-permute-done((f32[520,128]{1,0:T(8,128)S(1)}, f32[520,128]{1,0:T(8,128)S(1)}, u32[]{:S(2)}, u32[]{:S(2)}) %collective-permute-start.4) | collective-permute-done | bytes 266272 | tf_op jit(solution)/shard_map/ppermute | solution.py:432
  42.7 2.2 %collective-permute-done.5.refs_14_ = f32[520,128]{1,0:T(8,128)S(1)} collective-permute-done((f32[520,128]{1,0:T(8,128)S(1)}, f32[520,128]{1,0:T(8,128)S(1)}, u32[]{:S(2)}, u32[]{:S(2)}) %collective-permute-start.5) | collective-permute-done | bytes 266272 | tf_op jit(solution)/shard_map/ppermute | solution.py:432
  44.8 1.6 %collective-permute-done.6.refs_19_ = f32[520,128]{1,0:T(8,128)S(1)} collective-permute-done((f32[520,128]{1,0:T(8,128)S(1)}, f32[520,128]{1,0:T(8,128)S(1)}, u32[]{:S(2)}, u32[]{:S(2)}) %collective-permute-start.6) | collective-permute-done | bytes 266272 | tf_op jit(solution)/shard_map/ppermute | solution.py:432
  46.5 1.9 %attended.1 = (f32[128,512]{1,0:T(8,128)S(1)}, f32[128,512]{1,0:T(8,128)S(1)}, f32[128,512]{1,0:T(8,128)S(1)}, f32[128,512]{1,0:T(8,128)S(1)}, f32[8,128]{1,0:T(8,128)S(1)}) custom-call(s32[4]{0:T(128)S(1)} %iota_xor_fusion.g_ref, f32[16]{0:T(128)S(1)} %copy-done.13, s32[1,128]{1,0:T(1,128)S(1)} %bitcast.18, bf16[128,2048]{1,0:T(8,128)(2,1)S(1)} %copy-done.4, ...), custom_call_target="tpu_custom_call" | custom-call | flops 134217728 | bytes 4194304 | tf_op jit(solution)/shard_map/attended/pallas_call | solution.py:77
  48.4 0.7 copy-done.7
  49.0 0.7 copy-done.9
  49.8 0.7 copy-done.11
  50.5 2.4 %psum.7.refs_0_ = f32[8,128]{1,0:T(8,128)S(1)} all-reduce(f32[8,128]{1,0:T(8,128)S(1)} %get-tuple-element.53), channel_id=1, replica_groups=mesh['seq'=16,'head'=2] {'head'}, use_global_device_ids=true, to_apply=%region_0.0 | all-reduce | flops 1024 | bytes 8192 | tf_op jit(solution)/shard_map/psum | solution.py:485
  52.9 0.9 copy-done.12
  53.8 1.5 %back.4 = (f32[128,512]{1,0:T(8,128)S(1)}, f32[520,128]{1,0:T(8,128)S(1)}, f32[8,128]{1,0:T(8,128)S(1)}) custom-call(s32[4]{0:T(128)S(1)} %iota_xor_fusion.g_ref, f32[16]{0:T(128)S(1)} %copy-done.13, s32[1,128]{1,0:T(1,128)S(1)} %bitcast.19, f32[8,128]{1,0:T(8,128)S(1)} %psum.7.refs_0_, bf16[128,2048]{1,0:T(8,128)(2,1)S(1)} %copy-done.4, ...), custom_call_target="tpu_custom_call" | custom-call | flops 33554432 | bytes 1048576 | tf_op jit(solution)/shard_map/back/pallas_call | solution.py:77
  55.4 1.5 %back.5 = (f32[128,512]{1,0:T(8,128)S(1)}, f32[520,128]{1,0:T(8,128)S(1)}, f32[8,128]{1,0:T(8,128)S(1)}) custom-call(s32[4]{0:T(128)S(1)} %iota_xor_fusion.g_ref, f32[16]{0:T(128)S(1)} %copy-done.13, s32[1,128]{1,0:T(1,128)S(1)} %bitcast.20, f32[8,128]{1,0:T(8,128)S(1)} %psum.7.refs_0_, bf16[128,2048]{1,0:T(8,128)(2,1)S(1)} %copy-done.4, ...), custom_call_target="tpu_custom_call" | custom-call | flops 33554432 | bytes 1048576 | tf_op jit(solution)/shard_map/back/pallas_call | solution.py:77
  56.9 1.5 %back.6 = (f32[128,512]{1,0:T(8,128)S(1)}, f32[520,128]{1,0:T(8,128)S(1)}, f32[8,128]{1,0:T(8,128)S(1)}) custom-call(s32[4]{0:T(128)S(1)} %iota_xor_fusion.g_ref, f32[16]{0:T(128)S(1)} %copy-done.13, s32[1,128]{1,0:T(1,128)S(1)} %bitcast.21, f32[8,128]{1,0:T(8,128)S(1)} %psum.7.refs_0_, bf16[128,2048]{1,0:T(8,128)(2,1)S(1)} %copy-done.4, ...), custom_call_target="tpu_custom_call" | custom-call | flops 33554432 | bytes 1048576 | tf_op jit(solution)/shard_map/back/pallas_call | solution.py:77
  58.4 0.9 collective-permute-start.7
  59.3 1.5 %collective-permute-start.8 = (f32[520,128]{1,0:T(8,128)S(1)}, f32[520,128]{1,0:T(8,128)S(1)}, u32[]{:S(2)}, u32[]{:S(2)}) collective-permute-start(f32[520,128]{1,0:T(8,128)S(1)} %get-tuple-element.70), channel_id=1, source_target_pairs={{0,4},{2,6},{4,0},{6,2},{8,12},{10,14},{12,8},{14,10},{16,20},{18,... | collective-permute-start | bytes 798728 | tf_op jit(solution)/shard_map/ppermute | solution.py:432
  60.8 1.2 %collective-permute-start.9 = (f32[520,128]{1,0:T(8,128)S(1)}, f32[520,128]{1,0:T(8,128)S(1)}, u32[]{:S(2)}, u32[]{:S(2)}) collective-permute-start(f32[520,128]{1,0:T(8,128)S(1)} %get-tuple-element.71), channel_id=1, source_target_pairs={{0,6},{2,4},{4,2},{6,0},{8,14},{10,12},{12,10},{14,8},{16,22},{18,... | collective-permute-start | bytes 798728 | tf_op jit(solution)/shard_map/ppermute | solution.py:432
  61.9 1.5 %back.7 = (f32[128,512]{1,0:T(8,128)S(1)}, f32[520,128]{1,0:T(8,128)S(1)}, f32[32,128]{1,0:T(8,128)S(1)}) custom-call(s32[4]{0:T(128)S(1)} %iota_xor_fusion.g_ref, f32[16]{0:T(128)S(1)} %copy-done.13, s32[1,128]{1,0:T(1,128)S(1)} %bitcast.22, f32[8,128]{1,0:T(8,128)S(1)} %psum.7.refs_0_, bf16[128,2048]{1,0:T(8,128)(2,1)S(1)} %copy-done.4, ...), custom_call_target="tpu_custom_call" | custom-call | flops 33554432 | bytes 1048576 | tf_op jit(solution)/shard_map/back/pallas_call | solution.py:77
  63.4 4.2 %collective-permute-done.7.refs_1_ = f32[520,128]{1,0:T(8,128)S(1)} collective-permute-done((f32[520,128]{1,0:T(8,128)S(1)}, f32[520,128]{1,0:T(8,128)S(1)}, u32[]{:S(2)}, u32[]{:S(2)}) %collective-permute-start.7) | collective-permute-done | bytes 266272 | tf_op jit(solution)/shard_map/ppermute | solution.py:432
  67.7 5.5 %collective-permute-done.8.refs_2_ = f32[520,128]{1,0:T(8,128)S(1)} collective-permute-done((f32[520,128]{1,0:T(8,128)S(1)}, f32[520,128]{1,0:T(8,128)S(1)}, u32[]{:S(2)}, u32[]{:S(2)}) %collective-permute-start.8) | collective-permute-done | bytes 266272 | tf_op jit(solution)/shard_map/ppermute | solution.py:432
  73.2 1.2 %total.3 = f32[520,128]{1,0:T(8,128)S(1)} custom-call(s32[4]{0:T(128)S(1)} %iota_xor_fusion.g_ref, f32[16]{0:T(128)S(1)} %copy-done.13, s32[1,128]{1,0:T(1,128)S(1)} %bitcast.23, f32[520,128]{1,0:T(8,128)S(1)} %get-tuple-element.68.refs_0_, f32[520,128]{1,0:T(8,128)S(1)} %collective-permute-done.7.refs_1_, f32[520,128]{1,0:T(8,128)S(1)} %collective-permute-done.8.refs_2_, ...), custom_call_target="tpu_custom_call" | custom-call | flops 524288 | bytes 1310720 | tf_op jit(solution)/shard_map/total/pallas_call | solution.py:77
  74.4 1.5 %collective-permute-start.10 = (f32[520,128]{1,0:T(8,128)S(1)}, f32[520,128]{1,0:T(8,128)S(1)}, u32[]{:S(2)}, u32[]{:S(2)}) collective-permute-start(f32[520,128]{1,0:T(8,128)S(1)} %total.3), channel_id=1, source_target_pairs={{8,0},{10,2},{12,4},{14,6},{16,8},{18,10},{20,12},{22,14},{24,16},... | collective-permute-start | bytes 798728 | tf_op jit(solution)/shard_map/ppermute | solution.py:438
  75.8 3.2 %collective-permute-start.11 = (f32[32,128]{1,0:T(8,128)S(1)}, f32[32,128]{1,0:T(8,128)S(1)}, u32[]{:S(2)}, u32[]{:S(2)}) collective-permute-start(f32[32,128]{1,0:T(8,128)S(1)} %get-tuple-element.72), channel_id=1, source_target_pairs={{0,8},{2,10},{4,12},{6,14},{8,0},{10,2},{12,4},{14,6},{16,24},{18,... | collective-permute-start | bytes 49160 | tf_op jit(solution)/shard_map/ppermute | solution.py:432
  79.0 5.8 %collective-permute-done.11 = f32[32,128]{1,0:T(8,128)S(1)} collective-permute-done((f32[32,128]{1,0:T(8,128)S(1)}, f32[32,128]{1,0:T(8,128)S(1)}, u32[]{:S(2)}, u32[]{:S(2)}) %collective-permute-start.11) | collective-permute-done | bytes 16416 | tf_op jit(solution)/shard_map/ppermute | solution.py:432
  84.8 2.9 %collective-permute-start.12 = (f32[32,128]{1,0:T(8,128)S(1)}, f32[32,128]{1,0:T(8,128)S(1)}, u32[]{:S(2)}, u32[]{:S(2)}) collective-permute-start(f32[32,128]{1,0:T(8,128)S(1)} %add.8), channel_id=1, source_target_pairs={{0,16},{2,18},{4,20},{6,22},{8,24},{10,26},{12,28},{14,30},{16,0},... | collective-permute-start | bytes 49160 | tf_op jit(solution)/shard_map/ppermute | solution.py:432
  87.7 1.7 %collective-permute-done.12 = f32[32,128]{1,0:T(8,128)S(1)} collective-permute-done((f32[32,128]{1,0:T(8,128)S(1)}, f32[32,128]{1,0:T(8,128)S(1)}, u32[]{:S(2)}, u32[]{:S(2)}) %collective-permute-start.12) | collective-permute-done | bytes 16416 | tf_op jit(solution)/shard_map/ppermute | solution.py:432
  89.4 1.5 %prefixes.3 = (f32[552,128]{1,0:T(8,128)S(1)}, f32[552,128]{1,0:T(8,128)S(1)}, f32[552,128]{1,0:T(8,128)S(1)}, f32[552,128]{1,0:T(8,128)S(1)}) custom-call(s32[4]{0:T(128)S(1)} %iota_xor_fusion.g_ref, f32[16]{0:T(128)S(1)} %copy-done.13, s32[1,128]{1,0:T(1,128)S(1)} %bitcast.24, f32[520,128]{1,0:T(8,128)S(1)} %get-tuple-element.68.refs_0_, ...), custom_call_target="tpu_custom_call" | custom-call | flops 2621440 | bytes 2359296 | tf_op jit(solution)/shard_map/prefixes/pallas_call | solution.py:77
  91.0 1.5 %collective-permute-start.13 = (f32[552,128]{1,0:T(8,128)S(1)}, f32[552,128]{1,0:T(8,128)S(1)}, u32[]{:S(2)}, u32[]{:S(2)}) collective-permute-start(f32[552,128]{1,0:T(8,128)S(1)} %get-tuple-element.76), channel_id=1, source_target_pairs={{0,2},{2,0},{4,6},{6,4},{8,10},{10,8},{12,14},{14,12},{16,18},{18,... | collective-permute-start | bytes 847880 | tf_op jit(solution)/shard_map/ppermute | solution.py:432
  93.0 1.5 %collective-permute-start.15 = (f32[552,128]{1,0:T(8,128)S(1)}, f32[552,128]{1,0:T(8,128)S(1)}, u32[]{:S(2)}, u32[]{:S(2)}) collective-permute-start(f32[552,128]{1,0:T(8,128)S(1)} %get-tuple-element.82), channel_id=1, source_target_pairs={{0,6},{2,4},{4,2},{6,0},{8,14},{10,12},{12,10},{14,8},{16,22},{18,... | collective-permute-start | bytes 847880 | tf_op jit(solution)/shard_map/ppermute | solution.py:432
  94.5 7.8 %gradients.1 = (bf16[128,2048]{1,0:T(8,128)(2,1)}, f32[128,512]{1,0:T(8,128)S(1)}, f32[128,512]{1,0:T(8,128)S(1)}, f32[128,512]{1,0:T(8,128)S(1)}, f32[128,512]{...) custom-call(s32[4]{0:T(128)S(1)} %iota_xor_fusion.g_ref, ...), custom_call_target="tpu_custom_call" | custom-call | flops 872415232 | bytes 6291456 | tf_op jit(solution)/shard_map/gradients/pallas_call | solution.py:77
  102.4 2.1 %collective-permute-done.14.refs_14_ = f32[552,128]{1,0:T(8,128)S(1)} collective-permute-done((f32[552,128]{1,0:T(8,128)S(1)}, f32[552,128]{1,0:T(8,128)S(1)}, u32[]{:S(2)}, u32[]{:S(2)}) %collective-permute-start.14) | collective-permute-done | bytes 282656 | tf_op jit(solution)/shard_map/ppermute | solution.py:432
  104.5 2.8 %final.1 = (bf16[128,2048]{1,0:T(8,128)(2,1)}, bf16[128,2048]{1,0:T(8,128)(2,1)}, f32[1,2048]{1,0:T(1,128)}) custom-call(s32[4]{0:T(128)S(1)} %iota_xor_fusion.g_ref, f32[16]{0:T(128)S(1)} %copy-done.13, s32[1,128]{1,0:T(1,128)S(1)} %bitcast.26, bf16[128,2048]{1,0:T(8,128)(2,1)S(1)} %copy-done.1, bf16[128,2048]{1,0:T(8,128)(2,1)S(1)} %copy-done.3, ...), custom_call_target="tpu_custom_call" | custom-call | flops 268435456 | bytes 6291456 | tf_op jit(solution)/shard_map/final/pallas_call | solution.py:77
  (34 shorter events, 0.9 us)
Async XLA Ops:
  0.6 0.7 copy-start.13
  0.7 0.7 copy-start.14
  1.3 1.0 copy-start
  2.4 1.0 copy-start.2
  4.8 9.8 %collective-permute-start = (f32[520,128]{1,0:T(8,128)S(1)}, f32[520,128]{1,0:T(8,128)S(1)}, u32[]{:S(2)}, u32[]{:S(2)}) collective-permute-start(f32[520,128]{1,0:T(8,128)S(1)} %states.5), channel_id=1, source_target_pairs={{0,2},{2,0},{4,6},{6,4},{8,10},{10,8},{12,14},{14,12},{16,18},{18,... | collective-permute-start | bytes 798728 | tf_op jit(solution)/shard_map/ppermute | solution.py:432
  9.2 13.6 %collective-permute-start.1 = (f32[520,128]{1,0:T(8,128)S(1)}, f32[520,128]{1,0:T(8,128)S(1)}, u32[]{:S(2)}, u32[]{:S(2)}) collective-permute-start(f32[520,128]{1,0:T(8,128)S(1)} %states.6), channel_id=1, source_target_pairs={{0,4},{2,6},{4,0},{6,2},{8,12},{10,14},{12,8},{14,10},{16,20},{18,... | collective-permute-start | bytes 798728 | tf_op jit(solution)/shard_map/ppermute | solution.py:432
  12.3 10.6 %collective-permute-start.2 = (f32[520,128]{1,0:T(8,128)S(1)}, f32[520,128]{1,0:T(8,128)S(1)}, u32[]{:S(2)}, u32[]{:S(2)}) collective-permute-start(f32[520,128]{1,0:T(8,128)S(1)} %states.7), channel_id=1, source_target_pairs={{0,6},{2,4},{4,2},{6,0},{8,14},{10,12},{12,10},{14,8},{16,22},{18,... | collective-permute-start | bytes 798728 | tf_op jit(solution)/shard_map/ppermute | solution.py:432
  22.9 14.4 %copy-start.4 = (bf16[128,2048]{1,0:T(8,128)(2,1)S(1)}, bf16[128,2048]{1,0:T(8,128)(2,1)}, u32[]{:S(2)}) copy-start(bf16[128,2048]{1,0:T(8,128)(2,1)} %refs_15_.4) | copy-start | bytes 1572868
  24.1 13.2 %copy-start.1 = (bf16[128,2048]{1,0:T(8,128)(2,1)S(1)}, bf16[128,2048]{1,0:T(8,128)(2,1)}, u32[]{:S(2)}) copy-start(bf16[128,2048]{1,0:T(8,128)(2,1)} %refs_15_.5) | copy-start | bytes 1572868
  24.1 13.2 %copy-start.3 = (bf16[128,2048]{1,0:T(8,128)(2,1)S(1)}, bf16[128,2048]{1,0:T(8,128)(2,1)}, u32[]{:S(2)}) copy-start(bf16[128,2048]{1,0:T(8,128)(2,1)} %refs_16_.5) | copy-start | bytes 1572868
  24.1 8.1 %collective-permute-start.3 = (f32[520,128]{1,0:T(8,128)S(1)}, f32[520,128]{1,0:T(8,128)S(1)}, u32[]{:S(2)}, u32[]{:S(2)}) collective-permute-start(f32[520,128]{1,0:T(8,128)S(1)} %total.2), channel_id=1, source_target_pairs={{0,8},{2,10},{4,12},{6,14},{8,16},{10,18},{12,20},{14,22},{16,24},... | collective-permute-start | bytes 798728 | tf_op jit(solution)/shard_map/ppermute | solution.py:438
  33.7 8.9 %collective-permute-start.4 = (f32[520,128]{1,0:T(8,128)S(1)}, f32[520,128]{1,0:T(8,128)S(1)}, u32[]{:S(2)}, u32[]{:S(2)}) collective-permute-start(f32[520,128]{1,0:T(8,128)S(1)} %get-tuple-element.48), channel_id=1, source_target_pairs={{0,2},{2,0},{4,6},{6,4},{8,10},{10,8},{12,14},{14,12},{16,18},{18,... | collective-permute-start | bytes 798728 | tf_op jit(solution)/shard_map/ppermute | solution.py:432
  33.9 10.9 %collective-permute-start.5 = (f32[520,128]{1,0:T(8,128)S(1)}, f32[520,128]{1,0:T(8,128)S(1)}, u32[]{:S(2)}, u32[]{:S(2)}) collective-permute-start(f32[520,128]{1,0:T(8,128)S(1)} %get-tuple-element.50), channel_id=1, source_target_pairs={{0,4},{2,6},{4,0},{6,2},{8,12},{10,14},{12,8},{14,10},{16,20},{18,... | collective-permute-start | bytes 798728 | tf_op jit(solution)/shard_map/ppermute | solution.py:432
  35.8 10.6 %copy-start.5 = (bf16[128,2048]{1,0:T(8,128)(2,1)S(1)}, bf16[128,2048]{1,0:T(8,128)(2,1)}, u32[]{:S(2)}) copy-start(bf16[128,2048]{1,0:T(8,128)(2,1)} %refs_2_.10) | copy-start | bytes 1572868
  35.8 10.6 %collective-permute-start.6 = (f32[520,128]{1,0:T(8,128)S(1)}, f32[520,128]{1,0:T(8,128)S(1)}, u32[]{:S(2)}, u32[]{:S(2)}) collective-permute-start(f32[520,128]{1,0:T(8,128)S(1)} %get-tuple-element.52), channel_id=1, source_target_pairs={{0,6},{2,4},{4,2},{6,0},{8,14},{10,12},{12,10},{14,8},{16,22},{18,... | collective-permute-start | bytes 798728 | tf_op jit(solution)/shard_map/ppermute | solution.py:432
  41.0 5.4 %copy-start.6 = (f32[2048]{0:T(1024)S(1)}, f32[2048]{0:T(1024)}, u32[]{:S(2)}) copy-start(f32[2048]{0:T(1024)} %param.12) | copy-start | bytes 24580
  48.3 0.7 copy-start.7
  49.0 0.7 copy-start.9
  49.7 0.7 copy-start.11
  52.9 1.0 copy-start.12
  53.8 1.5 %copy-start.10 = (f32[128,512]{1,0:T(8,128)S(1)}, f32[128,512]{1,0:T(8,128)}, u32[]{:S(2)}) copy-start(f32[128,512]{1,0:T(8,128)} %copy-done.9) | copy-start | bytes 786436
  55.4 1.5 %copy-start.8 = (f32[128,512]{1,0:T(8,128)S(1)}, f32[128,512]{1,0:T(8,128)}, u32[]{:S(2)}) copy-start(f32[128,512]{1,0:T(8,128)} %copy-done.7) | copy-start | bytes 786436
  58.4 9.3 %collective-permute-start.7 = (f32[520,128]{1,0:T(8,128)S(1)}, f32[520,128]{1,0:T(8,128)S(1)}, u32[]{:S(2)}, u32[]{:S(2)}) collective-permute-start(f32[520,128]{1,0:T(8,128)S(1)} %get-tuple-element.69), channel_id=1, source_target_pairs={{0,2},{2,0},{4,6},{6,4},{8,10},{10,8},{12,14},{14,12},{16,18},{18,... | collective-permute-start | bytes 798728 | tf_op jit(solution)/shard_map/ppermute | solution.py:432
  59.3 13.9 %collective-permute-start.8 = (f32[520,128]{1,0:T(8,128)S(1)}, f32[520,128]{1,0:T(8,128)S(1)}, u32[]{:S(2)}, u32[]{:S(2)}) collective-permute-start(f32[520,128]{1,0:T(8,128)S(1)} %get-tuple-element.70), channel_id=1, source_target_pairs={{0,4},{2,6},{4,0},{6,2},{8,12},{10,14},{12,8},{14,10},{16,20},{18,... | collective-permute-start | bytes 798728 | tf_op jit(solution)/shard_map/ppermute | solution.py:432
  60.8 12.4 %collective-permute-start.9 = (f32[520,128]{1,0:T(8,128)S(1)}, f32[520,128]{1,0:T(8,128)S(1)}, u32[]{:S(2)}, u32[]{:S(2)}) collective-permute-start(f32[520,128]{1,0:T(8,128)S(1)} %get-tuple-element.71), channel_id=1, source_target_pairs={{0,6},{2,4},{4,2},{6,0},{8,14},{10,12},{12,10},{14,8},{16,22},{18,... | collective-permute-start | bytes 798728 | tf_op jit(solution)/shard_map/ppermute | solution.py:432
  74.4 15.1 %collective-permute-start.10 = (f32[520,128]{1,0:T(8,128)S(1)}, f32[520,128]{1,0:T(8,128)S(1)}, u32[]{:S(2)}, u32[]{:S(2)}) collective-permute-start(f32[520,128]{1,0:T(8,128)S(1)} %total.3), channel_id=1, source_target_pairs={{8,0},{10,2},{12,4},{14,6},{16,8},{18,10},{20,12},{22,14},{24,16},... | collective-permute-start | bytes 798728 | tf_op jit(solution)/shard_map/ppermute | solution.py:438
  75.8 8.9 %collective-permute-start.11 = (f32[32,128]{1,0:T(8,128)S(1)}, f32[32,128]{1,0:T(8,128)S(1)}, u32[]{:S(2)}, u32[]{:S(2)}) collective-permute-start(f32[32,128]{1,0:T(8,128)S(1)} %get-tuple-element.72), channel_id=1, source_target_pairs={{0,8},{2,10},{4,12},{6,14},{8,0},{10,2},{12,4},{14,6},{16,24},{18,... | collective-permute-start | bytes 49160 | tf_op jit(solution)/shard_map/ppermute | solution.py:432
  84.8 4.6 %collective-permute-start.12 = (f32[32,128]{1,0:T(8,128)S(1)}, f32[32,128]{1,0:T(8,128)S(1)}, u32[]{:S(2)}, u32[]{:S(2)}) collective-permute-start(f32[32,128]{1,0:T(8,128)S(1)} %add.8), channel_id=1, source_target_pairs={{0,16},{2,18},{4,20},{6,22},{8,24},{10,26},{12,28},{14,30},{16,0},... | collective-permute-start | bytes 49160 | tf_op jit(solution)/shard_map/ppermute | solution.py:432
  91.0 11.4 %collective-permute-start.13 = (f32[552,128]{1,0:T(8,128)S(1)}, f32[552,128]{1,0:T(8,128)S(1)}, u32[]{:S(2)}, u32[]{:S(2)}) collective-permute-start(f32[552,128]{1,0:T(8,128)S(1)} %get-tuple-element.76), channel_id=1, source_target_pairs={{0,2},{2,0},{4,6},{6,4},{8,10},{10,8},{12,14},{14,12},{16,18},{18,... | collective-permute-start | bytes 847880 | tf_op jit(solution)/shard_map/ppermute | solution.py:432
  92.5 12.0 %collective-permute-start.14 = (f32[552,128]{1,0:T(8,128)S(1)}, f32[552,128]{1,0:T(8,128)S(1)}, u32[]{:S(2)}, u32[]{:S(2)}) collective-permute-start(f32[552,128]{1,0:T(8,128)S(1)} %get-tuple-element.79), channel_id=1, source_target_pairs={{0,4},{2,6},{4,0},{6,2},{8,12},{10,14},{12,8},{14,10},{16,20},{18,... | collective-permute-start | bytes 847880 | tf_op jit(solution)/shard_map/ppermute | solution.py:432
  93.0 11.4 %collective-permute-start.15 = (f32[552,128]{1,0:T(8,128)S(1)}, f32[552,128]{1,0:T(8,128)S(1)}, u32[]{:S(2)}, u32[]{:S(2)}) collective-permute-start(f32[552,128]{1,0:T(8,128)S(1)} %get-tuple-element.82), channel_id=1, source_target_pairs={{0,6},{2,4},{4,2},{6,0},{8,14},{10,12},{12,10},{14,8},{16,22},{18,... | collective-permute-start | bytes 847880 | tf_op jit(solution)/shard_map/ppermute | solution.py:432

commit v2 on v1

v2 whole, which is shorter than its diff:
```python
import jax
import jax.numpy as jnp
from jax import lax
from jax.experimental import pallas as pl
from jax.experimental.pallas import tpu as pltpu
from jax.sharding import PartitionSpec as P

GROUP = 4
INFO = 8
FAR = 1e9
f32 = jnp.float32
bf16 = jnp.bfloat16
HBM = pl.BlockSpec(memory_space=pltpu.HBM)
VMEM = pl.BlockSpec(memory_space=pltpu.VMEM)


def dot(a, b, over_a=1, over_b=0):
    return lax.dot_general(a, b, (((over_a,), (over_b,)), ((), ())), preferred_element_type=f32)


def halves(x):
    high = x.astype(bf16)
    return high, (x - high.astype(f32)).astype(bf16)


def decay(steps, span):
    return jnp.exp(-steps / span)


class Sizes:
    def __init__(self, queries, decay_span):
        self.rows = queries.shape[0]
        self.heads = decay_span.shape[0]
        self.features = queries.shape[1]
        self.dim = self.features // self.heads
        self.per = self.heads // GROUP
        self.wide = self.per * self.dim
        self.state = self.per * self.dim
        self.pad = -(-self.per // 8) * 8
        self.payload = jax.ShapeDtypeStruct((self.state + INFO, self.dim), f32)
        self.block = jax.ShapeDtypeStruct((self.rows, self.features), f32)
        self.gains = jax.ShapeDtypeStruct((GROUP * self.pad, self.dim), f32)


def markers(seg_ref, size):
    row = seg_ref[...].astype(f32) + 1.0
    return row, jnp.broadcast_to(row, (size.dim, size.rows)).T


def position(size):
    return lax.broadcasted_iota(jnp.int32, (size.rows, size.dim), 0).astype(f32)


def pair_weight(row, size):
    shape = (size.rows, size.rows)
    here = jnp.broadcast_to(row, shape)
    at = lax.broadcasted_iota(jnp.int32, shape, 0)
    by = lax.broadcasted_iota(jnp.int32, shape, 1)
    live = jnp.logical_and(at >= by, here == here.T)
    return jnp.maximum(at - by, 0).astype(f32), live


def info_rows(first_row, second_row, dim):
    index = lax.broadcasted_iota(jnp.int32, (INFO, dim), 0)
    return jnp.where(index == 0, first_row, jnp.where(index == 1, second_row, 0.0))


def partners():
    me = jnp.bitwise_and(lax.axis_index("seq"), GROUP - 1)
    return [jnp.bitwise_xor(me, k) for k in range(GROUP)]


def places(backward):
    return [GROUP - 1 - p for p in partners()] if backward else partners()


def columns(size, group, h=None):
    if h is None:
        return pl.ds(pl.multiple_of(group * size.wide, size.wide), size.wide)
    return pl.ds(pl.multiple_of(group * size.wide + h * size.dim, size.dim), size.dim)


def span_of(spans_ref, size, group, h):
    return spans_ref[pl.ds(group * size.per + h, 1), :]


def square_span(span, size):
    return span[:, :1] if size.rows != size.dim else span


def call(body, name, inputs, outputs, flops, moved, scratch=(), in_specs=None, out_specs=None):
    return pl.pallas_call(
        body,
        out_shape=outputs,
        in_specs=in_specs if in_specs is not None else [VMEM] * len(inputs),
        out_specs=out_specs if out_specs is not None else [VMEM] * len(outputs),
        scratch_shapes=list(scratch),
        compiler_params=pltpu.CompilerParams(vmem_limit_bytes=16 * 1024 * 1024),
        cost_estimate=pl.CostEstimate(flops=flops, bytes_accessed=moved, transcendentals=0),
        name=name,
    )(*inputs)


def key_value_states(size, chunks, seg, spans, key_rows, value_rows):
    n = len(chunks)

    def body(seg_ref, spans_ref, key_hbm, value_hbm, *refs):
        outs, (keys, values, sems) = refs[:n], refs[n:]
        group = partners()
        copies = []
        for c, chunk in enumerate(chunks):
            here = columns(size, group[chunk])
            pair = (
                pltpu.make_async_copy(key_hbm.at[:, here], keys.at[c], sems.at[0, c]),
                pltpu.make_async_copy(value_hbm.at[:, here], values.at[c], sems.at[1, c]),
            )
            for copy in pair:
                copy.start()
            copies.append(pair)
        row, mark = markers(seg_ref, size)
        last, first = mark[size.rows - 1 :, :], mark[:1, :]
        ahead = (size.rows - 1.0) - position(size)
        for c, chunk in enumerate(chunks):
            for copy in copies[c]:
                copy.wait()
            for h in range(size.per):
                cols = slice(h * size.dim, (h + 1) * size.dim)
                span = span_of(spans_ref, size, group[chunk], h)
                weight = jnp.where(mark == last, decay(ahead, span), 0.0)
                key = keys[c, :, cols]
                high, low = halves(values[c, :, cols].astype(f32) * weight)
                outs[c][cols, :] = dot(
                    jnp.concatenate([key, key], 0), jnp.concatenate([high, low], 0), 0, 0
                )
            outs[c][size.state :, :] = info_rows(last, first, size.dim)

    held = (n, size.rows, size.wide)
    return call(
        body, "states", (seg, spans, key_rows, value_rows), [size.payload] * n,
        n * size.per * 4 * size.rows * size.dim * size.dim, n * size.wide * size.rows * 8,
        [pltpu.VMEM(held, bf16), pltpu.VMEM(held, bf16), pltpu.SemaphoreType.DMA((2, n))],
        [VMEM, VMEM, HBM, HBM],
    )


def nearby_attended(size, seg, spans, queries, key_rows, value_rows):
    def body(seg_ref, spans_ref, query_ref, key_ref, value_ref, out_ref):
        row, _ = markers(seg_ref, size)
        gap, live = pair_weight(row, size)
        for h in range(size.heads):
            cols = slice(h * size.dim, (h + 1) * size.dim)
            span = square_span(spans_ref[h : h + 1, :], size)
            weight = jnp.where(live, decay(gap, span), 0.0)
            query, key, value = query_ref[:, cols], key_ref[:, cols], value_ref[:, cols]
            high, low = halves(dot(query, key, 1, 1) * weight)
            out_ref[:, cols] = dot(
                jnp.concatenate([high, low], 1), jnp.concatenate([value, value], 0)
            )

    return call(
        body, "nearby", (seg, spans, queries, key_rows, value_rows), [size.block],
        size.heads * 6 * size.rows * size.dim * size.dim, size.features * size.rows * 10,
    )[0]


def group_total(size, backward, spans, parts, riders=()):
    mark_row = size.state + (1 if backward else 0)

    def body(spans_ref, *refs):
        ins, out = refs[:GROUP], refs[GROUP + len(riders)]
        place = places(backward)
        marks = [ref[mark_row : mark_row + 1, :] for ref in ins]
        end = marks[0]
        for mark in marks[1:]:
            end = jnp.minimum(end, mark) if backward else jnp.maximum(end, mark)
        me = partners()[0]
        for h in range(size.per):
            cols = slice(h * size.dim, (h + 1) * size.dim)
            span = span_of(spans_ref, size, me, h)
            total = None
            for k in range(GROUP):
                steps = ((GROUP - 1 - place[k]) * size.rows).astype(f32)
                factor = jnp.where(marks[k] == end, decay(steps, span), 0.0)
                term = factor * ins[k][cols, :]
                total = term if total is None else total + term
            out[cols, :] = total
        out[size.state :, :] = info_rows(end, end, size.dim)
        if riders:
            refs[-1][...] = refs[GROUP][...] + refs[GROUP + 1][...]

    outputs = [size.payload] + ([size.gains] if riders else [])
    return call(
        body, "total", (spans, *parts, *riders), outputs,
        size.state * size.dim * 8, size.state * size.dim * 20,
    )


def group_prefixes(size, backward, spans, parts, entering, riders=()):
    mark_row = size.state + (1 if backward else 0)
    extra = sum(r.shape[0] for r in riders)

    def body(spans_ref, *refs):
        ins, enter = refs[:GROUP], refs[GROUP]
        rides, outs = refs[GROUP + 1 : GROUP + 1 + len(riders)], refs[GROUP + 1 + len(riders) :]
        place = places(backward)
        me = partners()[0]
        marks = [ref[mark_row : mark_row + 1, :] for ref in ins]
        outer = enter[size.state : size.state + 1, :]
        if backward:
            outer = jnp.where(outer == 0.0, FAR, outer)
        carry = []
        for to in range(GROUP):
            now = outer
            for k in range(GROUP):
                if backward:
                    now = jnp.where(place[k] < place[to], jnp.minimum(now, marks[k]), now)
                else:
                    now = jnp.where(place[k] < place[to], jnp.maximum(now, marks[k]), now)
            carry.append(now)
            outs[to][size.state : size.state + INFO, :] = info_rows(now, now, size.dim)
            at = size.state + INFO
            for ride in rides:
                outs[to][at : at + ride.shape[0], :] = ride[...]
                at += ride.shape[0]
        for h in range(size.per):
            cols = slice(h * size.dim, (h + 1) * size.dim)
            span = span_of(spans_ref, size, me, h)
            for to in range(GROUP):
                steps = (place[to] * size.rows).astype(f32)
                total = jnp.where(outer == carry[to], decay(steps, span), 0.0) * enter[cols, :]
                for k in range(GROUP):
                    if k == to:
                        continue
                    gap = place[to] - 1 - place[k]
                    steps = (jnp.maximum(gap, 0) * size.rows).astype(f32)
                    live = jnp.logical_and(marks[k] == carry[to], gap >= 0)
                    total += jnp.where(live, decay(steps, span), 0.0) * ins[k][cols, :]
                outs[to][cols, :] = total

    shape = jax.ShapeDtypeStruct((size.state + INFO + extra, size.dim), f32)
    return call(
        body, "prefixes", (spans, *parts, entering, *riders), [shape] * GROUP,
        size.state * size.dim * 40, size.state * size.dim * 36,
    )


def whole_attended(size, seg, spans, queries, out_grad, gain, near, entering):
    def body(seg_ref, spans_ref, query_ref, grad_ref, gain_ref, near_ref, *refs):
        states, (out_ref, sums_ref) = refs[:GROUP], refs[GROUP:]
        group = partners()
        _, mark = markers(seg_ref, size)
        behind = position(size) + 1.0
        square = jnp.zeros((size.rows, size.dim), f32)
        cross = jnp.zeros((size.rows, size.dim), f32)
        for c in range(GROUP):
            live = mark == states[c][size.state : size.state + 1, :]
            for h in range(size.per):
                here = columns(size, group[c], h)
                span = span_of(spans_ref, size, group[c], h)
                weight = jnp.where(live, decay(behind, span), 0.0)
                query = query_ref[:, here]
                high, low = halves(states[c][h * size.dim : (h + 1) * size.dim, :])
                inter = dot(jnp.concatenate([query, query], 1), jnp.concatenate([high, low], 0))
                out = near_ref[:, here] + weight * inter
                out_ref[:, here] = out
                square += out * out
                cross += grad_ref[:, here].astype(f32) * gain_ref[:, here] * out
        square = jnp.sum(square.T, axis=0, keepdims=True)
        cross = jnp.sum(cross.T, axis=0, keepdims=True)
        index = lax.broadcasted_iota(jnp.int32, (8, size.rows), 0)
        sums_ref[...] = jnp.where(index == 0, square, jnp.where(index == 1, cross, 0.0))

    return call(
        body, "attended", (seg, spans, queries, out_grad, gain, near, *entering),
        [size.block, jax.ShapeDtypeStruct((8, size.rows), f32)],
        size.heads * 4 * size.rows * size.dim * size.dim, size.features * size.rows * 16,
    )


def output_grad_states(size, chunks, norm, seg, spans, queries, out_grad, gain, attended, sums, before=()):
    n = len(chunks)

    def body(seg_ref, spans_ref, query_ref, grad_ref, gain_ref, att_ref, sums_ref, *refs):
        outs = refs[len(before) :]
        group = partners()
        row, mark = markers(seg_ref, size)
        last, first = mark[size.rows - 1 :, :], mark[:1, :]
        wide = (size.dim, size.rows)
        square = jnp.broadcast_to(sums_ref[0:1, :], wide).T
        cross = jnp.broadcast_to(sums_ref[1:2, :], wide).T
        inv = lax.rsqrt(square / norm + 1e-06)
        pull = inv * inv * inv * cross / norm
        gone = position(size)
        for c, chunk in enumerate(chunks):
            back_ref, state_ref = outs[2 * c : 2 * c + 2]
            index = lax.broadcasted_iota(jnp.int32, (size.pad, size.dim), 0)
            gains = jnp.zeros((size.pad, size.dim), f32)
            for h in range(size.per):
                here = columns(size, group[chunk], h)
                cols = slice(h * size.dim, (h + 1) * size.dim)
                span = span_of(spans_ref, size, group[chunk], h)
                weight = jnp.where(mark == first, decay(gone, span), 0.0)
                grad = grad_ref[:, here].astype(f32) * inv
                att = att_ref[:, here]
                back = gain_ref[:, here] * grad - att * pull
                back_ref[:, cols] = back
                gains = jnp.where(index == h, jnp.sum(grad * att, axis=0, keepdims=True), gains)
                query = query_ref[:, here]
                high, low = halves(back * weight)
                state_ref[cols, :] = dot(
                    jnp.concatenate([query, query], 0), jnp.concatenate([high, low], 0), 0, 0
                )
            state_ref[size.state :, :] = info_rows(last, first, size.dim)
            outs[2 * n][chunk * size.pad : (chunk + 1) * size.pad, :] = gains
        for chunk in range(GROUP):
            if chunk not in chunks:
                at = slice(chunk * size.pad, (chunk + 1) * size.pad)
                held = refs[0][at, :] if before else jnp.zeros((size.pad, size.dim), f32)
                outs[2 * n][at, :] = held

    part = jax.ShapeDtypeStruct((size.rows, size.wide), f32)
    outs = call(
        body, "back", (seg, spans, queries, out_grad, gain, attended, sums, *before),
        [part, size.payload] * n + [size.gains],
        n * size.per * 4 * size.rows * size.dim * size.dim, n * size.wide * size.rows * 16,
    )
    return outs[0 : 2 * n : 2], outs[1 : 2 * n : 2], outs[2 * n]


def local_gradients(size, seg, spans, queries, key_rows, value_rows, back, entering):
    def body(seg_ref, spans_ref, query_ref, key_ref, value_ref, *refs):
        backs, states = refs[:GROUP], refs[GROUP : 2 * GROUP]
        out_hbm, local_key, local_value, done, sems = refs[2 * GROUP :]
        group = partners()
        row, mark = markers(seg_ref, size)
        gap, pairs = pair_weight(row, size)
        behind = position(size) + 1.0
        copies = []
        for c in range(GROUP):
            live = mark == states[c][size.state : size.state + 1, :]
            for h in range(size.per):
                here = columns(size, group[c], h)
                cols = slice(h * size.dim, (h + 1) * size.dim)
                span = span_of(spans_ref, size, group[c], h)
                weight = jnp.where(pairs, decay(gap, square_span(span, size)), 0.0)
                query, key, value = query_ref[:, here], key_ref[:, here], value_ref[:, here]
                high, low = halves(backs[c][:, cols])
                grads = dot(
                    jnp.concatenate([high, low], 1), jnp.concatenate([value, value], 1), 1, 1
                )
                grads_high, grads_low = halves(grads * weight)
                part = dot(
                    jnp.concatenate([grads_high, grads_low], 1), jnp.concatenate([key, key], 0)
                )
                state_high, state_low = halves(states[c][cols, :])
                inter = dot(
                    jnp.concatenate([high, high, low], 1),
                    jnp.concatenate([state_high, state_low, state_high], 1),
                    1, 1,
                )
                into = jnp.where(live, decay(behind, span), 0.0)
                done[c, :, cols] = (part + into * inter).astype(bf16)
                local_key[:, here] = dot(
                    jnp.concatenate([grads_high, grads_low], 0),
                    jnp.concatenate([query, query], 0),
                    0, 0,
                )
                score_high, score_low = halves(dot(query, key, 1, 1) * weight)
                local_value[:, here] = dot(
                    jnp.concatenate([score_high, score_high, score_low], 0),
                    jnp.concatenate([high, low, high], 0),
                    0, 0,
                )
            copies.append(
                pltpu.make_async_copy(
                    done.at[c], out_hbm.at[:, columns(size, group[c])], sems.at[c]
                )
            )
            copies[c].start()
        for copy in copies:
            copy.wait()

    return call(
        body, "gradients", (seg, spans, queries, key_rows, value_rows, *back, *entering),
        [jax.ShapeDtypeStruct((size.rows, size.features), bf16), size.block, size.block],
        size.heads * 26 * size.rows * size.dim * size.dim, size.features * size.rows * 24,
        [pltpu.VMEM((GROUP, size.rows, size.wide), bf16), pltpu.SemaphoreType.DMA((GROUP,))],
        None, [HBM, VMEM, VMEM],
    )


def final_gradients(size, seg, spans, key_rows, value_rows, local_key, local_value, entering):
    def body(seg_ref, spans_ref, key_ref, value_ref, local_key_ref, local_value_ref, *refs):
        states, (keys_hbm, values_hbm, gain_hbm) = refs[:GROUP], refs[GROUP : GROUP + 3]
        keys, values, gains, sems = refs[GROUP + 3 :]
        group = partners()
        _, mark = markers(seg_ref, size)
        left = size.rows - position(size)
        for c in range(GROUP):
            for h in range(size.per):
                total = None
                for k in range(GROUP):
                    at = size.state + INFO + (k ^ c) * size.pad + h
                    row = states[k][at : at + 1, :]
                    total = row if total is None else total + row
                gains[:, columns(size, group[c], h)] = total
        copies = [pltpu.make_async_copy(gains, gain_hbm, sems.at[2, 0])]
        copies[0].start()
        for c in range(GROUP):
            live = mark == states[c][size.state : size.state + 1, :]
            for h in range(size.per):
                here = columns(size, group[c], h)
                cols = slice(h * size.dim, (h + 1) * size.dim)
                span = span_of(spans_ref, size, group[c], h)
                weight = jnp.where(live, decay(left, span), 0.0)
                key, value = key_ref[:, here], value_ref[:, here]
                high, low = halves(states[c][cols, :])
                from_values = dot(
                    jnp.concatenate([value, value], 1), jnp.concatenate([high, low], 1), 1, 1
                )
                from_keys = dot(jnp.concatenate([key, key], 1), jnp.concatenate([high, low], 0))
                keys[c, :, cols] = (local_key_ref[:, here] + weight * from_values).astype(bf16)
                values[c, :, cols] = (local_value_ref[:, here] + weight * from_keys).astype(bf16)
            here = columns(size, group[c])
            for copy in (
                pltpu.make_async_copy(keys.at[c], keys_hbm.at[:, here], sems.at[0, c]),
                pltpu.make_async_copy(values.at[c], values_hbm.at[:, here], sems.at[1, c]),
            ):
                copy.start()
                copies.append(copy)
        for copy in copies:
            copy.wait()

    shape = jax.ShapeDtypeStruct((size.rows, size.features), bf16)
    held = pltpu.VMEM((GROUP, size.rows, size.wide), bf16)
    return call(
        body, "final", (seg, spans, key_rows, value_rows, local_key, local_value, *entering),
        [shape, shape, jax.ShapeDtypeStruct((1, size.features), f32)],
        size.heads * 8 * size.rows * size.dim * size.dim, size.features * size.rows * 24,
        [held, held, pltpu.VMEM((1, size.features), f32), pltpu.SemaphoreType.DMA((3, GROUP))],
        None, [HBM] * 3,
    )


def swap(array, distance):
    members = lax.axis_size("seq")
    return lax.ppermute(array, "seq", [(i, i ^ distance) for i in range(members)])


def shifted(array, by):
    members = lax.axis_size("seq")
    pairs = [(i, i + by) for i in range(members) if 0 <= i + by < members]
    return lax.ppermute(array, "seq", pairs)


def from_other_groups(size, backward, decay_span, total):
    members = lax.axis_size("seq")
    tokens = GROUP * size.rows
    longest = members * size.rows // 4
    needed = max(longest - 2, 0) // tokens + 1
    way = -GROUP if backward else GROUP
    result = shifted(total, way)
    reach = 1
    mine = lax.dynamic_slice(decay_span, (partners()[0] * size.per,), (size.per,))
    while reach < needed:
        incoming = shifted(result, way * reach)
        passes = incoming[size.state, 0] == result[size.state, 0]
        factor = jnp.where(passes, jnp.exp(-(reach * tokens) / mine), 0.0)
        factor = jnp.repeat(factor, size.dim)[:, None]
        result = result.at[: size.state].add(factor * incoming[: size.state])
        reach *= 2
    return result


def local(queries, key_rows, value_rows, segment_ids, decay_span, norm_gain, out_grad):
    size = Sizes(queries, decay_span)
    norm = size.features * lax.axis_size("head")
    members = lax.axis_size("seq")
    seg = segment_ids.reshape(1, size.rows)
    gain = norm_gain.reshape(1, size.features)
    spans = jnp.broadcast_to(decay_span[:, None], (size.heads, size.dim))
    common = (seg, spans)

    sent = key_value_states(size, (3, 1, 2), *common, key_rows, value_rows)
    kept = key_value_states(size, (0,), *common, key_rows, value_rows)
    states = [kept[0], sent[1], sent[2], sent[0]]
    near = nearby_attended(size, *common, queries, key_rows, value_rows)
    parts = [states[0]] + [swap(states[k], k) for k in range(1, GROUP)]
    total = group_total(size, False, spans, parts)[0]
    outer = from_other_groups(size, False, decay_span, total)
    outs = group_prefixes(size, False, spans, parts, outer)
    entering = [outs[0]] + [swap(outs[k], k) for k in range(1, GROUP)]

    attended, sums = whole_attended(size, *common, queries, out_grad, gain, near, entering)
    sums = lax.psum(sums, "head")
    normed = (norm, *common, queries, out_grad, gain, attended, sums)
    back_sent, sent, gains = output_grad_states(size, (3, 1, 2), *normed)
    back_kept, kept, gains = output_grad_states(size, (0,), *normed, (gains,))
    back = [back_kept[0], back_sent[1], back_sent[2], back_sent[0]]
    states = [kept[0], sent[1], sent[2], sent[0]]

    parts = [states[0]] + [swap(states[k], k) for k in range(1, GROUP)]
    distance, arrived = GROUP, jnp.zeros_like(gains)
    while distance < members:
        gains = gains + arrived if distance > GROUP else gains
        arrived = swap(gains, distance)
        distance *= 2
    total, gains = group_total(size, True, spans, parts, (gains, arrived))
    outer = from_other_groups(size, True, decay_span, total)
    outs = group_prefixes(size, True, spans, parts, outer, (gains,))
    leaving = [outs[0]] + [swap(outs[k], k) for k in range(1, GROUP)]

    query_grad, local_key, local_value = local_gradients(
        size, *common, queries, key_rows, value_rows, back, entering
    )
    key_grad, value_grad, gain_grad = final_gradients(
        size, *common, key_rows, value_rows, local_key, local_value, leaving
    )
    return query_grad, key_grad, value_grad, gain_grad.reshape(size.features)


def solution(mesh):
    rows = P("seq", "head")
    in_specs = (rows, rows, rows, P("seq"), P("head"), P("head"), rows)
    return jax.shard_map(
        local, mesh=mesh, in_specs=in_specs, out_specs=(rows, rows, rows, P("head")), check_vma=False
    )
```

time: 108 us -> 89.1 us (0.82)
  Pallas kernels: 33.3 us -> 15.5 us
  waiting for transfers between devices: 38.3 us -> 40.9 us
  local copies, waits for them, and re-layouts: 5.83 us -> 3.43 us
    pallas_call x16 -> x12, Pallas kernels: 33.3 us -> 15.5 us  [call(): pl.pallas_call(body, out_shape=outputs, in_specs=in_specs if in_specs is...]
    ppermute x2, waiting for transfers between devices: 4.43 us -> 13.2 us  [shifted(): return lax.ppermute(array, 'seq', pairs)]
    ppermute x14, waiting for transfers between devices: 33.9 us -> 27.7 us  [swap(): lax.ppermute(array, 'seq', [(i, i ^ distance) for i in range(members)])]
    unnamed x30, local copies, waits for them, and re-layouts: 5.83 us -> 3.36 us
  transfers between devices with their start and end apart: 16 -> 16, of which waited for: 11 -> 11; matrix products, arithmetic and copies ran while one was open for 0% -> 0% of each run, Pallas kernels for 16% -> 11%
where the time goes in v2:
time: 89.1 us; the launch traced here: 88.8 us
  waiting for transfers between devices  40.9 us (46%)
  starting transfers between devices  25.7 us (29%)
  Pallas kernels  15.5 us (17%)
  local copies, waits for them, and re-layouts  3.43 us (4%)
  blocking collectives  2.47 us (3%)
    ppermute x14, waiting for transfers between devices, swap(): lax.ppermute(array, 'seq', [(i, i ^ distance) for i in range(members)])  27.7 us
    ppermute x14, starting transfers between devices, swap(): lax.ppermute(array, 'seq', [(i, i ^ distance) for i in range(members)])  20.8 us
    pallas_call x12, Pallas kernels, call(): pl.pallas_call(body, out_shape=outputs, in_specs=in_specs if in_specs is...  15.5 us
    ppermute x2, waiting for transfers between devices, shifted(): return lax.ppermute(array, 'seq', pairs)  13.2 us
    ppermute x2, starting transfers between devices, shifted(): return lax.ppermute(array, 'seq', pairs)  4.92 us
    unnamed x30, local copies, waits for them, and re-layouts  3.36 us
    psum x1, blocking collectives, local(): sums = lax.psum(sums, 'head')  2.47 us
  transfers between devices with their start and end apart: 16, of which 11 were waited for; matrix products, arithmetic and copies ran while one was open for 0% of the time, Pallas kernels for 11%

profile of v2, /device:TPU:0, one launch (start us, length us, event | category | flops | bytes accessed | tf_op | source)
XLA Modules:
  0.0 88.8 jit_solution(3210052826647380154)
XLA Ops:
  0.6 0.6 copy-done.14
  1.3 0.1 broadcast_in_dim.2.spans_ref
  1.4 0.6 copy-done.13
  1.9 1.0 %copy-done.1 = bf16[128,2048]{1,0:T(8,128)(2,1)S(1)} copy-done((bf16[128,2048]{1,0:T(8,128)(2,1)S(1)}, bf16[128,2048]{1,0:T(8,128)(2,1)}, u32[]{:S(2)}) %copy-start.1) | copy-done | bytes 524312
  3.0 1.0 %copy-done.3 = bf16[128,2048]{1,0:T(8,128)(2,1)S(1)} copy-done((bf16[128,2048]{1,0:T(8,128)(2,1)S(1)}, bf16[128,2048]{1,0:T(8,128)(2,1)}, u32[]{:S(2)}) %copy-start.3) | copy-done | bytes 524312
  4.0 1.1 %states.3 = (f32[520,128]{1,0:T(8,128)S(1)}, f32[520,128]{1,0:T(8,128)S(1)}, f32[520,128]{1,0:T(8,128)S(1)}) custom-call(s32[1,128]{1,0:T(1,128)S(1)} %bitcast.6, f32[16,128]{1,0:T(8,128)S(1)} %broadcast_in_dim.2.spans_ref, bf16[128,2048]{1,0:T(8,128)(2,1)S(1)} %copy-done.1, bf16[128,2048]{1,0:T(8,128)(2,1)S(1)} %copy-done.3), custom_call_target="tpu_custom_call" | custom-call | flops 100663296 | bytes 1572864 | tf_op jit(solution)/shard_map/states/pallas_call | solution.py:92
  5.1 3.0 %collective-permute-start = (f32[520,128]{1,0:T(8,128)S(1)}, f32[520,128]{1,0:T(8,128)S(1)}, u32[]{:S(2)}, u32[]{:S(2)}) collective-permute-start(f32[520,128]{1,0:T(8,128)S(1)} %get-tuple-element.35), channel_id=1, source_target_pairs={{0,2},{2,0},{4,6},{6,4},{8,10},{10,8},{12,14},{14,12},{16,18},{18,... | collective-permute-start | bytes 798728 | tf_op jit(solution)/shard_map/ppermute | solution.py:447
  8.1 1.5 %collective-permute-start.1 = (f32[520,128]{1,0:T(8,128)S(1)}, f32[520,128]{1,0:T(8,128)S(1)}, u32[]{:S(2)}, u32[]{:S(2)}) collective-permute-start(f32[520,128]{1,0:T(8,128)S(1)} %get-tuple-element.36), channel_id=1, source_target_pairs={{0,4},{2,6},{4,0},{6,2},{8,12},{10,14},{12,8},{14,10},{16,20},{18,... | collective-permute-start | bytes 798728 | tf_op jit(solution)/shard_map/ppermute | solution.py:447
  9.7 0.0 collective-permute-start.2
  9.7 0.4 states.2.refs_0_
  10.1 5.2 %collective-permute-done.refs_1_ = f32[520,128]{1,0:T(8,128)S(1)} collective-permute-done((f32[520,128]{1,0:T(8,128)S(1)}, f32[520,128]{1,0:T(8,128)S(1)}, u32[]{:S(2)}, u32[]{:S(2)}) %collective-permute-start) | collective-permute-done | bytes 266272 | tf_op jit(solution)/shard_map/ppermute | solution.py:447
  15.4 6.3 %collective-permute-done.1.refs_2_ = f32[520,128]{1,0:T(8,128)S(1)} collective-permute-done((f32[520,128]{1,0:T(8,128)S(1)}, f32[520,128]{1,0:T(8,128)S(1)}, u32[]{:S(2)}, u32[]{:S(2)}) %collective-permute-start.1) | collective-permute-done | bytes 266272 | tf_op jit(solution)/shard_map/ppermute | solution.py:447
  21.7 0.1 total.2
  21.8 0.0 copy-start
  21.8 0.0 copy-start.2
  21.8 3.6 %collective-permute-start.3 = (f32[520,128]{1,0:T(8,128)S(1)}, f32[520,128]{1,0:T(8,128)S(1)}, u32[]{:S(2)}, u32[]{:S(2)}) collective-permute-start(f32[520,128]{1,0:T(8,128)S(1)} %total.2), channel_id=1, source_target_pairs={{0,8},{2,10},{4,12},{6,14},{8,16},{10,18},{12,20},{14,22},{16,24},... | collective-permute-start | bytes 798728 | tf_op jit(solution)/shard_map/ppermute | solution.py:453
  25.5 4.5 %collective-permute-done.3.refs_4_ = f32[520,128]{1,0:T(8,128)S(1)} collective-permute-done((f32[520,128]{1,0:T(8,128)S(1)}, f32[520,128]{1,0:T(8,128)S(1)}, u32[]{:S(2)}, u32[]{:S(2)}) %collective-permute-start.3) | collective-permute-done | bytes 266272 | tf_op jit(solution)/shard_map/ppermute | solution.py:453
  30.0 0.4 prefixes.2
  30.4 1.5 %collective-permute-start.4 = (f32[520,128]{1,0:T(8,128)S(1)}, f32[520,128]{1,0:T(8,128)S(1)}, u32[]{:S(2)}, u32[]{:S(2)}) collective-permute-start(f32[520,128]{1,0:T(8,128)S(1)} %get-tuple-element.39), channel_id=1, source_target_pairs={{0,2},{2,0},{4,6},{6,4},{8,10},{10,8},{12,14},{14,12},{16,18},{18,... | collective-permute-start | bytes 798728 | tf_op jit(solution)/shard_map/ppermute | solution.py:447
  31.9 0.5 collective-permute-start.5
  32.4 1.5 %collective-permute-start.6 = (f32[520,128]{1,0:T(8,128)S(1)}, f32[520,128]{1,0:T(8,128)S(1)}, u32[]{:S(2)}, u32[]{:S(2)}) collective-permute-start(f32[520,128]{1,0:T(8,128)S(1)} %get-tuple-element.41), channel_id=1, source_target_pairs={{0,6},{2,4},{4,2},{6,0},{8,14},{10,12},{12,10},{14,8},{16,22},{18,... | collective-permute-start | bytes 798728 | tf_op jit(solution)/shard_map/ppermute | solution.py:447
  33.9 2.7 %nearby.1.near_ref = f32[128,2048]{1,0:T(8,128)S(1)} custom-call(s32[1,128]{1,0:T(1,128)S(1)} %bitcast.8, f32[16,128]{1,0:T(8,128)S(1)} %broadcast_in_dim.2.spans_ref, bf16[128,2048]{1,0:T(8,128)(2,1)S(1)} %copy-done, bf16[128,2048]{1,0:T(8,128)(2,1)S(1)} %copy-done.2, bf16[128,2048]{1,0:T(8,128)(2,1)S(1)} %copy-done.4), custom_call_target="tpu_custom_call" | custom-call | flops 201326592 | bytes 2621440 | tf_op jit(solution)/shard_map/nearby/pallas_call | solution.py:92
  36.6 2.8 %collective-permute-done.4.refs_1_.refs_5_ = f32[520,128]{1,0:T(8,128)S(1)} collective-permute-done((f32[520,128]{1,0:T(8,128)S(1)}, f32[520,128]{1,0:T(8,128)S(1)}, u32[]{:S(2)}, u32[]{:S(2)}) %collective-permute-start.4) | collective-permute-done | bytes 266272 | tf_op jit(solution)/shard_map/ppermute | solution.py:447
  39.4 4.2 %collective-permute-done.5.refs_2_.refs_6_ = f32[520,128]{1,0:T(8,128)S(1)} collective-permute-done((f32[520,128]{1,0:T(8,128)S(1)}, f32[520,128]{1,0:T(8,128)S(1)}, u32[]{:S(2)}, u32[]{:S(2)}) %collective-permute-start.5) | collective-permute-done | bytes 266272 | tf_op jit(solution)/shard_map/ppermute | solution.py:447
  43.7 0.9 attended.1
  44.6 2.5 %psum.7.sums_ref = f32[8,128]{1,0:T(8,128)S(1)} all-reduce(f32[8,128]{1,0:T(8,128)S(1)} %get-tuple-element.43), channel_id=1, replica_groups=mesh['seq'=16,'head'=2] {'head'}, use_global_device_ids=true, to_apply=%region_0.0 | all-reduce | flops 1024 | bytes 8192 | tf_op jit(solution)/shard_map/psum | solution.py:495
  47.0 0.8 back.2
  47.8 0.4 collective-permute-start.7
  48.3 1.4 %collective-permute-start.8 = (f32[520,128]{1,0:T(8,128)S(1)}, f32[520,128]{1,0:T(8,128)S(1)}, u32[]{:S(2)}, u32[]{:S(2)}) collective-permute-start(f32[520,128]{1,0:T(8,128)S(1)} %get-tuple-element.54), channel_id=1, source_target_pairs={{0,4},{2,6},{4,0},{6,2},{8,12},{10,14},{12,8},{14,10},{16,20},{18,... | collective-permute-start | bytes 798728 | tf_op jit(solution)/shard_map/ppermute | solution.py:447
  49.6 1.8 %collective-permute-start.9 = (f32[520,128]{1,0:T(8,128)S(1)}, f32[520,128]{1,0:T(8,128)S(1)}, u32[]{:S(2)}, u32[]{:S(2)}) collective-permute-start(f32[520,128]{1,0:T(8,128)S(1)} %get-tuple-element.55), channel_id=1, source_target_pairs={{0,6},{2,4},{4,2},{6,0},{8,14},{10,12},{12,10},{14,8},{16,22},{18,... | collective-permute-start | bytes 798728 | tf_op jit(solution)/shard_map/ppermute | solution.py:447
  51.4 0.4 back.3
  51.8 2.5 %collective-permute-start.10 = (f32[32,128]{1,0:T(8,128)S(1)}, f32[32,128]{1,0:T(8,128)S(1)}, u32[]{:S(2)}, u32[]{:S(2)}) collective-permute-start(f32[32,128]{1,0:T(8,128)S(1)} %get-tuple-element.56), channel_id=1, source_target_pairs={{0,8},{2,10},{4,12},{6,14},{8,0},{10,2},{12,4},{14,6},{16,24},{18,... | collective-permute-start | bytes 49160 | tf_op jit(solution)/shard_map/ppermute | solution.py:447
  54.4 1.7 %collective-permute-done.10 = f32[32,128]{1,0:T(8,128)S(1)} collective-permute-done((f32[32,128]{1,0:T(8,128)S(1)}, f32[32,128]{1,0:T(8,128)S(1)}, u32[]{:S(2)}, u32[]{:S(2)}) %collective-permute-start.10) | collective-permute-done | bytes 16416 | tf_op jit(solution)/shard_map/ppermute | solution.py:447
  56.1 3.0 %collective-permute-start.11 = (f32[32,128]{1,0:T(8,128)S(1)}, f32[32,128]{1,0:T(8,128)S(1)}, u32[]{:S(2)}, u32[]{:S(2)}) collective-permute-start(f32[32,128]{1,0:T(8,128)S(1)} %add.5.refs_4_), channel_id=1, source_target_pairs={{0,16},{2,18},{4,20},{6,22},{8,24},{10,26},{12,28},{14,30},{16,0},... | collective-permute-start | bytes 49160 | tf_op jit(solution)/shard_map/ppermute | solution.py:447
  59.1 1.7 %collective-permute-done.11.refs_5_ = f32[32,128]{1,0:T(8,128)S(1)} collective-permute-done((f32[32,128]{1,0:T(8,128)S(1)}, f32[32,128]{1,0:T(8,128)S(1)}, u32[]{:S(2)}, u32[]{:S(2)}) %collective-permute-start.11) | collective-permute-done | bytes 16416 | tf_op jit(solution)/shard_map/ppermute | solution.py:447
  60.9 0.0 collective-permute-done.7.refs_1_
  60.9 1.3 %collective-permute-done.8.refs_2_ = f32[520,128]{1,0:T(8,128)S(1)} collective-permute-done((f32[520,128]{1,0:T(8,128)S(1)}, f32[520,128]{1,0:T(8,128)S(1)}, u32[]{:S(2)}, u32[]{:S(2)}) %collective-permute-start.8) | collective-permute-done | bytes 266272 | tf_op jit(solution)/shard_map/ppermute | solution.py:447
  62.2 0.1 total.3
  62.3 1.3 %collective-permute-start.12 = (f32[520,128]{1,0:T(8,128)S(1)}, f32[520,128]{1,0:T(8,128)S(1)}, u32[]{:S(2)}, u32[]{:S(2)}) collective-permute-start(f32[520,128]{1,0:T(8,128)S(1)} %get-tuple-element.57), channel_id=1, source_target_pairs={{8,0},{10,2},{12,4},{14,6},{16,8},{18,10},{20,12},{22,14},{24,16},... | collective-permute-start | bytes 798728 | tf_op jit(solution)/shard_map/ppermute | solution.py:453
  63.6 8.7 %collective-permute-done.12.refs_4_ = f32[520,128]{1,0:T(8,128)S(1)} collective-permute-done((f32[520,128]{1,0:T(8,128)S(1)}, f32[520,128]{1,0:T(8,128)S(1)}, u32[]{:S(2)}, u32[]{:S(2)}) %collective-permute-start.12) | collective-permute-done | bytes 266272 | tf_op jit(solution)/shard_map/ppermute | solution.py:453
  72.3 0.3 prefixes.3
  72.6 1.5 %collective-permute-start.13 = (f32[552,128]{1,0:T(8,128)S(1)}, f32[552,128]{1,0:T(8,128)S(1)}, u32[]{:S(2)}, u32[]{:S(2)}) collective-permute-start(f32[552,128]{1,0:T(8,128)S(1)} %get-tuple-element.60), channel_id=1, source_target_pairs={{0,2},{2,0},{4,6},{6,4},{8,10},{10,8},{12,14},{14,12},{16,18},{18,... | collective-permute-start | bytes 847880 | tf_op jit(solution)/shard_map/ppermute | solution.py:447
  74.1 0.7 collective-permute-start.14
  74.7 1.4 %collective-permute-start.15 = (f32[552,128]{1,0:T(8,128)S(1)}, f32[552,128]{1,0:T(8,128)S(1)}, u32[]{:S(2)}, u32[]{:S(2)}) collective-permute-start(f32[552,128]{1,0:T(8,128)S(1)} %get-tuple-element.62), channel_id=1, source_target_pairs={{0,6},{2,4},{4,2},{6,0},{8,14},{10,12},{12,10},{14,8},{16,22},{18,... | collective-permute-start | bytes 847880 | tf_op jit(solution)/shard_map/ppermute | solution.py:447
  76.2 6.7 %gradients.1 = (bf16[128,2048]{1,0:T(8,128)(2,1)}, f32[128,2048]{1,0:T(8,128)S(1)}, f32[128,2048]{1,0:T(8,128)S(1)}) custom-call(s32[1,128]{1,0:T(1,128)S(1)} %bitcast.12, f32[16,128]{1,0:T(8,128)S(1)} %broadcast_in_dim.2.spans_ref, bf16[128,2048]{1,0:T(8,128)(2,1)S(1)} %copy-done, bf16[128,2048]{1,0:T(8,128)(2,1)S(1)} %copy-done.2, ...), custom_call_target="tpu_custom_call" | custom-call | flops 872415232 | bytes 6291456 | tf_op jit(solution)/shard_map/gradients/pallas_call | solution.py:92
  82.9 2.5 %collective-permute-done.14.refs_2_ = f32[552,128]{1,0:T(8,128)S(1)} collective-permute-done((f32[552,128]{1,0:T(8,128)S(1)}, f32[552,128]{1,0:T(8,128)S(1)}, u32[]{:S(2)}, u32[]{:S(2)}) %collective-permute-start.14) | collective-permute-done | bytes 282656 | tf_op jit(solution)/shard_map/ppermute | solution.py:447
  85.4 1.8 %collective-permute-done.15.refs_3_ = f32[552,128]{1,0:T(8,128)S(1)} collective-permute-done((f32[552,128]{1,0:T(8,128)S(1)}, f32[552,128]{1,0:T(8,128)S(1)}, u32[]{:S(2)}, u32[]{:S(2)}) %collective-permute-start.15) | collective-permute-done | bytes 282656 | tf_op jit(solution)/shard_map/ppermute | solution.py:447
  87.2 1.6 %final.1 = (bf16[128,2048]{1,0:T(8,128)(2,1)}, bf16[128,2048]{1,0:T(8,128)(2,1)}, f32[1,2048]{1,0:T(1,128)}) custom-call(s32[1,128]{1,0:T(1,128)S(1)} %bitcast.13, f32[16,128]{1,0:T(8,128)S(1)} %broadcast_in_dim.2.spans_ref, bf16[128,2048]{1,0:T(8,128)(2,1)S(1)} %copy-done.2, bf16[128,2048]{1,0:T(8,128)(2,1)S(1)} %copy-done.4, ...), custom_call_target="tpu_custom_call" | custom-call | flops 268435456 | bytes 6291456 | tf_op jit(solution)/shard_map/final/pallas_call | solution.py:92
  (29 shorter events, 0.1 us)
Async XLA Ops:
  0.6 0.7 copy-start.14
  1.3 0.7 copy-start.13
  1.9 1.0 %copy-start.1 = (bf16[128,2048]{1,0:T(8,128)(2,1)S(1)}, bf16[128,2048]{1,0:T(8,128)(2,1)}, u32[]{:S(2)}) copy-start(bf16[128,2048]{1,0:T(8,128)(2,1)} %key_ref.5) | copy-start | bytes 1572868
  3.0 1.0 %copy-start.3 = (bf16[128,2048]{1,0:T(8,128)(2,1)S(1)}, bf16[128,2048]{1,0:T(8,128)(2,1)}, u32[]{:S(2)}) copy-start(bf16[128,2048]{1,0:T(8,128)(2,1)} %value_ref.5) | copy-start | bytes 1572868
  5.1 10.2 %collective-permute-start = (f32[520,128]{1,0:T(8,128)S(1)}, f32[520,128]{1,0:T(8,128)S(1)}, u32[]{:S(2)}, u32[]{:S(2)}) collective-permute-start(f32[520,128]{1,0:T(8,128)S(1)} %get-tuple-element.35), channel_id=1, source_target_pairs={{0,2},{2,0},{4,6},{6,4},{8,10},{10,8},{12,14},{14,12},{16,18},{18,... | collective-permute-start | bytes 798728 | tf_op jit(solution)/shard_map/ppermute | solution.py:447
  8.1 13.6 %collective-permute-start.1 = (f32[520,128]{1,0:T(8,128)S(1)}, f32[520,128]{1,0:T(8,128)S(1)}, u32[]{:S(2)}, u32[]{:S(2)}) collective-permute-start(f32[520,128]{1,0:T(8,128)S(1)} %get-tuple-element.36), channel_id=1, source_target_pairs={{0,4},{2,6},{4,0},{6,2},{8,12},{10,14},{12,8},{14,10},{16,20},{18,... | collective-permute-start | bytes 798728 | tf_op jit(solution)/shard_map/ppermute | solution.py:447
  9.7 12.0 %collective-permute-start.2 = (f32[520,128]{1,0:T(8,128)S(1)}, f32[520,128]{1,0:T(8,128)S(1)}, u32[]{:S(2)}, u32[]{:S(2)}) collective-permute-start(f32[520,128]{1,0:T(8,128)S(1)} %get-tuple-element.37), channel_id=1, source_target_pairs={{0,6},{2,4},{4,2},{6,0},{8,14},{10,12},{12,10},{14,8},{16,22},{18,... | collective-permute-start | bytes 798728 | tf_op jit(solution)/shard_map/ppermute | solution.py:447
  21.7 12.2 %copy-start.4 = (bf16[128,2048]{1,0:T(8,128)(2,1)S(1)}, bf16[128,2048]{1,0:T(8,128)(2,1)}, u32[]{:S(2)}) copy-start(bf16[128,2048]{1,0:T(8,128)(2,1)} %value_ref.5) | copy-start | bytes 1572868
  21.8 12.1 %copy-start = (bf16[128,2048]{1,0:T(8,128)(2,1)S(1)}, bf16[128,2048]{1,0:T(8,128)(2,1)}, u32[]{:S(2)}) copy-start(bf16[128,2048]{1,0:T(8,128)(2,1)} %query_ref.9) | copy-start | bytes 1572868
  21.8 12.1 %copy-start.2 = (bf16[128,2048]{1,0:T(8,128)(2,1)S(1)}, bf16[128,2048]{1,0:T(8,128)(2,1)}, u32[]{:S(2)}) copy-start(bf16[128,2048]{1,0:T(8,128)(2,1)} %key_ref.5) | copy-start | bytes 1572868
  21.8 8.2 %collective-permute-start.3 = (f32[520,128]{1,0:T(8,128)S(1)}, f32[520,128]{1,0:T(8,128)S(1)}, u32[]{:S(2)}, u32[]{:S(2)}) collective-permute-start(f32[520,128]{1,0:T(8,128)S(1)} %total.2), channel_id=1, source_target_pairs={{0,8},{2,10},{4,12},{6,14},{8,16},{10,18},{12,20},{14,22},{16,24},... | collective-permute-start | bytes 798728 | tf_op jit(solution)/shard_map/ppermute | solution.py:453
  30.4 9.0 %collective-permute-start.4 = (f32[520,128]{1,0:T(8,128)S(1)}, f32[520,128]{1,0:T(8,128)S(1)}, u32[]{:S(2)}, u32[]{:S(2)}) collective-permute-start(f32[520,128]{1,0:T(8,128)S(1)} %get-tuple-element.39), channel_id=1, source_target_pairs={{0,2},{2,0},{4,6},{6,4},{8,10},{10,8},{12,14},{14,12},{16,18},{18,... | collective-permute-start | bytes 798728 | tf_op jit(solution)/shard_map/ppermute | solution.py:447
  31.9 11.8 %collective-permute-start.5 = (f32[520,128]{1,0:T(8,128)S(1)}, f32[520,128]{1,0:T(8,128)S(1)}, u32[]{:S(2)}, u32[]{:S(2)}) collective-permute-start(f32[520,128]{1,0:T(8,128)S(1)} %get-tuple-element.40), channel_id=1, source_target_pairs={{0,4},{2,6},{4,0},{6,2},{8,12},{10,14},{12,8},{14,10},{16,20},{18,... | collective-permute-start | bytes 798728 | tf_op jit(solution)/shard_map/ppermute | solution.py:447
  32.4 11.2 %copy-start.5 = (bf16[128,2048]{1,0:T(8,128)(2,1)S(1)}, bf16[128,2048]{1,0:T(8,128)(2,1)}, u32[]{:S(2)}) copy-start(bf16[128,2048]{1,0:T(8,128)(2,1)} %grad_ref.5) | copy-start | bytes 1572868
  32.4 11.2 %collective-permute-start.6 = (f32[520,128]{1,0:T(8,128)S(1)}, f32[520,128]{1,0:T(8,128)S(1)}, u32[]{:S(2)}, u32[]{:S(2)}) collective-permute-start(f32[520,128]{1,0:T(8,128)S(1)} %get-tuple-element.41), channel_id=1, source_target_pairs={{0,6},{2,4},{4,2},{6,0},{8,14},{10,12},{12,10},{14,8},{16,22},{18,... | collective-permute-start | bytes 798728 | tf_op jit(solution)/shard_map/ppermute | solution.py:447
  33.9 9.7 %copy-start.12 = (f32[2048]{0:T(1024)S(1)}, f32[2048]{0:T(1024)}, u32[]{:S(2)}) copy-start(f32[2048]{0:T(1024)} %param.12) | copy-start | bytes 24580
  39.4 5.1 %copy-start.6 = (f32[520,128]{1,0:T(8,128)}, f32[520,128]{1,0:T(8,128)S(1)}, u32[]{:S(2)}) copy-start(f32[520,128]{1,0:T(8,128)S(1)} %collective-permute-done.4.refs_1_.refs_5_) | copy-start | bytes 798724
  43.6 0.9 %copy-start.8 = (f32[520,128]{1,0:T(8,128)}, f32[520,128]{1,0:T(8,128)S(1)}, u32[]{:S(2)}) copy-start(f32[520,128]{1,0:T(8,128)S(1)} %collective-permute-done.5.refs_2_.refs_6_) | copy-start | bytes 798724
  43.6 0.9 %copy-start.10 = (f32[520,128]{1,0:T(8,128)}, f32[520,128]{1,0:T(8,128)S(1)}, u32[]{:S(2)}) copy-start(f32[520,128]{1,0:T(8,128)S(1)} %collective-permute-done.6.refs_3_.refs_7_) | copy-start | bytes 798724
  47.8 13.0 %collective-permute-start.7 = (f32[520,128]{1,0:T(8,128)S(1)}, f32[520,128]{1,0:T(8,128)S(1)}, u32[]{:S(2)}, u32[]{:S(2)}) collective-permute-start(f32[520,128]{1,0:T(8,128)S(1)} %get-tuple-element.53), channel_id=1, source_target_pairs={{0,2},{2,0},{4,6},{6,4},{8,10},{10,8},{12,14},{14,12},{16,18},{18,... | collective-permute-start | bytes 798728 | tf_op jit(solution)/shard_map/ppermute | solution.py:447
  48.3 13.9 %collective-permute-start.8 = (f32[520,128]{1,0:T(8,128)S(1)}, f32[520,128]{1,0:T(8,128)S(1)}, u32[]{:S(2)}, u32[]{:S(2)}) collective-permute-start(f32[520,128]{1,0:T(8,128)S(1)} %get-tuple-element.54), channel_id=1, source_target_pairs={{0,4},{2,6},{4,0},{6,2},{8,12},{10,14},{12,8},{14,10},{16,20},{18,... | collective-permute-start | bytes 798728 | tf_op jit(solution)/shard_map/ppermute | solution.py:447
  49.6 12.6 %collective-permute-start.9 = (f32[520,128]{1,0:T(8,128)S(1)}, f32[520,128]{1,0:T(8,128)S(1)}, u32[]{:S(2)}, u32[]{:S(2)}) collective-permute-start(f32[520,128]{1,0:T(8,128)S(1)} %get-tuple-element.55), channel_id=1, source_target_pairs={{0,6},{2,4},{4,2},{6,0},{8,14},{10,12},{12,10},{14,8},{16,22},{18,... | collective-permute-start | bytes 798728 | tf_op jit(solution)/shard_map/ppermute | solution.py:447
  51.8 4.3 %collective-permute-start.10 = (f32[32,128]{1,0:T(8,128)S(1)}, f32[32,128]{1,0:T(8,128)S(1)}, u32[]{:S(2)}, u32[]{:S(2)}) collective-permute-start(f32[32,128]{1,0:T(8,128)S(1)} %get-tuple-element.56), channel_id=1, source_target_pairs={{0,8},{2,10},{4,12},{6,14},{8,0},{10,2},{12,4},{14,6},{16,24},{18,... | collective-permute-start | bytes 49160 | tf_op jit(solution)/shard_map/ppermute | solution.py:447
  56.1 4.7 %collective-permute-start.11 = (f32[32,128]{1,0:T(8,128)S(1)}, f32[32,128]{1,0:T(8,128)S(1)}, u32[]{:S(2)}, u32[]{:S(2)}) collective-permute-start(f32[32,128]{1,0:T(8,128)S(1)} %add.5.refs_4_), channel_id=1, source_target_pairs={{0,16},{2,18},{4,20},{6,22},{8,24},{10,26},{12,28},{14,30},{16,0},... | collective-permute-start | bytes 49160 | tf_op jit(solution)/shard_map/ppermute | solution.py:447
  62.3 10.0 %collective-permute-start.12 = (f32[520,128]{1,0:T(8,128)S(1)}, f32[520,128]{1,0:T(8,128)S(1)}, u32[]{:S(2)}, u32[]{:S(2)}) collective-permute-start(f32[520,128]{1,0:T(8,128)S(1)} %get-tuple-element.57), channel_id=1, source_target_pairs={{8,0},{10,2},{12,4},{14,6},{16,8},{18,10},{20,12},{22,14},{24,16},... | collective-permute-start | bytes 798728 | tf_op jit(solution)/shard_map/ppermute | solution.py:453
  72.3 3.9 %copy-start.7 = (f32[520,128]{1,0:T(8,128)S(1)}, f32[520,128]{1,0:T(8,128)}, u32[]{:S(2)}) copy-start(f32[520,128]{1,0:T(8,128)} %copy-done.6) | copy-start | bytes 798724
  72.3 3.9 %copy-start.9 = (f32[520,128]{1,0:T(8,128)S(1)}, f32[520,128]{1,0:T(8,128)}, u32[]{:S(2)}) copy-start(f32[520,128]{1,0:T(8,128)} %copy-done.8) | copy-start | bytes 798724
  72.3 3.9 %copy-start.11 = (f32[520,128]{1,0:T(8,128)S(1)}, f32[520,128]{1,0:T(8,128)}, u32[]{:S(2)}) copy-start(f32[520,128]{1,0:T(8,128)} %copy-done.10) | copy-start | bytes 798724
  72.6 10.2 %collective-permute-start.13 = (f32[552,128]{1,0:T(8,128)S(1)}, f32[552,128]{1,0:T(8,128)S(1)}, u32[]{:S(2)}, u32[]{:S(2)}) collective-permute-start(f32[552,128]{1,0:T(8,128)S(1)} %get-tuple-element.60), channel_id=1, source_target_pairs={{0,2},{2,0},{4,6},{6,4},{8,10},{10,8},{12,14},{14,12},{16,18},{18,... | collective-permute-start | bytes 847880 | tf_op jit(solution)/shard_map/ppermute | solution.py:447
  74.1 11.3 %collective-permute-start.14 = (f32[552,128]{1,0:T(8,128)S(1)}, f32[552,128]{1,0:T(8,128)S(1)}, u32[]{:S(2)}, u32[]{:S(2)}) collective-permute-start(f32[552,128]{1,0:T(8,128)S(1)} %get-tuple-element.61), channel_id=1, source_target_pairs={{0,4},{2,6},{4,0},{6,2},{8,12},{10,14},{12,8},{14,10},{16,20},{18,... | collective-permute-start | bytes 847880 | tf_op jit(solution)/shard_map/ppermute | solution.py:447
  74.7 12.5 %collective-permute-start.15 = (f32[552,128]{1,0:T(8,128)S(1)}, f32[552,128]{1,0:T(8,128)S(1)}, u32[]{:S(2)}, u32[]{:S(2)}) collective-permute-start(f32[552,128]{1,0:T(8,128)S(1)} %get-tuple-element.62), channel_id=1, source_target_pairs={{0,6},{2,4},{4,2},{6,0},{8,14},{10,12},{12,10},{14,8},{16,22},{18,... | collective-permute-start | bytes 847880 | tf_op jit(solution)/shard_map/ppermute | solution.py:447

commit v3 on v2

v3 whole, which is shorter than its diff:
```python
import jax
import jax.numpy as jnp
from jax import lax
from jax.experimental import pallas as pl
from jax.experimental.pallas import tpu as pltpu
from jax.sharding import PartitionSpec as P

GROUP = 4
INFO = 8
FAR = 1e9
f32 = jnp.float32
bf16 = jnp.bfloat16
HBM = pl.BlockSpec(memory_space=pltpu.HBM)
VMEM = pl.BlockSpec(memory_space=pltpu.VMEM)


def dot(a, b, over_a=1, over_b=0):
    return lax.dot_general(a, b, (((over_a,), (over_b,)), ((), ())), preferred_element_type=f32)


def halves(x):
    high = x.astype(bf16)
    return high, (x - high.astype(f32)).astype(bf16)


def decay(steps, span):
    return jnp.exp(-steps / span)


class Sizes:
    def __init__(self, queries, decay_span):
        self.rows = queries.shape[0]
        self.heads = decay_span.shape[0]
        self.features = queries.shape[1]
        self.dim = self.features // self.heads
        self.per = self.heads // GROUP
        self.wide = self.per * self.dim
        self.pad = -(-self.per // 8) * 8
        self.waves = 2 if self.per % 2 == 0 else 1
        self.each = self.per // self.waves
        self.state = self.each * self.dim
        self.payload = jax.ShapeDtypeStruct((self.state + INFO, self.dim), f32)
        self.block = jax.ShapeDtypeStruct((self.rows, self.features), f32)
        self.gains = jax.ShapeDtypeStruct((GROUP * self.pad, self.dim), f32)


def position(size):
    return lax.broadcasted_iota(jnp.int32, (size.rows, size.dim), 0).astype(f32)


def pair_weight(mark, size):
    shape = (size.rows, size.rows)
    here = mark if size.rows == size.dim else jnp.broadcast_to(mark[:, :1], shape)
    at = lax.broadcasted_iota(jnp.int32, shape, 0)
    by = lax.broadcasted_iota(jnp.int32, shape, 1)
    live = jnp.logical_and(at >= by, here == here.T)
    return jnp.maximum(at - by, 0).astype(f32), live


def info_rows(first_row, second_row, dim):
    index = lax.broadcasted_iota(jnp.int32, (INFO, dim), 0)
    return jnp.where(index == 0, first_row, jnp.where(index == 1, second_row, 0.0))


def partners():
    me = jnp.bitwise_and(lax.axis_index("seq"), GROUP - 1)
    return [jnp.bitwise_xor(me, k) for k in range(GROUP)]


def places(backward):
    return [GROUP - 1 - p for p in partners()] if backward else partners()


def columns(size, group, h=None):
    if h is None:
        return pl.ds(pl.multiple_of(group * size.wide, size.wide), size.wide)
    return pl.ds(pl.multiple_of(group * size.wide + h * size.dim, size.dim), size.dim)


def wave_heads(size, wave):
    return [(wave * size.each + i, slice(i * size.dim, (i + 1) * size.dim)) for i in range(size.each)]


def all_pieces(size):
    return [(chunk, wave) for wave in range(size.waves) for chunk in range(GROUP)]


def span_of(spans_ref, size, group, h):
    return spans_ref[pl.ds(group * size.per + h, 1), :]


def square_span(span, size):
    return span[:, :1] if size.rows != size.dim else span


def call(body, name, inputs, outputs, flops, moved, scratch=(), in_specs=None, out_specs=None, vmem=16):
    return pl.pallas_call(
        body,
        out_shape=outputs,
        in_specs=in_specs if in_specs is not None else [VMEM] * len(inputs),
        out_specs=out_specs if out_specs is not None else [VMEM] * len(outputs),
        scratch_shapes=list(scratch),
        compiler_params=pltpu.CompilerParams(vmem_limit_bytes=vmem * 1024 * 1024),
        cost_estimate=pl.CostEstimate(flops=flops, bytes_accessed=moved, transcendentals=0),
        name=name,
    )(*inputs)


def key_value_states(size, pieces, seg, decay_span, key_rows, value_rows):
    n = len(pieces)
    wide = size.each * size.dim

    def body(seg_hbm, span_hbm, key_hbm, value_hbm, *refs):
        outs, mark_ref, spans_ref = refs[:n], refs[n], refs[n + 1]
        seg_row, span_row, keys, values, sems = refs[n + 2 :]
        group = partners()
        small = (
            pltpu.make_async_copy(seg_hbm, seg_row, sems.at[2, 0]),
            pltpu.make_async_copy(span_hbm, span_row, sems.at[2, 1]),
        )
        copies = []
        for copy in small:
            copy.start()
        for c, (chunk, wave) in enumerate(pieces):
            here = pl.ds(pl.multiple_of(group[chunk] * size.wide + wave * wide, wide), wide)
            pair = (
                pltpu.make_async_copy(key_hbm.at[:, here], keys.at[c], sems.at[0, c]),
                pltpu.make_async_copy(value_hbm.at[:, here], values.at[c], sems.at[1, c]),
            )
            for copy in pair:
                copy.start()
            copies.append(pair)
        for copy in small:
            copy.wait()
        mark = jnp.broadcast_to(seg_row[...].astype(f32) + 1.0, (size.dim, size.rows)).T
        mark_ref[...] = mark
        spans_ref[...] = jnp.broadcast_to(span_row[...], (size.dim, size.heads)).T
        last, first = mark[size.rows - 1 :, :], mark[:1, :]
        ahead = (size.rows - 1.0) - position(size)
        for c, (chunk, wave) in enumerate(pieces):
            for copy in copies[c]:
                copy.wait()
            for h, cols in wave_heads(size, wave):
                span = span_of(spans_ref, size, group[chunk], h)
                weight = jnp.where(mark == last, decay(ahead, span), 0.0)
                key = keys[c, :, cols]
                high, low = halves(values[c, :, cols].astype(f32) * weight)
                outs[c][cols, :] = dot(
                    jnp.concatenate([key, key], 0), jnp.concatenate([high, low], 0), 0, 0
                )
            outs[c][size.state :, :] = info_rows(last, first, size.dim)

    held = (n, size.rows, wide)
    outs = call(
        body, "states", (seg, decay_span.reshape(1, size.heads), key_rows, value_rows),
        [size.payload] * n + [
            jax.ShapeDtypeStruct((size.rows, size.dim), f32),
            jax.ShapeDtypeStruct((size.heads, size.dim), f32),
        ],
        n * size.each * 4 * size.rows * size.dim * size.dim, n * wide * size.rows * 8,
        [
            pltpu.VMEM((1, size.rows), jnp.int32),
            pltpu.VMEM((1, size.heads), f32),
            pltpu.VMEM(held, bf16),
            pltpu.VMEM(held, bf16),
            pltpu.SemaphoreType.DMA((3, max(n, 2))),
        ],
        [HBM] * 4, vmem=60,
    )
    return outs[:n], outs[n], outs[n + 1]


def nearby_attended(size, mark, spans, queries, key_rows, value_rows):
    def body(mark_ref, spans_ref, query_ref, key_ref, value_ref, out_ref):
        gap, live = pair_weight(mark_ref[...], size)
        for h in range(size.heads):
            cols = slice(h * size.dim, (h + 1) * size.dim)
            span = square_span(spans_ref[h : h + 1, :], size)
            weight = jnp.where(live, decay(gap, span), 0.0)
            query, key, value = query_ref[:, cols], key_ref[:, cols], value_ref[:, cols]
            high, low = halves(dot(query, key, 1, 1) * weight)
            out_ref[:, cols] = dot(
                jnp.concatenate([high, low], 1), jnp.concatenate([value, value], 0)
            )

    return call(
        body, "nearby", (mark, spans, queries, key_rows, value_rows), [size.block],
        size.heads * 6 * size.rows * size.dim * size.dim, size.features * size.rows * 10,
    )[0]


def group_total(size, backward, wave, spans, parts, riders=()):
    mark_row = size.state + (1 if backward else 0)

    def body(spans_ref, *refs):
        ins, out = refs[:GROUP], refs[GROUP + len(riders)]
        place = places(backward)
        marks = [ref[mark_row : mark_row + 1, :] for ref in ins]
        end = marks[0]
        for mark in marks[1:]:
            end = jnp.minimum(end, mark) if backward else jnp.maximum(end, mark)
        me = partners()[0]
        for h, cols in wave_heads(size, wave):
            span = span_of(spans_ref, size, me, h)
            total = None
            for k in range(GROUP):
                steps = ((GROUP - 1 - place[k]) * size.rows).astype(f32)
                factor = jnp.where(marks[k] == end, decay(steps, span), 0.0)
                term = factor * ins[k][cols, :]
                total = term if total is None else total + term
            out[cols, :] = total
        out[size.state :, :] = info_rows(end, end, size.dim)
        if riders:
            refs[-1][...] = refs[GROUP][...] + refs[GROUP + 1][...]

    outputs = [size.payload] + ([size.gains] if riders else [])
    return call(
        body, "total", (spans, *parts, *riders), outputs,
        size.state * size.dim * 8, size.state * size.dim * 20,
    )


def group_prefixes(size, backward, wave, spans, parts, entering, riders=()):
    mark_row = size.state + (1 if backward else 0)
    extra = sum(r.shape[0] for r in riders)

    def body(spans_ref, *refs):
        ins, enter = refs[:GROUP], refs[GROUP]
        rides, outs = refs[GROUP + 1 : GROUP + 1 + len(riders)], refs[GROUP + 1 + len(riders) :]
        place = places(backward)
        me = partners()[0]
        marks = [ref[mark_row : mark_row + 1, :] for ref in ins]
        block, members = lax.axis_index("seq"), lax.axis_size("seq")
        first = block >= members - GROUP if backward else block < GROUP
        outer = jnp.where(first, FAR if backward else 0.0, enter[size.state : size.state + 1, :])
        enters = jnp.where(first, 0.0, 1.0)
        carry = []
        for to in range(GROUP):
            now = outer
            for k in range(GROUP):
                if backward:
                    now = jnp.where(place[k] < place[to], jnp.minimum(now, marks[k]), now)
                else:
                    now = jnp.where(place[k] < place[to], jnp.maximum(now, marks[k]), now)
            carry.append(now)
            outs[to][size.state : size.state + INFO, :] = info_rows(now, now, size.dim)
            at = size.state + INFO
            for ride in rides:
                outs[to][at : at + ride.shape[0], :] = ride[...]
                at += ride.shape[0]
        for h, cols in wave_heads(size, wave):
            span = span_of(spans_ref, size, me, h)
            for to in range(GROUP):
                steps = (place[to] * size.rows).astype(f32)
                factor = jnp.where(outer == carry[to], enters * decay(steps, span), 0.0)
                total = factor * enter[cols, :]
                for k in range(GROUP):
                    if k == to:
                        continue
                    gap = place[to] - 1 - place[k]
                    steps = (jnp.maximum(gap, 0) * size.rows).astype(f32)
                    live = jnp.logical_and(marks[k] == carry[to], gap >= 0)
                    total += jnp.where(live, decay(steps, span), 0.0) * ins[k][cols, :]
                outs[to][cols, :] = total

    shape = jax.ShapeDtypeStruct((size.state + INFO + extra, size.dim), f32)
    return call(
        body, "prefixes", (spans, *parts, entering, *riders), [shape] * GROUP,
        size.state * size.dim * 40, size.state * size.dim * 36,
    )


def whole_attended(size, mark, spans, queries, out_grad, gain, near, entering):
    def body(mark_ref, spans_ref, query_ref, grad_ref, gain_ref, near_ref, *refs):
        states, (out_ref, sums_ref) = refs[:-2], refs[-2:]
        group = partners()
        mark = mark_ref[...]
        behind = position(size) + 1.0
        square = jnp.zeros((size.rows, size.dim), f32)
        cross = jnp.zeros((size.rows, size.dim), f32)
        live = mark == states[0][size.state : size.state + 1, :]
        for i, (c, wave) in enumerate(all_pieces(size)):
            for h, cols in wave_heads(size, wave):
                here = columns(size, group[c], h)
                span = span_of(spans_ref, size, group[c], h)
                weight = jnp.where(live, decay(behind, span), 0.0)
                query = query_ref[:, here]
                high, low = halves(states[i][cols, :])
                inter = dot(jnp.concatenate([query, query], 1), jnp.concatenate([high, low], 0))
                out = near_ref[:, here] + weight * inter
                out_ref[:, here] = out
                square += out * out
                cross += grad_ref[:, here].astype(f32) * gain_ref[:, here] * out
        square = jnp.sum(square.T, axis=0, keepdims=True)
        cross = jnp.sum(cross.T, axis=0, keepdims=True)
        index = lax.broadcasted_iota(jnp.int32, (8, size.rows), 0)
        sums_ref[...] = jnp.where(index == 0, square, jnp.where(index == 1, cross, 0.0))

    return call(
        body, "attended", (mark, spans, queries, out_grad, gain, near, *entering),
        [size.block, jax.ShapeDtypeStruct((8, size.rows), f32)],
        size.heads * 4 * size.rows * size.dim * size.dim, size.features * size.rows * 16,
    )


def output_grad_states(size, pieces, norm, mark, spans, queries, out_grad, gain, attended, sums, count=False):
    n = len(pieces)

    def body(mark_ref, spans_ref, query_ref, grad_ref, gain_ref, att_ref, sums_ref, *outs):
        group = partners()
        mark = mark_ref[...]
        last, first = mark[size.rows - 1 :, :], mark[:1, :]
        wide = (size.dim, size.rows)
        square = jnp.broadcast_to(sums_ref[0:1, :], wide).T
        cross = jnp.broadcast_to(sums_ref[1:2, :], wide).T
        inv = lax.rsqrt(square / norm + 1e-06)
        pull = inv * inv * inv * cross / norm
        gone = position(size)
        for c, (chunk, wave) in enumerate(pieces):
            back_ref, state_ref = outs[2 * c : 2 * c + 2]
            for h, cols in wave_heads(size, wave):
                here = columns(size, group[chunk], h)
                span = span_of(spans_ref, size, group[chunk], h)
                weight = jnp.where(mark == first, decay(gone, span), 0.0)
                grad = grad_ref[:, here].astype(f32) * inv
                att = att_ref[:, here]
                back = gain_ref[:, here] * grad - att * pull
                back_ref[:, cols] = back
                query = query_ref[:, here]
                high, low = halves(back * weight)
                state_ref[cols, :] = dot(
                    jnp.concatenate([query, query], 0), jnp.concatenate([high, low], 0), 0, 0
                )
            state_ref[size.state :, :] = info_rows(last, first, size.dim)
        if count:
            outs[2 * n][...] = jnp.zeros(size.gains.shape, f32)
            for chunk in range(GROUP):
                for h in range(size.per):
                    here = columns(size, group[chunk], h)
                    part = grad_ref[:, here].astype(f32) * inv * att_ref[:, here]
                    at = chunk * size.pad + h
                    outs[2 * n][at : at + 1, :] = jnp.sum(part, axis=0, keepdims=True)

    part = jax.ShapeDtypeStruct((size.rows, size.state), f32)
    outs = call(
        body, "back", (mark, spans, queries, out_grad, gain, attended, sums),
        [part, size.payload] * n + [size.gains] * count,
        n * size.each * 4 * size.rows * size.dim * size.dim, n * size.state * size.rows * 16,
    )
    return outs[0 : 2 * n : 2], outs[1 : 2 * n : 2], outs[2 * n :]


def local_gradients(size, mark, spans, queries, key_rows, value_rows, back, entering):
    def body(mark_ref, spans_ref, query_ref, key_ref, value_ref, *refs):
        n = GROUP * size.waves
        backs, states = refs[:n], refs[n : 2 * n]
        out_hbm, local_key, local_value, done, sems = refs[2 * n :]
        group = partners()
        mark = mark_ref[...]
        gap, pairs = pair_weight(mark, size)
        behind = position(size) + 1.0
        copies = []
        live = mark == states[0][size.state : size.state + 1, :]
        for c in range(GROUP):
            for h in range(size.per):
                here = columns(size, group[c], h)
                piece = c + GROUP * (h // size.each)
                cols = slice(h % size.each * size.dim, (h % size.each + 1) * size.dim)
                span = span_of(spans_ref, size, group[c], h)
                weight = jnp.where(pairs, decay(gap, square_span(span, size)), 0.0)
                query, key, value = query_ref[:, here], key_ref[:, here], value_ref[:, here]
                high, low = halves(backs[piece][:, cols])
                grads = dot(
                    jnp.concatenate([high, low], 1), jnp.concatenate([value, value], 1), 1, 1
                )
                grads_high, grads_low = halves(grads * weight)
                part = dot(
                    jnp.concatenate([grads_high, grads_low], 1), jnp.concatenate([key, key], 0)
                )
                state_high, state_low = halves(states[piece][cols, :])
                inter = dot(
                    jnp.concatenate([high, high, low], 1),
                    jnp.concatenate([state_high, state_low, state_high], 1),
                    1, 1,
                )
                into = jnp.where(live, decay(behind, span), 0.0)
                done[c, :, h * size.dim : (h + 1) * size.dim] = (part + into * inter).astype(bf16)
                local_key[:, here] = dot(
                    jnp.concatenate([grads_high, grads_low], 0),
                    jnp.concatenate([query, query], 0),
                    0, 0,
                )
                score_high, score_low = halves(dot(query, key, 1, 1) * weight)
                local_value[:, here] = dot(
                    jnp.concatenate([score_high, score_high, score_low], 0),
                    jnp.concatenate([high, low, high], 0),
                    0, 0,
                )
            copies.append(
                pltpu.make_async_copy(
                    done.at[c], out_hbm.at[:, columns(size, group[c])], sems.at[c]
                )
            )
            copies[c].start()
        for copy in copies:
            copy.wait()

    return call(
        body, "gradients", (mark, spans, queries, key_rows, value_rows, *back, *entering),
        [jax.ShapeDtypeStruct((size.rows, size.features), bf16), size.block, size.block],
        size.heads * 26 * size.rows * size.dim * size.dim, size.features * size.rows * 24,
        [pltpu.VMEM((GROUP, size.rows, size.wide), bf16), pltpu.SemaphoreType.DMA((GROUP,))],
        None, [HBM, VMEM, VMEM],
    )


def final_gradients(size, mark, spans, key_rows, value_rows, local_key, local_value, entering):
    def body(mark_ref, spans_ref, key_ref, value_ref, local_key_ref, local_value_ref, *refs):
        n = GROUP * size.waves
        states, (keys_hbm, values_hbm, gain_hbm) = refs[:n], refs[n : n + 3]
        keys, values, gains, sems = refs[n + 3 :]
        group = partners()
        mark = mark_ref[...]
        left = size.rows - position(size)
        for c in range(GROUP):
            for h in range(size.per):
                total = None
                for k in range(GROUP):
                    at = size.state + INFO + (k ^ c) * size.pad + h
                    row = states[n - GROUP + k][at : at + 1, :]
                    total = row if total is None else total + row
                gains[:, columns(size, group[c], h)] = total
        copies = [pltpu.make_async_copy(gains, gain_hbm, sems.at[2, 0])]
        copies[0].start()
        live = mark == states[0][size.state : size.state + 1, :]
        for c in range(GROUP):
            for h in range(size.per):
                here = columns(size, group[c], h)
                piece = c + GROUP * (h // size.each)
                at = slice(h % size.each * size.dim, (h % size.each + 1) * size.dim)
                cols = slice(h * size.dim, (h + 1) * size.dim)
                span = span_of(spans_ref, size, group[c], h)
                weight = jnp.where(live, decay(left, span), 0.0)
                key, value = key_ref[:, here], value_ref[:, here]
                high, low = halves(states[piece][at, :])
                from_values = dot(
                    jnp.concatenate([value, value], 1), jnp.concatenate([high, low], 1), 1, 1
                )
                from_keys = dot(jnp.concatenate([key, key], 1), jnp.concatenate([high, low], 0))
                keys[c, :, cols] = (local_key_ref[:, here] + weight * from_values).astype(bf16)
                values[c, :, cols] = (local_value_ref[:, here] + weight * from_keys).astype(bf16)
            here = columns(size, group[c])
            for copy in (
                pltpu.make_async_copy(keys.at[c], keys_hbm.at[:, here], sems.at[0, c]),
                pltpu.make_async_copy(values.at[c], values_hbm.at[:, here], sems.at[1, c]),
            ):
                copy.start()
                copies.append(copy)
        for copy in copies:
            copy.wait()

    shape = jax.ShapeDtypeStruct((size.rows, size.features), bf16)
    held = pltpu.VMEM((GROUP, size.rows, size.wide), bf16)
    return call(
        body, "final", (mark, spans, key_rows, value_rows, local_key, local_value, *entering),
        [shape, shape, jax.ShapeDtypeStruct((1, size.features), f32)],
        size.heads * 8 * size.rows * size.dim * size.dim, size.features * size.rows * 24,
        [held, held, pltpu.VMEM((1, size.features), f32), pltpu.SemaphoreType.DMA((3, GROUP))],
        None, [HBM] * 3,
    )


def swap(array, distance):
    members = lax.axis_size("seq")
    return lax.ppermute(array, "seq", [(i, i ^ distance) for i in range(members)])


def exchange(payloads):
    return [payloads[0]] + [swap(payloads[k], k) for k in range(1, GROUP)]


def shifted(array, by):
    members = lax.axis_size("seq")
    pairs = [(i, i + by) for i in range(members) if 0 <= i + by < members]
    return lax.ppermute(array, "seq", pairs)


def from_other_groups(size, backward, wave, decay_span, total):
    members = lax.axis_size("seq")
    tokens = GROUP * size.rows
    longest = members * size.rows // 4
    needed = max(longest - 2, 0) // tokens + 1
    way = -GROUP if backward else GROUP
    if needed == 1:
        pairs = [(i, (i + way) % members) for i in range(members)]
        return lax.ppermute(total, "seq", pairs)
    result = shifted(total, way)
    reach = 1
    start = partners()[0] * size.per + wave * size.each
    mine = lax.dynamic_slice(decay_span, (start,), (size.each,))
    while reach < needed:
        incoming = shifted(result, way * reach)
        passes = incoming[size.state, 0] == result[size.state, 0]
        factor = jnp.where(passes, jnp.exp(-(reach * tokens) / mine), 0.0)
        factor = jnp.repeat(factor, size.dim)[:, None]
        result = result.at[: size.state].add(factor * incoming[: size.state])
        reach *= 2
    return result


def local(queries, key_rows, value_rows, segment_ids, decay_span, norm_gain, out_grad):
    size = Sizes(queries, decay_span)
    norm = size.features * lax.axis_size("head")
    members = lax.axis_size("seq")
    seg = segment_ids.reshape(1, size.rows)
    gain = norm_gain.reshape(1, size.features)
    waves = range(size.waves)
    sent = [[(chunk, wave) for chunk in (3, 1, 2)] for wave in waves]
    kept = [(0, wave) for wave in waves]
    every = all_pieces(size)

    states = {}
    for pieces in [*sent, kept]:
        outs, mark, spans = key_value_states(size, pieces, seg, decay_span, key_rows, value_rows)
        states |= zip(pieces, outs)
        if pieces is sent[0]:
            common = (mark, spans)
    spans = common[1]
    near = nearby_attended(size, *common, queries, key_rows, value_rows)
    entering = {}
    parts = {w: exchange({k: states[k, w] for k in range(GROUP)}) for w in waves}
    totals = {w: group_total(size, False, w, spans, parts[w])[0] for w in waves}
    outer = {w: from_other_groups(size, False, w, decay_span, totals[w]) for w in waves}
    for w in waves:
        outs = exchange(group_prefixes(size, False, w, spans, parts[w], outer[w]))
        entering |= {(k, w): outs[k] for k in range(GROUP)}
    entering = [entering[piece] for piece in every]

    attended, sums = whole_attended(size, *common, queries, out_grad, gain, near, entering)
    sums = lax.psum(sums, "head")
    back, states, gains = {}, {}, []
    for pieces in [*sent, kept]:
        backs, payloads, rows = output_grad_states(
            size, pieces, norm, *common, queries, out_grad, gain, attended, sums, pieces is sent[-1]
        )
        back |= zip(pieces, backs)
        states |= zip(pieces, payloads)
        gains += rows
    back = [back[piece] for piece in every]

    parts = {w: exchange({k: states[k, w] for k in range(GROUP)}) for w in waves}
    gains, distance = gains[0], GROUP
    while distance << size.waves < members:
        gains = gains + swap(gains, distance)
        distance *= 2
    leaving, totals = {}, {}
    for w in waves:
        riders = (gains, swap(gains, distance)) if distance < members else ()
        totals[w], *rows = group_total(size, True, w, spans, parts[w], riders)
        gains = rows[0] if rows else gains
        distance *= 2
    riders = {w: (gains,) if w == size.waves - 1 else () for w in waves}
    outer = {w: from_other_groups(size, True, w, decay_span, totals[w]) for w in waves}
    for w in waves:
        outs = exchange(group_prefixes(size, True, w, spans, parts[w], outer[w], riders[w]))
        leaving |= {(k, w): outs[k] for k in range(GROUP)}
    leaving = [leaving[piece] for piece in every]

    query_grad, local_key, local_value = local_gradients(
        size, *common, queries, key_rows, value_rows, back, entering
    )
    key_grad, value_grad, gain_grad = final_gradients(
        size, *common, key_rows, value_rows, local_key, local_value, leaving
    )
    return query_grad, key_grad, value_grad, gain_grad.reshape(size.features)


def solution(mesh):
    rows = P("seq", "head")
    in_specs = (rows, rows, rows, P("seq"), P("head"), P("head"), rows)
    return jax.shard_map(
        local, mesh=mesh, in_specs=in_specs, out_specs=(rows, rows, rows, P("head")), check_vma=False
    )
```

time: 89.1 us -> 80 us (0.90)
  waiting for transfers between devices: 40.9 us -> 16.9 us
  starting transfers between devices: 25.7 us -> 37.1 us
  Pallas kernels: 15.5 us -> 21.1 us
  local copies, waits for them, and re-layouts: 3.43 us -> 1 us
    ppermute x14 -> x26, waiting for transfers between devices: 27.7 us -> 12.5 us  [swap(): lax.ppermute(array, 'seq', [(i, i ^ distance) for i in range(members)])]
    ppermute x14 -> x26, starting transfers between devices: 20.8 us -> 30.9 us  [swap(): lax.ppermute(array, 'seq', [(i, i ^ distance) for i in range(members)])]
    ppermute x2 -> x4, waiting for transfers between devices: 13.2 us -> 4.4 us  [from_other_groups(): return lax.ppermute(total, 'seq', pairs)]
    pallas_call x12 -> x18, Pallas kernels: 15.5 us -> 21.1 us  [call(): pl.pallas_call(body, out_shape=outputs, in_specs=in_specs if in_specs is...]
    unnamed x30 -> x44, local copies, waits for them, and re-layouts: 3.36 us -> 1 us
    ppermute x2 -> x4, starting transfers between devices: 4.92 us -> 6.13 us  [from_other_groups(): return lax.ppermute(total, 'seq', pairs)]
  transfers between devices with their start and end apart: 16 -> 30, of which waited for: 11 -> 8; matrix products, arithmetic and copies ran while one was open for 0% -> 0% of each run, Pallas kernels for 11% -> 20%
where the time goes in v3:
time: 80 us; the launch traced here: 79.7 us
  starting transfers between devices  37.1 us (46%)
  Pallas kernels  21.1 us (26%)
  waiting for transfers between devices  16.9 us (21%)
  blocking collectives  2.47 us (3%)
  between operations  1.17 us (1%)
  local copies, waits for them, and re-layouts  1 us (1%)
    ppermute x26, starting transfers between devices, swap(): lax.ppermute(array, 'seq', [(i, i ^ distance) for i in range(members)])  30.9 us
    pallas_call x18, Pallas kernels, call(): pl.pallas_call(body, out_shape=outputs, in_specs=in_specs if in_specs is...  21.1 us
    ppermute x26, waiting for transfers between devices, swap(): lax.ppermute(array, 'seq', [(i, i ^ distance) for i in range(members)])  12.5 us
    ppermute x4, starting transfers between devices, from_other_groups(): return lax.ppermute(total, 'seq', pairs)  6.13 us
    ppermute x4, waiting for transfers between devices, from_other_groups(): return lax.ppermute(total, 'seq', pairs)  4.4 us
    psum x1, blocking collectives, local(): sums = lax.psum(sums, 'head')  2.47 us
  transfers between devices with their start and end apart: 30, of which 8 were waited for; matrix products, arithmetic and copies ran while one was open for 0% of the time, Pallas kernels for 20%

profile of v3, /device:TPU:0, one launch (start us, length us, event | category | flops | bytes accessed | tf_op | source)
XLA Modules:
  0.0 79.7 jit_solution(14848408240811157071)
XLA Ops:
  0.6 2.3 %states.3 = (f32[264,128]{1,0:T(8,128)}, f32[264,128]{1,0:T(8,128)}, f32[264,128]{1,0:T(8,128)}, f32[128,128]{1,0:T(8,128)}, f32[16,128]{1,0:T(8,128)}) custom-call(s32[1,128]{1,0:T(1,128)} %bitcast.8, f32[1,16]{1,0:T(1,128)} %bitcast.11, bf16[128,2048]{1,0:T(8,128)(2,1)} %key_ref.5, bf16[128,2048]{1,0:T(8,128)(2,1)} %value_ref.5), custom_call_target="tpu_custom_call" | custom-call | flops 50331648 | bytes 786432 | tf_op jit(solution)/shard_map/states/pallas_call | solution.py:97
  2.9 3.0 %collective-permute-start = (f32[264,128]{1,0:T(8,128)}, f32[264,128]{1,0:T(8,128)S(1)}, u32[]{:S(2)}, u32[]{:S(2)}) collective-permute-start(f32[264,128]{1,0:T(8,128)} %get-tuple-element.62), channel_id=1, source_target_pairs={{0,2},{2,0},{4,6},{6,4},{8,10},{10,8},{12,14},{14,12},{16,18},{18,... | collective-permute-start | bytes 405512 | tf_op jit(solution)/shard_map/ppermute | solution.py:475
  5.9 1.5 %collective-permute-start.1 = (f32[264,128]{1,0:T(8,128)}, f32[264,128]{1,0:T(8,128)S(1)}, u32[]{:S(2)}, u32[]{:S(2)}) collective-permute-start(f32[264,128]{1,0:T(8,128)} %get-tuple-element.63), channel_id=1, source_target_pairs={{0,4},{2,6},{4,0},{6,2},{8,12},{10,14},{12,8},{14,10},{16,20},{18,... | collective-permute-start | bytes 405512 | tf_op jit(solution)/shard_map/ppermute | solution.py:475
  7.5 2.3 %states.5 = (f32[264,128]{1,0:T(8,128)}, f32[264,128]{1,0:T(8,128)}, f32[264,128]{1,0:T(8,128)}, f32[128,128]{1,0:T(8,128)}, f32[16,128]{1,0:T(8,128)}) custom-call(s32[1,128]{1,0:T(1,128)} %bitcast.9, f32[1,16]{1,0:T(1,128)} %bitcast.12, bf16[128,2048]{1,0:T(8,128)(2,1)} %key_ref.5, bf16[128,2048]{1,0:T(8,128)(2,1)} %value_ref.5), custom_call_target="tpu_custom_call" | custom-call | flops 50331648 | bytes 786432 | tf_op jit(solution)/shard_map/states/pallas_call | solution.py:97
  9.8 2.0 %collective-permute-start.7 = (f32[264,128]{1,0:T(8,128)}, f32[264,128]{1,0:T(8,128)S(1)}, u32[]{:S(2)}, u32[]{:S(2)}) collective-permute-start(f32[264,128]{1,0:T(8,128)} %get-tuple-element.70), channel_id=1, source_target_pairs={{0,2},{2,0},{4,6},{6,4},{8,10},{10,8},{12,14},{14,12},{16,18},{18,... | collective-permute-start | bytes 405512 | tf_op jit(solution)/shard_map/ppermute | solution.py:475
  11.8 1.5 %collective-permute-start.8 = (f32[264,128]{1,0:T(8,128)}, f32[264,128]{1,0:T(8,128)S(1)}, u32[]{:S(2)}, u32[]{:S(2)}) collective-permute-start(f32[264,128]{1,0:T(8,128)} %get-tuple-element.71), channel_id=1, source_target_pairs={{0,4},{2,6},{4,0},{6,2},{8,12},{10,14},{12,8},{14,10},{16,20},{18,... | collective-permute-start | bytes 405512 | tf_op jit(solution)/shard_map/ppermute | solution.py:475
  13.3 2.1 %states.4 = (f32[264,128]{1,0:T(8,128)}, f32[264,128]{1,0:T(8,128)}, f32[128,128]{1,0:T(8,128)}, f32[16,128]{1,0:T(8,128)}) custom-call(s32[1,128]{1,0:T(1,128)} %bitcast.10, f32[1,16]{1,0:T(1,128)} %bitcast.13, bf16[128,2048]{1,0:T(8,128)(2,1)} %key_ref.5, bf16[128,2048]{1,0:T(8,128)(2,1)} %value_ref.5), custom_call_target="tpu_custom_call" | custom-call | flops 33554432 | bytes 524288 | tf_op jit(solution)/shard_map/states/pallas_call | solution.py:97
  15.5 0.9 %copy-done.19 = f32[264,128]{1,0:T(8,128)S(1)} copy-done((f32[264,128]{1,0:T(8,128)S(1)}, f32[264,128]{1,0:T(8,128)}, u32[]{:S(2)}) %copy-start.19) | copy-done | bytes 135192
  16.5 2.1 %collective-permute-start.3 = (f32[264,128]{1,0:T(8,128)S(1)}, f32[264,128]{1,0:T(8,128)S(1)}, u32[]{:S(2)}, u32[]{:S(2)}) collective-permute-start(f32[264,128]{1,0:T(8,128)S(1)} %total.4), channel_id=1, source_target_pairs={{0,8},{2,10},{4,12},{6,14},{8,16},{10,18},{12,20},{14,22},{16,24},... | collective-permute-start | bytes 405512 | tf_op jit(solution)/shard_map/ppermute | solution.py:496
  18.6 2.8 %collective-permute-done.9.refs_3_ = f32[264,128]{1,0:T(8,128)S(1)} collective-permute-done((f32[264,128]{1,0:T(8,128)S(1)}, f32[264,128]{1,0:T(8,128)S(1)}, u32[]{:S(2)}, u32[]{:S(2)}) %collective-permute-start.9) | collective-permute-done | bytes 135200 | tf_op jit(solution)/shard_map/ppermute | solution.py:475
  21.5 1.6 %collective-permute-start.10 = (f32[264,128]{1,0:T(8,128)S(1)}, f32[264,128]{1,0:T(8,128)S(1)}, u32[]{:S(2)}, u32[]{:S(2)}) collective-permute-start(f32[264,128]{1,0:T(8,128)S(1)} %total.5), channel_id=1, source_target_pairs={{0,8},{2,10},{4,12},{6,14},{8,16},{10,18},{12,20},{14,22},{16,24},... | collective-permute-start | bytes 405512 | tf_op jit(solution)/shard_map/ppermute | solution.py:496
  23.1 0.8 collective-permute-done.3.refs_4_
  23.9 0.2 prefixes.4
  24.1 2.7 %collective-permute-start.4 = (f32[264,128]{1,0:T(8,128)S(1)}, f32[264,128]{1,0:T(8,128)S(1)}, u32[]{:S(2)}, u32[]{:S(2)}) collective-permute-start(f32[264,128]{1,0:T(8,128)S(1)} %get-tuple-element.66), channel_id=1, source_target_pairs={{0,2},{2,0},{4,6},{6,4},{8,10},{10,8},{12,14},{14,12},{16,18},{18,... | collective-permute-start | bytes 405512 | tf_op jit(solution)/shard_map/ppermute | solution.py:475
  26.7 1.2 %collective-permute-start.5 = (f32[264,128]{1,0:T(8,128)S(1)}, f32[264,128]{1,0:T(8,128)S(1)}, u32[]{:S(2)}, u32[]{:S(2)}) collective-permute-start(f32[264,128]{1,0:T(8,128)S(1)} %get-tuple-element.67), channel_id=1, source_target_pairs={{0,4},{2,6},{4,0},{6,2},{8,12},{10,14},{12,8},{14,10},{16,20},{18,... | collective-permute-start | bytes 405512 | tf_op jit(solution)/shard_map/ppermute | solution.py:475
  27.9 0.6 collective-permute-start.6
  28.7 1.8 %collective-permute-start.11 = (f32[264,128]{1,0:T(8,128)S(1)}, f32[264,128]{1,0:T(8,128)S(1)}, u32[]{:S(2)}, u32[]{:S(2)}) collective-permute-start(f32[264,128]{1,0:T(8,128)S(1)} %get-tuple-element.74), channel_id=1, source_target_pairs={{0,2},{2,0},{4,6},{6,4},{8,10},{10,8},{12,14},{14,12},{16,18},{18,... | collective-permute-start | bytes 405512 | tf_op jit(solution)/shard_map/ppermute | solution.py:475
  30.5 1.2 %collective-permute-start.12 = (f32[264,128]{1,0:T(8,128)S(1)}, f32[264,128]{1,0:T(8,128)S(1)}, u32[]{:S(2)}, u32[]{:S(2)}) collective-permute-start(f32[264,128]{1,0:T(8,128)S(1)} %get-tuple-element.75), channel_id=1, source_target_pairs={{0,4},{2,6},{4,0},{6,2},{8,12},{10,14},{12,8},{14,10},{16,20},{18,... | collective-permute-start | bytes 405512 | tf_op jit(solution)/shard_map/ppermute | solution.py:475
  31.7 1.0 %collective-permute-start.13 = (f32[264,128]{1,0:T(8,128)S(1)}, f32[264,128]{1,0:T(8,128)S(1)}, u32[]{:S(2)}, u32[]{:S(2)}) collective-permute-start(f32[264,128]{1,0:T(8,128)S(1)} %get-tuple-element.76), channel_id=1, source_target_pairs={{0,6},{2,4},{4,2},{6,0},{8,14},{10,12},{12,10},{14,8},{16,22},{18,... | collective-permute-start | bytes 405512 | tf_op jit(solution)/shard_map/ppermute | solution.py:475
  32.7 2.7 %nearby.1.near_ref = f32[128,2048]{1,0:T(8,128)S(1)} custom-call(f32[128,128]{1,0:T(8,128)S(1)} %copy-done.4, f32[16,128]{1,0:T(8,128)S(1)} %copy-done.5, bf16[128,2048]{1,0:T(8,128)(2,1)S(1)} %copy-done.2, bf16[128,2048]{1,0:T(8,128)(2,1)S(1)} %copy-done, bf16[128,2048]{1,0:T(8,128)(2,1)S(1)} %copy-done.1), custom_call_target="tpu_custom_call" | custom-call | flops 201326592 | bytes 2621440 | tf_op jit(solution)/shard_map/nearby/pallas_call | solution.py:97
  35.5 0.9 %collective-permute-done.12.refs_6_.refs_14_ = f32[264,128]{1,0:T(8,128)S(1)} collective-permute-done((f32[264,128]{1,0:T(8,128)S(1)}, f32[264,128]{1,0:T(8,128)S(1)}, u32[]{:S(2)}, u32[]{:S(2)}) %collective-permute-start.12) | collective-permute-done | bytes 135200 | tf_op jit(solution)/shard_map/ppermute | solution.py:475
  36.4 1.4 %collective-permute-done.13.refs_7_.refs_15_ = f32[264,128]{1,0:T(8,128)S(1)} collective-permute-done((f32[264,128]{1,0:T(8,128)S(1)}, f32[264,128]{1,0:T(8,128)S(1)}, u32[]{:S(2)}, u32[]{:S(2)}) %collective-permute-start.13) | collective-permute-done | bytes 135200 | tf_op jit(solution)/shard_map/ppermute | solution.py:475
  37.9 0.9 %attended.1 = (f32[128,2048]{1,0:T(8,128)S(1)}, f32[8,128]{1,0:T(8,128)S(1)}) custom-call(f32[128,128]{1,0:T(8,128)S(1)} %copy-done.4, f32[16,128]{1,0:T(8,128)S(1)} %copy-done.5, bf16[128,2048]{1,0:T(8,128)(2,1)S(1)} %copy-done.2, bf16[128,2048]{1,0:T(8,128)(2,1)S(1)} %copy-done.3, f32[1,2048]{1,0:T(1,128)S(1)} %bitcast.4, f32[128,2048]{1,0:T(8,128)S(1)} %nearby.1.near_ref, ...), custom_call_target="tpu_custom_call" | custom-call | flops 134217728 | bytes 4194304 | tf_op jit(solution)/shard_map/attended/pallas_call | solution.py:97
  38.8 2.5 %psum.7.sums_ref = f32[8,128]{1,0:T(8,128)S(1)} all-reduce(f32[8,128]{1,0:T(8,128)S(1)} %get-tuple-element.78), channel_id=1, replica_groups=mesh['seq'=16,'head'=2] {'head'}, use_global_device_ids=true, to_apply=%region_0.0 | all-reduce | flops 1024 | bytes 8192 | tf_op jit(solution)/shard_map/psum | solution.py:540
  41.3 0.5 back.4
  41.8 1.3 %collective-permute-start.14 = (f32[264,128]{1,0:T(8,128)S(1)}, f32[264,128]{1,0:T(8,128)S(1)}, u32[]{:S(2)}, u32[]{:S(2)}) collective-permute-start(f32[264,128]{1,0:T(8,128)S(1)} %get-tuple-element.91), channel_id=1, source_target_pairs={{0,2},{2,0},{4,6},{6,4},{8,10},{10,8},{12,14},{14,12},{16,18},{18,... | collective-permute-start | bytes 405512 | tf_op jit(solution)/shard_map/ppermute | solution.py:475
  43.0 1.1 %collective-permute-start.15 = (f32[264,128]{1,0:T(8,128)S(1)}, f32[264,128]{1,0:T(8,128)S(1)}, u32[]{:S(2)}, u32[]{:S(2)}) collective-permute-start(f32[264,128]{1,0:T(8,128)S(1)} %get-tuple-element.92), channel_id=1, source_target_pairs={{0,4},{2,6},{4,0},{6,2},{8,12},{10,14},{12,8},{14,10},{16,20},{18,... | collective-permute-start | bytes 405512 | tf_op jit(solution)/shard_map/ppermute | solution.py:475
  44.1 1.2 %collective-permute-start.16 = (f32[264,128]{1,0:T(8,128)S(1)}, f32[264,128]{1,0:T(8,128)S(1)}, u32[]{:S(2)}, u32[]{:S(2)}) collective-permute-start(f32[264,128]{1,0:T(8,128)S(1)} %get-tuple-element.93), channel_id=1, source_target_pairs={{0,6},{2,4},{4,2},{6,0},{8,14},{10,12},{12,10},{14,8},{16,22},{18,... | collective-permute-start | bytes 405512 | tf_op jit(solution)/shard_map/ppermute | solution.py:475
  45.3 0.7 back.5
  46.1 1.3 %collective-permute-start.22 = (f32[264,128]{1,0:T(8,128)S(1)}, f32[264,128]{1,0:T(8,128)S(1)}, u32[]{:S(2)}, u32[]{:S(2)}) collective-permute-start(f32[264,128]{1,0:T(8,128)S(1)} %get-tuple-element.101), channel_id=1, source_target_pairs={{0,2},{2,0},{4,6},{6,4},{8,10},{10,8},{12,14},{14,12},{16,18},{18,... | collective-permute-start | bytes 405512 | tf_op jit(solution)/shard_map/ppermute | solution.py:475
  47.4 2.5 %collective-permute-done.17.refs_5_ = f32[32,128]{1,0:T(8,128)S(1)} collective-permute-done((f32[32,128]{1,0:T(8,128)S(1)}, f32[32,128]{1,0:T(8,128)S(1)}, u32[]{:S(2)}, u32[]{:S(2)}) %collective-permute-start.17) | collective-permute-done | bytes 16416 | tf_op jit(solution)/shard_map/ppermute | solution.py:475
  49.9 1.5 %collective-permute-start.23 = (f32[264,128]{1,0:T(8,128)S(1)}, f32[264,128]{1,0:T(8,128)S(1)}, u32[]{:S(2)}, u32[]{:S(2)}) collective-permute-start(f32[264,128]{1,0:T(8,128)S(1)} %get-tuple-element.102), channel_id=1, source_target_pairs={{0,4},{2,6},{4,0},{6,2},{8,12},{10,14},{12,8},{14,10},{16,20},{18,... | collective-permute-start | bytes 405512 | tf_op jit(solution)/shard_map/ppermute | solution.py:475
  51.4 1.2 %collective-permute-start.24 = (f32[264,128]{1,0:T(8,128)S(1)}, f32[264,128]{1,0:T(8,128)S(1)}, u32[]{:S(2)}, u32[]{:S(2)}) collective-permute-start(f32[264,128]{1,0:T(8,128)S(1)} %get-tuple-element.103), channel_id=1, source_target_pairs={{0,6},{2,4},{4,2},{6,0},{8,14},{10,12},{12,10},{14,8},{16,22},{18,... | collective-permute-start | bytes 405512 | tf_op jit(solution)/shard_map/ppermute | solution.py:475
  52.5 0.4 back.3
  53.0 1.9 %collective-permute-start.18 = (f32[264,128]{1,0:T(8,128)S(1)}, f32[264,128]{1,0:T(8,128)S(1)}, u32[]{:S(2)}, u32[]{:S(2)}) collective-permute-start(f32[264,128]{1,0:T(8,128)S(1)} %get-tuple-element.95), channel_id=1, source_target_pairs={{0,24},{2,26},{4,28},{6,30},{8,0},{10,2},{12,4},{14,6},{16,8},{18,... | collective-permute-start | bytes 405512 | tf_op jit(solution)/shard_map/ppermute | solution.py:496
  54.9 2.8 %collective-permute-done.23.refs_2_ = f32[264,128]{1,0:T(8,128)S(1)} collective-permute-done((f32[264,128]{1,0:T(8,128)S(1)}, f32[264,128]{1,0:T(8,128)S(1)}, u32[]{:S(2)}, u32[]{:S(2)}) %collective-permute-start.23) | collective-permute-done | bytes 135200 | tf_op jit(solution)/shard_map/ppermute | solution.py:475
  57.8 2.0 %collective-permute-done.25.refs_5_ = f32[32,128]{1,0:T(8,128)S(1)} collective-permute-done((f32[32,128]{1,0:T(8,128)S(1)}, f32[32,128]{1,0:T(8,128)S(1)}, u32[]{:S(2)}, u32[]{:S(2)}) %collective-permute-start.25) | collective-permute-done | bytes 16416 | tf_op jit(solution)/shard_map/ppermute | solution.py:475
  59.8 0.5 collective-permute-start.26
  60.5 0.9 %collective-permute-start.19 = (f32[264,128]{1,0:T(8,128)S(1)}, f32[264,128]{1,0:T(8,128)S(1)}, u32[]{:S(2)}, u32[]{:S(2)}) collective-permute-start(f32[264,128]{1,0:T(8,128)S(1)} %get-tuple-element.97), channel_id=1, source_target_pairs={{0,2},{2,0},{4,6},{6,4},{8,10},{10,8},{12,14},{14,12},{16,18},{18,... | collective-permute-start | bytes 405512 | tf_op jit(solution)/shard_map/ppermute | solution.py:475
  61.4 3.6 %collective-permute-done.26.refs_4_ = f32[264,128]{1,0:T(8,128)S(1)} collective-permute-done((f32[264,128]{1,0:T(8,128)S(1)}, f32[264,128]{1,0:T(8,128)S(1)}, u32[]{:S(2)}, u32[]{:S(2)}) %collective-permute-start.26) | collective-permute-done | bytes 135200 | tf_op jit(solution)/shard_map/ppermute | solution.py:496
  65.1 0.2 prefixes.7
  65.3 0.9 %collective-permute-start.27 = (f32[296,128]{1,0:T(8,128)S(1)}, f32[296,128]{1,0:T(8,128)S(1)}, u32[]{:S(2)}, u32[]{:S(2)}) collective-permute-start(f32[296,128]{1,0:T(8,128)S(1)} %get-tuple-element.108), channel_id=1, source_target_pairs={{0,2},{2,0},{4,6},{6,4},{8,10},{10,8},{12,14},{14,12},{16,18},{18,... | collective-permute-start | bytes 454664 | tf_op jit(solution)/shard_map/ppermute | solution.py:475
  66.2 1.4 %collective-permute-start.28 = (f32[296,128]{1,0:T(8,128)S(1)}, f32[296,128]{1,0:T(8,128)S(1)}, u32[]{:S(2)}, u32[]{:S(2)}) collective-permute-start(f32[296,128]{1,0:T(8,128)S(1)} %get-tuple-element.109), channel_id=1, source_target_pairs={{0,4},{2,6},{4,0},{6,2},{8,12},{10,14},{12,8},{14,10},{16,20},{18,... | collective-permute-start | bytes 454664 | tf_op jit(solution)/shard_map/ppermute | solution.py:475
  67.6 1.3 %collective-permute-start.29 = (f32[296,128]{1,0:T(8,128)S(1)}, f32[296,128]{1,0:T(8,128)S(1)}, u32[]{:S(2)}, u32[]{:S(2)}) collective-permute-start(f32[296,128]{1,0:T(8,128)S(1)} %get-tuple-element.110), channel_id=1, source_target_pairs={{0,6},{2,4},{4,2},{6,0},{8,14},{10,12},{12,10},{14,8},{16,22},{18,... | collective-permute-start | bytes 454664 | tf_op jit(solution)/shard_map/ppermute | solution.py:475
  68.9 1.0 %collective-permute-start.20 = (f32[264,128]{1,0:T(8,128)S(1)}, f32[264,128]{1,0:T(8,128)S(1)}, u32[]{:S(2)}, u32[]{:S(2)}) collective-permute-start(f32[264,128]{1,0:T(8,128)S(1)} %get-tuple-element.98), channel_id=1, source_target_pairs={{0,4},{2,6},{4,0},{6,2},{8,12},{10,14},{12,8},{14,10},{16,20},{18,... | collective-permute-start | bytes 405512 | tf_op jit(solution)/shard_map/ppermute | solution.py:475
  69.8 1.3 %collective-permute-start.21 = (f32[264,128]{1,0:T(8,128)S(1)}, f32[264,128]{1,0:T(8,128)S(1)}, u32[]{:S(2)}, u32[]{:S(2)}) collective-permute-start(f32[264,128]{1,0:T(8,128)S(1)} %get-tuple-element.99), channel_id=1, source_target_pairs={{0,6},{2,4},{4,2},{6,0},{8,14},{10,12},{12,10},{14,8},{16,22},{18,... | collective-permute-start | bytes 405512 | tf_op jit(solution)/shard_map/ppermute | solution.py:475
  71.2 6.7 %gradients.1 = (bf16[128,2048]{1,0:T(8,128)(2,1)}, f32[128,2048]{1,0:T(8,128)S(1)}, f32[128,2048]{1,0:T(8,128)S(1)}) custom-call(f32[128,128]{1,0:T(8,128)S(1)} %copy-done.4, f32[16,128]{1,0:T(8,128)S(1)} %copy-done.5, bf16[128,2048]{1,0:T(8,128)(2,1)S(1)} %copy-done.2, bf16[128,2048]{1,0:T(8,128)(2,1)S(1)} %copy-done, bf16[128,2048]{1,0:T(8,128)(2,1)S(1)} %copy-done.1, ...), custom_call_target="tpu_custom_call" | custom-call | flops 872415232 | bytes 6291456 | tf_op jit(solution)/shard_map/gradients/pallas_call | solution.py:97
  77.9 1.6 %final.1 = (bf16[128,2048]{1,0:T(8,128)(2,1)}, bf16[128,2048]{1,0:T(8,128)(2,1)}, f32[1,2048]{1,0:T(1,128)}) custom-call(f32[128,128]{1,0:T(8,128)S(1)} %copy-done.4, f32[16,128]{1,0:T(8,128)S(1)} %copy-done.5, bf16[128,2048]{1,0:T(8,128)(2,1)S(1)} %copy-done, bf16[128,2048]{1,0:T(8,128)(2,1)S(1)} %copy-done.1, ...), custom_call_target="tpu_custom_call" | custom-call | flops 268435456 | bytes 6291456 | tf_op jit(solution)/shard_map/final/pallas_call | solution.py:97
  (75 shorter events, 1.0 us)
Async XLA Ops:
  2.9 12.4 %collective-permute-start = (f32[264,128]{1,0:T(8,128)}, f32[264,128]{1,0:T(8,128)S(1)}, u32[]{:S(2)}, u32[]{:S(2)}) collective-permute-start(f32[264,128]{1,0:T(8,128)} %get-tuple-element.62), channel_id=1, source_target_pairs={{0,2},{2,0},{4,6},{6,4},{8,10},{10,8},{12,14},{14,12},{16,18},{18,... | collective-permute-start | bytes 405512 | tf_op jit(solution)/shard_map/ppermute | solution.py:475
  5.9 9.6 %collective-permute-start.1 = (f32[264,128]{1,0:T(8,128)}, f32[264,128]{1,0:T(8,128)S(1)}, u32[]{:S(2)}, u32[]{:S(2)}) collective-permute-start(f32[264,128]{1,0:T(8,128)} %get-tuple-element.63), channel_id=1, source_target_pairs={{0,4},{2,6},{4,0},{6,2},{8,12},{10,14},{12,8},{14,10},{16,20},{18,... | collective-permute-start | bytes 405512 | tf_op jit(solution)/shard_map/ppermute | solution.py:475
  7.4 8.1 %collective-permute-start.2 = (f32[264,128]{1,0:T(8,128)}, f32[264,128]{1,0:T(8,128)S(1)}, u32[]{:S(2)}, u32[]{:S(2)}) collective-permute-start(f32[264,128]{1,0:T(8,128)} %get-tuple-element.64), channel_id=1, source_target_pairs={{0,6},{2,4},{4,2},{6,0},{8,14},{10,12},{12,10},{14,8},{16,22},{18,... | collective-permute-start | bytes 405512 | tf_op jit(solution)/shard_map/ppermute | solution.py:475
  9.8 8.8 %collective-permute-start.7 = (f32[264,128]{1,0:T(8,128)}, f32[264,128]{1,0:T(8,128)S(1)}, u32[]{:S(2)}, u32[]{:S(2)}) collective-permute-start(f32[264,128]{1,0:T(8,128)} %get-tuple-element.70), channel_id=1, source_target_pairs={{0,2},{2,0},{4,6},{6,4},{8,10},{10,8},{12,14},{14,12},{16,18},{18,... | collective-permute-start | bytes 405512 | tf_op jit(solution)/shard_map/ppermute | solution.py:475
  11.8 3.6 %copy-start.21 = (f32[264,128]{1,0:T(8,128)S(1)}, f32[264,128]{1,0:T(8,128)}, u32[]{:S(2)}) copy-start(f32[264,128]{1,0:T(8,128)} %get-tuple-element.72) | copy-start | bytes 405508
  11.8 6.8 %collective-permute-start.8 = (f32[264,128]{1,0:T(8,128)}, f32[264,128]{1,0:T(8,128)S(1)}, u32[]{:S(2)}, u32[]{:S(2)}) collective-permute-start(f32[264,128]{1,0:T(8,128)} %get-tuple-element.71), channel_id=1, source_target_pairs={{0,4},{2,6},{4,0},{6,2},{8,12},{10,14},{12,8},{14,10},{16,20},{18,... | collective-permute-start | bytes 405512 | tf_op jit(solution)/shard_map/ppermute | solution.py:475
  15.4 6.0 %collective-permute-start.9 = (f32[264,128]{1,0:T(8,128)S(1)}, f32[264,128]{1,0:T(8,128)S(1)}, u32[]{:S(2)}, u32[]{:S(2)}) collective-permute-start(f32[264,128]{1,0:T(8,128)S(1)} %copy-done.21), channel_id=1, source_target_pairs={{0,6},{2,4},{4,2},{6,0},{8,14},{10,12},{12,10},{14,8},{16,22},{18,... | collective-permute-start | bytes 405512 | tf_op jit(solution)/shard_map/ppermute | solution.py:475
  16.4 5.0 %copy-start.18 = (f32[264,128]{1,0:T(8,128)S(1)}, f32[264,128]{1,0:T(8,128)}, u32[]{:S(2)}) copy-start(f32[264,128]{1,0:T(8,128)} %get-tuple-element.69.refs_0_) | copy-start | bytes 405508
  16.5 7.4 %collective-permute-start.3 = (f32[264,128]{1,0:T(8,128)S(1)}, f32[264,128]{1,0:T(8,128)S(1)}, u32[]{:S(2)}, u32[]{:S(2)}) collective-permute-start(f32[264,128]{1,0:T(8,128)S(1)} %total.4), channel_id=1, source_target_pairs={{0,8},{2,10},{4,12},{6,14},{8,16},{10,18},{12,20},{14,22},{16,24},... | collective-permute-start | bytes 405512 | tf_op jit(solution)/shard_map/ppermute | solution.py:496
  21.4 11.3 %copy-start.2 = (bf16[128,2048]{1,0:T(8,128)(2,1)S(1)}, bf16[128,2048]{1,0:T(8,128)(2,1)}, u32[]{:S(2)}) copy-start(bf16[128,2048]{1,0:T(8,128)(2,1)} %query_ref.11) | copy-start | bytes 1572868
  21.4 11.3 %copy-start = (bf16[128,2048]{1,0:T(8,128)(2,1)S(1)}, bf16[128,2048]{1,0:T(8,128)(2,1)}, u32[]{:S(2)}) copy-start(bf16[128,2048]{1,0:T(8,128)(2,1)} %key_ref.5) | copy-start | bytes 1572868
  21.5 11.2 %copy-start.1 = (bf16[128,2048]{1,0:T(8,128)(2,1)S(1)}, bf16[128,2048]{1,0:T(8,128)(2,1)}, u32[]{:S(2)}) copy-start(bf16[128,2048]{1,0:T(8,128)(2,1)} %value_ref.5) | copy-start | bytes 1572868
  21.5 7.0 %collective-permute-start.10 = (f32[264,128]{1,0:T(8,128)S(1)}, f32[264,128]{1,0:T(8,128)S(1)}, u32[]{:S(2)}, u32[]{:S(2)}) collective-permute-start(f32[264,128]{1,0:T(8,128)S(1)} %total.5), channel_id=1, source_target_pairs={{0,8},{2,10},{4,12},{6,14},{8,16},{10,18},{12,20},{14,22},{16,24},... | collective-permute-start | bytes 405512 | tf_op jit(solution)/shard_map/ppermute | solution.py:496
  24.1 7.6 %collective-permute-start.4 = (f32[264,128]{1,0:T(8,128)S(1)}, f32[264,128]{1,0:T(8,128)S(1)}, u32[]{:S(2)}, u32[]{:S(2)}) collective-permute-start(f32[264,128]{1,0:T(8,128)S(1)} %get-tuple-element.66), channel_id=1, source_target_pairs={{0,2},{2,0},{4,6},{6,4},{8,10},{10,8},{12,14},{14,12},{16,18},{18,... | collective-permute-start | bytes 405512 | tf_op jit(solution)/shard_map/ppermute | solution.py:475
  26.7 8.7 %collective-permute-start.5 = (f32[264,128]{1,0:T(8,128)S(1)}, f32[264,128]{1,0:T(8,128)S(1)}, u32[]{:S(2)}, u32[]{:S(2)}) collective-permute-start(f32[264,128]{1,0:T(8,128)S(1)} %get-tuple-element.67), channel_id=1, source_target_pairs={{0,4},{2,6},{4,0},{6,2},{8,12},{10,14},{12,8},{14,10},{16,20},{18,... | collective-permute-start | bytes 405512 | tf_op jit(solution)/shard_map/ppermute | solution.py:475
  27.9 4.8 %copy-start.4 = (f32[128,128]{1,0:T(8,128)S(1)}, f32[128,128]{1,0:T(8,128)}, u32[]{:S(2)}) copy-start(f32[128,128]{1,0:T(8,128)} %get-tuple-element.59.mark_ref) | copy-start | bytes 196612
  27.9 7.5 %collective-permute-start.6 = (f32[264,128]{1,0:T(8,128)S(1)}, f32[264,128]{1,0:T(8,128)S(1)}, u32[]{:S(2)}, u32[]{:S(2)}) collective-permute-start(f32[264,128]{1,0:T(8,128)S(1)} %get-tuple-element.68), channel_id=1, source_target_pairs={{0,6},{2,4},{4,2},{6,0},{8,14},{10,12},{12,10},{14,8},{16,22},{18,... | collective-permute-start | bytes 405512 | tf_op jit(solution)/shard_map/ppermute | solution.py:475
  28.7 9.2 %copy-start.10 = (f32[264,128]{1,0:T(8,128)}, f32[264,128]{1,0:T(8,128)S(1)}, u32[]{:S(2)}) copy-start(f32[264,128]{1,0:T(8,128)S(1)} %get-tuple-element.73.refs_4_.refs_12_) | copy-start | bytes 405508
  28.7 6.8 %collective-permute-start.11 = (f32[264,128]{1,0:T(8,128)S(1)}, f32[264,128]{1,0:T(8,128)S(1)}, u32[]{:S(2)}, u32[]{:S(2)}) collective-permute-start(f32[264,128]{1,0:T(8,128)S(1)} %get-tuple-element.74), channel_id=1, source_target_pairs={{0,2},{2,0},{4,6},{6,4},{8,10},{10,8},{12,14},{14,12},{16,18},{18,... | collective-permute-start | bytes 405512 | tf_op jit(solution)/shard_map/ppermute | solution.py:475
  30.5 5.9 %collective-permute-start.12 = (f32[264,128]{1,0:T(8,128)S(1)}, f32[264,128]{1,0:T(8,128)S(1)}, u32[]{:S(2)}, u32[]{:S(2)}) collective-permute-start(f32[264,128]{1,0:T(8,128)S(1)} %get-tuple-element.75), channel_id=1, source_target_pairs={{0,4},{2,6},{4,0},{6,2},{8,12},{10,14},{12,8},{14,10},{16,20},{18,... | collective-permute-start | bytes 405512 | tf_op jit(solution)/shard_map/ppermute | solution.py:475
  31.7 6.2 %collective-permute-start.13 = (f32[264,128]{1,0:T(8,128)S(1)}, f32[264,128]{1,0:T(8,128)S(1)}, u32[]{:S(2)}, u32[]{:S(2)}) collective-permute-start(f32[264,128]{1,0:T(8,128)S(1)} %get-tuple-element.76), channel_id=1, source_target_pairs={{0,6},{2,4},{4,2},{6,0},{8,14},{10,12},{12,10},{14,8},{16,22},{18,... | collective-permute-start | bytes 405512 | tf_op jit(solution)/shard_map/ppermute | solution.py:475
  32.7 5.2 %copy-start.3 = (bf16[128,2048]{1,0:T(8,128)(2,1)S(1)}, bf16[128,2048]{1,0:T(8,128)(2,1)}, u32[]{:S(2)}) copy-start(bf16[128,2048]{1,0:T(8,128)(2,1)} %grad_ref.7) | copy-start | bytes 1572868
  32.7 5.1 %copy-start.20 = (f32[2048]{0:T(1024)S(1)}, f32[2048]{0:T(1024)}, u32[]{:S(2)}) copy-start(f32[2048]{0:T(1024)} %param.12) | copy-start | bytes 24580
  35.4 3.3 %copy-start.6 = (f32[264,128]{1,0:T(8,128)}, f32[264,128]{1,0:T(8,128)S(1)}, u32[]{:S(2)}) copy-start(f32[264,128]{1,0:T(8,128)S(1)} %collective-permute-done.5.refs_2_.refs_10_) | copy-start | bytes 405508
  35.4 3.3 %copy-start.8 = (f32[264,128]{1,0:T(8,128)}, f32[264,128]{1,0:T(8,128)S(1)}, u32[]{:S(2)}) copy-start(f32[264,128]{1,0:T(8,128)S(1)} %collective-permute-done.6.refs_3_.refs_11_) | copy-start | bytes 405508
  35.5 3.3 %copy-start.12 = (f32[264,128]{1,0:T(8,128)}, f32[264,128]{1,0:T(8,128)S(1)}, u32[]{:S(2)}) copy-start(f32[264,128]{1,0:T(8,128)S(1)} %collective-permute-done.11.refs_5_.refs_13_) | copy-start | bytes 405508
  41.8 9.6 %collective-permute-start.14 = (f32[264,128]{1,0:T(8,128)S(1)}, f32[264,128]{1,0:T(8,128)S(1)}, u32[]{:S(2)}, u32[]{:S(2)}) collective-permute-start(f32[264,128]{1,0:T(8,128)S(1)} %get-tuple-element.91), channel_id=1, source_target_pairs={{0,2},{2,0},{4,6},{6,4},{8,10},{10,8},{12,14},{14,12},{16,18},{18,... | collective-permute-start | bytes 405512 | tf_op jit(solution)/shard_map/ppermute | solution.py:475
  43.0 9.9 %collective-permute-start.15 = (f32[264,128]{1,0:T(8,128)S(1)}, f32[264,128]{1,0:T(8,128)S(1)}, u32[]{:S(2)}, u32[]{:S(2)}) collective-permute-start(f32[264,128]{1,0:T(8,128)S(1)} %get-tuple-element.92), channel_id=1, source_target_pairs={{0,4},{2,6},{4,0},{6,2},{8,12},{10,14},{12,8},{14,10},{16,20},{18,... | collective-permute-start | bytes 405512 | tf_op jit(solution)/shard_map/ppermute | solution.py:475
  44.1 8.8 %collective-permute-start.16 = (f32[264,128]{1,0:T(8,128)S(1)}, f32[264,128]{1,0:T(8,128)S(1)}, u32[]{:S(2)}, u32[]{:S(2)}) collective-permute-start(f32[264,128]{1,0:T(8,128)S(1)} %get-tuple-element.93), channel_id=1, source_target_pairs={{0,6},{2,4},{4,2},{6,0},{8,14},{10,12},{12,10},{14,8},{16,22},{18,... | collective-permute-start | bytes 405512 | tf_op jit(solution)/shard_map/ppermute | solution.py:475
  46.1 3.8 %collective-permute-start.17 = (f32[32,128]{1,0:T(8,128)S(1)}, f32[32,128]{1,0:T(8,128)S(1)}, u32[]{:S(2)}, u32[]{:S(2)}) collective-permute-start(f32[32,128]{1,0:T(8,128)S(1)} %get-tuple-element.94.refs_4_), channel_id=1, source_target_pairs={{0,8},{2,10},{4,12},{6,14},{8,0},{10,2},{12,4},{14,6},{16,24},{18,... | collective-permute-start | bytes 49160 | tf_op jit(solution)/shard_map/ppermute | solution.py:475
  46.1 8.8 %collective-permute-start.22 = (f32[264,128]{1,0:T(8,128)S(1)}, f32[264,128]{1,0:T(8,128)S(1)}, u32[]{:S(2)}, u32[]{:S(2)}) collective-permute-start(f32[264,128]{1,0:T(8,128)S(1)} %get-tuple-element.101), channel_id=1, source_target_pairs={{0,2},{2,0},{4,6},{6,4},{8,10},{10,8},{12,14},{14,12},{16,18},{18,... | collective-permute-start | bytes 405512 | tf_op jit(solution)/shard_map/ppermute | solution.py:475
  49.9 7.9 %collective-permute-start.23 = (f32[264,128]{1,0:T(8,128)S(1)}, f32[264,128]{1,0:T(8,128)S(1)}, u32[]{:S(2)}, u32[]{:S(2)}) collective-permute-start(f32[264,128]{1,0:T(8,128)S(1)} %get-tuple-element.102), channel_id=1, source_target_pairs={{0,4},{2,6},{4,0},{6,2},{8,12},{10,14},{12,8},{14,10},{16,20},{18,... | collective-permute-start | bytes 405512 | tf_op jit(solution)/shard_map/ppermute | solution.py:475
  51.4 6.4 %collective-permute-start.24 = (f32[264,128]{1,0:T(8,128)S(1)}, f32[264,128]{1,0:T(8,128)S(1)}, u32[]{:S(2)}, u32[]{:S(2)}) collective-permute-start(f32[264,128]{1,0:T(8,128)S(1)} %get-tuple-element.103), channel_id=1, source_target_pairs={{0,6},{2,4},{4,2},{6,0},{8,14},{10,12},{12,10},{14,8},{16,22},{18,... | collective-permute-start | bytes 405512 | tf_op jit(solution)/shard_map/ppermute | solution.py:475
  53.0 7.3 %collective-permute-start.18 = (f32[264,128]{1,0:T(8,128)S(1)}, f32[264,128]{1,0:T(8,128)S(1)}, u32[]{:S(2)}, u32[]{:S(2)}) collective-permute-start(f32[264,128]{1,0:T(8,128)S(1)} %get-tuple-element.95), channel_id=1, source_target_pairs={{0,24},{2,26},{4,28},{6,30},{8,0},{10,2},{12,4},{14,6},{16,8},{18,... | collective-permute-start | bytes 405512 | tf_op jit(solution)/shard_map/ppermute | solution.py:496
  54.9 4.8 %collective-permute-start.25 = (f32[32,128]{1,0:T(8,128)S(1)}, f32[32,128]{1,0:T(8,128)S(1)}, u32[]{:S(2)}, u32[]{:S(2)}) collective-permute-start(f32[32,128]{1,0:T(8,128)S(1)} %get-tuple-element.104.refs_4_), channel_id=1, source_target_pairs={{0,16},{2,18},{4,20},{6,22},{8,24},{10,26},{12,28},{14,30},{16,0},... | collective-permute-start | bytes 49160 | tf_op jit(solution)/shard_map/ppermute | solution.py:475
  59.8 5.2 %collective-permute-start.26 = (f32[264,128]{1,0:T(8,128)S(1)}, f32[264,128]{1,0:T(8,128)S(1)}, u32[]{:S(2)}, u32[]{:S(2)}) collective-permute-start(f32[264,128]{1,0:T(8,128)S(1)} %get-tuple-element.105), channel_id=1, source_target_pairs={{0,24},{2,26},{4,28},{6,30},{8,0},{10,2},{12,4},{14,6},{16,8},{18,... | collective-permute-start | bytes 405512 | tf_op jit(solution)/shard_map/ppermute | solution.py:496
  60.3 10.8 %copy-start.17 = (f32[264,128]{1,0:T(8,128)S(1)}, f32[264,128]{1,0:T(8,128)}, u32[]{:S(2)}) copy-start(f32[264,128]{1,0:T(8,128)} %copy-done.16) | copy-start | bytes 405508
  60.5 9.3 %collective-permute-start.19 = (f32[264,128]{1,0:T(8,128)S(1)}, f32[264,128]{1,0:T(8,128)S(1)}, u32[]{:S(2)}, u32[]{:S(2)}) collective-permute-start(f32[264,128]{1,0:T(8,128)S(1)} %get-tuple-element.97), channel_id=1, source_target_pairs={{0,2},{2,0},{4,6},{6,4},{8,10},{10,8},{12,14},{14,12},{16,18},{18,... | collective-permute-start | bytes 405512 | tf_op jit(solution)/shard_map/ppermute | solution.py:475
  65.1 6.1 %copy-start.7 = (f32[264,128]{1,0:T(8,128)S(1)}, f32[264,128]{1,0:T(8,128)}, u32[]{:S(2)}) copy-start(f32[264,128]{1,0:T(8,128)} %copy-done.6) | copy-start | bytes 405508
  65.1 6.1 %copy-start.9 = (f32[264,128]{1,0:T(8,128)S(1)}, f32[264,128]{1,0:T(8,128)}, u32[]{:S(2)}) copy-start(f32[264,128]{1,0:T(8,128)} %copy-done.8) | copy-start | bytes 405508
  65.1 6.1 %copy-start.11 = (f32[264,128]{1,0:T(8,128)S(1)}, f32[264,128]{1,0:T(8,128)}, u32[]{:S(2)}) copy-start(f32[264,128]{1,0:T(8,128)} %copy-done.10) | copy-start | bytes 405508
  65.1 6.1 %copy-start.13 = (f32[264,128]{1,0:T(8,128)S(1)}, f32[264,128]{1,0:T(8,128)}, u32[]{:S(2)}) copy-start(f32[264,128]{1,0:T(8,128)} %copy-done.12) | copy-start | bytes 405508
  65.1 6.1 %copy-start.15 = (f32[264,128]{1,0:T(8,128)S(1)}, f32[264,128]{1,0:T(8,128)}, u32[]{:S(2)}) copy-start(f32[264,128]{1,0:T(8,128)} %copy-done.14) | copy-start | bytes 405508
  65.3 12.6 %collective-permute-start.27 = (f32[296,128]{1,0:T(8,128)S(1)}, f32[296,128]{1,0:T(8,128)S(1)}, u32[]{:S(2)}, u32[]{:S(2)}) collective-permute-start(f32[296,128]{1,0:T(8,128)S(1)} %get-tuple-element.108), channel_id=1, source_target_pairs={{0,2},{2,0},{4,6},{6,4},{8,10},{10,8},{12,14},{14,12},{16,18},{18,... | collective-permute-start | bytes 454664 | tf_op jit(solution)/shard_map/ppermute | solution.py:475
  66.2 11.7 %collective-permute-start.28 = (f32[296,128]{1,0:T(8,128)S(1)}, f32[296,128]{1,0:T(8,128)S(1)}, u32[]{:S(2)}, u32[]{:S(2)}) collective-permute-start(f32[296,128]{1,0:T(8,128)S(1)} %get-tuple-element.109), channel_id=1, source_target_pairs={{0,4},{2,6},{4,0},{6,2},{8,12},{10,14},{12,8},{14,10},{16,20},{18,... | collective-permute-start | bytes 454664 | tf_op jit(solution)/shard_map/ppermute | solution.py:475
  67.6 10.3 %collective-permute-start.29 = (f32[296,128]{1,0:T(8,128)S(1)}, f32[296,128]{1,0:T(8,128)S(1)}, u32[]{:S(2)}, u32[]{:S(2)}) collective-permute-start(f32[296,128]{1,0:T(8,128)S(1)} %get-tuple-element.110), channel_id=1, source_target_pairs={{0,6},{2,4},{4,2},{6,0},{8,14},{10,12},{12,10},{14,8},{16,22},{18,... | collective-permute-start | bytes 454664 | tf_op jit(solution)/shard_map/ppermute | solution.py:475
  68.9 9.0 %collective-permute-start.20 = (f32[264,128]{1,0:T(8,128)S(1)}, f32[264,128]{1,0:T(8,128)S(1)}, u32[]{:S(2)}, u32[]{:S(2)}) collective-permute-start(f32[264,128]{1,0:T(8,128)S(1)} %get-tuple-element.98), channel_id=1, source_target_pairs={{0,4},{2,6},{4,0},{6,2},{8,12},{10,14},{12,8},{14,10},{16,20},{18,... | collective-permute-start | bytes 405512 | tf_op jit(solution)/shard_map/ppermute | solution.py:475
  69.8 8.0 %collective-permute-start.21 = (f32[264,128]{1,0:T(8,128)S(1)}, f32[264,128]{1,0:T(8,128)S(1)}, u32[]{:S(2)}, u32[]{:S(2)}) collective-permute-start(f32[264,128]{1,0:T(8,128)S(1)} %get-tuple-element.99), channel_id=1, source_target_pairs={{0,6},{2,4},{4,2},{6,0},{8,14},{10,12},{12,10},{14,8},{16,22},{18,... | collective-permute-start | bytes 405512 | tf_op jit(solution)/shard_map/ppermute | solution.py:475
  (4 other events, 6.4 us)

commit v4 on v3

v4 whole, which is shorter than its diff:
```python
import jax
import jax.numpy as jnp
from jax import lax
from jax.experimental import pallas as pl
from jax.experimental.pallas import tpu as pltpu
from jax.sharding import PartitionSpec as P

GROUP = 4
INFO = 8
FAR = 1e9
NEVER = 1e30
f32 = jnp.float32
bf16 = jnp.bfloat16
HBM = pl.BlockSpec(memory_space=pltpu.HBM)
VMEM = pl.BlockSpec(memory_space=pltpu.VMEM)


def dot(a, b, over_a=1, over_b=0):
    return lax.dot_general(a, b, (((over_a,), (over_b,)), ((), ())), preferred_element_type=f32)


def halves(x):
    high = x.astype(bf16)
    return high, (x - high.astype(f32)).astype(bf16)


def decay(steps, rate):
    return jnp.exp(steps * rate)


class Sizes:
    def __init__(self, queries, decay_span):
        self.rows = queries.shape[0]
        self.heads = decay_span.shape[0]
        self.features = queries.shape[1]
        self.dim = self.features // self.heads
        self.per = self.heads // GROUP
        self.wide = self.per * self.dim
        self.pad = -(-self.heads // 8) * 8
        self.waves = 2 if self.per % 2 == 0 else 1
        self.each = self.per // self.waves
        self.state = self.each * self.dim
        self.payload = jax.ShapeDtypeStruct((self.state + INFO, self.dim), f32)
        self.block = jax.ShapeDtypeStruct((self.rows, self.features), f32)
        self.gains = jax.ShapeDtypeStruct((self.pad, self.dim), f32)


def position(size):
    return lax.broadcasted_iota(jnp.int32, (size.rows, size.dim), 0).astype(f32)


def steps_if(live, steps):
    return jnp.where(live, steps, NEVER)


def pair_steps(mark, size, earlier=1):
    shape = (size.rows, size.rows)
    here = mark if size.rows == size.dim else jnp.broadcast_to(mark[:, :1], shape)
    later = lax.broadcasted_iota(jnp.int32, shape, 1 - earlier)
    gap = later - lax.broadcasted_iota(jnp.int32, shape, earlier)
    return steps_if(jnp.logical_and(gap >= 0, here == here.T), gap.astype(f32))


def token_product(a, high, low):
    turned = a.T
    return dot(jnp.concatenate([turned, turned], 1), jnp.concatenate([high, low], 0))


def info_rows(first_row, second_row, dim):
    index = lax.broadcasted_iota(jnp.int32, (INFO, dim), 0)
    return jnp.where(index == 0, first_row, jnp.where(index == 1, second_row, 0.0))


def partners():
    me = jnp.bitwise_and(lax.axis_index("seq"), GROUP - 1)
    return [jnp.bitwise_xor(me, k) for k in range(GROUP)]


def places(backward):
    return [GROUP - 1 - p for p in partners()] if backward else partners()


def columns(size, group, h=None):
    if h is None:
        return pl.ds(pl.multiple_of(group * size.wide, size.wide), size.wide)
    return pl.ds(pl.multiple_of(group * size.wide + h * size.dim, size.dim), size.dim)


def wave_heads(size, wave):
    return [(wave * size.each + i, slice(i * size.dim, (i + 1) * size.dim)) for i in range(size.each)]


def all_pieces(size):
    return [(chunk, wave) for wave in range(size.waves) for chunk in range(GROUP)]


def rate_of(rates_ref, size, group, h):
    return rates_ref[pl.ds(group * size.per + h, 1), :]


def square_rate(rate, size):
    return rate[:, :1] if size.rows != size.dim else rate


def call(body, name, inputs, outputs, flops, moved, scratch=(), in_specs=None, out_specs=None, vmem=16):
    return pl.pallas_call(
        body,
        out_shape=outputs,
        in_specs=in_specs if in_specs is not None else [VMEM] * len(inputs),
        out_specs=out_specs if out_specs is not None else [VMEM] * len(outputs),
        scratch_shapes=list(scratch),
        compiler_params=pltpu.CompilerParams(vmem_limit_bytes=vmem * 1024 * 1024),
        cost_estimate=pl.CostEstimate(flops=flops, bytes_accessed=moved, transcendentals=0),
        name=name,
    )(*inputs)


def state_payloads(size, pieces, mark, rates_ref, group, outs, key_of, value_of):
    last, first = mark[size.rows - 1 :, :], mark[:1, :]
    ahead = steps_if(mark == last, (size.rows - 1.0) - position(size))
    for c, (chunk, wave) in enumerate(pieces):
        for h, cols in wave_heads(size, wave):
            weight = decay(ahead, rate_of(rates_ref, size, group[chunk], h))
            high, low = halves(value_of(c, h, cols).astype(f32) * weight)
            outs[c][cols, :] = token_product(key_of(c, h, cols), high, low)
        outs[c][size.state :, :] = info_rows(last, first, size.dim)


def first_states(size, pieces, seg, decay_span, key_rows, value_rows):
    n = len(pieces)
    wide = size.each * size.dim

    def body(seg_hbm, span_hbm, key_hbm, value_hbm, *refs):
        outs, mark_ref, rates_ref = refs[:n], refs[n], refs[n + 1]
        seg_row, span_row, keys, values, sems = refs[n + 2 :]
        group = partners()
        small = (
            pltpu.make_async_copy(seg_hbm, seg_row, sems.at[2, 0]),
            pltpu.make_async_copy(span_hbm, span_row, sems.at[2, 1]),
        )
        copies = []
        for copy in small:
            copy.start()
        for c, (chunk, wave) in enumerate(pieces):
            here = pl.ds(pl.multiple_of(group[chunk] * size.wide + wave * wide, wide), wide)
            copies += [
                pltpu.make_async_copy(key_hbm.at[:, here], keys.at[c], sems.at[0, c]),
                pltpu.make_async_copy(value_hbm.at[:, here], values.at[c], sems.at[1, c]),
            ]
        for copy in copies:
            copy.start()
        for copy in small:
            copy.wait()
        mark = jnp.broadcast_to(seg_row[...].astype(f32) + 1.0, (size.dim, size.rows)).T
        mark_ref[...] = mark
        rates_ref[...] = jnp.broadcast_to(-1.0 / span_row[...], (size.dim, size.heads)).T
        for copy in copies:
            copy.wait()
        state_payloads(
            size, pieces, mark, rates_ref, group, outs,
            lambda c, h, cols: keys[c, :, cols], lambda c, h, cols: values[c, :, cols],
        )

    held = (n, size.rows, wide)
    outs = call(
        body, "states", (seg, decay_span.reshape(1, size.heads), key_rows, value_rows),
        [size.payload] * n + [
            jax.ShapeDtypeStruct((size.rows, size.dim), f32),
            jax.ShapeDtypeStruct((size.heads, size.dim), f32),
        ],
        n * size.each * 4 * size.rows * size.dim * size.dim, n * wide * size.rows * 8,
        [
            pltpu.VMEM((1, size.rows), jnp.int32),
            pltpu.VMEM((1, size.heads), f32),
            pltpu.VMEM(held, bf16),
            pltpu.VMEM(held, bf16),
            pltpu.SemaphoreType.DMA((3, max(n, 2))),
        ],
        [HBM] * 4, vmem=60,
    )
    return outs[:n], outs[n], outs[n + 1]


def more_states(size, pieces, mark, rates, key_rows, value_rows):
    def body(mark_ref, rates_ref, key_ref, value_ref, *outs):
        group = partners()

        def head(ref):
            return lambda c, h, cols: ref[:, columns(size, group[pieces[c][0]], h)]

        state_payloads(
            size, pieces, mark_ref[...], rates_ref, group, outs, head(key_ref), head(value_ref)
        )

    n = len(pieces)
    return call(
        body, "states", (mark, rates, key_rows, value_rows), [size.payload] * n,
        n * size.each * 4 * size.rows * size.dim * size.dim, n * size.state * size.rows * 8,
    )


def nearby_attended(size, mark, rates, queries, key_rows, value_rows):
    def body(mark_ref, rates_ref, query_ref, key_ref, value_ref, out_ref):
        gap = pair_steps(mark_ref[...], size)
        for h in range(size.heads):
            cols = slice(h * size.dim, (h + 1) * size.dim)
            rate = square_rate(rates_ref[h : h + 1, :], size)
            weight = decay(gap, rate)
            query, key, value = query_ref[:, cols], key_ref[:, cols], value_ref[:, cols]
            high, low = halves(dot(query, key, 1, 1) * weight)
            out_ref[:, cols] = dot(
                jnp.concatenate([high, low], 1), jnp.concatenate([value, value], 0)
            )

    return call(
        body, "nearby", (mark, rates, queries, key_rows, value_rows), [size.block],
        size.heads * 6 * size.rows * size.dim * size.dim, size.features * size.rows * 10,
    )[0]


def put_rows(ref, at, rows):
    ref[at : at + rows.shape[0], :] = rows


def group_total(size, backward, wave, rates, parts, extra=0, riders=()):
    mark_row = size.state + (1 if backward else 0)

    def body(rates_ref, *refs):
        ins, out = refs[:GROUP], refs[-1]
        place = places(backward)
        marks = [ref[mark_row : mark_row + 1, :] for ref in ins]
        end = marks[0]
        for mark in marks[1:]:
            end = jnp.minimum(end, mark) if backward else jnp.maximum(end, mark)
        steps = [
            steps_if(marks[k] == end, ((GROUP - 1 - place[k]) * size.rows).astype(f32))
            for k in range(GROUP)
        ]
        me = partners()[0]
        for h, cols in wave_heads(size, wave):
            rate = rate_of(rates_ref, size, me, h)
            total = None
            for k in range(GROUP):
                term = decay(steps[k], rate) * ins[k][cols, :]
                total = term if total is None else total + term
            out[cols, :] = total
        put_rows(out, size.state, info_rows(end, end, size.dim))
        if extra:
            rows = refs[GROUP][...] if riders else jnp.zeros((extra, size.dim), f32)
            put_rows(out, size.state + INFO, rows)

    return call(
        body, "total", (rates, *parts, *riders),
        [jax.ShapeDtypeStruct((size.state + INFO + extra, size.dim), f32)],
        size.state * size.dim * 8, size.state * size.dim * 20,
    )[0]


def group_prefixes(size, backward, wave, rates, parts, entering, extra=0, riders=(), collect=()):
    mark_row = size.state + (1 if backward else 0)

    def body(rates_ref, *refs):
        ins, enter = refs[:GROUP], refs[GROUP]
        rides, outs = refs[GROUP + 1 : GROUP + 1 + len(riders)], refs[GROUP + 1 + len(riders) :]
        if collect:
            outs[-1][...] = outs[0][...] + enter[size.state + INFO :, :]
            outs = outs[1:-1]
        place = places(backward)
        me = partners()[0]
        marks = [ref[mark_row : mark_row + 1, :] for ref in ins]
        block, members = lax.axis_index("seq"), lax.axis_size("seq")
        first = block >= members - GROUP if backward else block < GROUP
        outer = jnp.where(first, FAR if backward else 0.0, enter[size.state : size.state + 1, :])
        steps = []
        for to in range(GROUP):
            now = outer
            for k in range(GROUP):
                if backward:
                    now = jnp.where(place[k] < place[to], jnp.minimum(now, marks[k]), now)
                else:
                    now = jnp.where(place[k] < place[to], jnp.maximum(now, marks[k]), now)
            put_rows(outs[to], size.state, info_rows(now, now, size.dim))
            if extra:
                total = jnp.zeros((extra, size.dim), f32)
                for ride in rides:
                    total = total + ride[...]
                put_rows(outs[to], size.state + INFO, total)
            far = (place[to] * size.rows).astype(f32)
            steps.append([steps_if(jnp.logical_and(outer == now, jnp.logical_not(first)), far)])
            for k in range(GROUP):
                gap = place[to] - 1 - place[k]
                live = jnp.logical_and(marks[k] == now, gap >= 0)
                steps[to].append(steps_if(live, (gap * size.rows).astype(f32)))
        for h, cols in wave_heads(size, wave):
            rate = rate_of(rates_ref, size, me, h)
            for to in range(GROUP):
                total = decay(steps[to][0], rate) * enter[cols, :]
                for k in range(GROUP):
                    if k != to:
                        total += decay(steps[to][1 + k], rate) * ins[k][cols, :]
                outs[to][cols, :] = total

    shape = jax.ShapeDtypeStruct((size.state + INFO + extra, size.dim), f32)
    return call(
        body, "prefixes", (rates, *parts, entering, *riders, *collect),
        [shape] * GROUP + [size.gains] * len(collect),
        size.state * size.dim * 40, size.state * size.dim * 36,
    )


def whole_attended(size, mark, rates, queries, out_grad, gain, near, entering):
    def body(mark_ref, rates_ref, query_ref, grad_ref, gain_ref, near_ref, *refs):
        states, (out_ref, sums_ref) = refs[:-2], refs[-2:]
        group = partners()
        mark = mark_ref[...]
        behind = steps_if(mark == states[0][size.state : size.state + 1, :], position(size) + 1.0)
        square = jnp.zeros((size.rows, size.dim), f32)
        cross = jnp.zeros((size.rows, size.dim), f32)
        for i, (c, wave) in enumerate(all_pieces(size)):
            for h, cols in wave_heads(size, wave):
                here = columns(size, group[c], h)
                rate = rate_of(rates_ref, size, group[c], h)
                weight = decay(behind, rate)
                query = query_ref[:, here]
                high, low = halves(states[i][cols, :])
                inter = dot(jnp.concatenate([query, query], 1), jnp.concatenate([high, low], 0))
                out = near_ref[:, here] + weight * inter
                out_ref[:, here] = out
                square += out * out
                cross += grad_ref[:, here].astype(f32) * gain_ref[:, here] * out
        square = jnp.sum(square.T, axis=0, keepdims=True)
        cross = jnp.sum(cross.T, axis=0, keepdims=True)
        index = lax.broadcasted_iota(jnp.int32, (8, size.rows), 0)
        sums_ref[...] = jnp.where(index == 0, square, jnp.where(index == 1, cross, 0.0))

    return call(
        body, "attended", (mark, rates, queries, out_grad, gain, near, *entering),
        [size.block, jax.ShapeDtypeStruct((8, size.rows), f32)],
        size.heads * 4 * size.rows * size.dim * size.dim, size.features * size.rows * 16,
    )


def output_grad_states(size, pieces, norm, mark, rates, queries, out_grad, gain, attended, sums, count=False):
    n = len(pieces)

    def body(mark_ref, rates_ref, query_ref, grad_ref, gain_ref, att_ref, sums_ref, *outs):
        group = partners()
        mark = mark_ref[...]
        last, first = mark[size.rows - 1 :, :], mark[:1, :]
        wide = (size.dim, size.rows)
        square = jnp.broadcast_to(sums_ref[0:1, :], wide).T
        cross = jnp.broadcast_to(sums_ref[1:2, :], wide).T
        inv = lax.rsqrt(square / norm + 1e-06)
        pull = inv * inv * inv * cross / norm
        gone = steps_if(mark == first, position(size))
        for c, (chunk, wave) in enumerate(pieces):
            back_ref, state_ref = outs[2 * c : 2 * c + 2]
            for h, cols in wave_heads(size, wave):
                here = columns(size, group[chunk], h)
                rate = rate_of(rates_ref, size, group[chunk], h)
                weight = decay(gone, rate)
                grad = grad_ref[:, here].astype(f32) * inv
                att = att_ref[:, here]
                back = gain_ref[:, here] * grad - att * pull
                back_ref[:, cols] = back
                high, low = halves(back * weight)
                state_ref[cols, :] = token_product(query_ref[:, here], high, low)
            put_rows(state_ref, size.state, info_rows(last, first, size.dim))
            put_rows(state_ref, size.state + INFO, jnp.zeros((size.pad, size.dim), f32))
        if count:
            outs[2 * n][...] = jnp.zeros(size.gains.shape, f32)
            for chunk in range(GROUP):
                for h in range(size.per):
                    here = columns(size, group[chunk], h)
                    part = grad_ref[:, here].astype(f32) * inv * att_ref[:, here]
                    at = chunk * size.per + h
                    outs[2 * n][at : at + 1, :] = jnp.sum(part, axis=0, keepdims=True)

    part = jax.ShapeDtypeStruct((size.rows, size.state), f32)
    outs = call(
        body, "back", (mark, rates, queries, out_grad, gain, attended, sums),
        [part, jax.ShapeDtypeStruct((size.state + INFO + size.pad, size.dim), f32)] * n + [size.gains] * count,
        n * size.each * 4 * size.rows * size.dim * size.dim, n * size.state * size.rows * 16,
    )
    return outs[0 : 2 * n : 2], outs[1 : 2 * n : 2], outs[2 * n :]


def local_gradients(size, mark, rates, queries, key_rows, value_rows, back, entering):
    def body(mark_ref, rates_ref, query_ref, key_ref, value_ref, *refs):
        n = GROUP * size.waves
        backs, states = refs[:n], refs[n : 2 * n]
        out_hbm, local_key, local_value, done, sems = refs[2 * n :]
        group = partners()
        mark = mark_ref[...]
        gap, turned_gap = pair_steps(mark, size), pair_steps(mark, size, 0)
        behind = steps_if(mark == states[0][size.state : size.state + 1, :], position(size) + 1.0)
        copies = []
        for c in range(GROUP):
            for h in range(size.per):
                here = columns(size, group[c], h)
                piece = c + GROUP * (h // size.each)
                cols = slice(h % size.each * size.dim, (h % size.each + 1) * size.dim)
                rate = rate_of(rates_ref, size, group[c], h)
                rows_rate = square_rate(rate, size)
                weight, turned_weight = decay(gap, rows_rate), decay(turned_gap, rows_rate)
                query, key, value = query_ref[:, here], key_ref[:, here], value_ref[:, here]
                high, low = halves(backs[piece][:, cols])
                both, values = jnp.concatenate([high, low], 1), jnp.concatenate([value, value], 1)
                grads_high, grads_low = halves(dot(both, values, 1, 1) * weight)
                part = dot(
                    jnp.concatenate([grads_high, grads_low], 1), jnp.concatenate([key, key], 0)
                )
                state_high, state_low = halves(states[piece][cols, :])
                inter = dot(
                    jnp.concatenate([high, high, low], 1),
                    jnp.concatenate([state_high, state_low, state_high], 1),
                    1, 1,
                )
                done[c, :, h * size.dim : (h + 1) * size.dim] = (
                    part + decay(behind, rate) * inter
                ).astype(bf16)
                grads_high, grads_low = halves(dot(values, both, 1, 1) * turned_weight)
                local_key[:, here] = dot(
                    jnp.concatenate([grads_high, grads_low], 1),
                    jnp.concatenate([query, query], 0),
                )
                score_high, score_low = halves(dot(key, query, 1, 1) * turned_weight)
                local_value[:, here] = dot(
                    jnp.concatenate([score_high, score_high, score_low], 1),
                    jnp.concatenate([high, low, high], 0),
                )
            copies.append(
                pltpu.make_async_copy(
                    done.at[c], out_hbm.at[:, columns(size, group[c])], sems.at[c]
                )
            )
            copies[c].start()
        for copy in copies:
            copy.wait()

    return call(
        body, "gradients", (mark, rates, queries, key_rows, value_rows, *back, *entering),
        [jax.ShapeDtypeStruct((size.rows, size.features), bf16), size.block, size.block],
        size.heads * 26 * size.rows * size.dim * size.dim, size.features * size.rows * 24,
        [pltpu.VMEM((GROUP, size.rows, size.wide), bf16), pltpu.SemaphoreType.DMA((GROUP,))],
        None, [HBM, VMEM, VMEM],
    )


def final_gradients(size, mark, rates, key_rows, value_rows, local_key, local_value, entering):
    def body(mark_ref, rates_ref, key_ref, value_ref, local_key_ref, local_value_ref, *refs):
        n = GROUP * size.waves
        states, (keys_hbm, values_hbm, gain_hbm) = refs[:n], refs[n : n + 3]
        keys, values, gains, sems = refs[n + 3 :]
        group = partners()
        mark = mark_ref[...]
        left = steps_if(mark == states[0][size.state : size.state + 1, :], size.rows - position(size))
        for c in range(GROUP):
            for h in range(size.per):
                total = None
                for k in range(GROUP):
                    at = size.state + INFO + (k ^ c) * size.per + h
                    row = states[n - GROUP + k][at : at + 1, :]
                    total = row if total is None else total + row
                gains[:, columns(size, group[c], h)] = total
        copies = [pltpu.make_async_copy(gains, gain_hbm, sems.at[2, 0])]
        copies[0].start()
        for c in range(GROUP):
            for h in range(size.per):
                here = columns(size, group[c], h)
                piece = c + GROUP * (h // size.each)
                at = slice(h % size.each * size.dim, (h % size.each + 1) * size.dim)
                cols = slice(h * size.dim, (h + 1) * size.dim)
                rate = rate_of(rates_ref, size, group[c], h)
                weight = decay(left, rate)
                key, value = key_ref[:, here], value_ref[:, here]
                high, low = halves(states[piece][at, :])
                from_values = dot(
                    jnp.concatenate([value, value], 1), jnp.concatenate([high, low], 1), 1, 1
                )
                from_keys = dot(jnp.concatenate([key, key], 1), jnp.concatenate([high, low], 0))
                keys[c, :, cols] = (local_key_ref[:, here] + weight * from_values).astype(bf16)
                values[c, :, cols] = (local_value_ref[:, here] + weight * from_keys).astype(bf16)
            here = columns(size, group[c])
            for copy in (
                pltpu.make_async_copy(keys.at[c], keys_hbm.at[:, here], sems.at[0, c]),
                pltpu.make_async_copy(values.at[c], values_hbm.at[:, here], sems.at[1, c]),
            ):
                copy.start()
                copies.append(copy)
        for copy in copies:
            copy.wait()

    shape = jax.ShapeDtypeStruct((size.rows, size.features), bf16)
    held = pltpu.VMEM((GROUP, size.rows, size.wide), bf16)
    return call(
        body, "final", (mark, rates, key_rows, value_rows, local_key, local_value, *entering),
        [shape, shape, jax.ShapeDtypeStruct((1, size.features), f32)],
        size.heads * 8 * size.rows * size.dim * size.dim, size.features * size.rows * 24,
        [held, held, pltpu.VMEM((1, size.features), f32), pltpu.SemaphoreType.DMA((3, GROUP))],
        None, [HBM] * 3,
    )


def swap(array, distance):
    members = lax.axis_size("seq")
    return lax.ppermute(array, "seq", [(i, i ^ distance) for i in range(members)])


def exchange(payloads):
    return [payloads[0]] + [swap(payloads[k], k) for k in range(1, GROUP)]


def shifted(array, by):
    members = lax.axis_size("seq")
    pairs = [(i, i + by) for i in range(members) if 0 <= i + by < members]
    return lax.ppermute(array, "seq", pairs)


def cyclic(array, by):
    members = lax.axis_size("seq")
    return lax.ppermute(array, "seq", [(i, (i + by) % members) for i in range(members)])


def reach_of_documents(size):
    longest = lax.axis_size("seq") * size.rows // 4
    return max(longest - 2, 0) // (GROUP * size.rows) + 1


def from_other_groups(size, backward, wave, decay_span, total):
    needed = reach_of_documents(size)
    way = -GROUP if backward else GROUP
    if needed == 1:
        return cyclic(total, way)
    result = shifted(total, way)
    reach = 1
    start = partners()[0] * size.per + wave * size.each
    mine = lax.dynamic_slice(decay_span, (start,), (size.each,))
    while reach < needed:
        incoming = shifted(result, way * reach)
        passes = incoming[size.state, 0] == result[size.state, 0]
        factor = jnp.where(passes, jnp.exp(-(reach * GROUP * size.rows) / mine), 0.0)
        factor = jnp.repeat(factor, size.dim)[:, None]
        result = result.at[: size.state].add(factor * incoming[: size.state])
        reach *= 2
    return result


def local(queries, key_rows, value_rows, segment_ids, decay_span, norm_gain, out_grad):
    size = Sizes(queries, decay_span)
    norm = size.features * lax.axis_size("head")
    members = lax.axis_size("seq")
    seg = segment_ids.reshape(1, size.rows)
    gain = norm_gain.reshape(1, size.features)
    waves = range(size.waves)
    sent = [[(chunk, wave) for chunk in (3, 1, 2)] for wave in waves]
    kept = [(0, wave) for wave in waves]
    every = all_pieces(size)
    calls = [sent[0], sum(sent[1:], []) + kept]

    outs, mark, rates = first_states(size, calls[0], seg, decay_span, key_rows, value_rows)
    common = (mark, rates)
    states = dict(zip(calls[0], outs))
    states |= zip(calls[1], more_states(size, calls[1], *common, key_rows, value_rows))
    near = nearby_attended(size, *common, queries, key_rows, value_rows)
    entering = {}
    parts = {w: exchange({k: states[k, w] for k in range(GROUP)}) for w in waves}
    totals = {w: group_total(size, False, w, rates, parts[w]) for w in waves}
    outer = {w: from_other_groups(size, False, w, decay_span, totals[w]) for w in waves}
    for w in waves:
        outs = exchange(group_prefixes(size, False, w, rates, parts[w], outer[w]))
        entering |= {(k, w): outs[k] for k in range(GROUP)}
    entering = [entering[piece] for piece in every]

    attended, sums = whole_attended(size, *common, queries, out_grad, gain, near, entering)
    sums = lax.psum(sums, "head")
    back, states = {}, {}
    for pieces in calls:
        backs, payloads, gains = output_grad_states(
            size, pieces, norm, *common, queries, out_grad, gain, attended, sums, pieces is calls[1]
        )
        back |= zip(pieces, backs)
        states |= zip(pieces, payloads)
    back = [back[piece] for piece in every]

    parts = {w: exchange({k: states[k, w] for k in range(GROUP)}) for w in waves}
    leaving, summed = {}, 1
    rides = size.waves > 1 and reach_of_documents(size) == 1 and members > GROUP
    totals = {}
    for w in waves:
        riders = gains if rides and w == 0 else ()
        totals[w] = group_total(size, True, w, rates, parts[w], size.pad * rides, riders)
    outer = {w: from_other_groups(size, True, w, decay_span, totals[w]) for w in waves}
    for w in waves:
        if w < size.waves - 1:
            riders, collect = (), (gains if rides and w == 0 else ())
        else:
            while summed * GROUP < members:
                gains = [sum(gains), cyclic(sum(gains), -summed * GROUP)]
                summed *= 2
            riders, collect = gains, ()
        outs = group_prefixes(
            size, True, w, rates, parts[w], outer[w], size.pad, riders, collect
        )
        if collect:
            gains, summed = outs[GROUP:], 2
        outs = exchange(outs[:GROUP])
        leaving |= {(k, w): outs[k] for k in range(GROUP)}
    leaving = [leaving[piece] for piece in every]

    query_grad, local_key, local_value = local_gradients(
        size, *common, queries, key_rows, value_rows, back, entering
    )
    key_grad, value_grad, gain_grad = final_gradients(
        size, *common, key_rows, value_rows, local_key, local_value, leaving
    )
    return query_grad, key_grad, value_grad, gain_grad.reshape(size.features)


def solution(mesh):
    rows = P("seq", "head")
    in_specs = (rows, rows, rows, P("seq"), P("head"), P("head"), rows)
    return jax.shard_map(
        local, mesh=mesh, in_specs=in_specs, out_specs=(rows, rows, rows, P("head")), check_vma=False
    )
```

time: 80 us -> 76.1 us (0.951)
  Pallas kernels: 21.1 us -> 15.1 us
  starting transfers between devices: 37.1 us -> 40.3 us
    pallas_call x18 -> x16, Pallas kernels: 21.1 us -> 15.1 us  [call(): pl.pallas_call(body, out_shape=outputs, in_specs=in_specs if in_specs is...]
    ppermute x4 -> x5, waiting for transfers between devices: 4.4 us -> 1.91 us  [cyclic(): lax.ppermute(array, 'seq', [(i, (i + by) % members) for i in range(member...]
    ppermute x4 -> x5, starting transfers between devices: 6.13 us -> 8.3 us  [cyclic(): lax.ppermute(array, 'seq', [(i, (i + by) % members) for i in range(member...]
    ppermute x26 -> x24, waiting for transfers between devices: 12.5 us -> 14.2 us  [swap(): lax.ppermute(array, 'seq', [(i, i ^ distance) for i in range(members)])]
    ppermute x26 -> x24, starting transfers between devices: 30.9 us -> 32 us  [swap(): lax.ppermute(array, 'seq', [(i, i ^ distance) for i in range(members)])]
  transfers between devices with their start and end apart: 30 -> 29, of which waited for: 8 -> 14; matrix products, arithmetic and copies ran while one was open for 0% -> 0% of each run, Pallas kernels for 20% -> 13%
where the time goes in v4:
time: 76.1 us; the launch traced here: 75.9 us
  starting transfers between devices  40.3 us (53%)
  waiting for transfers between devices  16.1 us (21%)
  Pallas kernels  15.1 us (20%)
  blocking collectives  2.47 us (3%)
  between operations  1.08 us (1%)
  local copies, waits for them, and re-layouts  0.92 us (1%)
    ppermute x24, starting transfers between devices, swap(): lax.ppermute(array, 'seq', [(i, i ^ distance) for i in range(members)])  32 us
    pallas_call x16, Pallas kernels, call(): pl.pallas_call(body, out_shape=outputs, in_specs=in_specs if in_specs is...  15.1 us
    ppermute x24, waiting for transfers between devices, swap(): lax.ppermute(array, 'seq', [(i, i ^ distance) for i in range(members)])  14.2 us
    ppermute x5, starting transfers between devices, cyclic(): lax.ppermute(array, 'seq', [(i, (i + by) % members) for i in range(member...  8.3 us
    psum x1, blocking collectives, local(): sums = lax.psum(sums, 'head')  2.47 us
    ppermute x5, waiting for transfers between devices, cyclic(): lax.ppermute(array, 'seq', [(i, (i + by) % members) for i in range(member...  1.91 us
  transfers between devices with their start and end apart: 29, of which 14 were waited for; matrix products, arithmetic and copies ran while one was open for 0% of the time, Pallas kernels for 13%

profile of v4, /device:TPU:0, one launch (start us, length us, event | category | flops | bytes accessed | tf_op | source)
XLA Modules:
  0.0 75.9 jit_solution(12938626665860533611)
XLA Ops:
  0.7 2.2 %states.2 = (f32[264,128]{1,0:T(8,128)}, f32[264,128]{1,0:T(8,128)}, f32[264,128]{1,0:T(8,128)}, f32[128,128]{1,0:T(8,128)}, f32[16,128]{1,0:T(8,128)}) custom-call(s32[1,128]{1,0:T(1,128)} %bitcast.7, f32[1,16]{1,0:T(1,128)} %bitcast.8, bf16[128,2048]{1,0:T(8,128)(2,1)} %key_ref.7, bf16[128,2048]{1,0:T(8,128)(2,1)} %value_ref.7), custom_call_target="tpu_custom_call" | custom-call | flops 50331648 | bytes 786432 | tf_op jit(solution)/shard_map/states/pallas_call | solution.py:106
  2.8 3.0 %collective-permute-start = (f32[264,128]{1,0:T(8,128)}, f32[264,128]{1,0:T(8,128)S(1)}, u32[]{:S(2)}, u32[]{:S(2)}) collective-permute-start(f32[264,128]{1,0:T(8,128)} %get-tuple-element.59), channel_id=1, source_target_pairs={{0,2},{2,0},{4,6},{6,4},{8,10},{10,8},{12,14},{14,12},{16,18},{18,... | collective-permute-start | bytes 405512 | tf_op jit(solution)/shard_map/ppermute | solution.py:507
  5.8 1.5 %collective-permute-start.1 = (f32[264,128]{1,0:T(8,128)}, f32[264,128]{1,0:T(8,128)S(1)}, u32[]{:S(2)}, u32[]{:S(2)}) collective-permute-start(f32[264,128]{1,0:T(8,128)} %get-tuple-element.60), channel_id=1, source_target_pairs={{0,4},{2,6},{4,0},{6,2},{8,12},{10,14},{12,8},{14,10},{16,20},{18,... | collective-permute-start | bytes 405512 | tf_op jit(solution)/shard_map/ppermute | solution.py:507
  7.4 0.8 %copy-done.4 = f32[128,128]{1,0:T(8,128)S(1)} copy-done((f32[128,128]{1,0:T(8,128)S(1)}, f32[128,128]{1,0:T(8,128)}, u32[]{:S(2)}) %copy-start.4) | copy-done | bytes 65560
  8.6 2.0 %collective-permute-start.7 = (f32[264,128]{1,0:T(8,128)S(1)}, f32[264,128]{1,0:T(8,128)S(1)}, u32[]{:S(2)}, u32[]{:S(2)}) collective-permute-start(f32[264,128]{1,0:T(8,128)S(1)} %get-tuple-element.67), channel_id=1, source_target_pairs={{0,2},{2,0},{4,6},{6,4},{8,10},{10,8},{12,14},{14,12},{16,18},{18,... | collective-permute-start | bytes 405512 | tf_op jit(solution)/shard_map/ppermute | solution.py:507
  10.7 1.5 %collective-permute-start.8 = (f32[264,128]{1,0:T(8,128)S(1)}, f32[264,128]{1,0:T(8,128)S(1)}, u32[]{:S(2)}, u32[]{:S(2)}) collective-permute-start(f32[264,128]{1,0:T(8,128)S(1)} %get-tuple-element.68), channel_id=1, source_target_pairs={{0,4},{2,6},{4,0},{6,2},{8,12},{10,14},{12,8},{14,10},{16,20},{18,... | collective-permute-start | bytes 405512 | tf_op jit(solution)/shard_map/ppermute | solution.py:507
  12.2 1.3 %collective-permute-start.9 = (f32[264,128]{1,0:T(8,128)S(1)}, f32[264,128]{1,0:T(8,128)S(1)}, u32[]{:S(2)}, u32[]{:S(2)}) collective-permute-start(f32[264,128]{1,0:T(8,128)S(1)} %get-tuple-element.69), channel_id=1, source_target_pairs={{0,6},{2,4},{4,2},{6,0},{8,14},{10,12},{12,10},{14,8},{16,22},{18,... | collective-permute-start | bytes 405512 | tf_op jit(solution)/shard_map/ppermute | solution.py:507
  13.5 1.1 %collective-permute-done.1.refs_2_ = f32[264,128]{1,0:T(8,128)S(1)} collective-permute-done((f32[264,128]{1,0:T(8,128)}, f32[264,128]{1,0:T(8,128)S(1)}, u32[]{:S(2)}, u32[]{:S(2)}) %collective-permute-start.1) | collective-permute-done | bytes 135200 | tf_op jit(solution)/shard_map/ppermute | solution.py:507
  14.6 0.5 collective-permute-done.2.refs_3_
  15.1 1.6 %collective-permute-start.3 = (f32[264,128]{1,0:T(8,128)S(1)}, f32[264,128]{1,0:T(8,128)S(1)}, u32[]{:S(2)}, u32[]{:S(2)}) collective-permute-start(f32[264,128]{1,0:T(8,128)S(1)} %total.4), channel_id=1, source_target_pairs={{0,8},{2,10},{4,12},{6,14},{8,16},{10,18},{12,20},{14,22},{16,24},... | collective-permute-start | bytes 405512 | tf_op jit(solution)/shard_map/ppermute | solution.py:522
  16.9 2.9 %collective-permute-done.8.refs_2_ = f32[264,128]{1,0:T(8,128)S(1)} collective-permute-done((f32[264,128]{1,0:T(8,128)S(1)}, f32[264,128]{1,0:T(8,128)S(1)}, u32[]{:S(2)}, u32[]{:S(2)}) %collective-permute-start.8) | collective-permute-done | bytes 135200 | tf_op jit(solution)/shard_map/ppermute | solution.py:507
  19.9 1.6 %collective-permute-start.10 = (f32[264,128]{1,0:T(8,128)S(1)}, f32[264,128]{1,0:T(8,128)S(1)}, u32[]{:S(2)}, u32[]{:S(2)}) collective-permute-start(f32[264,128]{1,0:T(8,128)S(1)} %total.5), channel_id=1, source_target_pairs={{0,8},{2,10},{4,12},{6,14},{8,16},{10,18},{12,20},{14,22},{16,24},... | collective-permute-start | bytes 405512 | tf_op jit(solution)/shard_map/ppermute | solution.py:522
  21.5 0.5 collective-permute-done.3.refs_4_
  22.2 1.4 %collective-permute-start.4 = (f32[264,128]{1,0:T(8,128)S(1)}, f32[264,128]{1,0:T(8,128)S(1)}, u32[]{:S(2)}, u32[]{:S(2)}) collective-permute-start(f32[264,128]{1,0:T(8,128)S(1)} %get-tuple-element.63), channel_id=1, source_target_pairs={{0,2},{2,0},{4,6},{6,4},{8,10},{10,8},{12,14},{14,12},{16,18},{18,... | collective-permute-start | bytes 405512 | tf_op jit(solution)/shard_map/ppermute | solution.py:507
  23.6 1.2 %collective-permute-start.5 = (f32[264,128]{1,0:T(8,128)S(1)}, f32[264,128]{1,0:T(8,128)S(1)}, u32[]{:S(2)}, u32[]{:S(2)}) collective-permute-start(f32[264,128]{1,0:T(8,128)S(1)} %get-tuple-element.64), channel_id=1, source_target_pairs={{0,4},{2,6},{4,0},{6,2},{8,12},{10,14},{12,8},{14,10},{16,20},{18,... | collective-permute-start | bytes 405512 | tf_op jit(solution)/shard_map/ppermute | solution.py:507
  24.7 1.4 %collective-permute-start.6 = (f32[264,128]{1,0:T(8,128)S(1)}, f32[264,128]{1,0:T(8,128)S(1)}, u32[]{:S(2)}, u32[]{:S(2)}) collective-permute-start(f32[264,128]{1,0:T(8,128)S(1)} %get-tuple-element.65), channel_id=1, source_target_pairs={{0,6},{2,4},{4,2},{6,0},{8,14},{10,12},{12,10},{14,8},{16,22},{18,... | collective-permute-start | bytes 405512 | tf_op jit(solution)/shard_map/ppermute | solution.py:507
  26.1 0.6 collective-permute-done.10.refs_4_
  26.9 1.3 %collective-permute-start.11 = (f32[264,128]{1,0:T(8,128)S(1)}, f32[264,128]{1,0:T(8,128)S(1)}, u32[]{:S(2)}, u32[]{:S(2)}) collective-permute-start(f32[264,128]{1,0:T(8,128)S(1)} %get-tuple-element.71), channel_id=1, source_target_pairs={{0,2},{2,0},{4,6},{6,4},{8,10},{10,8},{12,14},{14,12},{16,18},{18,... | collective-permute-start | bytes 405512 | tf_op jit(solution)/shard_map/ppermute | solution.py:507
  28.2 0.8 %collective-permute-start.12 = (f32[264,128]{1,0:T(8,128)S(1)}, f32[264,128]{1,0:T(8,128)S(1)}, u32[]{:S(2)}, u32[]{:S(2)}) collective-permute-start(f32[264,128]{1,0:T(8,128)S(1)} %get-tuple-element.72), channel_id=1, source_target_pairs={{0,4},{2,6},{4,0},{6,2},{8,12},{10,14},{12,8},{14,10},{16,20},{18,... | collective-permute-start | bytes 405512 | tf_op jit(solution)/shard_map/ppermute | solution.py:507
  29.1 1.4 %collective-permute-start.13 = (f32[264,128]{1,0:T(8,128)S(1)}, f32[264,128]{1,0:T(8,128)S(1)}, u32[]{:S(2)}, u32[]{:S(2)}) collective-permute-start(f32[264,128]{1,0:T(8,128)S(1)} %get-tuple-element.73), channel_id=1, source_target_pairs={{0,6},{2,4},{4,2},{6,0},{8,14},{10,12},{12,10},{14,8},{16,22},{18,... | collective-permute-start | bytes 405512 | tf_op jit(solution)/shard_map/ppermute | solution.py:507
  30.5 2.7 %nearby.1.near_ref = f32[128,2048]{1,0:T(8,128)S(1)} custom-call(f32[128,128]{1,0:T(8,128)S(1)} %copy-done.5, f32[16,128]{1,0:T(8,128)S(1)} %copy-done.6, bf16[128,2048]{1,0:T(8,128)(2,1)S(1)} %copy-done.2, bf16[128,2048]{1,0:T(8,128)(2,1)S(1)} %copy-done, bf16[128,2048]{1,0:T(8,128)(2,1)S(1)} %copy-done.1), custom_call_target="tpu_custom_call" | custom-call | flops 201326592 | bytes 2621440 | tf_op jit(solution)/shard_map/nearby/pallas_call | solution.py:106
  33.2 0.7 collective-permute-done.11.refs_5_.refs_13_
  33.9 1.0 %collective-permute-done.12.refs_6_.refs_14_ = f32[264,128]{1,0:T(8,128)S(1)} collective-permute-done((f32[264,128]{1,0:T(8,128)S(1)}, f32[264,128]{1,0:T(8,128)S(1)}, u32[]{:S(2)}, u32[]{:S(2)}) %collective-permute-start.12) | collective-permute-done | bytes 135200 | tf_op jit(solution)/shard_map/ppermute | solution.py:507
  34.9 1.4 %collective-permute-done.13.refs_7_.refs_15_ = f32[264,128]{1,0:T(8,128)S(1)} collective-permute-done((f32[264,128]{1,0:T(8,128)S(1)}, f32[264,128]{1,0:T(8,128)S(1)}, u32[]{:S(2)}, u32[]{:S(2)}) %collective-permute-start.13) | collective-permute-done | bytes 135200 | tf_op jit(solution)/shard_map/ppermute | solution.py:507
  36.4 0.8 %attended.1 = (f32[128,2048]{1,0:T(8,128)S(1)}, f32[8,128]{1,0:T(8,128)S(1)}) custom-call(f32[128,128]{1,0:T(8,128)S(1)} %copy-done.5, f32[16,128]{1,0:T(8,128)S(1)} %copy-done.6, bf16[128,2048]{1,0:T(8,128)(2,1)S(1)} %copy-done.2, bf16[128,2048]{1,0:T(8,128)(2,1)S(1)} %copy-done.3, f32[1,2048]{1,0:T(1,128)S(1)} %bitcast.4, f32[128,2048]{1,0:T(8,128)S(1)} %nearby.1.near_ref, ...), custom_call_target="tpu_custom_call" | custom-call | flops 134217728 | bytes 4194304 | tf_op jit(solution)/shard_map/attended/pallas_call | solution.py:106
  37.2 2.5 %psum.7.sums_ref = f32[8,128]{1,0:T(8,128)S(1)} all-reduce(f32[8,128]{1,0:T(8,128)S(1)} %get-tuple-element.75), channel_id=1, replica_groups=mesh['seq'=16,'head'=2] {'head'}, use_global_device_ids=true, to_apply=%region_0.0 | all-reduce | flops 1024 | bytes 8192 | tf_op jit(solution)/shard_map/psum | solution.py:576
  40.2 1.3 %collective-permute-start.14 = (f32[280,128]{1,0:T(8,128)S(1)}, f32[280,128]{1,0:T(8,128)S(1)}, u32[]{:S(2)}, u32[]{:S(2)}) collective-permute-start(f32[280,128]{1,0:T(8,128)S(1)} %get-tuple-element.88), channel_id=1, source_target_pairs={{0,2},{2,0},{4,6},{6,4},{8,10},{10,8},{12,14},{14,12},{16,18},{18,... | collective-permute-start | bytes 430088 | tf_op jit(solution)/shard_map/ppermute | solution.py:507
  41.5 1.3 %collective-permute-start.15 = (f32[280,128]{1,0:T(8,128)S(1)}, f32[280,128]{1,0:T(8,128)S(1)}, u32[]{:S(2)}, u32[]{:S(2)}) collective-permute-start(f32[280,128]{1,0:T(8,128)S(1)} %get-tuple-element.89), channel_id=1, source_target_pairs={{0,4},{2,6},{4,0},{6,2},{8,12},{10,14},{12,8},{14,10},{16,20},{18,... | collective-permute-start | bytes 430088 | tf_op jit(solution)/shard_map/ppermute | solution.py:507
  42.8 0.9 %collective-permute-start.16 = (f32[280,128]{1,0:T(8,128)S(1)}, f32[280,128]{1,0:T(8,128)S(1)}, u32[]{:S(2)}, u32[]{:S(2)}) collective-permute-start(f32[280,128]{1,0:T(8,128)S(1)} %get-tuple-element.90), channel_id=1, source_target_pairs={{0,6},{2,4},{4,2},{6,0},{8,14},{10,12},{12,10},{14,8},{16,22},{18,... | collective-permute-start | bytes 430088 | tf_op jit(solution)/shard_map/ppermute | solution.py:507
  43.7 0.9 %back.2 = (f32[128,256]{1,0:T(8,128)S(1)}, f32[280,128]{1,0:T(8,128)S(1)}, f32[128,256]{1,0:T(8,128)S(1)}, f32[280,128]{1,0:T(8,128)S(1)}, f32[128,256]{1,0:T(8,...) custom-call(f32[128,128]{1,0:T(8,128)S(1)} %copy-done.5, ...), custom_call_target="tpu_custom_call" | custom-call | flops 83886080 | bytes 2621440 | tf_op jit(solution)/shard_map/back/pallas_call | solution.py:106
  44.6 1.3 %collective-permute-start.21 = (f32[280,128]{1,0:T(8,128)S(1)}, f32[280,128]{1,0:T(8,128)S(1)}, u32[]{:S(2)}, u32[]{:S(2)}) collective-permute-start(f32[280,128]{1,0:T(8,128)S(1)} %get-tuple-element.97), channel_id=1, source_target_pairs={{0,2},{2,0},{4,6},{6,4},{8,10},{10,8},{12,14},{14,12},{16,18},{18,... | collective-permute-start | bytes 430088 | tf_op jit(solution)/shard_map/ppermute | solution.py:507
  46.0 1.3 %collective-permute-start.22 = (f32[280,128]{1,0:T(8,128)S(1)}, f32[280,128]{1,0:T(8,128)S(1)}, u32[]{:S(2)}, u32[]{:S(2)}) collective-permute-start(f32[280,128]{1,0:T(8,128)S(1)} %get-tuple-element.98), channel_id=1, source_target_pairs={{0,4},{2,6},{4,0},{6,2},{8,12},{10,14},{12,8},{14,10},{16,20},{18,... | collective-permute-start | bytes 430088 | tf_op jit(solution)/shard_map/ppermute | solution.py:507
  47.3 1.6 %collective-permute-start.23 = (f32[280,128]{1,0:T(8,128)S(1)}, f32[280,128]{1,0:T(8,128)S(1)}, u32[]{:S(2)}, u32[]{:S(2)}) collective-permute-start(f32[280,128]{1,0:T(8,128)S(1)} %get-tuple-element.99), channel_id=1, source_target_pairs={{0,6},{2,4},{4,2},{6,0},{8,14},{10,12},{12,10},{14,8},{16,22},{18,... | collective-permute-start | bytes 430088 | tf_op jit(solution)/shard_map/ppermute | solution.py:507
  48.9 1.6 %collective-permute-done.15.refs_2_ = f32[280,128]{1,0:T(8,128)S(1)} collective-permute-done((f32[280,128]{1,0:T(8,128)S(1)}, f32[280,128]{1,0:T(8,128)S(1)}, u32[]{:S(2)}, u32[]{:S(2)}) %collective-permute-start.15) | collective-permute-done | bytes 143392 | tf_op jit(solution)/shard_map/ppermute | solution.py:507
  50.6 2.1 %collective-permute-start.17 = (f32[280,128]{1,0:T(8,128)S(1)}, f32[280,128]{1,0:T(8,128)S(1)}, u32[]{:S(2)}, u32[]{:S(2)}) collective-permute-start(f32[280,128]{1,0:T(8,128)S(1)} %total.6), channel_id=1, source_target_pairs={{0,24},{2,26},{4,28},{6,30},{8,0},{10,2},{12,4},{14,6},{16,8},{18,... | collective-permute-start | bytes 430088 | tf_op jit(solution)/shard_map/ppermute | solution.py:522
  53.0 3.3 %collective-permute-done.22.refs_2_ = f32[280,128]{1,0:T(8,128)S(1)} collective-permute-done((f32[280,128]{1,0:T(8,128)S(1)}, f32[280,128]{1,0:T(8,128)S(1)}, u32[]{:S(2)}, u32[]{:S(2)}) %collective-permute-start.22) | collective-permute-done | bytes 143392 | tf_op jit(solution)/shard_map/ppermute | solution.py:507
  56.3 2.3 %collective-permute-start.24 = (f32[280,128]{1,0:T(8,128)S(1)}, f32[280,128]{1,0:T(8,128)S(1)}, u32[]{:S(2)}, u32[]{:S(2)}) collective-permute-start(f32[280,128]{1,0:T(8,128)S(1)} %total.7), channel_id=1, source_target_pairs={{0,24},{2,26},{4,28},{6,30},{8,0},{10,2},{12,4},{14,6},{16,8},{18,... | collective-permute-start | bytes 430088 | tf_op jit(solution)/shard_map/ppermute | solution.py:522
  58.8 0.7 collective-permute-start.18
  59.5 0.7 collective-permute-start.25
  60.2 1.3 %collective-permute-start.19 = (f32[280,128]{1,0:T(8,128)S(1)}, f32[280,128]{1,0:T(8,128)S(1)}, u32[]{:S(2)}, u32[]{:S(2)}) collective-permute-start(f32[280,128]{1,0:T(8,128)S(1)} %get-tuple-element.94), channel_id=1, source_target_pairs={{0,4},{2,6},{4,0},{6,2},{8,12},{10,14},{12,8},{14,10},{16,20},{18,... | collective-permute-start | bytes 430088 | tf_op jit(solution)/shard_map/ppermute | solution.py:507
  61.5 1.8 %collective-permute-start.20 = (f32[280,128]{1,0:T(8,128)S(1)}, f32[280,128]{1,0:T(8,128)S(1)}, u32[]{:S(2)}, u32[]{:S(2)}) collective-permute-start(f32[280,128]{1,0:T(8,128)S(1)} %get-tuple-element.95), channel_id=1, source_target_pairs={{0,6},{2,4},{4,2},{6,0},{8,14},{10,12},{12,10},{14,8},{16,22},{18,... | collective-permute-start | bytes 430088 | tf_op jit(solution)/shard_map/ppermute | solution.py:507
  63.2 0.8 %collective-permute-done.25.refs_6_ = f32[16,128]{1,0:T(8,128)S(1)} collective-permute-done((f32[16,128]{1,0:T(8,128)S(1)}, f32[16,128]{1,0:T(8,128)S(1)}, u32[]{:S(2)}, u32[]{:S(2)}) %collective-permute-start.25) | collective-permute-done | bytes 8224 | tf_op jit(solution)/shard_map/ppermute | solution.py:522
  64.2 1.5 %collective-permute-start.26 = (f32[280,128]{1,0:T(8,128)S(1)}, f32[280,128]{1,0:T(8,128)S(1)}, u32[]{:S(2)}, u32[]{:S(2)}) collective-permute-start(f32[280,128]{1,0:T(8,128)S(1)} %get-tuple-element.102), channel_id=1, source_target_pairs={{0,2},{2,0},{4,6},{6,4},{8,10},{10,8},{12,14},{14,12},{16,18},{18,... | collective-permute-start | bytes 430088 | tf_op jit(solution)/shard_map/ppermute | solution.py:507
  65.7 0.9 %collective-permute-start.27 = (f32[280,128]{1,0:T(8,128)S(1)}, f32[280,128]{1,0:T(8,128)S(1)}, u32[]{:S(2)}, u32[]{:S(2)}) collective-permute-start(f32[280,128]{1,0:T(8,128)S(1)} %get-tuple-element.103), channel_id=1, source_target_pairs={{0,4},{2,6},{4,0},{6,2},{8,12},{10,14},{12,8},{14,10},{16,20},{18,... | collective-permute-start | bytes 430088 | tf_op jit(solution)/shard_map/ppermute | solution.py:507
  66.6 1.2 %collective-permute-start.28 = (f32[280,128]{1,0:T(8,128)S(1)}, f32[280,128]{1,0:T(8,128)S(1)}, u32[]{:S(2)}, u32[]{:S(2)}) collective-permute-start(f32[280,128]{1,0:T(8,128)S(1)} %get-tuple-element.104), channel_id=1, source_target_pairs={{0,6},{2,4},{4,2},{6,0},{8,14},{10,12},{12,10},{14,8},{16,22},{18,... | collective-permute-start | bytes 430088 | tf_op jit(solution)/shard_map/ppermute | solution.py:507
  67.8 5.1 %gradients.1 = (bf16[128,2048]{1,0:T(8,128)(2,1)}, f32[128,2048]{1,0:T(8,128)S(1)}, f32[128,2048]{1,0:T(8,128)S(1)}) custom-call(f32[128,128]{1,0:T(8,128)S(1)} %copy-done.5, f32[16,128]{1,0:T(8,128)S(1)} %copy-done.6, bf16[128,2048]{1,0:T(8,128)(2,1)S(1)} %copy-done.2, bf16[128,2048]{1,0:T(8,128)(2,1)S(1)} %copy-done, bf16[128,2048]{1,0:T(8,128)(2,1)S(1)} %copy-done.1, ...), custom_call_target="tpu_custom_call" | custom-call | flops 872415232 | bytes 6291456 | tf_op jit(solution)/shard_map/gradients/pallas_call | solution.py:106
  73.0 1.2 %collective-permute-done.27.refs_6_ = f32[280,128]{1,0:T(8,128)S(1)} collective-permute-done((f32[280,128]{1,0:T(8,128)S(1)}, f32[280,128]{1,0:T(8,128)S(1)}, u32[]{:S(2)}, u32[]{:S(2)}) %collective-permute-start.27) | collective-permute-done | bytes 143392 | tf_op jit(solution)/shard_map/ppermute | solution.py:507
  74.2 1.6 %final.1 = (bf16[128,2048]{1,0:T(8,128)(2,1)}, bf16[128,2048]{1,0:T(8,128)(2,1)}, f32[1,2048]{1,0:T(1,128)}) custom-call(f32[128,128]{1,0:T(8,128)S(1)} %copy-done.5, f32[16,128]{1,0:T(8,128)S(1)} %copy-done.6, bf16[128,2048]{1,0:T(8,128)(2,1)S(1)} %copy-done, bf16[128,2048]{1,0:T(8,128)(2,1)S(1)} %copy-done.1, ...), custom_call_target="tpu_custom_call" | custom-call | flops 268435456 | bytes 6291456 | tf_op jit(solution)/shard_map/final/pallas_call | solution.py:106
  (67 shorter events, 2.5 us)
Async XLA Ops:
  0.6 6.8 %copy-start = (bf16[128,2048]{1,0:T(8,128)(2,1)S(1)}, bf16[128,2048]{1,0:T(8,128)(2,1)}, u32[]{:S(2)}) copy-start(bf16[128,2048]{1,0:T(8,128)(2,1)} %key_ref.7) | copy-start | bytes 1572868
  0.6 6.7 %copy-start.1 = (bf16[128,2048]{1,0:T(8,128)(2,1)S(1)}, bf16[128,2048]{1,0:T(8,128)(2,1)}, u32[]{:S(2)}) copy-start(bf16[128,2048]{1,0:T(8,128)(2,1)} %value_ref.7) | copy-start | bytes 1572868
  2.8 4.6 %copy-start.6 = (f32[16,128]{1,0:T(8,128)S(1)}, f32[16,128]{1,0:T(8,128)}, u32[]{:S(2)}) copy-start(f32[16,128]{1,0:T(8,128)} %get-tuple-element.57.rates_ref) | copy-start | bytes 24580
  2.8 9.3 %collective-permute-start = (f32[264,128]{1,0:T(8,128)}, f32[264,128]{1,0:T(8,128)S(1)}, u32[]{:S(2)}, u32[]{:S(2)}) collective-permute-start(f32[264,128]{1,0:T(8,128)} %get-tuple-element.59), channel_id=1, source_target_pairs={{0,2},{2,0},{4,6},{6,4},{8,10},{10,8},{12,14},{14,12},{16,18},{18,... | collective-permute-start | bytes 405512 | tf_op jit(solution)/shard_map/ppermute | solution.py:507
  5.8 8.7 %collective-permute-start.1 = (f32[264,128]{1,0:T(8,128)}, f32[264,128]{1,0:T(8,128)S(1)}, u32[]{:S(2)}, u32[]{:S(2)}) collective-permute-start(f32[264,128]{1,0:T(8,128)} %get-tuple-element.60), channel_id=1, source_target_pairs={{0,4},{2,6},{4,0},{6,2},{8,12},{10,14},{12,8},{14,10},{16,20},{18,... | collective-permute-start | bytes 405512 | tf_op jit(solution)/shard_map/ppermute | solution.py:507
  7.4 7.7 %collective-permute-start.2 = (f32[264,128]{1,0:T(8,128)}, f32[264,128]{1,0:T(8,128)S(1)}, u32[]{:S(2)}, u32[]{:S(2)}) collective-permute-start(f32[264,128]{1,0:T(8,128)} %get-tuple-element.61), channel_id=1, source_target_pairs={{0,6},{2,4},{4,2},{6,0},{8,14},{10,12},{12,10},{14,8},{16,22},{18,... | collective-permute-start | bytes 405512 | tf_op jit(solution)/shard_map/ppermute | solution.py:507
  8.6 8.3 %collective-permute-start.7 = (f32[264,128]{1,0:T(8,128)S(1)}, f32[264,128]{1,0:T(8,128)S(1)}, u32[]{:S(2)}, u32[]{:S(2)}) collective-permute-start(f32[264,128]{1,0:T(8,128)S(1)} %get-tuple-element.67), channel_id=1, source_target_pairs={{0,2},{2,0},{4,6},{6,4},{8,10},{10,8},{12,14},{14,12},{16,18},{18,... | collective-permute-start | bytes 405512 | tf_op jit(solution)/shard_map/ppermute | solution.py:507
  10.7 9.1 %collective-permute-start.8 = (f32[264,128]{1,0:T(8,128)S(1)}, f32[264,128]{1,0:T(8,128)S(1)}, u32[]{:S(2)}, u32[]{:S(2)}) collective-permute-start(f32[264,128]{1,0:T(8,128)S(1)} %get-tuple-element.68), channel_id=1, source_target_pairs={{0,4},{2,6},{4,0},{6,2},{8,12},{10,14},{12,8},{14,10},{16,20},{18,... | collective-permute-start | bytes 405512 | tf_op jit(solution)/shard_map/ppermute | solution.py:507
  12.2 7.6 %collective-permute-start.9 = (f32[264,128]{1,0:T(8,128)S(1)}, f32[264,128]{1,0:T(8,128)S(1)}, u32[]{:S(2)}, u32[]{:S(2)}) collective-permute-start(f32[264,128]{1,0:T(8,128)S(1)} %get-tuple-element.69), channel_id=1, source_target_pairs={{0,6},{2,4},{4,2},{6,0},{8,14},{10,12},{12,10},{14,8},{16,22},{18,... | collective-permute-start | bytes 405512 | tf_op jit(solution)/shard_map/ppermute | solution.py:507
  15.1 6.9 %collective-permute-start.3 = (f32[264,128]{1,0:T(8,128)S(1)}, f32[264,128]{1,0:T(8,128)S(1)}, u32[]{:S(2)}, u32[]{:S(2)}) collective-permute-start(f32[264,128]{1,0:T(8,128)S(1)} %total.4), channel_id=1, source_target_pairs={{0,8},{2,10},{4,12},{6,14},{8,16},{10,18},{12,20},{14,22},{16,24},... | collective-permute-start | bytes 405512 | tf_op jit(solution)/shard_map/ppermute | solution.py:522
  19.9 10.6 %copy-start.2 = (bf16[128,2048]{1,0:T(8,128)(2,1)S(1)}, bf16[128,2048]{1,0:T(8,128)(2,1)}, u32[]{:S(2)}) copy-start(bf16[128,2048]{1,0:T(8,128)(2,1)} %query_ref.9) | copy-start | bytes 1572868
  19.9 6.9 %collective-permute-start.10 = (f32[264,128]{1,0:T(8,128)S(1)}, f32[264,128]{1,0:T(8,128)S(1)}, u32[]{:S(2)}, u32[]{:S(2)}) collective-permute-start(f32[264,128]{1,0:T(8,128)S(1)} %total.5), channel_id=1, source_target_pairs={{0,8},{2,10},{4,12},{6,14},{8,16},{10,18},{12,20},{14,22},{16,24},... | collective-permute-start | bytes 405512 | tf_op jit(solution)/shard_map/ppermute | solution.py:522
  22.2 6.9 %collective-permute-start.4 = (f32[264,128]{1,0:T(8,128)S(1)}, f32[264,128]{1,0:T(8,128)S(1)}, u32[]{:S(2)}, u32[]{:S(2)}) collective-permute-start(f32[264,128]{1,0:T(8,128)S(1)} %get-tuple-element.63), channel_id=1, source_target_pairs={{0,2},{2,0},{4,6},{6,4},{8,10},{10,8},{12,14},{14,12},{16,18},{18,... | collective-permute-start | bytes 405512 | tf_op jit(solution)/shard_map/ppermute | solution.py:507
  23.6 9.6 %collective-permute-start.5 = (f32[264,128]{1,0:T(8,128)S(1)}, f32[264,128]{1,0:T(8,128)S(1)}, u32[]{:S(2)}, u32[]{:S(2)}) collective-permute-start(f32[264,128]{1,0:T(8,128)S(1)} %get-tuple-element.64), channel_id=1, source_target_pairs={{0,4},{2,6},{4,0},{6,2},{8,12},{10,14},{12,8},{14,10},{16,20},{18,... | collective-permute-start | bytes 405512 | tf_op jit(solution)/shard_map/ppermute | solution.py:507
  24.7 5.8 %copy-start.5 = (f32[128,128]{1,0:T(8,128)S(1)}, f32[128,128]{1,0:T(8,128)}, u32[]{:S(2)}) copy-start(f32[128,128]{1,0:T(8,128)} %get-tuple-element.56.mark_ref) | copy-start | bytes 196612
  24.7 8.5 %collective-permute-start.6 = (f32[264,128]{1,0:T(8,128)S(1)}, f32[264,128]{1,0:T(8,128)S(1)}, u32[]{:S(2)}, u32[]{:S(2)}) collective-permute-start(f32[264,128]{1,0:T(8,128)S(1)} %get-tuple-element.65), channel_id=1, source_target_pairs={{0,6},{2,4},{4,2},{6,0},{8,14},{10,12},{12,10},{14,8},{16,22},{18,... | collective-permute-start | bytes 405512 | tf_op jit(solution)/shard_map/ppermute | solution.py:507
  26.9 9.4 %copy-start.11 = (f32[264,128]{1,0:T(8,128)}, f32[264,128]{1,0:T(8,128)S(1)}, u32[]{:S(2)}) copy-start(f32[264,128]{1,0:T(8,128)S(1)} %get-tuple-element.70.refs_4_.refs_12_) | copy-start | bytes 405508
  26.9 7.0 %collective-permute-start.11 = (f32[264,128]{1,0:T(8,128)S(1)}, f32[264,128]{1,0:T(8,128)S(1)}, u32[]{:S(2)}, u32[]{:S(2)}) collective-permute-start(f32[264,128]{1,0:T(8,128)S(1)} %get-tuple-element.71), channel_id=1, source_target_pairs={{0,2},{2,0},{4,6},{6,4},{8,10},{10,8},{12,14},{14,12},{16,18},{18,... | collective-permute-start | bytes 405512 | tf_op jit(solution)/shard_map/ppermute | solution.py:507
  28.2 6.7 %collective-permute-start.12 = (f32[264,128]{1,0:T(8,128)S(1)}, f32[264,128]{1,0:T(8,128)S(1)}, u32[]{:S(2)}, u32[]{:S(2)}) collective-permute-start(f32[264,128]{1,0:T(8,128)S(1)} %get-tuple-element.72), channel_id=1, source_target_pairs={{0,4},{2,6},{4,0},{6,2},{8,12},{10,14},{12,8},{14,10},{16,20},{18,... | collective-permute-start | bytes 405512 | tf_op jit(solution)/shard_map/ppermute | solution.py:507
  29.1 7.3 %copy-start.3 = (bf16[128,2048]{1,0:T(8,128)(2,1)S(1)}, bf16[128,2048]{1,0:T(8,128)(2,1)}, u32[]{:S(2)}) copy-start(bf16[128,2048]{1,0:T(8,128)(2,1)} %grad_ref.5) | copy-start | bytes 1572868
  29.1 7.3 %collective-permute-start.13 = (f32[264,128]{1,0:T(8,128)S(1)}, f32[264,128]{1,0:T(8,128)S(1)}, u32[]{:S(2)}, u32[]{:S(2)}) collective-permute-start(f32[264,128]{1,0:T(8,128)S(1)} %get-tuple-element.73), channel_id=1, source_target_pairs={{0,6},{2,4},{4,2},{6,0},{8,14},{10,12},{12,10},{14,8},{16,22},{18,... | collective-permute-start | bytes 405512 | tf_op jit(solution)/shard_map/ppermute | solution.py:507
  30.5 5.9 %copy-start.19 = (f32[2048]{0:T(1024)S(1)}, f32[2048]{0:T(1024)}, u32[]{:S(2)}) copy-start(f32[2048]{0:T(1024)} %param.12) | copy-start | bytes 24580
  33.2 4.0 %copy-start.7 = (f32[264,128]{1,0:T(8,128)}, f32[264,128]{1,0:T(8,128)S(1)}, u32[]{:S(2)}) copy-start(f32[264,128]{1,0:T(8,128)S(1)} %collective-permute-done.5.refs_2_.refs_10_) | copy-start | bytes 405508
  33.2 4.0 %copy-start.9 = (f32[264,128]{1,0:T(8,128)}, f32[264,128]{1,0:T(8,128)S(1)}, u32[]{:S(2)}) copy-start(f32[264,128]{1,0:T(8,128)S(1)} %collective-permute-done.6.refs_3_.refs_11_) | copy-start | bytes 405508
  33.9 3.3 %copy-start.13 = (f32[264,128]{1,0:T(8,128)}, f32[264,128]{1,0:T(8,128)S(1)}, u32[]{:S(2)}) copy-start(f32[264,128]{1,0:T(8,128)S(1)} %collective-permute-done.11.refs_5_.refs_13_) | copy-start | bytes 405508
  34.9 2.3 %copy-start.15 = (f32[264,128]{1,0:T(8,128)}, f32[264,128]{1,0:T(8,128)S(1)}, u32[]{:S(2)}) copy-start(f32[264,128]{1,0:T(8,128)S(1)} %collective-permute-done.12.refs_6_.refs_14_) | copy-start | bytes 405508
  36.3 0.9 %copy-start.17 = (f32[264,128]{1,0:T(8,128)}, f32[264,128]{1,0:T(8,128)S(1)}, u32[]{:S(2)}) copy-start(f32[264,128]{1,0:T(8,128)S(1)} %collective-permute-done.13.refs_7_.refs_15_) | copy-start | bytes 405508
  40.2 7.1 %collective-permute-start.14 = (f32[280,128]{1,0:T(8,128)S(1)}, f32[280,128]{1,0:T(8,128)S(1)}, u32[]{:S(2)}, u32[]{:S(2)}) collective-permute-start(f32[280,128]{1,0:T(8,128)S(1)} %get-tuple-element.88), channel_id=1, source_target_pairs={{0,2},{2,0},{4,6},{6,4},{8,10},{10,8},{12,14},{14,12},{16,18},{18,... | collective-permute-start | bytes 430088 | tf_op jit(solution)/shard_map/ppermute | solution.py:507
  41.5 9.0 %collective-permute-start.15 = (f32[280,128]{1,0:T(8,128)S(1)}, f32[280,128]{1,0:T(8,128)S(1)}, u32[]{:S(2)}, u32[]{:S(2)}) collective-permute-start(f32[280,128]{1,0:T(8,128)S(1)} %get-tuple-element.89), channel_id=1, source_target_pairs={{0,4},{2,6},{4,0},{6,2},{8,12},{10,14},{12,8},{14,10},{16,20},{18,... | collective-permute-start | bytes 430088 | tf_op jit(solution)/shard_map/ppermute | solution.py:507
  42.8 7.7 %collective-permute-start.16 = (f32[280,128]{1,0:T(8,128)S(1)}, f32[280,128]{1,0:T(8,128)S(1)}, u32[]{:S(2)}, u32[]{:S(2)}) collective-permute-start(f32[280,128]{1,0:T(8,128)S(1)} %get-tuple-element.90), channel_id=1, source_target_pairs={{0,6},{2,4},{4,2},{6,0},{8,14},{10,12},{12,10},{14,8},{16,22},{18,... | collective-permute-start | bytes 430088 | tf_op jit(solution)/shard_map/ppermute | solution.py:507
  44.6 8.4 %collective-permute-start.21 = (f32[280,128]{1,0:T(8,128)S(1)}, f32[280,128]{1,0:T(8,128)S(1)}, u32[]{:S(2)}, u32[]{:S(2)}) collective-permute-start(f32[280,128]{1,0:T(8,128)S(1)} %get-tuple-element.97), channel_id=1, source_target_pairs={{0,2},{2,0},{4,6},{6,4},{8,10},{10,8},{12,14},{14,12},{16,18},{18,... | collective-permute-start | bytes 430088 | tf_op jit(solution)/shard_map/ppermute | solution.py:507
  46.0 10.3 %collective-permute-start.22 = (f32[280,128]{1,0:T(8,128)S(1)}, f32[280,128]{1,0:T(8,128)S(1)}, u32[]{:S(2)}, u32[]{:S(2)}) collective-permute-start(f32[280,128]{1,0:T(8,128)S(1)} %get-tuple-element.98), channel_id=1, source_target_pairs={{0,4},{2,6},{4,0},{6,2},{8,12},{10,14},{12,8},{14,10},{16,20},{18,... | collective-permute-start | bytes 430088 | tf_op jit(solution)/shard_map/ppermute | solution.py:507
  47.3 9.0 %collective-permute-start.23 = (f32[280,128]{1,0:T(8,128)S(1)}, f32[280,128]{1,0:T(8,128)S(1)}, u32[]{:S(2)}, u32[]{:S(2)}) collective-permute-start(f32[280,128]{1,0:T(8,128)S(1)} %get-tuple-element.99), channel_id=1, source_target_pairs={{0,6},{2,4},{4,2},{6,0},{8,14},{10,12},{12,10},{14,8},{16,22},{18,... | collective-permute-start | bytes 430088 | tf_op jit(solution)/shard_map/ppermute | solution.py:507
  50.6 8.0 %collective-permute-start.17 = (f32[280,128]{1,0:T(8,128)S(1)}, f32[280,128]{1,0:T(8,128)S(1)}, u32[]{:S(2)}, u32[]{:S(2)}) collective-permute-start(f32[280,128]{1,0:T(8,128)S(1)} %total.6), channel_id=1, source_target_pairs={{0,24},{2,26},{4,28},{6,30},{8,0},{10,2},{12,4},{14,6},{16,8},{18,... | collective-permute-start | bytes 430088 | tf_op jit(solution)/shard_map/ppermute | solution.py:522
  56.3 6.9 %collective-permute-start.24 = (f32[280,128]{1,0:T(8,128)S(1)}, f32[280,128]{1,0:T(8,128)S(1)}, u32[]{:S(2)}, u32[]{:S(2)}) collective-permute-start(f32[280,128]{1,0:T(8,128)S(1)} %total.7), channel_id=1, source_target_pairs={{0,24},{2,26},{4,28},{6,30},{8,0},{10,2},{12,4},{14,6},{16,8},{18,... | collective-permute-start | bytes 430088 | tf_op jit(solution)/shard_map/ppermute | solution.py:522
  58.6 9.2 %copy-start.18 = (f32[264,128]{1,0:T(8,128)S(1)}, f32[264,128]{1,0:T(8,128)}, u32[]{:S(2)}) copy-start(f32[264,128]{1,0:T(8,128)} %copy-done.17) | copy-start | bytes 405508
  58.8 7.8 %collective-permute-start.18 = (f32[280,128]{1,0:T(8,128)S(1)}, f32[280,128]{1,0:T(8,128)S(1)}, u32[]{:S(2)}, u32[]{:S(2)}) collective-permute-start(f32[280,128]{1,0:T(8,128)S(1)} %get-tuple-element.93), channel_id=1, source_target_pairs={{0,2},{2,0},{4,6},{6,4},{8,10},{10,8},{12,14},{14,12},{16,18},{18,... | collective-permute-start | bytes 430088 | tf_op jit(solution)/shard_map/ppermute | solution.py:507
  59.5 4.5 %collective-permute-start.25 = (f32[16,128]{1,0:T(8,128)S(1)}, f32[16,128]{1,0:T(8,128)S(1)}, u32[]{:S(2)}, u32[]{:S(2)}) collective-permute-start(f32[16,128]{1,0:T(8,128)S(1)} %get-tuple-element.100.refs_5_), channel_id=1, source_target_pairs={{0,16},{2,18},{4,20},{6,22},{8,24},{10,26},{12,28},{14,30},{16,0},... | collective-permute-start | bytes 24584 | tf_op jit(solution)/shard_map/ppermute | solution.py:522
  60.2 12.8 %collective-permute-start.19 = (f32[280,128]{1,0:T(8,128)S(1)}, f32[280,128]{1,0:T(8,128)S(1)}, u32[]{:S(2)}, u32[]{:S(2)}) collective-permute-start(f32[280,128]{1,0:T(8,128)S(1)} %get-tuple-element.94), channel_id=1, source_target_pairs={{0,4},{2,6},{4,0},{6,2},{8,12},{10,14},{12,8},{14,10},{16,20},{18,... | collective-permute-start | bytes 430088 | tf_op jit(solution)/shard_map/ppermute | solution.py:507
  61.4 6.4 %copy-start.8 = (f32[264,128]{1,0:T(8,128)S(1)}, f32[264,128]{1,0:T(8,128)}, u32[]{:S(2)}) copy-start(f32[264,128]{1,0:T(8,128)} %copy-done.7) | copy-start | bytes 405508
  61.4 6.4 %copy-start.10 = (f32[264,128]{1,0:T(8,128)S(1)}, f32[264,128]{1,0:T(8,128)}, u32[]{:S(2)}) copy-start(f32[264,128]{1,0:T(8,128)} %copy-done.9) | copy-start | bytes 405508
  61.4 6.4 %copy-start.12 = (f32[264,128]{1,0:T(8,128)S(1)}, f32[264,128]{1,0:T(8,128)}, u32[]{:S(2)}) copy-start(f32[264,128]{1,0:T(8,128)} %copy-done.11) | copy-start | bytes 405508
  61.4 6.4 %copy-start.14 = (f32[264,128]{1,0:T(8,128)S(1)}, f32[264,128]{1,0:T(8,128)}, u32[]{:S(2)}) copy-start(f32[264,128]{1,0:T(8,128)} %copy-done.13) | copy-start | bytes 405508
  61.4 6.4 %copy-start.16 = (f32[264,128]{1,0:T(8,128)S(1)}, f32[264,128]{1,0:T(8,128)}, u32[]{:S(2)}) copy-start(f32[264,128]{1,0:T(8,128)} %copy-done.15) | copy-start | bytes 405508
  61.5 11.5 %collective-permute-start.20 = (f32[280,128]{1,0:T(8,128)S(1)}, f32[280,128]{1,0:T(8,128)S(1)}, u32[]{:S(2)}, u32[]{:S(2)}) collective-permute-start(f32[280,128]{1,0:T(8,128)S(1)} %get-tuple-element.95), channel_id=1, source_target_pairs={{0,6},{2,4},{4,2},{6,0},{8,14},{10,12},{12,10},{14,8},{16,22},{18,... | collective-permute-start | bytes 430088 | tf_op jit(solution)/shard_map/ppermute | solution.py:507
  64.2 8.8 %collective-permute-start.26 = (f32[280,128]{1,0:T(8,128)S(1)}, f32[280,128]{1,0:T(8,128)S(1)}, u32[]{:S(2)}, u32[]{:S(2)}) collective-permute-start(f32[280,128]{1,0:T(8,128)S(1)} %get-tuple-element.102), channel_id=1, source_target_pairs={{0,2},{2,0},{4,6},{6,4},{8,10},{10,8},{12,14},{14,12},{16,18},{18,... | collective-permute-start | bytes 430088 | tf_op jit(solution)/shard_map/ppermute | solution.py:507
  65.7 8.5 %collective-permute-start.27 = (f32[280,128]{1,0:T(8,128)S(1)}, f32[280,128]{1,0:T(8,128)S(1)}, u32[]{:S(2)}, u32[]{:S(2)}) collective-permute-start(f32[280,128]{1,0:T(8,128)S(1)} %get-tuple-element.103), channel_id=1, source_target_pairs={{0,4},{2,6},{4,0},{6,2},{8,12},{10,14},{12,8},{14,10},{16,20},{18,... | collective-permute-start | bytes 430088 | tf_op jit(solution)/shard_map/ppermute | solution.py:507
  66.6 7.6 %collective-permute-start.28 = (f32[280,128]{1,0:T(8,128)S(1)}, f32[280,128]{1,0:T(8,128)S(1)}, u32[]{:S(2)}, u32[]{:S(2)}) collective-permute-start(f32[280,128]{1,0:T(8,128)S(1)} %get-tuple-element.104), channel_id=1, source_target_pairs={{0,6},{2,4},{4,2},{6,0},{8,14},{10,12},{12,10},{14,8},{16,22},{18,... | collective-permute-start | bytes 430088 | tf_op jit(solution)/shard_map/ppermute | solution.py:507
  (1 other events, 0.8 us)

commit v5 on v4

--- a/solution.py
+++ b/solution.py
@@ -6,7 +6,7 @@
 from jax.sharding import PartitionSpec as P
 
 GROUP = 4
-INFO = 8
+MARKS = 2
 FAR = 1e9
 NEVER = 1e30
 f32 = jnp.float32
@@ -36,13 +36,13 @@
         self.dim = self.features // self.heads
         self.per = self.heads // GROUP
         self.wide = self.per * self.dim
-        self.pad = -(-self.heads // 8) * 8
+        self.info = -(-(MARKS + self.per) // 8) * 8
         self.waves = 2 if self.per % 2 == 0 else 1
         self.each = self.per // self.waves
         self.state = self.each * self.dim
-        self.payload = jax.ShapeDtypeStruct((self.state + INFO, self.dim), f32)
+        self.payload = jax.ShapeDtypeStruct((self.state + self.info, self.dim), f32)
         self.block = jax.ShapeDtypeStruct((self.rows, self.features), f32)
-        self.gains = jax.ShapeDtypeStruct((self.pad, self.dim), f32)
+        self.rows_of_gain = jax.ShapeDtypeStruct((self.info, self.dim), f32)
 
 
 def position(size):
@@ -66,9 +66,17 @@
     return dot(jnp.concatenate([turned, turned], 1), jnp.concatenate([high, low], 0))
 
 
-def info_rows(first_row, second_row, dim):
-    index = lax.broadcasted_iota(jnp.int32, (INFO, dim), 0)
-    return jnp.where(index == 0, first_row, jnp.where(index == 1, second_row, 0.0))
+def info_rows(size, last, first, more=()):
+    index = lax.broadcasted_iota(jnp.int32, (size.info, size.dim), 0)
+    rows = jnp.zeros((size.info, size.dim), f32)
+    for i, row in enumerate((last, first, *more)):
+        rows = jnp.where(index == i, row, rows)
+    return rows
+
+
+def with_marks(size, last, first, rows):
+    index = lax.broadcasted_iota(jnp.int32, (size.info, size.dim), 0)
+    return jnp.where(index == 0, last, jnp.where(index == 1, first, rows))
 
 
 def partners():
@@ -88,6 +96,10 @@
 
 def wave_heads(size, wave):
     return [(wave * size.each + i, slice(i * size.dim, (i + 1) * size.dim)) for i in range(size.each)]
+
+
+def wave_columns(size, h):
+    return slice(h % size.each * size.dim, (h % size.each + 1) * size.dim)
 
 
 def all_pieces(size):
@@ -123,7 +135,7 @@
             weight = decay(ahead, rate_of(rates_ref, size, group[chunk], h))
             high, low = halves(value_of(c, h, cols).astype(f32) * weight)
             outs[c][cols, :] = token_product(key_of(c, h, cols), high, low)
-        outs[c][size.state :, :] = info_rows(last, first, size.dim)
+        outs[c][size.state :, :] = info_rows(size, last, first)
 
 
 def first_states(size, pieces, seg, decay_span, key_rows, value_rows):
@@ -222,11 +234,11 @@
     ref[at : at + rows.shape[0], :] = rows
 
 
-def group_total(size, backward, wave, rates, parts, extra=0, riders=()):
+def group_total(size, backward, wave, rates, parts):
     mark_row = size.state + (1 if backward else 0)
 
     def body(rates_ref, *refs):
-        ins, out = refs[:GROUP], refs[-1]
+        ins, out = refs[:GROUP], refs[GROUP]
         place = places(backward)
         marks = [ref[mark_row : mark_row + 1, :] for ref in ins]
         end = marks[0]
@@ -244,27 +256,29 @@
                 term = decay(steps[k], rate) * ins[k][cols, :]
                 total = term if total is None else total + term
             out[cols, :] = total
-        put_rows(out, size.state, info_rows(end, end, size.dim))
-        if extra:
-            rows = refs[GROUP][...] if riders else jnp.zeros((extra, size.dim), f32)
-            put_rows(out, size.state + INFO, rows)
+        gains = ins[0][size.state :, :]
+        for k in range(1, GROUP):
+            gains = gains + ins[k][size.state :, :]
+        put_rows(out, size.state, with_marks(size, end, end, gains))
 
     return call(
-        body, "total", (rates, *parts, *riders),
-        [jax.ShapeDtypeStruct((size.state + INFO + extra, size.dim), f32)],
+        body, "total", (rates, *parts), [size.payload],
         size.state * size.dim * 8, size.state * size.dim * 20,
     )[0]
 
 
-def group_prefixes(size, backward, wave, rates, parts, entering, extra=0, riders=(), collect=()):
+def group_prefixes(size, backward, wave, rates, parts, entering, riders=(), collect=()):
     mark_row = size.state + (1 if backward else 0)
 
     def body(rates_ref, *refs):
         ins, enter = refs[:GROUP], refs[GROUP]
         rides, outs = refs[GROUP + 1 : GROUP + 1 + len(riders)], refs[GROUP + 1 + len(riders) :]
         if collect:
-            outs[-1][...] = outs[0][...] + enter[size.state + INFO :, :]
+            put_rows(outs[-1], 0, outs[0][size.state :, :] + enter[size.state :, :])
             outs = outs[1:-1]
+        gains = jnp.zeros((size.info, size.dim), f32)
+        for ride in rides:
+            gains = gains + ride[: size.info, :]
         place = places(backward)
         me = partners()[0]
         marks = [ref[mark_row : mark_row + 1, :] for ref in ins]
@@ -279,12 +293,7 @@
                     now = jnp.where(place[k] < place[to], jnp.minimum(now, marks[k]), now)
                 else:
                     now = jnp.where(place[k] < place[to], jnp.maximum(now, marks[k]), now)
-            put_rows(outs[to], size.state, info_rows(now, now, size.dim))
-            if extra:
-                total = jnp.zeros((extra, size.dim), f32)
-                for ride in rides:
-                    total = total + ride[...]
-                put_rows(outs[to], size.state + INFO, total)
+            put_rows(outs[to], size.state, with_marks(size, now, now, gains))
             far = (place[to] * size.rows).astype(f32)
             steps.append([steps_if(jnp.logical_and(outer == now, jnp.logical_not(first)), far)])
             for k in range(GROUP):
@@ -300,10 +309,9 @@
                         total += decay(steps[to][1 + k], rate) * ins[k][cols, :]
                 outs[to][cols, :] = total
 
-    shape = jax.ShapeDtypeStruct((size.state + INFO + extra, size.dim), f32)
     return call(
         body, "prefixes", (rates, *parts, entering, *riders, *collect),
-        [shape] * GROUP + [size.gains] * len(collect),
+        [size.payload] * GROUP + [size.rows_of_gain] * len(collect),
         size.state * size.dim * 40, size.state * size.dim * 36,
     )
 
@@ -340,10 +348,10 @@
     )
 
 
-def output_grad_states(size, pieces, norm, mark, rates, queries, out_grad, gain, attended, sums, count=False):
+def output_grad_states(size, pieces, norm, mark, rates, queries, out_grad, gain, sums, attended):
     n = len(pieces)
 
-    def body(mark_ref, rates_ref, query_ref, grad_ref, gain_ref, att_ref, sums_ref, *outs):
+    def body(mark_ref, rates_ref, query_ref, grad_ref, gain_ref, sums_ref, att_ref, *outs):
         group = partners()
         mark = mark_ref[...]
         last, first = mark[size.rows - 1 :, :], mark[:1, :]
@@ -355,34 +363,30 @@
         gone = steps_if(mark == first, position(size))
         for c, (chunk, wave) in enumerate(pieces):
             back_ref, state_ref = outs[2 * c : 2 * c + 2]
-            for h, cols in wave_heads(size, wave):
-                here = columns(size, group[chunk], h)
-                rate = rate_of(rates_ref, size, group[chunk], h)
-                weight = decay(gone, rate)
+            gains = []
+            for h in range(size.per):
+                if wave > 0 and h // size.each != wave:
+                    continue
+                here, cols = columns(size, group[chunk], h), wave_columns(size, h)
                 grad = grad_ref[:, here].astype(f32) * inv
                 att = att_ref[:, here]
-                back = gain_ref[:, here] * grad - att * pull
-                back_ref[:, cols] = back
-                high, low = halves(back * weight)
-                state_ref[cols, :] = token_product(query_ref[:, here], high, low)
-            put_rows(state_ref, size.state, info_rows(last, first, size.dim))
-            put_rows(state_ref, size.state + INFO, jnp.zeros((size.pad, size.dim), f32))
-        if count:
-            outs[2 * n][...] = jnp.zeros(size.gains.shape, f32)
-            for chunk in range(GROUP):
-                for h in range(size.per):
-                    here = columns(size, group[chunk], h)
-                    part = grad_ref[:, here].astype(f32) * inv * att_ref[:, here]
-                    at = chunk * size.per + h
-                    outs[2 * n][at : at + 1, :] = jnp.sum(part, axis=0, keepdims=True)
+                if wave == 0:
+                    gains.append(jnp.sum(grad * att, axis=0, keepdims=True))
+                if h // size.each == wave:
+                    weight = decay(gone, rate_of(rates_ref, size, group[chunk], h))
+                    back = gain_ref[:, here] * grad - att * pull
+                    back_ref[:, cols] = back
+                    high, low = halves(back * weight)
+                    state_ref[cols, :] = token_product(query_ref[:, here], high, low)
+            put_rows(state_ref, size.state, info_rows(size, last, first, gains))
 
     part = jax.ShapeDtypeStruct((size.rows, size.state), f32)
     outs = call(
-        body, "back", (mark, rates, queries, out_grad, gain, attended, sums),
-        [part, jax.ShapeDtypeStruct((size.state + INFO + size.pad, size.dim), f32)] * n + [size.gains] * count,
+        body, "back", (mark, rates, queries, out_grad, gain, sums, attended),
+        [part, size.payload] * n,
         n * size.each * 4 * size.rows * size.dim * size.dim, n * size.state * size.rows * 16,
     )
-    return outs[0 : 2 * n : 2], outs[1 : 2 * n : 2], outs[2 * n :]
+    return outs[0::2], outs[1::2]
 
 
 def local_gradients(size, mark, rates, queries, key_rows, value_rows, back, entering):
@@ -457,12 +461,8 @@
         left = steps_if(mark == states[0][size.state : size.state + 1, :], size.rows - position(size))
         for c in range(GROUP):
             for h in range(size.per):
-                total = None
-                for k in range(GROUP):
-                    at = size.state + INFO + (k ^ c) * size.per + h
-                    row = states[n - GROUP + k][at : at + 1, :]
-                    total = row if total is None else total + row
-                gains[:, columns(size, group[c], h)] = total
+                at = size.state + MARKS + h
+                gains[:, columns(size, group[c], h)] = states[n - GROUP + c][at : at + 1, :]
         copies = [pltpu.make_async_copy(gains, gain_hbm, sems.at[2, 0])]
         copies[0].start()
         for c in range(GROUP):
@@ -556,60 +556,51 @@
     sent = [[(chunk, wave) for chunk in (3, 1, 2)] for wave in waves]
     kept = [(0, wave) for wave in waves]
     every = all_pieces(size)
-    calls = [sent[0], sum(sent[1:], []) + kept]
-
-    outs, mark, rates = first_states(size, calls[0], seg, decay_span, key_rows, value_rows)
+
+    outs, mark, rates = first_states(size, sent[0], seg, decay_span, key_rows, value_rows)
     common = (mark, rates)
-    states = dict(zip(calls[0], outs))
-    states |= zip(calls[1], more_states(size, calls[1], *common, key_rows, value_rows))
+    states = dict(zip(sent[0], outs))
+    later = sum(sent[1:], []) + kept
+    states |= zip(later, more_states(size, later, *common, key_rows, value_rows))
     near = nearby_attended(size, *common, queries, key_rows, value_rows)
-    entering = {}
     parts = {w: exchange({k: states[k, w] for k in range(GROUP)}) for w in waves}
     totals = {w: group_total(size, False, w, rates, parts[w]) for w in waves}
     outer = {w: from_other_groups(size, False, w, decay_span, totals[w]) for w in waves}
+    entering = {}
     for w in waves:
-        outs = exchange(group_prefixes(size, False, w, rates, parts[w], outer[w]))
-        entering |= {(k, w): outs[k] for k in range(GROUP)}
-    entering = [entering[piece] for piece in every]
-
+        entering[w] = exchange(group_prefixes(size, False, w, rates, parts[w], outer[w]))
+
+    entering = sum([entering[w] for w in waves], [])
     attended, sums = whole_attended(size, *common, queries, out_grad, gain, near, entering)
     sums = lax.psum(sums, "head")
     back, states = {}, {}
-    for pieces in calls:
-        backs, payloads, gains = output_grad_states(
-            size, pieces, norm, *common, queries, out_grad, gain, attended, sums, pieces is calls[1]
+    for pieces in [*sent, kept]:
+        backs, payloads = output_grad_states(
+            size, pieces, norm, *common, queries, out_grad, gain, sums, attended
         )
         back |= zip(pieces, backs)
         states |= zip(pieces, payloads)
-    back = [back[piece] for piece in every]
 
     parts = {w: exchange({k: states[k, w] for k in range(GROUP)}) for w in waves}
-    leaving, summed = {}, 1
+    totals = {w: group_total(size, True, w, rates, parts[w]) for w in waves}
+    outer = {w: from_other_groups(size, True, w, decay_span, totals[w]) for w in waves}
     rides = size.waves > 1 and reach_of_documents(size) == 1 and members > GROUP
-    totals = {}
-    for w in waves:
-        riders = gains if rides and w == 0 else ()
-        totals[w] = group_total(size, True, w, rates, parts[w], size.pad * rides, riders)
-    outer = {w: from_other_groups(size, True, w, decay_span, totals[w]) for w in waves}
+    gains, summed, leaving = [totals[0][size.state :, :]], 1, []
     for w in waves:
         if w < size.waves - 1:
-            riders, collect = (), (gains if rides and w == 0 else ())
+            riders, collect = (), ((totals[0],) if rides and w == 0 else ())
         else:
             while summed * GROUP < members:
                 gains = [sum(gains), cyclic(sum(gains), -summed * GROUP)]
                 summed *= 2
             riders, collect = gains, ()
-        outs = group_prefixes(
-            size, True, w, rates, parts[w], outer[w], size.pad, riders, collect
-        )
+        outs = group_prefixes(size, True, w, rates, parts[w], outer[w], riders, collect)
         if collect:
             gains, summed = outs[GROUP:], 2
-        outs = exchange(outs[:GROUP])
-        leaving |= {(k, w): outs[k] for k in range(GROUP)}
-    leaving = [leaving[piece] for piece in every]
+        leaving += exchange(outs[:GROUP])
 
     query_grad, local_key, local_value = local_gradients(
-        size, *common, queries, key_rows, value_rows, back, entering
+        size, *common, queries, key_rows, value_rows, [back[piece] for piece in every], entering
     )
     key_grad, value_grad, gain_grad = final_gradients(
         size, *common, key_rows, value_rows, local_key, local_value, leaving

time: 76.1 us -> 74.9 us (0.984)
  waiting for transfers between devices: 16.1 us -> 14.6 us
    ppermute x24, waiting for transfers between devices: 14.2 us -> 12.7 us  [swap(): lax.ppermute(array, 'seq', [(i, i ^ distance) for i in range(members)])]
    pallas_call x16 -> x17, Pallas kernels: 15.1 us -> 15.2 us  [call(): pl.pallas_call(body, out_shape=outputs, in_specs=in_specs if in_specs is...]
where the time goes in v5:
time: 74.9 us; the launch traced here: 74.7 us
  starting transfers between devices  40.5 us (54%)
  Pallas kernels  15.2 us (20%)
  waiting for transfers between devices  14.6 us (19%)
  blocking collectives  2.47 us (3%)
  between operations  1.08 us (1%)
  local copies, waits for them, and re-layouts  0.92 us (1%)
    ppermute x24, starting transfers between devices, swap(): lax.ppermute(array, 'seq', [(i, i ^ distance) for i in range(members)])  32.2 us
    pallas_call x17, Pallas kernels, call(): pl.pallas_call(body, out_shape=outputs, in_specs=in_specs if in_specs is...  15.2 us
    ppermute x24, waiting for transfers between devices, swap(): lax.ppermute(array, 'seq', [(i, i ^ distance) for i in range(members)])  12.7 us
    ppermute x5, starting transfers between devices, cyclic(): lax.ppermute(array, 'seq', [(i, (i + by) % members) for i in range(member...  8.25 us
    psum x1, blocking collectives, local(): sums = lax.psum(sums, 'head')  2.47 us
    ppermute x5, waiting for transfers between devices, cyclic(): lax.ppermute(array, 'seq', [(i, (i + by) % members) for i in range(member...  1.87 us
  transfers between devices with their start and end apart: 29, of which 14 were waited for; matrix products, arithmetic and copies ran while one was open for 0% of the time, Pallas kernels for 13%

profile of v5, /device:TPU:0, one launch (start us, length us, event | category | flops | bytes accessed | tf_op | source)
XLA Modules:
  0.0 74.7 jit_solution(6718284301918190617)
XLA Ops:
  0.7 2.2 %states.2 = (f32[264,128]{1,0:T(8,128)}, f32[264,128]{1,0:T(8,128)}, f32[264,128]{1,0:T(8,128)}, f32[128,128]{1,0:T(8,128)}, f32[16,128]{1,0:T(8,128)}) custom-call(s32[1,128]{1,0:T(1,128)} %bitcast.8, f32[1,16]{1,0:T(1,128)} %bitcast.9, bf16[128,2048]{1,0:T(8,128)(2,1)} %key_ref.7, bf16[128,2048]{1,0:T(8,128)(2,1)} %value_ref.7), custom_call_target="tpu_custom_call" | custom-call | flops 50331648 | bytes 786432 | tf_op jit(solution)/shard_map/states/pallas_call | solution.py:118
  2.8 3.0 %collective-permute-start = (f32[264,128]{1,0:T(8,128)}, f32[264,128]{1,0:T(8,128)S(1)}, u32[]{:S(2)}, u32[]{:S(2)}) collective-permute-start(f32[264,128]{1,0:T(8,128)} %get-tuple-element.58), channel_id=1, source_target_pairs={{0,2},{2,0},{4,6},{6,4},{8,10},{10,8},{12,14},{14,12},{16,18},{18,... | collective-permute-start | bytes 405512 | tf_op jit(solution)/shard_map/ppermute | solution.py:507
  5.8 1.5 %collective-permute-start.1 = (f32[264,128]{1,0:T(8,128)}, f32[264,128]{1,0:T(8,128)S(1)}, u32[]{:S(2)}, u32[]{:S(2)}) collective-permute-start(f32[264,128]{1,0:T(8,128)} %get-tuple-element.59), channel_id=1, source_target_pairs={{0,4},{2,6},{4,0},{6,2},{8,12},{10,14},{12,8},{14,10},{16,20},{18,... | collective-permute-start | bytes 405512 | tf_op jit(solution)/shard_map/ppermute | solution.py:507
  7.4 0.8 %copy-done.4 = f32[128,128]{1,0:T(8,128)S(1)} copy-done((f32[128,128]{1,0:T(8,128)S(1)}, f32[128,128]{1,0:T(8,128)}, u32[]{:S(2)}) %copy-start.4) | copy-done | bytes 65560
  8.6 2.0 %collective-permute-start.7 = (f32[264,128]{1,0:T(8,128)S(1)}, f32[264,128]{1,0:T(8,128)S(1)}, u32[]{:S(2)}, u32[]{:S(2)}) collective-permute-start(f32[264,128]{1,0:T(8,128)S(1)} %get-tuple-element.66), channel_id=1, source_target_pairs={{0,2},{2,0},{4,6},{6,4},{8,10},{10,8},{12,14},{14,12},{16,18},{18,... | collective-permute-start | bytes 405512 | tf_op jit(solution)/shard_map/ppermute | solution.py:507
  10.7 1.5 %collective-permute-start.8 = (f32[264,128]{1,0:T(8,128)S(1)}, f32[264,128]{1,0:T(8,128)S(1)}, u32[]{:S(2)}, u32[]{:S(2)}) collective-permute-start(f32[264,128]{1,0:T(8,128)S(1)} %get-tuple-element.67), channel_id=1, source_target_pairs={{0,4},{2,6},{4,0},{6,2},{8,12},{10,14},{12,8},{14,10},{16,20},{18,... | collective-permute-start | bytes 405512 | tf_op jit(solution)/shard_map/ppermute | solution.py:507
  12.2 1.3 %collective-permute-start.9 = (f32[264,128]{1,0:T(8,128)S(1)}, f32[264,128]{1,0:T(8,128)S(1)}, u32[]{:S(2)}, u32[]{:S(2)}) collective-permute-start(f32[264,128]{1,0:T(8,128)S(1)} %get-tuple-element.68), channel_id=1, source_target_pairs={{0,6},{2,4},{4,2},{6,0},{8,14},{10,12},{12,10},{14,8},{16,22},{18,... | collective-permute-start | bytes 405512 | tf_op jit(solution)/shard_map/ppermute | solution.py:507
  13.5 1.1 %collective-permute-done.1.refs_2_ = f32[264,128]{1,0:T(8,128)S(1)} collective-permute-done((f32[264,128]{1,0:T(8,128)}, f32[264,128]{1,0:T(8,128)S(1)}, u32[]{:S(2)}, u32[]{:S(2)}) %collective-permute-start.1) | collective-permute-done | bytes 135200 | tf_op jit(solution)/shard_map/ppermute | solution.py:507
  14.6 0.5 collective-permute-done.2.refs_3_
  15.1 1.6 %collective-permute-start.3 = (f32[264,128]{1,0:T(8,128)S(1)}, f32[264,128]{1,0:T(8,128)S(1)}, u32[]{:S(2)}, u32[]{:S(2)}) collective-permute-start(f32[264,128]{1,0:T(8,128)S(1)} %total.4), channel_id=1, source_target_pairs={{0,8},{2,10},{4,12},{6,14},{8,16},{10,18},{12,20},{14,22},{16,24},... | collective-permute-start | bytes 405512 | tf_op jit(solution)/shard_map/ppermute | solution.py:522
  16.9 2.9 %collective-permute-done.8.refs_2_ = f32[264,128]{1,0:T(8,128)S(1)} collective-permute-done((f32[264,128]{1,0:T(8,128)S(1)}, f32[264,128]{1,0:T(8,128)S(1)}, u32[]{:S(2)}, u32[]{:S(2)}) %collective-permute-start.8) | collective-permute-done | bytes 135200 | tf_op jit(solution)/shard_map/ppermute | solution.py:507
  19.9 1.6 %collective-permute-start.10 = (f32[264,128]{1,0:T(8,128)S(1)}, f32[264,128]{1,0:T(8,128)S(1)}, u32[]{:S(2)}, u32[]{:S(2)}) collective-permute-start(f32[264,128]{1,0:T(8,128)S(1)} %total.5), channel_id=1, source_target_pairs={{0,8},{2,10},{4,12},{6,14},{8,16},{10,18},{12,20},{14,22},{16,24},... | collective-permute-start | bytes 405512 | tf_op jit(solution)/shard_map/ppermute | solution.py:522
  21.5 0.5 collective-permute-done.3.refs_4_
  22.2 1.4 %collective-permute-start.4 = (f32[264,128]{1,0:T(8,128)S(1)}, f32[264,128]{1,0:T(8,128)S(1)}, u32[]{:S(2)}, u32[]{:S(2)}) collective-permute-start(f32[264,128]{1,0:T(8,128)S(1)} %get-tuple-element.62), channel_id=1, source_target_pairs={{0,2},{2,0},{4,6},{6,4},{8,10},{10,8},{12,14},{14,12},{16,18},{18,... | collective-permute-start | bytes 405512 | tf_op jit(solution)/shard_map/ppermute | solution.py:507
  23.6 1.2 %collective-permute-start.5 = (f32[264,128]{1,0:T(8,128)S(1)}, f32[264,128]{1,0:T(8,128)S(1)}, u32[]{:S(2)}, u32[]{:S(2)}) collective-permute-start(f32[264,128]{1,0:T(8,128)S(1)} %get-tuple-element.63), channel_id=1, source_target_pairs={{0,4},{2,6},{4,0},{6,2},{8,12},{10,14},{12,8},{14,10},{16,20},{18,... | collective-permute-start | bytes 405512 | tf_op jit(solution)/shard_map/ppermute | solution.py:507
  24.7 1.4 %collective-permute-start.6 = (f32[264,128]{1,0:T(8,128)S(1)}, f32[264,128]{1,0:T(8,128)S(1)}, u32[]{:S(2)}, u32[]{:S(2)}) collective-permute-start(f32[264,128]{1,0:T(8,128)S(1)} %get-tuple-element.64), channel_id=1, source_target_pairs={{0,6},{2,4},{4,2},{6,0},{8,14},{10,12},{12,10},{14,8},{16,22},{18,... | collective-permute-start | bytes 405512 | tf_op jit(solution)/shard_map/ppermute | solution.py:507
  26.1 0.6 collective-permute-done.10.refs_4_
  26.9 1.3 %collective-permute-start.11 = (f32[264,128]{1,0:T(8,128)S(1)}, f32[264,128]{1,0:T(8,128)S(1)}, u32[]{:S(2)}, u32[]{:S(2)}) collective-permute-start(f32[264,128]{1,0:T(8,128)S(1)} %get-tuple-element.70), channel_id=1, source_target_pairs={{0,2},{2,0},{4,6},{6,4},{8,10},{10,8},{12,14},{14,12},{16,18},{18,... | collective-permute-start | bytes 405512 | tf_op jit(solution)/shard_map/ppermute | solution.py:507
  28.2 0.8 %collective-permute-start.12 = (f32[264,128]{1,0:T(8,128)S(1)}, f32[264,128]{1,0:T(8,128)S(1)}, u32[]{:S(2)}, u32[]{:S(2)}) collective-permute-start(f32[264,128]{1,0:T(8,128)S(1)} %get-tuple-element.71), channel_id=1, source_target_pairs={{0,4},{2,6},{4,0},{6,2},{8,12},{10,14},{12,8},{14,10},{16,20},{18,... | collective-permute-start | bytes 405512 | tf_op jit(solution)/shard_map/ppermute | solution.py:507
  29.1 1.4 %collective-permute-start.13 = (f32[264,128]{1,0:T(8,128)S(1)}, f32[264,128]{1,0:T(8,128)S(1)}, u32[]{:S(2)}, u32[]{:S(2)}) collective-permute-start(f32[264,128]{1,0:T(8,128)S(1)} %get-tuple-element.72), channel_id=1, source_target_pairs={{0,6},{2,4},{4,2},{6,0},{8,14},{10,12},{12,10},{14,8},{16,22},{18,... | collective-permute-start | bytes 405512 | tf_op jit(solution)/shard_map/ppermute | solution.py:507
  30.5 2.7 %nearby.1.near_ref = f32[128,2048]{1,0:T(8,128)S(1)} custom-call(f32[128,128]{1,0:T(8,128)S(1)} %copy-done.5, f32[16,128]{1,0:T(8,128)S(1)} %copy-done.6, bf16[128,2048]{1,0:T(8,128)(2,1)S(1)} %copy-done, bf16[128,2048]{1,0:T(8,128)(2,1)S(1)} %copy-done.1, bf16[128,2048]{1,0:T(8,128)(2,1)S(1)} %copy-done.2), custom_call_target="tpu_custom_call" | custom-call | flops 201326592 | bytes 2621440 | tf_op jit(solution)/shard_map/nearby/pallas_call | solution.py:118
  33.2 0.7 collective-permute-done.11.refs_5_.refs_13_
  33.9 1.0 %collective-permute-done.12.refs_6_.refs_14_ = f32[264,128]{1,0:T(8,128)S(1)} collective-permute-done((f32[264,128]{1,0:T(8,128)S(1)}, f32[264,128]{1,0:T(8,128)S(1)}, u32[]{:S(2)}, u32[]{:S(2)}) %collective-permute-start.12) | collective-permute-done | bytes 135200 | tf_op jit(solution)/shard_map/ppermute | solution.py:507
  34.9 1.4 %collective-permute-done.13.refs_7_.refs_15_ = f32[264,128]{1,0:T(8,128)S(1)} collective-permute-done((f32[264,128]{1,0:T(8,128)S(1)}, f32[264,128]{1,0:T(8,128)S(1)}, u32[]{:S(2)}, u32[]{:S(2)}) %collective-permute-start.13) | collective-permute-done | bytes 135200 | tf_op jit(solution)/shard_map/ppermute | solution.py:507
  36.4 0.8 %attended.1 = (f32[128,2048]{1,0:T(8,128)S(1)}, f32[8,128]{1,0:T(8,128)S(1)}) custom-call(f32[128,128]{1,0:T(8,128)S(1)} %copy-done.5, f32[16,128]{1,0:T(8,128)S(1)} %copy-done.6, bf16[128,2048]{1,0:T(8,128)(2,1)S(1)} %copy-done, bf16[128,2048]{1,0:T(8,128)(2,1)S(1)} %copy-done.3, f32[1,2048]{1,0:T(1,128)S(1)} %bitcast.4, f32[128,2048]{1,0:T(8,128)S(1)} %nearby.1.near_ref, ...), custom_call_target="tpu_custom_call" | custom-call | flops 134217728 | bytes 4194304 | tf_op jit(solution)/shard_map/attended/pallas_call | solution.py:118
  37.2 2.5 %psum.7.sums_ref = f32[8,128]{1,0:T(8,128)S(1)} all-reduce(f32[8,128]{1,0:T(8,128)S(1)} %get-tuple-element.73), channel_id=1, replica_groups=mesh['seq'=16,'head'=2] {'head'}, use_global_device_ids=true, to_apply=%region_0.0 | all-reduce | flops 1024 | bytes 8192 | tf_op jit(solution)/shard_map/psum | solution.py:575
  39.7 0.6 back.4
  40.3 1.3 %collective-permute-start.14 = (f32[264,128]{1,0:T(8,128)S(1)}, f32[264,128]{1,0:T(8,128)S(1)}, u32[]{:S(2)}, u32[]{:S(2)}) collective-permute-start(f32[264,128]{1,0:T(8,128)S(1)} %get-tuple-element.87), channel_id=1, source_target_pairs={{0,2},{2,0},{4,6},{6,4},{8,10},{10,8},{12,14},{14,12},{16,18},{18,... | collective-permute-start | bytes 405512 | tf_op jit(solution)/shard_map/ppermute | solution.py:507
  41.6 1.3 %collective-permute-start.15 = (f32[264,128]{1,0:T(8,128)S(1)}, f32[264,128]{1,0:T(8,128)S(1)}, u32[]{:S(2)}, u32[]{:S(2)}) collective-permute-start(f32[264,128]{1,0:T(8,128)S(1)} %get-tuple-element.88), channel_id=1, source_target_pairs={{0,4},{2,6},{4,0},{6,2},{8,12},{10,14},{12,8},{14,10},{16,20},{18,... | collective-permute-start | bytes 405512 | tf_op jit(solution)/shard_map/ppermute | solution.py:507
  43.0 0.9 %collective-permute-start.16 = (f32[264,128]{1,0:T(8,128)S(1)}, f32[264,128]{1,0:T(8,128)S(1)}, u32[]{:S(2)}, u32[]{:S(2)}) collective-permute-start(f32[264,128]{1,0:T(8,128)S(1)} %get-tuple-element.89), channel_id=1, source_target_pairs={{0,6},{2,4},{4,2},{6,0},{8,14},{10,12},{12,10},{14,8},{16,22},{18,... | collective-permute-start | bytes 405512 | tf_op jit(solution)/shard_map/ppermute | solution.py:507
  44.3 1.3 %collective-permute-start.21 = (f32[264,128]{1,0:T(8,128)S(1)}, f32[264,128]{1,0:T(8,128)S(1)}, u32[]{:S(2)}, u32[]{:S(2)}) collective-permute-start(f32[264,128]{1,0:T(8,128)S(1)} %get-tuple-element.95), channel_id=1, source_target_pairs={{0,2},{2,0},{4,6},{6,4},{8,10},{10,8},{12,14},{14,12},{16,18},{18,... | collective-permute-start | bytes 405512 | tf_op jit(solution)/shard_map/ppermute | solution.py:507
  45.6 1.3 %collective-permute-start.22 = (f32[264,128]{1,0:T(8,128)S(1)}, f32[264,128]{1,0:T(8,128)S(1)}, u32[]{:S(2)}, u32[]{:S(2)}) collective-permute-start(f32[264,128]{1,0:T(8,128)S(1)} %get-tuple-element.96), channel_id=1, source_target_pairs={{0,4},{2,6},{4,0},{6,2},{8,12},{10,14},{12,8},{14,10},{16,20},{18,... | collective-permute-start | bytes 405512 | tf_op jit(solution)/shard_map/ppermute | solution.py:507
  47.0 1.8 %collective-permute-start.23 = (f32[264,128]{1,0:T(8,128)S(1)}, f32[264,128]{1,0:T(8,128)S(1)}, u32[]{:S(2)}, u32[]{:S(2)}) collective-permute-start(f32[264,128]{1,0:T(8,128)S(1)} %get-tuple-element.97), channel_id=1, source_target_pairs={{0,6},{2,4},{4,2},{6,0},{8,14},{10,12},{12,10},{14,8},{16,22},{18,... | collective-permute-start | bytes 405512 | tf_op jit(solution)/shard_map/ppermute | solution.py:507
  49.2 0.9 %collective-permute-done.15.refs_2_ = f32[264,128]{1,0:T(8,128)S(1)} collective-permute-done((f32[264,128]{1,0:T(8,128)S(1)}, f32[264,128]{1,0:T(8,128)S(1)}, u32[]{:S(2)}, u32[]{:S(2)}) %collective-permute-start.15) | collective-permute-done | bytes 135200 | tf_op jit(solution)/shard_map/ppermute | solution.py:507
  50.5 2.0 %collective-permute-start.17 = (f32[264,128]{1,0:T(8,128)S(1)}, f32[264,128]{1,0:T(8,128)S(1)}, u32[]{:S(2)}, u32[]{:S(2)}) collective-permute-start(f32[264,128]{1,0:T(8,128)S(1)} %total.6.refs_5_), channel_id=1, source_target_pairs={{0,24},{2,26},{4,28},{6,30},{8,0},{10,2},{12,4},{14,6},{16,8},{18,... | collective-permute-start | bytes 405512 | tf_op jit(solution)/shard_map/ppermute | solution.py:522
  52.5 3.2 %collective-permute-done.22.refs_2_ = f32[264,128]{1,0:T(8,128)S(1)} collective-permute-done((f32[264,128]{1,0:T(8,128)S(1)}, f32[264,128]{1,0:T(8,128)S(1)}, u32[]{:S(2)}, u32[]{:S(2)}) %collective-permute-start.22) | collective-permute-done | bytes 135200 | tf_op jit(solution)/shard_map/ppermute | solution.py:507
  55.8 2.3 %collective-permute-start.24 = (f32[264,128]{1,0:T(8,128)S(1)}, f32[264,128]{1,0:T(8,128)S(1)}, u32[]{:S(2)}, u32[]{:S(2)}) collective-permute-start(f32[264,128]{1,0:T(8,128)S(1)} %total.7), channel_id=1, source_target_pairs={{0,24},{2,26},{4,28},{6,30},{8,0},{10,2},{12,4},{14,6},{16,8},{18,... | collective-permute-start | bytes 405512 | tf_op jit(solution)/shard_map/ppermute | solution.py:522
  58.2 0.7 collective-permute-start.18
  58.9 0.7 collective-permute-start.25
  59.6 1.3 %collective-permute-start.19 = (f32[264,128]{1,0:T(8,128)S(1)}, f32[264,128]{1,0:T(8,128)S(1)}, u32[]{:S(2)}, u32[]{:S(2)}) collective-permute-start(f32[264,128]{1,0:T(8,128)S(1)} %get-tuple-element.92), channel_id=1, source_target_pairs={{0,4},{2,6},{4,0},{6,2},{8,12},{10,14},{12,8},{14,10},{16,20},{18,... | collective-permute-start | bytes 405512 | tf_op jit(solution)/shard_map/ppermute | solution.py:507
  60.9 1.8 %collective-permute-start.20 = (f32[264,128]{1,0:T(8,128)S(1)}, f32[264,128]{1,0:T(8,128)S(1)}, u32[]{:S(2)}, u32[]{:S(2)}) collective-permute-start(f32[264,128]{1,0:T(8,128)S(1)} %get-tuple-element.93), channel_id=1, source_target_pairs={{0,6},{2,4},{4,2},{6,0},{8,14},{10,12},{12,10},{14,8},{16,22},{18,... | collective-permute-start | bytes 405512 | tf_op jit(solution)/shard_map/ppermute | solution.py:507
  62.7 0.8 %collective-permute-done.25.refs_6_ = f32[8,128]{1,0:T(8,128)S(1)} collective-permute-done((f32[8,128]{1,0:T(8,128)S(1)}, f32[8,128]{1,0:T(8,128)S(1)}, u32[]{:S(2)}, u32[]{:S(2)}) %collective-permute-start.25) | collective-permute-done | bytes 4128 | tf_op jit(solution)/shard_map/ppermute | solution.py:522
  63.6 1.5 %collective-permute-start.26 = (f32[264,128]{1,0:T(8,128)S(1)}, f32[264,128]{1,0:T(8,128)S(1)}, u32[]{:S(2)}, u32[]{:S(2)}) collective-permute-start(f32[264,128]{1,0:T(8,128)S(1)} %get-tuple-element.100), channel_id=1, source_target_pairs={{0,2},{2,0},{4,6},{6,4},{8,10},{10,8},{12,14},{14,12},{16,18},{18,... | collective-permute-start | bytes 405512 | tf_op jit(solution)/shard_map/ppermute | solution.py:507
  65.1 0.9 %collective-permute-start.27 = (f32[264,128]{1,0:T(8,128)S(1)}, f32[264,128]{1,0:T(8,128)S(1)}, u32[]{:S(2)}, u32[]{:S(2)}) collective-permute-start(f32[264,128]{1,0:T(8,128)S(1)} %get-tuple-element.101), channel_id=1, source_target_pairs={{0,4},{2,6},{4,0},{6,2},{8,12},{10,14},{12,8},{14,10},{16,20},{18,... | collective-permute-start | bytes 405512 | tf_op jit(solution)/shard_map/ppermute | solution.py:507
  66.0 1.2 %collective-permute-start.28 = (f32[264,128]{1,0:T(8,128)S(1)}, f32[264,128]{1,0:T(8,128)S(1)}, u32[]{:S(2)}, u32[]{:S(2)}) collective-permute-start(f32[264,128]{1,0:T(8,128)S(1)} %get-tuple-element.102), channel_id=1, source_target_pairs={{0,6},{2,4},{4,2},{6,0},{8,14},{10,12},{12,10},{14,8},{16,22},{18,... | collective-permute-start | bytes 405512 | tf_op jit(solution)/shard_map/ppermute | solution.py:507
  67.2 5.1 %gradients.1 = (bf16[128,2048]{1,0:T(8,128)(2,1)}, f32[128,2048]{1,0:T(8,128)S(1)}, f32[128,2048]{1,0:T(8,128)S(1)}) custom-call(f32[128,128]{1,0:T(8,128)S(1)} %copy-done.5, f32[16,128]{1,0:T(8,128)S(1)} %copy-done.6, bf16[128,2048]{1,0:T(8,128)(2,1)S(1)} %copy-done, bf16[128,2048]{1,0:T(8,128)(2,1)S(1)} %copy-done.1, bf16[128,2048]{1,0:T(8,128)(2,1)S(1)} %copy-done.2, ...), custom_call_target="tpu_custom_call" | custom-call | flops 872415232 | bytes 6291456 | tf_op jit(solution)/shard_map/gradients/pallas_call | solution.py:118
  72.4 0.6 collective-permute-done.27.refs_6_
  73.0 1.6 %final.1 = (bf16[128,2048]{1,0:T(8,128)(2,1)}, bf16[128,2048]{1,0:T(8,128)(2,1)}, f32[1,2048]{1,0:T(1,128)}) custom-call(f32[128,128]{1,0:T(8,128)S(1)} %copy-done.5, f32[16,128]{1,0:T(8,128)S(1)} %copy-done.6, bf16[128,2048]{1,0:T(8,128)(2,1)S(1)} %copy-done.1, bf16[128,2048]{1,0:T(8,128)(2,1)S(1)} %copy-done.2, ...), custom_call_target="tpu_custom_call" | custom-call | flops 268435456 | bytes 6291456 | tf_op jit(solution)/shard_map/final/pallas_call | solution.py:118
  (68 shorter events, 2.8 us)
Async XLA Ops:
  0.6 6.8 %copy-start.1 = (bf16[128,2048]{1,0:T(8,128)(2,1)S(1)}, bf16[128,2048]{1,0:T(8,128)(2,1)}, u32[]{:S(2)}) copy-start(bf16[128,2048]{1,0:T(8,128)(2,1)} %key_ref.7) | copy-start | bytes 1572868
  0.6 6.7 %copy-start.2 = (bf16[128,2048]{1,0:T(8,128)(2,1)S(1)}, bf16[128,2048]{1,0:T(8,128)(2,1)}, u32[]{:S(2)}) copy-start(bf16[128,2048]{1,0:T(8,128)(2,1)} %value_ref.7) | copy-start | bytes 1572868
  2.8 4.6 %copy-start.6 = (f32[16,128]{1,0:T(8,128)S(1)}, f32[16,128]{1,0:T(8,128)}, u32[]{:S(2)}) copy-start(f32[16,128]{1,0:T(8,128)} %get-tuple-element.56.rates_ref) | copy-start | bytes 24580
  2.8 9.3 %collective-permute-start = (f32[264,128]{1,0:T(8,128)}, f32[264,128]{1,0:T(8,128)S(1)}, u32[]{:S(2)}, u32[]{:S(2)}) collective-permute-start(f32[264,128]{1,0:T(8,128)} %get-tuple-element.58), channel_id=1, source_target_pairs={{0,2},{2,0},{4,6},{6,4},{8,10},{10,8},{12,14},{14,12},{16,18},{18,... | collective-permute-start | bytes 405512 | tf_op jit(solution)/shard_map/ppermute | solution.py:507
  5.8 8.7 %collective-permute-start.1 = (f32[264,128]{1,0:T(8,128)}, f32[264,128]{1,0:T(8,128)S(1)}, u32[]{:S(2)}, u32[]{:S(2)}) collective-permute-start(f32[264,128]{1,0:T(8,128)} %get-tuple-element.59), channel_id=1, source_target_pairs={{0,4},{2,6},{4,0},{6,2},{8,12},{10,14},{12,8},{14,10},{16,20},{18,... | collective-permute-start | bytes 405512 | tf_op jit(solution)/shard_map/ppermute | solution.py:507
  7.4 7.7 %collective-permute-start.2 = (f32[264,128]{1,0:T(8,128)}, f32[264,128]{1,0:T(8,128)S(1)}, u32[]{:S(2)}, u32[]{:S(2)}) collective-permute-start(f32[264,128]{1,0:T(8,128)} %get-tuple-element.60), channel_id=1, source_target_pairs={{0,6},{2,4},{4,2},{6,0},{8,14},{10,12},{12,10},{14,8},{16,22},{18,... | collective-permute-start | bytes 405512 | tf_op jit(solution)/shard_map/ppermute | solution.py:507
  8.6 8.3 %collective-permute-start.7 = (f32[264,128]{1,0:T(8,128)S(1)}, f32[264,128]{1,0:T(8,128)S(1)}, u32[]{:S(2)}, u32[]{:S(2)}) collective-permute-start(f32[264,128]{1,0:T(8,128)S(1)} %get-tuple-element.66), channel_id=1, source_target_pairs={{0,2},{2,0},{4,6},{6,4},{8,10},{10,8},{12,14},{14,12},{16,18},{18,... | collective-permute-start | bytes 405512 | tf_op jit(solution)/shard_map/ppermute | solution.py:507
  10.7 9.1 %collective-permute-start.8 = (f32[264,128]{1,0:T(8,128)S(1)}, f32[264,128]{1,0:T(8,128)S(1)}, u32[]{:S(2)}, u32[]{:S(2)}) collective-permute-start(f32[264,128]{1,0:T(8,128)S(1)} %get-tuple-element.67), channel_id=1, source_target_pairs={{0,4},{2,6},{4,0},{6,2},{8,12},{10,14},{12,8},{14,10},{16,20},{18,... | collective-permute-start | bytes 405512 | tf_op jit(solution)/shard_map/ppermute | solution.py:507
  12.2 7.6 %collective-permute-start.9 = (f32[264,128]{1,0:T(8,128)S(1)}, f32[264,128]{1,0:T(8,128)S(1)}, u32[]{:S(2)}, u32[]{:S(2)}) collective-permute-start(f32[264,128]{1,0:T(8,128)S(1)} %get-tuple-element.68), channel_id=1, source_target_pairs={{0,6},{2,4},{4,2},{6,0},{8,14},{10,12},{12,10},{14,8},{16,22},{18,... | collective-permute-start | bytes 405512 | tf_op jit(solution)/shard_map/ppermute | solution.py:507
  15.1 6.9 %collective-permute-start.3 = (f32[264,128]{1,0:T(8,128)S(1)}, f32[264,128]{1,0:T(8,128)S(1)}, u32[]{:S(2)}, u32[]{:S(2)}) collective-permute-start(f32[264,128]{1,0:T(8,128)S(1)} %total.4), channel_id=1, source_target_pairs={{0,8},{2,10},{4,12},{6,14},{8,16},{10,18},{12,20},{14,22},{16,24},... | collective-permute-start | bytes 405512 | tf_op jit(solution)/shard_map/ppermute | solution.py:522
  19.9 10.6 %copy-start = (bf16[128,2048]{1,0:T(8,128)(2,1)S(1)}, bf16[128,2048]{1,0:T(8,128)(2,1)}, u32[]{:S(2)}) copy-start(bf16[128,2048]{1,0:T(8,128)(2,1)} %query_ref.11) | copy-start | bytes 1572868
  19.9 6.9 %collective-permute-start.10 = (f32[264,128]{1,0:T(8,128)S(1)}, f32[264,128]{1,0:T(8,128)S(1)}, u32[]{:S(2)}, u32[]{:S(2)}) collective-permute-start(f32[264,128]{1,0:T(8,128)S(1)} %total.5), channel_id=1, source_target_pairs={{0,8},{2,10},{4,12},{6,14},{8,16},{10,18},{12,20},{14,22},{16,24},... | collective-permute-start | bytes 405512 | tf_op jit(solution)/shard_map/ppermute | solution.py:522
  22.2 6.9 %collective-permute-start.4 = (f32[264,128]{1,0:T(8,128)S(1)}, f32[264,128]{1,0:T(8,128)S(1)}, u32[]{:S(2)}, u32[]{:S(2)}) collective-permute-start(f32[264,128]{1,0:T(8,128)S(1)} %get-tuple-element.62), channel_id=1, source_target_pairs={{0,2},{2,0},{4,6},{6,4},{8,10},{10,8},{12,14},{14,12},{16,18},{18,... | collective-permute-start | bytes 405512 | tf_op jit(solution)/shard_map/ppermute | solution.py:507
  23.6 9.6 %collective-permute-start.5 = (f32[264,128]{1,0:T(8,128)S(1)}, f32[264,128]{1,0:T(8,128)S(1)}, u32[]{:S(2)}, u32[]{:S(2)}) collective-permute-start(f32[264,128]{1,0:T(8,128)S(1)} %get-tuple-element.63), channel_id=1, source_target_pairs={{0,4},{2,6},{4,0},{6,2},{8,12},{10,14},{12,8},{14,10},{16,20},{18,... | collective-permute-start | bytes 405512 | tf_op jit(solution)/shard_map/ppermute | solution.py:507
  24.7 5.8 %copy-start.5 = (f32[128,128]{1,0:T(8,128)S(1)}, f32[128,128]{1,0:T(8,128)}, u32[]{:S(2)}) copy-start(f32[128,128]{1,0:T(8,128)} %get-tuple-element.55.mark_ref) | copy-start | bytes 196612
  24.7 8.5 %collective-permute-start.6 = (f32[264,128]{1,0:T(8,128)S(1)}, f32[264,128]{1,0:T(8,128)S(1)}, u32[]{:S(2)}, u32[]{:S(2)}) collective-permute-start(f32[264,128]{1,0:T(8,128)S(1)} %get-tuple-element.64), channel_id=1, source_target_pairs={{0,6},{2,4},{4,2},{6,0},{8,14},{10,12},{12,10},{14,8},{16,22},{18,... | collective-permute-start | bytes 405512 | tf_op jit(solution)/shard_map/ppermute | solution.py:507
  26.9 9.4 %copy-start.11 = (f32[264,128]{1,0:T(8,128)}, f32[264,128]{1,0:T(8,128)S(1)}, u32[]{:S(2)}) copy-start(f32[264,128]{1,0:T(8,128)S(1)} %get-tuple-element.69.refs_4_.refs_12_) | copy-start | bytes 405508
  26.9 7.0 %collective-permute-start.11 = (f32[264,128]{1,0:T(8,128)S(1)}, f32[264,128]{1,0:T(8,128)S(1)}, u32[]{:S(2)}, u32[]{:S(2)}) collective-permute-start(f32[264,128]{1,0:T(8,128)S(1)} %get-tuple-element.70), channel_id=1, source_target_pairs={{0,2},{2,0},{4,6},{6,4},{8,10},{10,8},{12,14},{14,12},{16,18},{18,... | collective-permute-start | bytes 405512 | tf_op jit(solution)/shard_map/ppermute | solution.py:507
  28.2 6.7 %collective-permute-start.12 = (f32[264,128]{1,0:T(8,128)S(1)}, f32[264,128]{1,0:T(8,128)S(1)}, u32[]{:S(2)}, u32[]{:S(2)}) collective-permute-start(f32[264,128]{1,0:T(8,128)S(1)} %get-tuple-element.71), channel_id=1, source_target_pairs={{0,4},{2,6},{4,0},{6,2},{8,12},{10,14},{12,8},{14,10},{16,20},{18,... | collective-permute-start | bytes 405512 | tf_op jit(solution)/shard_map/ppermute | solution.py:507
  29.1 7.3 %copy-start.3 = (bf16[128,2048]{1,0:T(8,128)(2,1)S(1)}, bf16[128,2048]{1,0:T(8,128)(2,1)}, u32[]{:S(2)}) copy-start(bf16[128,2048]{1,0:T(8,128)(2,1)} %grad_ref.7) | copy-start | bytes 1572868
  29.1 7.3 %collective-permute-start.13 = (f32[264,128]{1,0:T(8,128)S(1)}, f32[264,128]{1,0:T(8,128)S(1)}, u32[]{:S(2)}, u32[]{:S(2)}) collective-permute-start(f32[264,128]{1,0:T(8,128)S(1)} %get-tuple-element.72), channel_id=1, source_target_pairs={{0,6},{2,4},{4,2},{6,0},{8,14},{10,12},{12,10},{14,8},{16,22},{18,... | collective-permute-start | bytes 405512 | tf_op jit(solution)/shard_map/ppermute | solution.py:507
  30.5 5.9 %copy-start.19 = (f32[2048]{0:T(1024)S(1)}, f32[2048]{0:T(1024)}, u32[]{:S(2)}) copy-start(f32[2048]{0:T(1024)} %param.12) | copy-start | bytes 24580
  33.2 4.0 %copy-start.7 = (f32[264,128]{1,0:T(8,128)}, f32[264,128]{1,0:T(8,128)S(1)}, u32[]{:S(2)}) copy-start(f32[264,128]{1,0:T(8,128)S(1)} %collective-permute-done.5.refs_2_.refs_10_) | copy-start | bytes 405508
  33.2 4.0 %copy-start.9 = (f32[264,128]{1,0:T(8,128)}, f32[264,128]{1,0:T(8,128)S(1)}, u32[]{:S(2)}) copy-start(f32[264,128]{1,0:T(8,128)S(1)} %collective-permute-done.6.refs_3_.refs_11_) | copy-start | bytes 405508
  33.9 3.3 %copy-start.13 = (f32[264,128]{1,0:T(8,128)}, f32[264,128]{1,0:T(8,128)S(1)}, u32[]{:S(2)}) copy-start(f32[264,128]{1,0:T(8,128)S(1)} %collective-permute-done.11.refs_5_.refs_13_) | copy-start | bytes 405508
  34.9 2.3 %copy-start.15 = (f32[264,128]{1,0:T(8,128)}, f32[264,128]{1,0:T(8,128)S(1)}, u32[]{:S(2)}) copy-start(f32[264,128]{1,0:T(8,128)S(1)} %collective-permute-done.12.refs_6_.refs_14_) | copy-start | bytes 405508
  36.3 0.9 %copy-start.17 = (f32[264,128]{1,0:T(8,128)}, f32[264,128]{1,0:T(8,128)S(1)}, u32[]{:S(2)}) copy-start(f32[264,128]{1,0:T(8,128)S(1)} %collective-permute-done.13.refs_7_.refs_15_) | copy-start | bytes 405508
  40.3 6.7 %collective-permute-start.14 = (f32[264,128]{1,0:T(8,128)S(1)}, f32[264,128]{1,0:T(8,128)S(1)}, u32[]{:S(2)}, u32[]{:S(2)}) collective-permute-start(f32[264,128]{1,0:T(8,128)S(1)} %get-tuple-element.87), channel_id=1, source_target_pairs={{0,2},{2,0},{4,6},{6,4},{8,10},{10,8},{12,14},{14,12},{16,18},{18,... | collective-permute-start | bytes 405512 | tf_op jit(solution)/shard_map/ppermute | solution.py:507
  41.6 8.5 %collective-permute-start.15 = (f32[264,128]{1,0:T(8,128)S(1)}, f32[264,128]{1,0:T(8,128)S(1)}, u32[]{:S(2)}, u32[]{:S(2)}) collective-permute-start(f32[264,128]{1,0:T(8,128)S(1)} %get-tuple-element.88), channel_id=1, source_target_pairs={{0,4},{2,6},{4,0},{6,2},{8,12},{10,14},{12,8},{14,10},{16,20},{18,... | collective-permute-start | bytes 405512 | tf_op jit(solution)/shard_map/ppermute | solution.py:507
  43.0 7.4 %collective-permute-start.16 = (f32[264,128]{1,0:T(8,128)S(1)}, f32[264,128]{1,0:T(8,128)S(1)}, u32[]{:S(2)}, u32[]{:S(2)}) collective-permute-start(f32[264,128]{1,0:T(8,128)S(1)} %get-tuple-element.89), channel_id=1, source_target_pairs={{0,6},{2,4},{4,2},{6,0},{8,14},{10,12},{12,10},{14,8},{16,22},{18,... | collective-permute-start | bytes 405512 | tf_op jit(solution)/shard_map/ppermute | solution.py:507
  44.3 8.2 %collective-permute-start.21 = (f32[264,128]{1,0:T(8,128)S(1)}, f32[264,128]{1,0:T(8,128)S(1)}, u32[]{:S(2)}, u32[]{:S(2)}) collective-permute-start(f32[264,128]{1,0:T(8,128)S(1)} %get-tuple-element.95), channel_id=1, source_target_pairs={{0,2},{2,0},{4,6},{6,4},{8,10},{10,8},{12,14},{14,12},{16,18},{18,... | collective-permute-start | bytes 405512 | tf_op jit(solution)/shard_map/ppermute | solution.py:507
  45.6 10.0 %collective-permute-start.22 = (f32[264,128]{1,0:T(8,128)S(1)}, f32[264,128]{1,0:T(8,128)S(1)}, u32[]{:S(2)}, u32[]{:S(2)}) collective-permute-start(f32[264,128]{1,0:T(8,128)S(1)} %get-tuple-element.96), channel_id=1, source_target_pairs={{0,4},{2,6},{4,0},{6,2},{8,12},{10,14},{12,8},{14,10},{16,20},{18,... | collective-permute-start | bytes 405512 | tf_op jit(solution)/shard_map/ppermute | solution.py:507
  47.0 8.7 %collective-permute-start.23 = (f32[264,128]{1,0:T(8,128)S(1)}, f32[264,128]{1,0:T(8,128)S(1)}, u32[]{:S(2)}, u32[]{:S(2)}) collective-permute-start(f32[264,128]{1,0:T(8,128)S(1)} %get-tuple-element.97), channel_id=1, source_target_pairs={{0,6},{2,4},{4,2},{6,0},{8,14},{10,12},{12,10},{14,8},{16,22},{18,... | collective-permute-start | bytes 405512 | tf_op jit(solution)/shard_map/ppermute | solution.py:507
  50.5 7.6 %collective-permute-start.17 = (f32[264,128]{1,0:T(8,128)S(1)}, f32[264,128]{1,0:T(8,128)S(1)}, u32[]{:S(2)}, u32[]{:S(2)}) collective-permute-start(f32[264,128]{1,0:T(8,128)S(1)} %total.6.refs_5_), channel_id=1, source_target_pairs={{0,24},{2,26},{4,28},{6,30},{8,0},{10,2},{12,4},{14,6},{16,8},{18,... | collective-permute-start | bytes 405512 | tf_op jit(solution)/shard_map/ppermute | solution.py:522
  55.8 6.9 %collective-permute-start.24 = (f32[264,128]{1,0:T(8,128)S(1)}, f32[264,128]{1,0:T(8,128)S(1)}, u32[]{:S(2)}, u32[]{:S(2)}) collective-permute-start(f32[264,128]{1,0:T(8,128)S(1)} %total.7), channel_id=1, source_target_pairs={{0,24},{2,26},{4,28},{6,30},{8,0},{10,2},{12,4},{14,6},{16,8},{18,... | collective-permute-start | bytes 405512 | tf_op jit(solution)/shard_map/ppermute | solution.py:522
  58.0 9.1 %copy-start.18 = (f32[264,128]{1,0:T(8,128)S(1)}, f32[264,128]{1,0:T(8,128)}, u32[]{:S(2)}) copy-start(f32[264,128]{1,0:T(8,128)} %copy-done.17) | copy-start | bytes 405508
  58.2 7.7 %collective-permute-start.18 = (f32[264,128]{1,0:T(8,128)S(1)}, f32[264,128]{1,0:T(8,128)S(1)}, u32[]{:S(2)}, u32[]{:S(2)}) collective-permute-start(f32[264,128]{1,0:T(8,128)S(1)} %get-tuple-element.91), channel_id=1, source_target_pairs={{0,2},{2,0},{4,6},{6,4},{8,10},{10,8},{12,14},{14,12},{16,18},{18,... | collective-permute-start | bytes 405512 | tf_op jit(solution)/shard_map/ppermute | solution.py:507
  58.9 4.5 %collective-permute-start.25 = (f32[8,128]{1,0:T(8,128)S(1)}, f32[8,128]{1,0:T(8,128)S(1)}, u32[]{:S(2)}, u32[]{:S(2)}) collective-permute-start(f32[8,128]{1,0:T(8,128)S(1)} %get-tuple-element.98.refs_5_), channel_id=1, source_target_pairs={{0,16},{2,18},{4,20},{6,22},{8,24},{10,26},{12,28},{14,30},{16,0},... | collective-permute-start | bytes 12296 | tf_op jit(solution)/shard_map/ppermute | solution.py:522
  59.6 12.8 %collective-permute-start.19 = (f32[264,128]{1,0:T(8,128)S(1)}, f32[264,128]{1,0:T(8,128)S(1)}, u32[]{:S(2)}, u32[]{:S(2)}) collective-permute-start(f32[264,128]{1,0:T(8,128)S(1)} %get-tuple-element.92), channel_id=1, source_target_pairs={{0,4},{2,6},{4,0},{6,2},{8,12},{10,14},{12,8},{14,10},{16,20},{18,... | collective-permute-start | bytes 405512 | tf_op jit(solution)/shard_map/ppermute | solution.py:507
  60.9 6.3 %copy-start.8 = (f32[264,128]{1,0:T(8,128)S(1)}, f32[264,128]{1,0:T(8,128)}, u32[]{:S(2)}) copy-start(f32[264,128]{1,0:T(8,128)} %copy-done.7) | copy-start | bytes 405508
  60.9 6.3 %copy-start.10 = (f32[264,128]{1,0:T(8,128)S(1)}, f32[264,128]{1,0:T(8,128)}, u32[]{:S(2)}) copy-start(f32[264,128]{1,0:T(8,128)} %copy-done.9) | copy-start | bytes 405508
  60.9 6.3 %copy-start.12 = (f32[264,128]{1,0:T(8,128)S(1)}, f32[264,128]{1,0:T(8,128)}, u32[]{:S(2)}) copy-start(f32[264,128]{1,0:T(8,128)} %copy-done.11) | copy-start | bytes 405508
  60.9 6.3 %copy-start.14 = (f32[264,128]{1,0:T(8,128)S(1)}, f32[264,128]{1,0:T(8,128)}, u32[]{:S(2)}) copy-start(f32[264,128]{1,0:T(8,128)} %copy-done.13) | copy-start | bytes 405508
  60.9 6.3 %copy-start.16 = (f32[264,128]{1,0:T(8,128)S(1)}, f32[264,128]{1,0:T(8,128)}, u32[]{:S(2)}) copy-start(f32[264,128]{1,0:T(8,128)} %copy-done.15) | copy-start | bytes 405508
  60.9 11.5 %collective-permute-start.20 = (f32[264,128]{1,0:T(8,128)S(1)}, f32[264,128]{1,0:T(8,128)S(1)}, u32[]{:S(2)}, u32[]{:S(2)}) collective-permute-start(f32[264,128]{1,0:T(8,128)S(1)} %get-tuple-element.93), channel_id=1, source_target_pairs={{0,6},{2,4},{4,2},{6,0},{8,14},{10,12},{12,10},{14,8},{16,22},{18,... | collective-permute-start | bytes 405512 | tf_op jit(solution)/shard_map/ppermute | solution.py:507
  63.6 8.8 %collective-permute-start.26 = (f32[264,128]{1,0:T(8,128)S(1)}, f32[264,128]{1,0:T(8,128)S(1)}, u32[]{:S(2)}, u32[]{:S(2)}) collective-permute-start(f32[264,128]{1,0:T(8,128)S(1)} %get-tuple-element.100), channel_id=1, source_target_pairs={{0,2},{2,0},{4,6},{6,4},{8,10},{10,8},{12,14},{14,12},{16,18},{18,... | collective-permute-start | bytes 405512 | tf_op jit(solution)/shard_map/ppermute | solution.py:507
  65.1 7.9 %collective-permute-start.27 = (f32[264,128]{1,0:T(8,128)S(1)}, f32[264,128]{1,0:T(8,128)S(1)}, u32[]{:S(2)}, u32[]{:S(2)}) collective-permute-start(f32[264,128]{1,0:T(8,128)S(1)} %get-tuple-element.101), channel_id=1, source_target_pairs={{0,4},{2,6},{4,0},{6,2},{8,12},{10,14},{12,8},{14,10},{16,20},{18,... | collective-permute-start | bytes 405512 | tf_op jit(solution)/shard_map/ppermute | solution.py:507
  66.0 7.1 %collective-permute-start.28 = (f32[264,128]{1,0:T(8,128)S(1)}, f32[264,128]{1,0:T(8,128)S(1)}, u32[]{:S(2)}, u32[]{:S(2)}) collective-permute-start(f32[264,128]{1,0:T(8,128)S(1)} %get-tuple-element.102), channel_id=1, source_target_pairs={{0,6},{2,4},{4,2},{6,0},{8,14},{10,12},{12,10},{14,8},{16,22},{18,... | collective-permute-start | bytes 405512 | tf_op jit(solution)/shard_map/ppermute | solution.py:507
  (1 other events, 0.8 us)

commit v6 on v5

--- a/solution.py
+++ b/solution.py
@@ -106,6 +106,11 @@
     return [(chunk, wave) for wave in range(size.waves) for chunk in range(GROUP)]
 
 
+def last_order(size):
+    usual = list(range(GROUP * (size.waves - 1)))
+    return usual + [GROUP * (size.waves - 1) + k for k in reversed(range(GROUP))]
+
+
 def rate_of(rates_ref, size, group, h):
     return rates_ref[pl.ds(group * size.per + h, 1), :]
 
@@ -114,13 +119,14 @@
     return rate[:, :1] if size.rows != size.dim else rate
 
 
-def call(body, name, inputs, outputs, flops, moved, scratch=(), in_specs=None, out_specs=None, vmem=16):
+def call(body, name, inputs, outputs, flops, moved, scratch=(), in_specs=None, out_specs=None, vmem=16, aliases=None):
     return pl.pallas_call(
         body,
         out_shape=outputs,
         in_specs=in_specs if in_specs is not None else [VMEM] * len(inputs),
         out_specs=out_specs if out_specs is not None else [VMEM] * len(outputs),
         scratch_shapes=list(scratch),
+        input_output_aliases=aliases or {},
         compiler_params=pltpu.CompilerParams(vmem_limit_bytes=vmem * 1024 * 1024),
         cost_estimate=pl.CostEstimate(flops=flops, bytes_accessed=moved, transcendentals=0),
         name=name,
@@ -234,11 +240,12 @@
     ref[at : at + rows.shape[0], :] = rows
 
 
-def group_total(size, backward, wave, rates, parts):
+def group_total(size, backward, wave, rates, parts, riders=(), count=False):
     mark_row = size.state + (1 if backward else 0)
 
     def body(rates_ref, *refs):
-        ins, out = refs[:GROUP], refs[GROUP]
+        ins, rides = refs[:GROUP], refs[GROUP : GROUP + len(riders)]
+        outs = refs[GROUP + len(riders) :]
         place = places(backward)
         marks = [ref[mark_row : mark_row + 1, :] for ref in ins]
         end = marks[0]
@@ -255,30 +262,29 @@
             for k in range(GROUP):
                 term = decay(steps[k], rate) * ins[k][cols, :]
                 total = term if total is None else total + term
-            out[cols, :] = total
-        gains = ins[0][size.state :, :]
-        for k in range(1, GROUP):
-            gains = gains + ins[k][size.state :, :]
-        put_rows(out, size.state, with_marks(size, end, end, gains))
+            outs[0][cols, :] = total
+        rows = [ride[...] for ride in rides] or [ref[size.state :, :] for ref in ins]
+        put_rows(outs[0], size.state, with_marks(size, end, end, sum(rows)))
+        if count:
+            outs[1][...] = sum(rows)
 
     return call(
-        body, "total", (rates, *parts), [size.payload],
+        body, "total", (rates, *parts, *riders), [size.payload] + [size.rows_of_gain] * count,
         size.state * size.dim * 8, size.state * size.dim * 20,
-    )[0]
-
-
-def group_prefixes(size, backward, wave, rates, parts, entering, riders=(), collect=()):
+    )
+
+
+def group_prefixes(size, backward, wave, rates, parts, entering, riders=(), own=()):
     mark_row = size.state + (1 if backward else 0)
 
     def body(rates_ref, *refs):
-        ins, enter = refs[:GROUP], refs[GROUP]
-        rides, outs = refs[GROUP + 1 : GROUP + 1 + len(riders)], refs[GROUP + 1 + len(riders) :]
-        if collect:
-            put_rows(outs[-1], 0, outs[0][size.state :, :] + enter[size.state :, :])
-            outs = outs[1:-1]
-        gains = jnp.zeros((size.info, size.dim), f32)
-        for ride in rides:
-            gains = gains + ride[: size.info, :]
+        ins, enter, refs = refs[:GROUP], refs[GROUP], refs[GROUP + 1 :]
+        rows = [ref[...] for ref in refs[: len(riders)]]
+        rows += [ref[size.state :, :] for ref in refs[len(riders) : len(riders) + len(own)]]
+        outs = refs[len(riders) + len(own) :]
+        gains = sum(rows) + enter[size.state :, :] if own else sum(rows)
+        if not rows:
+            gains = jnp.zeros((size.info, size.dim), f32)
         place = places(backward)
         me = partners()[0]
         marks = [ref[mark_row : mark_row + 1, :] for ref in ins]
@@ -310,41 +316,49 @@
                 outs[to][cols, :] = total
 
     return call(
-        body, "prefixes", (rates, *parts, entering, *riders, *collect),
-        [size.payload] * GROUP + [size.rows_of_gain] * len(collect),
+        body, "prefixes", (rates, *parts, entering, *riders, *own), [size.payload] * GROUP,
         size.state * size.dim * 40, size.state * size.dim * 36,
     )
 
 
-def whole_attended(size, mark, rates, queries, out_grad, gain, near, entering):
+def whole_attended(size, wave, mark, rates, queries, out_grad, gain, near, entering, before=()):
+    last = wave == size.waves - 1
+
     def body(mark_ref, rates_ref, query_ref, grad_ref, gain_ref, near_ref, *refs):
-        states, (out_ref, sums_ref) = refs[:-2], refs[-2:]
+        states, earlier, outs = refs[:GROUP], refs[GROUP : GROUP + len(before)], refs[GROUP + len(before) :]
         group = partners()
         mark = mark_ref[...]
         behind = steps_if(mark == states[0][size.state : size.state + 1, :], position(size) + 1.0)
-        square = jnp.zeros((size.rows, size.dim), f32)
-        cross = jnp.zeros((size.rows, size.dim), f32)
-        for i, (c, wave) in enumerate(all_pieces(size)):
+        square = earlier[1][...] if before else jnp.zeros((size.rows, size.dim), f32)
+        cross = earlier[2][...] if before else jnp.zeros((size.rows, size.dim), f32)
+        for c in range(GROUP):
             for h, cols in wave_heads(size, wave):
                 here = columns(size, group[c], h)
-                rate = rate_of(rates_ref, size, group[c], h)
-                weight = decay(behind, rate)
+                weight = decay(behind, rate_of(rates_ref, size, group[c], h))
                 query = query_ref[:, here]
-                high, low = halves(states[i][cols, :])
+                high, low = halves(states[c][cols, :])
                 inter = dot(jnp.concatenate([query, query], 1), jnp.concatenate([high, low], 0))
                 out = near_ref[:, here] + weight * inter
-                out_ref[:, here] = out
+                outs[0][:, here] = out
                 square += out * out
                 cross += grad_ref[:, here].astype(f32) * gain_ref[:, here] * out
-        square = jnp.sum(square.T, axis=0, keepdims=True)
-        cross = jnp.sum(cross.T, axis=0, keepdims=True)
-        index = lax.broadcasted_iota(jnp.int32, (8, size.rows), 0)
-        sums_ref[...] = jnp.where(index == 0, square, jnp.where(index == 1, cross, 0.0))
-
+        if last:
+            square = jnp.sum(square.T, axis=0, keepdims=True)
+            cross = jnp.sum(cross.T, axis=0, keepdims=True)
+            index = lax.broadcasted_iota(jnp.int32, (8, size.rows), 0)
+            outs[1][...] = jnp.where(index == 0, square, jnp.where(index == 1, cross, 0.0))
+        else:
+            outs[1][...], outs[2][...] = square, cross
+
+    if last:
+        sums = [jax.ShapeDtypeStruct((8, size.rows), f32)]
+    else:
+        sums = [jax.ShapeDtypeStruct((size.rows, size.dim), f32)] * 2
+    inputs = (mark, rates, queries, out_grad, gain, near, *entering, *before)
     return call(
-        body, "attended", (mark, rates, queries, out_grad, gain, near, *entering),
-        [size.block, jax.ShapeDtypeStruct((8, size.rows), f32)],
-        size.heads * 4 * size.rows * size.dim * size.dim, size.features * size.rows * 16,
+        body, "attended", inputs, [size.block] + sums,
+        GROUP * size.each * 4 * size.rows * size.dim * size.dim, GROUP * size.state * size.rows * 16,
+        aliases={len(inputs) - len(before): 0} if before else {},
     )
 
 
@@ -390,8 +404,10 @@
 
 
 def local_gradients(size, mark, rates, queries, key_rows, value_rows, back, entering):
+    pieces = all_pieces(size)
+    n = len(pieces)
+
     def body(mark_ref, rates_ref, query_ref, key_ref, value_ref, *refs):
-        n = GROUP * size.waves
         backs, states = refs[:n], refs[n : 2 * n]
         out_hbm, local_key, local_value, done, sems = refs[2 * n :]
         group = partners()
@@ -402,7 +418,8 @@
         for c in range(GROUP):
             for h in range(size.per):
                 here = columns(size, group[c], h)
-                piece = c + GROUP * (h // size.each)
+                piece = pieces.index((c, h // size.each))
+                near = slice(c * size.wide + h * size.dim, c * size.wide + (h + 1) * size.dim)
                 cols = slice(h % size.each * size.dim, (h % size.each + 1) * size.dim)
                 rate = rate_of(rates_ref, size, group[c], h)
                 rows_rate = square_rate(rate, size)
@@ -424,12 +441,12 @@
                     part + decay(behind, rate) * inter
                 ).astype(bf16)
                 grads_high, grads_low = halves(dot(values, both, 1, 1) * turned_weight)
-                local_key[:, here] = dot(
+                local_key[:, near] = dot(
                     jnp.concatenate([grads_high, grads_low], 1),
                     jnp.concatenate([query, query], 0),
                 )
                 score_high, score_low = halves(dot(key, query, 1, 1) * turned_weight)
-                local_value[:, here] = dot(
+                local_value[:, near] = dot(
                     jnp.concatenate([score_high, score_high, score_low], 1),
                     jnp.concatenate([high, low, high], 0),
                 )
@@ -455,6 +472,7 @@
     def body(mark_ref, rates_ref, key_ref, value_ref, local_key_ref, local_value_ref, *refs):
         n = GROUP * size.waves
         states, (keys_hbm, values_hbm, gain_hbm) = refs[:n], refs[n : n + 3]
+        states = [states[last_order(size).index(i)] for i in range(n)]
         keys, values, gains, sems = refs[n + 3 :]
         group = partners()
         mark = mark_ref[...]
@@ -479,8 +497,9 @@
                     jnp.concatenate([value, value], 1), jnp.concatenate([high, low], 1), 1, 1
                 )
                 from_keys = dot(jnp.concatenate([key, key], 1), jnp.concatenate([high, low], 0))
-                keys[c, :, cols] = (local_key_ref[:, here] + weight * from_values).astype(bf16)
-                values[c, :, cols] = (local_value_ref[:, here] + weight * from_keys).astype(bf16)
+                near = slice(c * size.wide + h * size.dim, c * size.wide + (h + 1) * size.dim)
+                keys[c, :, cols] = (local_key_ref[:, near] + weight * from_values).astype(bf16)
+                values[c, :, cols] = (local_value_ref[:, near] + weight * from_keys).astype(bf16)
             here = columns(size, group[c])
             for copy in (
                 pltpu.make_async_copy(keys.at[c], keys_hbm.at[:, here], sems.at[0, c]),
@@ -494,7 +513,11 @@
     shape = jax.ShapeDtypeStruct((size.rows, size.features), bf16)
     held = pltpu.VMEM((GROUP, size.rows, size.wide), bf16)
     return call(
-        body, "final", (mark, rates, key_rows, value_rows, local_key, local_value, *entering),
+        body, "final",
+        (
+            mark, rates, key_rows, value_rows, local_key, local_value,
+            *[entering[i] for i in last_order(size)],
+        ),
         [shape, shape, jax.ShapeDtypeStruct((1, size.features), f32)],
         size.heads * 8 * size.rows * size.dim * size.dim, size.features * size.rows * 24,
         [held, held, pltpu.VMEM((1, size.features), f32), pltpu.SemaphoreType.DMA((3, GROUP))],
@@ -564,14 +587,18 @@
     states |= zip(later, more_states(size, later, *common, key_rows, value_rows))
     near = nearby_attended(size, *common, queries, key_rows, value_rows)
     parts = {w: exchange({k: states[k, w] for k in range(GROUP)}) for w in waves}
-    totals = {w: group_total(size, False, w, rates, parts[w]) for w in waves}
+    totals = {w: group_total(size, False, w, rates, parts[w])[0] for w in waves}
     outer = {w: from_other_groups(size, False, w, decay_span, totals[w]) for w in waves}
     entering = {}
     for w in waves:
         entering[w] = exchange(group_prefixes(size, False, w, rates, parts[w], outer[w]))
 
     entering = sum([entering[w] for w in waves], [])
-    attended, sums = whole_attended(size, *common, queries, out_grad, gain, near, entering)
+    outs = ()
+    for w in waves:
+        states = entering[w * GROUP : (w + 1) * GROUP]
+        outs = whole_attended(size, w, *common, queries, out_grad, gain, near, states, outs)
+    attended, sums = outs
     sums = lax.psum(sums, "head")
     back, states = {}, {}
     for pieces in [*sent, kept]:
@@ -582,25 +609,27 @@
         states |= zip(pieces, payloads)
 
     parts = {w: exchange({k: states[k, w] for k in range(GROUP)}) for w in waves}
-    totals = {w: group_total(size, True, w, rates, parts[w]) for w in waves}
+    back = [back[piece] for piece in every]
+    totals, leaving, last = {}, [], size.waves - 1
+    rides = size.waves > 1 and reach_of_documents(size) == 1 and members > GROUP
+    totals[0], *gains = group_total(size, True, 0, rates, parts[0], (), True)
+    apart = 2 if rides else 1
+    while apart * GROUP < members:
+        gains = [sum(gains), cyclic(sum(gains), -apart * GROUP)]
+        apart *= 2
+    for w in waves[1:]:
+        riders = gains if rides and w == last else ()
+        totals[w] = group_total(size, True, w, rates, parts[w], riders)[0]
     outer = {w: from_other_groups(size, True, w, decay_span, totals[w]) for w in waves}
-    rides = size.waves > 1 and reach_of_documents(size) == 1 and members > GROUP
-    gains, summed, leaving = [totals[0][size.state :, :]], 1, []
     for w in waves:
-        if w < size.waves - 1:
-            riders, collect = (), ((totals[0],) if rides and w == 0 else ())
-        else:
-            while summed * GROUP < members:
-                gains = [sum(gains), cyclic(sum(gains), -summed * GROUP)]
-                summed *= 2
-            riders, collect = gains, ()
-        outs = group_prefixes(size, True, w, rates, parts[w], outer[w], riders, collect)
-        if collect:
-            gains, summed = outs[GROUP:], 2
-        leaving += exchange(outs[:GROUP])
+        riders = gains if w == last and not rides else ()
+        own = (totals[w],) if w == last and rides else ()
+        leaving += exchange(
+            group_prefixes(size, True, w, rates, parts[w], outer[w], riders, own)
+        )
 
     query_grad, local_key, local_value = local_gradients(
-        size, *common, queries, key_rows, value_rows, [back[piece] for piece in every], entering
+        size, *common, queries, key_rows, value_rows, back, entering
     )
     key_grad, value_grad, gain_grad = final_gradients(
         size, *common, key_rows, value_rows, local_key, local_value, leaving

time: 74.9 us -> 74.2 us (level)
  waiting for transfers between devices: 14.6 us -> 13.4 us
    ppermute x24, waiting for transfers between devices: 12.7 us -> 11 us  [swap(): lax.ppermute(array, 'seq', [(i, i ^ distance) for i in range(members)])]
    pallas_call x17 -> x18, Pallas kernels: 15.2 us -> 15.2 us  [call(): pl.pallas_call(body, out_shape=outputs, in_specs=in_specs if in_specs is...]
  transfers between devices with their start and end apart: 29 -> 29, of which waited for: 14 -> 14; matrix products, arithmetic and copies ran while one was open for 0% -> 0% of each run, Pallas kernels for 13% -> 14%
where the time goes in v6:
time: 74.2 us; the launch traced here: 74 us
  starting transfers between devices  40.5 us (55%)
  Pallas kernels  15.2 us (20%)
  waiting for transfers between devices  13.4 us (18%)
  blocking collectives  2.44 us (3%)
  local copies, waits for them, and re-layouts  1.35 us (2%)
  between operations  1.1 us (1%)
    ppermute x24, starting transfers between devices, swap(): lax.ppermute(array, 'seq', [(i, i ^ distance) for i in range(members)])  32 us
    pallas_call x18, Pallas kernels, call(): pl.pallas_call(body, out_shape=outputs, in_specs=in_specs if in_specs is...  15.2 us
    ppermute x24, waiting for transfers between devices, swap(): lax.ppermute(array, 'seq', [(i, i ^ distance) for i in range(members)])  11 us
    ppermute x5, starting transfers between devices, cyclic(): lax.ppermute(array, 'seq', [(i, (i + by) % members) for i in range(member...  8.49 us
    psum x1, blocking collectives, local(): sums = lax.psum(sums, 'head')  2.44 us
    ppermute x5, waiting for transfers between devices, cyclic(): lax.ppermute(array, 'seq', [(i, (i + by) % members) for i in range(member...  2.41 us
  transfers between devices with their start and end apart: 29, of which 14 were waited for; matrix products, arithmetic and copies ran while one was open for 0% of the time, Pallas kernels for 14%

profile of v6, /device:TPU:0, one launch (start us, length us, event | category | flops | bytes accessed | tf_op | source)
XLA Modules:
  0.0 74.0 jit_solution(16496893721945111242)
XLA Ops:
  0.7 2.2 %states.2 = (f32[264,128]{1,0:T(8,128)}, f32[264,128]{1,0:T(8,128)}, f32[264,128]{1,0:T(8,128)}, f32[128,128]{1,0:T(8,128)}, f32[16,128]{1,0:T(8,128)}) custom-call(s32[1,128]{1,0:T(1,128)} %bitcast.9, f32[1,16]{1,0:T(1,128)} %bitcast.10, bf16[128,2048]{1,0:T(8,128)(2,1)} %key_ref.7, bf16[128,2048]{1,0:T(8,128)(2,1)} %value_ref.7), custom_call_target="tpu_custom_call" | custom-call | flops 50331648 | bytes 786432 | tf_op jit(solution)/shard_map/states/pallas_call | solution.py:123
  2.8 3.0 %collective-permute-start.7 = (f32[264,128]{1,0:T(8,128)}, f32[264,128]{1,0:T(8,128)S(1)}, u32[]{:S(2)}, u32[]{:S(2)}) collective-permute-start(f32[264,128]{1,0:T(8,128)} %get-tuple-element.70), channel_id=1, source_target_pairs={{0,2},{2,0},{4,6},{6,4},{8,10},{10,8},{12,14},{14,12},{16,18},{18,... | collective-permute-start | bytes 405512 | tf_op jit(solution)/shard_map/ppermute | solution.py:530
  5.8 1.5 %collective-permute-start.8 = (f32[264,128]{1,0:T(8,128)}, f32[264,128]{1,0:T(8,128)S(1)}, u32[]{:S(2)}, u32[]{:S(2)}) collective-permute-start(f32[264,128]{1,0:T(8,128)} %get-tuple-element.71), channel_id=1, source_target_pairs={{0,4},{2,6},{4,0},{6,2},{8,12},{10,14},{12,8},{14,10},{16,20},{18,... | collective-permute-start | bytes 405512 | tf_op jit(solution)/shard_map/ppermute | solution.py:530
  7.4 0.8 %copy-done.4 = f32[128,128]{1,0:T(8,128)S(1)} copy-done((f32[128,128]{1,0:T(8,128)S(1)}, f32[128,128]{1,0:T(8,128)}, u32[]{:S(2)}) %copy-start.4) | copy-done | bytes 65560
  8.6 2.0 %collective-permute-start = (f32[264,128]{1,0:T(8,128)S(1)}, f32[264,128]{1,0:T(8,128)S(1)}, u32[]{:S(2)}, u32[]{:S(2)}) collective-permute-start(f32[264,128]{1,0:T(8,128)S(1)} %get-tuple-element.62), channel_id=1, source_target_pairs={{0,2},{2,0},{4,6},{6,4},{8,10},{10,8},{12,14},{14,12},{16,18},{18,... | collective-permute-start | bytes 405512 | tf_op jit(solution)/shard_map/ppermute | solution.py:530
  10.7 1.5 %collective-permute-start.1 = (f32[264,128]{1,0:T(8,128)S(1)}, f32[264,128]{1,0:T(8,128)S(1)}, u32[]{:S(2)}, u32[]{:S(2)}) collective-permute-start(f32[264,128]{1,0:T(8,128)S(1)} %get-tuple-element.63), channel_id=1, source_target_pairs={{0,4},{2,6},{4,0},{6,2},{8,12},{10,14},{12,8},{14,10},{16,20},{18,... | collective-permute-start | bytes 405512 | tf_op jit(solution)/shard_map/ppermute | solution.py:530
  12.2 1.3 %collective-permute-start.2 = (f32[264,128]{1,0:T(8,128)S(1)}, f32[264,128]{1,0:T(8,128)S(1)}, u32[]{:S(2)}, u32[]{:S(2)}) collective-permute-start(f32[264,128]{1,0:T(8,128)S(1)} %get-tuple-element.64), channel_id=1, source_target_pairs={{0,6},{2,4},{4,2},{6,0},{8,14},{10,12},{12,10},{14,8},{16,22},{18,... | collective-permute-start | bytes 405512 | tf_op jit(solution)/shard_map/ppermute | solution.py:530
  13.5 1.1 %collective-permute-done.8.refs_2_ = f32[264,128]{1,0:T(8,128)S(1)} collective-permute-done((f32[264,128]{1,0:T(8,128)}, f32[264,128]{1,0:T(8,128)S(1)}, u32[]{:S(2)}, u32[]{:S(2)}) %collective-permute-start.8) | collective-permute-done | bytes 135200 | tf_op jit(solution)/shard_map/ppermute | solution.py:530
  14.6 0.5 collective-permute-done.9.refs_3_
  15.1 1.6 %collective-permute-start.10 = (f32[264,128]{1,0:T(8,128)S(1)}, f32[264,128]{1,0:T(8,128)S(1)}, u32[]{:S(2)}, u32[]{:S(2)}) collective-permute-start(f32[264,128]{1,0:T(8,128)S(1)} %total.5), channel_id=1, source_target_pairs={{0,8},{2,10},{4,12},{6,14},{8,16},{10,18},{12,20},{14,22},{16,24},... | collective-permute-start | bytes 405512 | tf_op jit(solution)/shard_map/ppermute | solution.py:545
  16.9 2.9 %collective-permute-done.1.refs_2_ = f32[264,128]{1,0:T(8,128)S(1)} collective-permute-done((f32[264,128]{1,0:T(8,128)S(1)}, f32[264,128]{1,0:T(8,128)S(1)}, u32[]{:S(2)}, u32[]{:S(2)}) %collective-permute-start.1) | collective-permute-done | bytes 135200 | tf_op jit(solution)/shard_map/ppermute | solution.py:530
  19.9 1.6 %collective-permute-start.3 = (f32[264,128]{1,0:T(8,128)S(1)}, f32[264,128]{1,0:T(8,128)S(1)}, u32[]{:S(2)}, u32[]{:S(2)}) collective-permute-start(f32[264,128]{1,0:T(8,128)S(1)} %total.4), channel_id=1, source_target_pairs={{0,8},{2,10},{4,12},{6,14},{8,16},{10,18},{12,20},{14,22},{16,24},... | collective-permute-start | bytes 405512 | tf_op jit(solution)/shard_map/ppermute | solution.py:545
  21.5 0.5 collective-permute-done.10.refs_4_
  22.2 1.4 %collective-permute-start.11 = (f32[264,128]{1,0:T(8,128)S(1)}, f32[264,128]{1,0:T(8,128)S(1)}, u32[]{:S(2)}, u32[]{:S(2)}) collective-permute-start(f32[264,128]{1,0:T(8,128)S(1)} %get-tuple-element.74), channel_id=1, source_target_pairs={{0,2},{2,0},{4,6},{6,4},{8,10},{10,8},{12,14},{14,12},{16,18},{18,... | collective-permute-start | bytes 405512 | tf_op jit(solution)/shard_map/ppermute | solution.py:530
  23.6 1.2 %collective-permute-start.12 = (f32[264,128]{1,0:T(8,128)S(1)}, f32[264,128]{1,0:T(8,128)S(1)}, u32[]{:S(2)}, u32[]{:S(2)}) collective-permute-start(f32[264,128]{1,0:T(8,128)S(1)} %get-tuple-element.75), channel_id=1, source_target_pairs={{0,4},{2,6},{4,0},{6,2},{8,12},{10,14},{12,8},{14,10},{16,20},{18,... | collective-permute-start | bytes 405512 | tf_op jit(solution)/shard_map/ppermute | solution.py:530
  24.7 1.4 %collective-permute-start.13 = (f32[264,128]{1,0:T(8,128)S(1)}, f32[264,128]{1,0:T(8,128)S(1)}, u32[]{:S(2)}, u32[]{:S(2)}) collective-permute-start(f32[264,128]{1,0:T(8,128)S(1)} %get-tuple-element.76), channel_id=1, source_target_pairs={{0,6},{2,4},{4,2},{6,0},{8,14},{10,12},{12,10},{14,8},{16,22},{18,... | collective-permute-start | bytes 405512 | tf_op jit(solution)/shard_map/ppermute | solution.py:530
  26.1 0.6 collective-permute-done.3.refs_4_
  26.9 1.3 %collective-permute-start.4 = (f32[264,128]{1,0:T(8,128)S(1)}, f32[264,128]{1,0:T(8,128)S(1)}, u32[]{:S(2)}, u32[]{:S(2)}) collective-permute-start(f32[264,128]{1,0:T(8,128)S(1)} %get-tuple-element.66), channel_id=1, source_target_pairs={{0,2},{2,0},{4,6},{6,4},{8,10},{10,8},{12,14},{14,12},{16,18},{18,... | collective-permute-start | bytes 405512 | tf_op jit(solution)/shard_map/ppermute | solution.py:530
  28.2 0.8 %collective-permute-start.5 = (f32[264,128]{1,0:T(8,128)S(1)}, f32[264,128]{1,0:T(8,128)S(1)}, u32[]{:S(2)}, u32[]{:S(2)}) collective-permute-start(f32[264,128]{1,0:T(8,128)S(1)} %get-tuple-element.67), channel_id=1, source_target_pairs={{0,4},{2,6},{4,0},{6,2},{8,12},{10,14},{12,8},{14,10},{16,20},{18,... | collective-permute-start | bytes 405512 | tf_op jit(solution)/shard_map/ppermute | solution.py:530
  29.1 1.4 %collective-permute-start.6 = (f32[264,128]{1,0:T(8,128)S(1)}, f32[264,128]{1,0:T(8,128)S(1)}, u32[]{:S(2)}, u32[]{:S(2)}) collective-permute-start(f32[264,128]{1,0:T(8,128)S(1)} %get-tuple-element.68), channel_id=1, source_target_pairs={{0,6},{2,4},{4,2},{6,0},{8,14},{10,12},{12,10},{14,8},{16,22},{18,... | collective-permute-start | bytes 405512 | tf_op jit(solution)/shard_map/ppermute | solution.py:530
  30.5 2.7 %nearby.1.near_ref = f32[128,2048]{1,0:T(8,128)S(1)} custom-call(f32[128,128]{1,0:T(8,128)S(1)} %copy-done.5, f32[16,128]{1,0:T(8,128)S(1)} %copy-done.6, bf16[128,2048]{1,0:T(8,128)(2,1)S(1)} %copy-done, bf16[128,2048]{1,0:T(8,128)(2,1)S(1)} %copy-done.1, bf16[128,2048]{1,0:T(8,128)(2,1)S(1)} %copy-done.2), custom_call_target="tpu_custom_call" | custom-call | flops 201326592 | bytes 2621440 | tf_op jit(solution)/shard_map/nearby/pallas_call | solution.py:123
  33.9 1.0 %collective-permute-done.5.refs_2_.refs_14_ = f32[264,128]{1,0:T(8,128)S(1)} collective-permute-done((f32[264,128]{1,0:T(8,128)S(1)}, f32[264,128]{1,0:T(8,128)S(1)}, u32[]{:S(2)}, u32[]{:S(2)}) %collective-permute-start.5) | collective-permute-done | bytes 135200 | tf_op jit(solution)/shard_map/ppermute | solution.py:530
  34.9 1.4 %collective-permute-done.6.refs_3_.refs_15_ = f32[264,128]{1,0:T(8,128)S(1)} collective-permute-done((f32[264,128]{1,0:T(8,128)S(1)}, f32[264,128]{1,0:T(8,128)S(1)}, u32[]{:S(2)}, u32[]{:S(2)}) %collective-permute-start.6) | collective-permute-done | bytes 135200 | tf_op jit(solution)/shard_map/ppermute | solution.py:530
  36.3 0.5 attended.3
  37.0 2.4 %psum.7.sums_ref = f32[8,128]{1,0:T(8,128)S(1)} all-reduce(f32[8,128]{1,0:T(8,128)S(1)} %get-tuple-element.80), channel_id=1, replica_groups=mesh['seq'=16,'head'=2] {'head'}, use_global_device_ids=true, to_apply=%region_0.0 | all-reduce | flops 1024 | bytes 8192 | tf_op jit(solution)/shard_map/psum | solution.py:602
  39.4 0.6 back.4
  40.0 1.4 %collective-permute-start.14 = (f32[264,128]{1,0:T(8,128)S(1)}, f32[264,128]{1,0:T(8,128)S(1)}, u32[]{:S(2)}, u32[]{:S(2)}) collective-permute-start(f32[264,128]{1,0:T(8,128)S(1)} %get-tuple-element.94), channel_id=1, source_target_pairs={{0,2},{2,0},{4,6},{6,4},{8,10},{10,8},{12,14},{14,12},{16,18},{18,... | collective-permute-start | bytes 405512 | tf_op jit(solution)/shard_map/ppermute | solution.py:530
  41.4 1.3 %collective-permute-start.15 = (f32[264,128]{1,0:T(8,128)S(1)}, f32[264,128]{1,0:T(8,128)S(1)}, u32[]{:S(2)}, u32[]{:S(2)}) collective-permute-start(f32[264,128]{1,0:T(8,128)S(1)} %get-tuple-element.95), channel_id=1, source_target_pairs={{0,4},{2,6},{4,0},{6,2},{8,12},{10,14},{12,8},{14,10},{16,20},{18,... | collective-permute-start | bytes 405512 | tf_op jit(solution)/shard_map/ppermute | solution.py:530
  42.7 0.8 %collective-permute-start.16 = (f32[264,128]{1,0:T(8,128)S(1)}, f32[264,128]{1,0:T(8,128)S(1)}, u32[]{:S(2)}, u32[]{:S(2)}) collective-permute-start(f32[264,128]{1,0:T(8,128)S(1)} %get-tuple-element.96), channel_id=1, source_target_pairs={{0,6},{2,4},{4,2},{6,0},{8,14},{10,12},{12,10},{14,8},{16,22},{18,... | collective-permute-start | bytes 405512 | tf_op jit(solution)/shard_map/ppermute | solution.py:530
  43.6 0.5 back.5
  44.0 1.4 %collective-permute-start.21 = (f32[264,128]{1,0:T(8,128)S(1)}, f32[264,128]{1,0:T(8,128)S(1)}, u32[]{:S(2)}, u32[]{:S(2)}) collective-permute-start(f32[264,128]{1,0:T(8,128)S(1)} %get-tuple-element.103), channel_id=1, source_target_pairs={{0,2},{2,0},{4,6},{6,4},{8,10},{10,8},{12,14},{14,12},{16,18},{18,... | collective-permute-start | bytes 405512 | tf_op jit(solution)/shard_map/ppermute | solution.py:530
  45.4 1.3 %collective-permute-start.22 = (f32[264,128]{1,0:T(8,128)S(1)}, f32[264,128]{1,0:T(8,128)S(1)}, u32[]{:S(2)}, u32[]{:S(2)}) collective-permute-start(f32[264,128]{1,0:T(8,128)S(1)} %get-tuple-element.104), channel_id=1, source_target_pairs={{0,4},{2,6},{4,0},{6,2},{8,12},{10,14},{12,8},{14,10},{16,20},{18,... | collective-permute-start | bytes 405512 | tf_op jit(solution)/shard_map/ppermute | solution.py:530
  46.8 1.8 %collective-permute-start.23 = (f32[264,128]{1,0:T(8,128)S(1)}, f32[264,128]{1,0:T(8,128)S(1)}, u32[]{:S(2)}, u32[]{:S(2)}) collective-permute-start(f32[264,128]{1,0:T(8,128)S(1)} %get-tuple-element.105), channel_id=1, source_target_pairs={{0,6},{2,4},{4,2},{6,0},{8,14},{10,12},{12,10},{14,8},{16,22},{18,... | collective-permute-start | bytes 405512 | tf_op jit(solution)/shard_map/ppermute | solution.py:530
  48.6 0.4 back.3
  49.0 0.9 %collective-permute-done.15.refs_2_ = f32[264,128]{1,0:T(8,128)S(1)} collective-permute-done((f32[264,128]{1,0:T(8,128)S(1)}, f32[264,128]{1,0:T(8,128)S(1)}, u32[]{:S(2)}, u32[]{:S(2)}) %collective-permute-start.15) | collective-permute-done | bytes 135200 | tf_op jit(solution)/shard_map/ppermute | solution.py:530
  50.2 2.0 %collective-permute-start.17 = (f32[264,128]{1,0:T(8,128)S(1)}, f32[264,128]{1,0:T(8,128)S(1)}, u32[]{:S(2)}, u32[]{:S(2)}) collective-permute-start(f32[264,128]{1,0:T(8,128)S(1)} %get-tuple-element.97), channel_id=1, source_target_pairs={{0,24},{2,26},{4,28},{6,30},{8,0},{10,2},{12,4},{14,6},{16,8},{18,... | collective-permute-start | bytes 405512 | tf_op jit(solution)/shard_map/ppermute | solution.py:545
  52.3 0.8 %collective-permute-start.24 = (f32[8,128]{1,0:T(8,128)S(1)}, f32[8,128]{1,0:T(8,128)S(1)}, u32[]{:S(2)}, u32[]{:S(2)}) collective-permute-start(f32[8,128]{1,0:T(8,128)S(1)} %get-tuple-element.106.refs_4_), channel_id=1, source_target_pairs={{0,16},{2,18},{4,20},{6,22},{8,24},{10,26},{12,28},{14,30},{16,0},... | collective-permute-start | bytes 12296 | tf_op jit(solution)/shard_map/ppermute | solution.py:545
  53.1 2.4 %collective-permute-done.22.refs_2_ = f32[264,128]{1,0:T(8,128)S(1)} collective-permute-done((f32[264,128]{1,0:T(8,128)S(1)}, f32[264,128]{1,0:T(8,128)S(1)}, u32[]{:S(2)}, u32[]{:S(2)}) %collective-permute-start.22) | collective-permute-done | bytes 135200 | tf_op jit(solution)/shard_map/ppermute | solution.py:530
  55.5 1.3 %collective-permute-done.24.refs_5_ = f32[8,128]{1,0:T(8,128)S(1)} collective-permute-done((f32[8,128]{1,0:T(8,128)S(1)}, f32[8,128]{1,0:T(8,128)S(1)}, u32[]{:S(2)}, u32[]{:S(2)}) %collective-permute-start.24) | collective-permute-done | bytes 4128 | tf_op jit(solution)/shard_map/ppermute | solution.py:545
  56.8 2.4 %collective-permute-start.25 = (f32[264,128]{1,0:T(8,128)S(1)}, f32[264,128]{1,0:T(8,128)S(1)}, u32[]{:S(2)}, u32[]{:S(2)}) collective-permute-start(f32[264,128]{1,0:T(8,128)S(1)} %total.7.refs_5_), channel_id=1, source_target_pairs={{0,24},{2,26},{4,28},{6,30},{8,0},{10,2},{12,4},{14,6},{16,8},{18,... | collective-permute-start | bytes 405512 | tf_op jit(solution)/shard_map/ppermute | solution.py:545
  59.5 0.9 %collective-permute-start.18 = (f32[264,128]{1,0:T(8,128)S(1)}, f32[264,128]{1,0:T(8,128)S(1)}, u32[]{:S(2)}, u32[]{:S(2)}) collective-permute-start(f32[264,128]{1,0:T(8,128)S(1)} %get-tuple-element.99), channel_id=1, source_target_pairs={{0,2},{2,0},{4,6},{6,4},{8,10},{10,8},{12,14},{14,12},{16,18},{18,... | collective-permute-start | bytes 405512 | tf_op jit(solution)/shard_map/ppermute | solution.py:530
  60.4 1.3 %collective-permute-start.19 = (f32[264,128]{1,0:T(8,128)S(1)}, f32[264,128]{1,0:T(8,128)S(1)}, u32[]{:S(2)}, u32[]{:S(2)}) collective-permute-start(f32[264,128]{1,0:T(8,128)S(1)} %get-tuple-element.100), channel_id=1, source_target_pairs={{0,4},{2,6},{4,0},{6,2},{8,12},{10,14},{12,8},{14,10},{16,20},{18,... | collective-permute-start | bytes 405512 | tf_op jit(solution)/shard_map/ppermute | solution.py:530
  61.7 1.4 %collective-permute-start.20 = (f32[264,128]{1,0:T(8,128)S(1)}, f32[264,128]{1,0:T(8,128)S(1)}, u32[]{:S(2)}, u32[]{:S(2)}) collective-permute-start(f32[264,128]{1,0:T(8,128)S(1)} %get-tuple-element.101), channel_id=1, source_target_pairs={{0,6},{2,4},{4,2},{6,0},{8,14},{10,12},{12,10},{14,8},{16,22},{18,... | collective-permute-start | bytes 405512 | tf_op jit(solution)/shard_map/ppermute | solution.py:530
  63.3 1.6 %collective-permute-start.26 = (f32[264,128]{1,0:T(8,128)S(1)}, f32[264,128]{1,0:T(8,128)S(1)}, u32[]{:S(2)}, u32[]{:S(2)}) collective-permute-start(f32[264,128]{1,0:T(8,128)S(1)} %get-tuple-element.107), channel_id=1, source_target_pairs={{0,6},{2,4},{4,2},{6,0},{8,14},{10,12},{12,10},{14,8},{16,22},{18,... | collective-permute-start | bytes 405512 | tf_op jit(solution)/shard_map/ppermute | solution.py:530
  64.9 0.7 collective-permute-start.27
  65.8 1.1 %collective-permute-start.28 = (f32[264,128]{1,0:T(8,128)S(1)}, f32[264,128]{1,0:T(8,128)S(1)}, u32[]{:S(2)}, u32[]{:S(2)}) collective-permute-start(f32[264,128]{1,0:T(8,128)S(1)} %get-tuple-element.109), channel_id=1, source_target_pairs={{0,2},{2,0},{4,6},{6,4},{8,10},{10,8},{12,14},{14,12},{16,18},{18,... | collective-permute-start | bytes 405512 | tf_op jit(solution)/shard_map/ppermute | solution.py:530
  66.9 5.1 %gradients.1 = (bf16[128,2048]{1,0:T(8,128)(2,1)}, f32[128,2048]{1,0:T(8,128)S(1)}, f32[128,2048]{1,0:T(8,128)S(1)}) custom-call(f32[128,128]{1,0:T(8,128)S(1)} %copy-done.5, f32[16,128]{1,0:T(8,128)S(1)} %copy-done.6, bf16[128,2048]{1,0:T(8,128)(2,1)S(1)} %copy-done, bf16[128,2048]{1,0:T(8,128)(2,1)S(1)} %copy-done.1, bf16[128,2048]{1,0:T(8,128)(2,1)S(1)} %copy-done.2, ...), custom_call_target="tpu_custom_call" | custom-call | flops 872415232 | bytes 6291456 | tf_op jit(solution)/shard_map/gradients/pallas_call | solution.py:123
  72.3 1.5 %final.1 = (bf16[128,2048]{1,0:T(8,128)(2,1)}, bf16[128,2048]{1,0:T(8,128)(2,1)}, f32[1,2048]{1,0:T(1,128)}) custom-call(f32[128,128]{1,0:T(8,128)S(1)} %copy-done.5, f32[16,128]{1,0:T(8,128)S(1)} %copy-done.6, bf16[128,2048]{1,0:T(8,128)(2,1)S(1)} %copy-done.1, bf16[128,2048]{1,0:T(8,128)(2,1)S(1)} %copy-done.2, ...), custom_call_target="tpu_custom_call" | custom-call | flops 268435456 | bytes 6291456 | tf_op jit(solution)/shard_map/final/pallas_call | solution.py:123
  (69 shorter events, 3.1 us)
Async XLA Ops:
  0.6 6.8 %copy-start.1 = (bf16[128,2048]{1,0:T(8,128)(2,1)S(1)}, bf16[128,2048]{1,0:T(8,128)(2,1)}, u32[]{:S(2)}) copy-start(bf16[128,2048]{1,0:T(8,128)(2,1)} %key_ref.7) | copy-start | bytes 1572868
  0.6 6.7 %copy-start.2 = (bf16[128,2048]{1,0:T(8,128)(2,1)S(1)}, bf16[128,2048]{1,0:T(8,128)(2,1)}, u32[]{:S(2)}) copy-start(bf16[128,2048]{1,0:T(8,128)(2,1)} %value_ref.7) | copy-start | bytes 1572868
  2.8 4.6 %copy-start.6 = (f32[16,128]{1,0:T(8,128)S(1)}, f32[16,128]{1,0:T(8,128)}, u32[]{:S(2)}) copy-start(f32[16,128]{1,0:T(8,128)} %get-tuple-element.60.rates_ref) | copy-start | bytes 24580
  2.8 9.3 %collective-permute-start.7 = (f32[264,128]{1,0:T(8,128)}, f32[264,128]{1,0:T(8,128)S(1)}, u32[]{:S(2)}, u32[]{:S(2)}) collective-permute-start(f32[264,128]{1,0:T(8,128)} %get-tuple-element.70), channel_id=1, source_target_pairs={{0,2},{2,0},{4,6},{6,4},{8,10},{10,8},{12,14},{14,12},{16,18},{18,... | collective-permute-start | bytes 405512 | tf_op jit(solution)/shard_map/ppermute | solution.py:530
  5.8 8.7 %collective-permute-start.8 = (f32[264,128]{1,0:T(8,128)}, f32[264,128]{1,0:T(8,128)S(1)}, u32[]{:S(2)}, u32[]{:S(2)}) collective-permute-start(f32[264,128]{1,0:T(8,128)} %get-tuple-element.71), channel_id=1, source_target_pairs={{0,4},{2,6},{4,0},{6,2},{8,12},{10,14},{12,8},{14,10},{16,20},{18,... | collective-permute-start | bytes 405512 | tf_op jit(solution)/shard_map/ppermute | solution.py:530
  7.4 7.7 %collective-permute-start.9 = (f32[264,128]{1,0:T(8,128)}, f32[264,128]{1,0:T(8,128)S(1)}, u32[]{:S(2)}, u32[]{:S(2)}) collective-permute-start(f32[264,128]{1,0:T(8,128)} %get-tuple-element.72), channel_id=1, source_target_pairs={{0,6},{2,4},{4,2},{6,0},{8,14},{10,12},{12,10},{14,8},{16,22},{18,... | collective-permute-start | bytes 405512 | tf_op jit(solution)/shard_map/ppermute | solution.py:530
  7.4 0.8 %copy-start.4 = (f32[128,128]{1,0:T(8,128)S(1)}, f32[128,128]{1,0:T(8,128)}, u32[]{:S(2)}) copy-start(f32[128,128]{1,0:T(8,128)} %get-tuple-element.59.mark_ref) | copy-start | bytes 196612
  8.6 8.3 %collective-permute-start = (f32[264,128]{1,0:T(8,128)S(1)}, f32[264,128]{1,0:T(8,128)S(1)}, u32[]{:S(2)}, u32[]{:S(2)}) collective-permute-start(f32[264,128]{1,0:T(8,128)S(1)} %get-tuple-element.62), channel_id=1, source_target_pairs={{0,2},{2,0},{4,6},{6,4},{8,10},{10,8},{12,14},{14,12},{16,18},{18,... | collective-permute-start | bytes 405512 | tf_op jit(solution)/shard_map/ppermute | solution.py:530
  10.7 9.1 %collective-permute-start.1 = (f32[264,128]{1,0:T(8,128)S(1)}, f32[264,128]{1,0:T(8,128)S(1)}, u32[]{:S(2)}, u32[]{:S(2)}) collective-permute-start(f32[264,128]{1,0:T(8,128)S(1)} %get-tuple-element.63), channel_id=1, source_target_pairs={{0,4},{2,6},{4,0},{6,2},{8,12},{10,14},{12,8},{14,10},{16,20},{18,... | collective-permute-start | bytes 405512 | tf_op jit(solution)/shard_map/ppermute | solution.py:530
  12.2 7.6 %collective-permute-start.2 = (f32[264,128]{1,0:T(8,128)S(1)}, f32[264,128]{1,0:T(8,128)S(1)}, u32[]{:S(2)}, u32[]{:S(2)}) collective-permute-start(f32[264,128]{1,0:T(8,128)S(1)} %get-tuple-element.64), channel_id=1, source_target_pairs={{0,6},{2,4},{4,2},{6,0},{8,14},{10,12},{12,10},{14,8},{16,22},{18,... | collective-permute-start | bytes 405512 | tf_op jit(solution)/shard_map/ppermute | solution.py:530
  15.1 6.9 %collective-permute-start.10 = (f32[264,128]{1,0:T(8,128)S(1)}, f32[264,128]{1,0:T(8,128)S(1)}, u32[]{:S(2)}, u32[]{:S(2)}) collective-permute-start(f32[264,128]{1,0:T(8,128)S(1)} %total.5), channel_id=1, source_target_pairs={{0,8},{2,10},{4,12},{6,14},{8,16},{10,18},{12,20},{14,22},{16,24},... | collective-permute-start | bytes 405512 | tf_op jit(solution)/shard_map/ppermute | solution.py:545
  19.9 10.6 %copy-start = (bf16[128,2048]{1,0:T(8,128)(2,1)S(1)}, bf16[128,2048]{1,0:T(8,128)(2,1)}, u32[]{:S(2)}) copy-start(bf16[128,2048]{1,0:T(8,128)(2,1)} %query_ref.13) | copy-start | bytes 1572868
  19.9 6.9 %collective-permute-start.3 = (f32[264,128]{1,0:T(8,128)S(1)}, f32[264,128]{1,0:T(8,128)S(1)}, u32[]{:S(2)}, u32[]{:S(2)}) collective-permute-start(f32[264,128]{1,0:T(8,128)S(1)} %total.4), channel_id=1, source_target_pairs={{0,8},{2,10},{4,12},{6,14},{8,16},{10,18},{12,20},{14,22},{16,24},... | collective-permute-start | bytes 405512 | tf_op jit(solution)/shard_map/ppermute | solution.py:545
  22.2 11.1 %copy-start.11 = (f32[264,128]{1,0:T(8,128)}, f32[264,128]{1,0:T(8,128)S(1)}, u32[]{:S(2)}) copy-start(f32[264,128]{1,0:T(8,128)S(1)} %get-tuple-element.73.refs_0_.refs_8_) | copy-start | bytes 405508
  22.2 6.9 %collective-permute-start.11 = (f32[264,128]{1,0:T(8,128)S(1)}, f32[264,128]{1,0:T(8,128)S(1)}, u32[]{:S(2)}, u32[]{:S(2)}) collective-permute-start(f32[264,128]{1,0:T(8,128)S(1)} %get-tuple-element.74), channel_id=1, source_target_pairs={{0,2},{2,0},{4,6},{6,4},{8,10},{10,8},{12,14},{14,12},{16,18},{18,... | collective-permute-start | bytes 405512 | tf_op jit(solution)/shard_map/ppermute | solution.py:530
  23.6 9.6 %collective-permute-start.12 = (f32[264,128]{1,0:T(8,128)S(1)}, f32[264,128]{1,0:T(8,128)S(1)}, u32[]{:S(2)}, u32[]{:S(2)}) collective-permute-start(f32[264,128]{1,0:T(8,128)S(1)} %get-tuple-element.75), channel_id=1, source_target_pairs={{0,4},{2,6},{4,0},{6,2},{8,12},{10,14},{12,8},{14,10},{16,20},{18,... | collective-permute-start | bytes 405512 | tf_op jit(solution)/shard_map/ppermute | solution.py:530
  24.7 5.8 %copy-start.5 = (f32[128,128]{1,0:T(8,128)S(1)}, f32[128,128]{1,0:T(8,128)}, u32[]{:S(2)}) copy-start(f32[128,128]{1,0:T(8,128)} %get-tuple-element.59.mark_ref) | copy-start | bytes 196612
  24.7 8.5 %collective-permute-start.13 = (f32[264,128]{1,0:T(8,128)S(1)}, f32[264,128]{1,0:T(8,128)S(1)}, u32[]{:S(2)}, u32[]{:S(2)}) collective-permute-start(f32[264,128]{1,0:T(8,128)S(1)} %get-tuple-element.76), channel_id=1, source_target_pairs={{0,6},{2,4},{4,2},{6,0},{8,14},{10,12},{12,10},{14,8},{16,22},{18,... | collective-permute-start | bytes 405512 | tf_op jit(solution)/shard_map/ppermute | solution.py:530
  26.9 7.0 %collective-permute-start.4 = (f32[264,128]{1,0:T(8,128)S(1)}, f32[264,128]{1,0:T(8,128)S(1)}, u32[]{:S(2)}, u32[]{:S(2)}) collective-permute-start(f32[264,128]{1,0:T(8,128)S(1)} %get-tuple-element.66), channel_id=1, source_target_pairs={{0,2},{2,0},{4,6},{6,4},{8,10},{10,8},{12,14},{14,12},{16,18},{18,... | collective-permute-start | bytes 405512 | tf_op jit(solution)/shard_map/ppermute | solution.py:530
  28.2 6.7 %collective-permute-start.5 = (f32[264,128]{1,0:T(8,128)S(1)}, f32[264,128]{1,0:T(8,128)S(1)}, u32[]{:S(2)}, u32[]{:S(2)}) collective-permute-start(f32[264,128]{1,0:T(8,128)S(1)} %get-tuple-element.67), channel_id=1, source_target_pairs={{0,4},{2,6},{4,0},{6,2},{8,12},{10,14},{12,8},{14,10},{16,20},{18,... | collective-permute-start | bytes 405512 | tf_op jit(solution)/shard_map/ppermute | solution.py:530
  29.1 4.2 %copy-start.13 = (f32[264,128]{1,0:T(8,128)}, f32[264,128]{1,0:T(8,128)S(1)}, u32[]{:S(2)}) copy-start(f32[264,128]{1,0:T(8,128)S(1)} %collective-permute-done.11.refs_1_.refs_9_) | copy-start | bytes 405508
  29.1 4.2 %copy-start.3 = (bf16[128,2048]{1,0:T(8,128)(2,1)S(1)}, bf16[128,2048]{1,0:T(8,128)(2,1)}, u32[]{:S(2)}) copy-start(bf16[128,2048]{1,0:T(8,128)(2,1)} %grad_ref.9) | copy-start | bytes 1572868
  29.1 7.3 %collective-permute-start.6 = (f32[264,128]{1,0:T(8,128)S(1)}, f32[264,128]{1,0:T(8,128)S(1)}, u32[]{:S(2)}, u32[]{:S(2)}) collective-permute-start(f32[264,128]{1,0:T(8,128)S(1)} %get-tuple-element.68), channel_id=1, source_target_pairs={{0,6},{2,4},{4,2},{6,0},{8,14},{10,12},{12,10},{14,8},{16,22},{18,... | collective-permute-start | bytes 405512 | tf_op jit(solution)/shard_map/ppermute | solution.py:530
  30.5 2.7 %copy-start.19 = (f32[2048]{0:T(1024)S(1)}, f32[2048]{0:T(1024)}, u32[]{:S(2)}) copy-start(f32[2048]{0:T(1024)} %param.12) | copy-start | bytes 24580
  33.2 0.7 copy-start.15
  33.2 0.7 copy-start.17
  34.9 1.9 %copy-start.7 = (f32[264,128]{1,0:T(8,128)}, f32[264,128]{1,0:T(8,128)S(1)}, u32[]{:S(2)}) copy-start(f32[264,128]{1,0:T(8,128)S(1)} %collective-permute-done.5.refs_2_.refs_14_) | copy-start | bytes 405508
  40.0 6.7 %collective-permute-start.14 = (f32[264,128]{1,0:T(8,128)S(1)}, f32[264,128]{1,0:T(8,128)S(1)}, u32[]{:S(2)}, u32[]{:S(2)}) collective-permute-start(f32[264,128]{1,0:T(8,128)S(1)} %get-tuple-element.94), channel_id=1, source_target_pairs={{0,2},{2,0},{4,6},{6,4},{8,10},{10,8},{12,14},{14,12},{16,18},{18,... | collective-permute-start | bytes 405512 | tf_op jit(solution)/shard_map/ppermute | solution.py:530
  41.4 8.5 %collective-permute-start.15 = (f32[264,128]{1,0:T(8,128)S(1)}, f32[264,128]{1,0:T(8,128)S(1)}, u32[]{:S(2)}, u32[]{:S(2)}) collective-permute-start(f32[264,128]{1,0:T(8,128)S(1)} %get-tuple-element.95), channel_id=1, source_target_pairs={{0,4},{2,6},{4,0},{6,2},{8,12},{10,14},{12,8},{14,10},{16,20},{18,... | collective-permute-start | bytes 405512 | tf_op jit(solution)/shard_map/ppermute | solution.py:530
  42.7 7.4 %collective-permute-start.16 = (f32[264,128]{1,0:T(8,128)S(1)}, f32[264,128]{1,0:T(8,128)S(1)}, u32[]{:S(2)}, u32[]{:S(2)}) collective-permute-start(f32[264,128]{1,0:T(8,128)S(1)} %get-tuple-element.96), channel_id=1, source_target_pairs={{0,6},{2,4},{4,2},{6,0},{8,14},{10,12},{12,10},{14,8},{16,22},{18,... | collective-permute-start | bytes 405512 | tf_op jit(solution)/shard_map/ppermute | solution.py:530
  44.0 9.0 %collective-permute-start.21 = (f32[264,128]{1,0:T(8,128)S(1)}, f32[264,128]{1,0:T(8,128)S(1)}, u32[]{:S(2)}, u32[]{:S(2)}) collective-permute-start(f32[264,128]{1,0:T(8,128)S(1)} %get-tuple-element.103), channel_id=1, source_target_pairs={{0,2},{2,0},{4,6},{6,4},{8,10},{10,8},{12,14},{14,12},{16,18},{18,... | collective-permute-start | bytes 405512 | tf_op jit(solution)/shard_map/ppermute | solution.py:530
  45.4 10.0 %collective-permute-start.22 = (f32[264,128]{1,0:T(8,128)S(1)}, f32[264,128]{1,0:T(8,128)S(1)}, u32[]{:S(2)}, u32[]{:S(2)}) collective-permute-start(f32[264,128]{1,0:T(8,128)S(1)} %get-tuple-element.104), channel_id=1, source_target_pairs={{0,4},{2,6},{4,0},{6,2},{8,12},{10,14},{12,8},{14,10},{16,20},{18,... | collective-permute-start | bytes 405512 | tf_op jit(solution)/shard_map/ppermute | solution.py:530
  46.8 8.7 %collective-permute-start.23 = (f32[264,128]{1,0:T(8,128)S(1)}, f32[264,128]{1,0:T(8,128)S(1)}, u32[]{:S(2)}, u32[]{:S(2)}) collective-permute-start(f32[264,128]{1,0:T(8,128)S(1)} %get-tuple-element.105), channel_id=1, source_target_pairs={{0,6},{2,4},{4,2},{6,0},{8,14},{10,12},{12,10},{14,8},{16,22},{18,... | collective-permute-start | bytes 405512 | tf_op jit(solution)/shard_map/ppermute | solution.py:530
  50.2 9.0 %collective-permute-start.17 = (f32[264,128]{1,0:T(8,128)S(1)}, f32[264,128]{1,0:T(8,128)S(1)}, u32[]{:S(2)}, u32[]{:S(2)}) collective-permute-start(f32[264,128]{1,0:T(8,128)S(1)} %get-tuple-element.97), channel_id=1, source_target_pairs={{0,24},{2,26},{4,28},{6,30},{8,0},{10,2},{12,4},{14,6},{16,8},{18,... | collective-permute-start | bytes 405512 | tf_op jit(solution)/shard_map/ppermute | solution.py:545
  52.3 4.5 %collective-permute-start.24 = (f32[8,128]{1,0:T(8,128)S(1)}, f32[8,128]{1,0:T(8,128)S(1)}, u32[]{:S(2)}, u32[]{:S(2)}) collective-permute-start(f32[8,128]{1,0:T(8,128)S(1)} %get-tuple-element.106.refs_4_), channel_id=1, source_target_pairs={{0,16},{2,18},{4,20},{6,22},{8,24},{10,26},{12,28},{14,30},{16,0},... | collective-permute-start | bytes 12296 | tf_op jit(solution)/shard_map/ppermute | solution.py:545
  56.8 6.3 %collective-permute-start.25 = (f32[264,128]{1,0:T(8,128)S(1)}, f32[264,128]{1,0:T(8,128)S(1)}, u32[]{:S(2)}, u32[]{:S(2)}) collective-permute-start(f32[264,128]{1,0:T(8,128)S(1)} %total.7.refs_5_), channel_id=1, source_target_pairs={{0,24},{2,26},{4,28},{6,30},{8,0},{10,2},{12,4},{14,6},{16,8},{18,... | collective-permute-start | bytes 405512 | tf_op jit(solution)/shard_map/ppermute | solution.py:545
  59.5 6.3 %collective-permute-start.18 = (f32[264,128]{1,0:T(8,128)S(1)}, f32[264,128]{1,0:T(8,128)S(1)}, u32[]{:S(2)}, u32[]{:S(2)}) collective-permute-start(f32[264,128]{1,0:T(8,128)S(1)} %get-tuple-element.99), channel_id=1, source_target_pairs={{0,2},{2,0},{4,6},{6,4},{8,10},{10,8},{12,14},{14,12},{16,18},{18,... | collective-permute-start | bytes 405512 | tf_op jit(solution)/shard_map/ppermute | solution.py:530
  60.4 11.7 %collective-permute-start.19 = (f32[264,128]{1,0:T(8,128)S(1)}, f32[264,128]{1,0:T(8,128)S(1)}, u32[]{:S(2)}, u32[]{:S(2)}) collective-permute-start(f32[264,128]{1,0:T(8,128)S(1)} %get-tuple-element.100), channel_id=1, source_target_pairs={{0,4},{2,6},{4,0},{6,2},{8,12},{10,14},{12,8},{14,10},{16,20},{18,... | collective-permute-start | bytes 405512 | tf_op jit(solution)/shard_map/ppermute | solution.py:530
  61.7 5.2 %copy-start.8 = (f32[264,128]{1,0:T(8,128)S(1)}, f32[264,128]{1,0:T(8,128)}, u32[]{:S(2)}) copy-start(f32[264,128]{1,0:T(8,128)} %copy-done.7) | copy-start | bytes 405508
  61.7 5.2 %copy-start.10 = (f32[264,128]{1,0:T(8,128)S(1)}, f32[264,128]{1,0:T(8,128)}, u32[]{:S(2)}) copy-start(f32[264,128]{1,0:T(8,128)} %copy-done.9) | copy-start | bytes 405508
  61.7 5.2 %copy-start.12 = (f32[264,128]{1,0:T(8,128)S(1)}, f32[264,128]{1,0:T(8,128)}, u32[]{:S(2)}) copy-start(f32[264,128]{1,0:T(8,128)} %copy-done.11) | copy-start | bytes 405508
  61.7 5.2 %copy-start.14 = (f32[264,128]{1,0:T(8,128)S(1)}, f32[264,128]{1,0:T(8,128)}, u32[]{:S(2)}) copy-start(f32[264,128]{1,0:T(8,128)} %copy-done.13) | copy-start | bytes 405508
  61.7 5.2 %copy-start.16 = (f32[264,128]{1,0:T(8,128)S(1)}, f32[264,128]{1,0:T(8,128)}, u32[]{:S(2)}) copy-start(f32[264,128]{1,0:T(8,128)} %copy-done.15) | copy-start | bytes 405508
  61.7 5.2 %copy-start.18 = (f32[264,128]{1,0:T(8,128)S(1)}, f32[264,128]{1,0:T(8,128)}, u32[]{:S(2)}) copy-start(f32[264,128]{1,0:T(8,128)} %copy-done.17) | copy-start | bytes 405508
  61.7 10.4 %collective-permute-start.20 = (f32[264,128]{1,0:T(8,128)S(1)}, f32[264,128]{1,0:T(8,128)S(1)}, u32[]{:S(2)}, u32[]{:S(2)}) collective-permute-start(f32[264,128]{1,0:T(8,128)S(1)} %get-tuple-element.101), channel_id=1, source_target_pairs={{0,6},{2,4},{4,2},{6,0},{8,14},{10,12},{12,10},{14,8},{16,22},{18,... | collective-permute-start | bytes 405512 | tf_op jit(solution)/shard_map/ppermute | solution.py:530
  63.3 8.8 %collective-permute-start.26 = (f32[264,128]{1,0:T(8,128)S(1)}, f32[264,128]{1,0:T(8,128)S(1)}, u32[]{:S(2)}, u32[]{:S(2)}) collective-permute-start(f32[264,128]{1,0:T(8,128)S(1)} %get-tuple-element.107), channel_id=1, source_target_pairs={{0,6},{2,4},{4,2},{6,0},{8,14},{10,12},{12,10},{14,8},{16,22},{18,... | collective-permute-start | bytes 405512 | tf_op jit(solution)/shard_map/ppermute | solution.py:530
  64.9 7.3 %collective-permute-start.27 = (f32[264,128]{1,0:T(8,128)S(1)}, f32[264,128]{1,0:T(8,128)S(1)}, u32[]{:S(2)}, u32[]{:S(2)}) collective-permute-start(f32[264,128]{1,0:T(8,128)S(1)} %get-tuple-element.108), channel_id=1, source_target_pairs={{0,4},{2,6},{4,0},{6,2},{8,12},{10,14},{12,8},{14,10},{16,20},{18,... | collective-permute-start | bytes 405512 | tf_op jit(solution)/shard_map/ppermute | solution.py:530
  65.8 6.5 %collective-permute-start.28 = (f32[264,128]{1,0:T(8,128)S(1)}, f32[264,128]{1,0:T(8,128)S(1)}, u32[]{:S(2)}, u32[]{:S(2)}) collective-permute-start(f32[264,128]{1,0:T(8,128)S(1)} %get-tuple-element.109), channel_id=1, source_target_pairs={{0,2},{2,0},{4,6},{6,4},{8,10},{10,8},{12,14},{14,12},{16,18},{18,... | collective-permute-start | bytes 405512 | tf_op jit(solution)/shard_map/ppermute | solution.py:530
  (1 other events, 0.7 us)

commit v7 on v6

--- a/solution.py
+++ b/solution.py
@@ -365,13 +365,14 @@
 def output_grad_states(size, pieces, norm, mark, rates, queries, out_grad, gain, sums, attended):
     n = len(pieces)
 
-    def body(mark_ref, rates_ref, query_ref, grad_ref, gain_ref, sums_ref, att_ref, *outs):
+    def body(mark_ref, rates_ref, query_ref, grad_ref, gain_ref, att_ref, *refs):
+        sums_refs, outs = refs[: len(sums)], refs[len(sums) :]
         group = partners()
         mark = mark_ref[...]
         last, first = mark[size.rows - 1 :, :], mark[:1, :]
         wide = (size.dim, size.rows)
-        square = jnp.broadcast_to(sums_ref[0:1, :], wide).T
-        cross = jnp.broadcast_to(sums_ref[1:2, :], wide).T
+        square = jnp.broadcast_to(sum(ref[0:1, :] for ref in sums_refs), wide).T
+        cross = jnp.broadcast_to(sum(ref[1:2, :] for ref in sums_refs), wide).T
         inv = lax.rsqrt(square / norm + 1e-06)
         pull = inv * inv * inv * cross / norm
         gone = steps_if(mark == first, position(size))
@@ -396,7 +397,7 @@
 
     part = jax.ShapeDtypeStruct((size.rows, size.state), f32)
     outs = call(
-        body, "back", (mark, rates, queries, out_grad, gain, sums, attended),
+        body, "back", (mark, rates, queries, out_grad, gain, attended, *sums),
         [part, size.payload] * n,
         n * size.each * 4 * size.rows * size.dim * size.dim, n * size.state * size.rows * 16,
     )
@@ -599,7 +600,10 @@
         states = entering[w * GROUP : (w + 1) * GROUP]
         outs = whole_attended(size, w, *common, queries, out_grad, gain, near, states, outs)
     attended, sums = outs
-    sums = lax.psum(sums, "head")
+    if lax.axis_size("head") == 2:
+        sums = (sums, lax.ppermute(sums, "head", [(0, 1), (1, 0)]))
+    else:
+        sums = (lax.psum(sums, "head"),)
     back, states = {}, {}
     for pieces in [*sent, kept]:
         backs, payloads = output_grad_states(

time: 74.2 us -> 72.5 us (0.977)
  blocking collectives: 2.44 us -> 0 us
  waiting for transfers between devices: 13.4 us -> 14.9 us
    psum x1 -> x0, blocking collectives: 2.44 us -> none  [local(): sums = lax.psum(sums, 'head')]
    ppermute x0 -> x1, waiting for transfers between devices: none -> 1.15 us  [local(): sums = (sums, lax.ppermute(sums, 'head', [(0, 1), (1, 0)]))]
  transfers between devices with their start and end apart: 29 -> 30, of which waited for: 14 -> 16; matrix products, arithmetic and copies ran while one was open for 0% -> 0% of each run, Pallas kernels for 14% -> 14%
where the time goes in v7:
time: 72.5 us; the launch traced here: 72.3 us
  starting transfers between devices  40.4 us (56%)
  Pallas kernels  15.1 us (21%)
  waiting for transfers between devices  14.9 us (21%)
  between operations  1.02 us (1%)
  local copies, waits for them, and re-layouts  0.87 us (1%)
    ppermute x24, starting transfers between devices, swap(): lax.ppermute(array, 'seq', [(i, i ^ distance) for i in range(members)])  31.8 us
    pallas_call x18, Pallas kernels, call(): pl.pallas_call(body, out_shape=outputs, in_specs=in_specs if in_specs is...  15.1 us
    ppermute x24, waiting for transfers between devices, swap(): lax.ppermute(array, 'seq', [(i, i ^ distance) for i in range(members)])  11.4 us
    ppermute x5, starting transfers between devices, cyclic(): lax.ppermute(array, 'seq', [(i, (i + by) % members) for i in range(member...  8.5 us
    ppermute x5, waiting for transfers between devices, cyclic(): lax.ppermute(array, 'seq', [(i, (i + by) % members) for i in range(member...  2.43 us
  transfers between devices with their start and end apart: 30, of which 16 were waited for; matrix products, arithmetic and copies ran while one was open for 0% of the time, Pallas kernels for 14%

profile of v7, /device:TPU:0, one launch (start us, length us, event | category | flops | bytes accessed | tf_op | source)
XLA Modules:
  0.0 72.3 jit_solution(11625183969466504927)
XLA Ops:
  0.7 2.2 %states.2 = (f32[264,128]{1,0:T(8,128)}, f32[264,128]{1,0:T(8,128)}, f32[264,128]{1,0:T(8,128)}, f32[128,128]{1,0:T(8,128)}, f32[16,128]{1,0:T(8,128)}) custom-call(s32[1,128]{1,0:T(1,128)} %bitcast.9, f32[1,16]{1,0:T(1,128)} %bitcast.10, bf16[128,2048]{1,0:T(8,128)(2,1)} %key_ref.7, bf16[128,2048]{1,0:T(8,128)(2,1)} %value_ref.7), custom_call_target="tpu_custom_call" | custom-call | flops 50331648 | bytes 786432 | tf_op jit(solution)/shard_map/states/pallas_call | solution.py:123
  2.8 3.0 %collective-permute-start.7 = (f32[264,128]{1,0:T(8,128)}, f32[264,128]{1,0:T(8,128)S(1)}, u32[]{:S(2)}, u32[]{:S(2)}) collective-permute-start(f32[264,128]{1,0:T(8,128)} %get-tuple-element.70), channel_id=1, source_target_pairs={{0,2},{2,0},{4,6},{6,4},{8,10},{10,8},{12,14},{14,12},{16,18},{18,... | collective-permute-start | bytes 405512 | tf_op jit(solution)/shard_map/ppermute | solution.py:531
  5.8 1.5 %collective-permute-start.8 = (f32[264,128]{1,0:T(8,128)}, f32[264,128]{1,0:T(8,128)S(1)}, u32[]{:S(2)}, u32[]{:S(2)}) collective-permute-start(f32[264,128]{1,0:T(8,128)} %get-tuple-element.71), channel_id=1, source_target_pairs={{0,4},{2,6},{4,0},{6,2},{8,12},{10,14},{12,8},{14,10},{16,20},{18,... | collective-permute-start | bytes 405512 | tf_op jit(solution)/shard_map/ppermute | solution.py:531
  7.4 0.8 %copy-done.4 = f32[128,128]{1,0:T(8,128)S(1)} copy-done((f32[128,128]{1,0:T(8,128)S(1)}, f32[128,128]{1,0:T(8,128)}, u32[]{:S(2)}) %copy-start.4) | copy-done | bytes 65560
  8.6 2.0 %collective-permute-start = (f32[264,128]{1,0:T(8,128)S(1)}, f32[264,128]{1,0:T(8,128)S(1)}, u32[]{:S(2)}, u32[]{:S(2)}) collective-permute-start(f32[264,128]{1,0:T(8,128)S(1)} %get-tuple-element.62), channel_id=1, source_target_pairs={{0,2},{2,0},{4,6},{6,4},{8,10},{10,8},{12,14},{14,12},{16,18},{18,... | collective-permute-start | bytes 405512 | tf_op jit(solution)/shard_map/ppermute | solution.py:531
  10.7 1.5 %collective-permute-start.1 = (f32[264,128]{1,0:T(8,128)S(1)}, f32[264,128]{1,0:T(8,128)S(1)}, u32[]{:S(2)}, u32[]{:S(2)}) collective-permute-start(f32[264,128]{1,0:T(8,128)S(1)} %get-tuple-element.63), channel_id=1, source_target_pairs={{0,4},{2,6},{4,0},{6,2},{8,12},{10,14},{12,8},{14,10},{16,20},{18,... | collective-permute-start | bytes 405512 | tf_op jit(solution)/shard_map/ppermute | solution.py:531
  12.2 1.3 %collective-permute-start.2 = (f32[264,128]{1,0:T(8,128)S(1)}, f32[264,128]{1,0:T(8,128)S(1)}, u32[]{:S(2)}, u32[]{:S(2)}) collective-permute-start(f32[264,128]{1,0:T(8,128)S(1)} %get-tuple-element.64), channel_id=1, source_target_pairs={{0,6},{2,4},{4,2},{6,0},{8,14},{10,12},{12,10},{14,8},{16,22},{18,... | collective-permute-start | bytes 405512 | tf_op jit(solution)/shard_map/ppermute | solution.py:531
  13.5 1.1 %collective-permute-done.8.refs_2_ = f32[264,128]{1,0:T(8,128)S(1)} collective-permute-done((f32[264,128]{1,0:T(8,128)}, f32[264,128]{1,0:T(8,128)S(1)}, u32[]{:S(2)}, u32[]{:S(2)}) %collective-permute-start.8) | collective-permute-done | bytes 135200 | tf_op jit(solution)/shard_map/ppermute | solution.py:531
  14.6 0.5 collective-permute-done.9.refs_3_
  15.1 1.6 %collective-permute-start.10 = (f32[264,128]{1,0:T(8,128)S(1)}, f32[264,128]{1,0:T(8,128)S(1)}, u32[]{:S(2)}, u32[]{:S(2)}) collective-permute-start(f32[264,128]{1,0:T(8,128)S(1)} %total.5), channel_id=1, source_target_pairs={{0,8},{2,10},{4,12},{6,14},{8,16},{10,18},{12,20},{14,22},{16,24},... | collective-permute-start | bytes 405512 | tf_op jit(solution)/shard_map/ppermute | solution.py:546
  16.9 2.9 %collective-permute-done.1.refs_2_ = f32[264,128]{1,0:T(8,128)S(1)} collective-permute-done((f32[264,128]{1,0:T(8,128)S(1)}, f32[264,128]{1,0:T(8,128)S(1)}, u32[]{:S(2)}, u32[]{:S(2)}) %collective-permute-start.1) | collective-permute-done | bytes 135200 | tf_op jit(solution)/shard_map/ppermute | solution.py:531
  19.9 1.6 %collective-permute-start.3 = (f32[264,128]{1,0:T(8,128)S(1)}, f32[264,128]{1,0:T(8,128)S(1)}, u32[]{:S(2)}, u32[]{:S(2)}) collective-permute-start(f32[264,128]{1,0:T(8,128)S(1)} %total.4), channel_id=1, source_target_pairs={{0,8},{2,10},{4,12},{6,14},{8,16},{10,18},{12,20},{14,22},{16,24},... | collective-permute-start | bytes 405512 | tf_op jit(solution)/shard_map/ppermute | solution.py:546
  21.5 0.5 collective-permute-done.10.refs_4_
  22.2 1.4 %collective-permute-start.11 = (f32[264,128]{1,0:T(8,128)S(1)}, f32[264,128]{1,0:T(8,128)S(1)}, u32[]{:S(2)}, u32[]{:S(2)}) collective-permute-start(f32[264,128]{1,0:T(8,128)S(1)} %get-tuple-element.74), channel_id=1, source_target_pairs={{0,2},{2,0},{4,6},{6,4},{8,10},{10,8},{12,14},{14,12},{16,18},{18,... | collective-permute-start | bytes 405512 | tf_op jit(solution)/shard_map/ppermute | solution.py:531
  23.6 1.2 %collective-permute-start.12 = (f32[264,128]{1,0:T(8,128)S(1)}, f32[264,128]{1,0:T(8,128)S(1)}, u32[]{:S(2)}, u32[]{:S(2)}) collective-permute-start(f32[264,128]{1,0:T(8,128)S(1)} %get-tuple-element.75), channel_id=1, source_target_pairs={{0,4},{2,6},{4,0},{6,2},{8,12},{10,14},{12,8},{14,10},{16,20},{18,... | collective-permute-start | bytes 405512 | tf_op jit(solution)/shard_map/ppermute | solution.py:531
  24.7 1.4 %collective-permute-start.13 = (f32[264,128]{1,0:T(8,128)S(1)}, f32[264,128]{1,0:T(8,128)S(1)}, u32[]{:S(2)}, u32[]{:S(2)}) collective-permute-start(f32[264,128]{1,0:T(8,128)S(1)} %get-tuple-element.76), channel_id=1, source_target_pairs={{0,6},{2,4},{4,2},{6,0},{8,14},{10,12},{12,10},{14,8},{16,22},{18,... | collective-permute-start | bytes 405512 | tf_op jit(solution)/shard_map/ppermute | solution.py:531
  26.1 0.6 collective-permute-done.3.refs_4_
  26.9 1.3 %collective-permute-start.4 = (f32[264,128]{1,0:T(8,128)S(1)}, f32[264,128]{1,0:T(8,128)S(1)}, u32[]{:S(2)}, u32[]{:S(2)}) collective-permute-start(f32[264,128]{1,0:T(8,128)S(1)} %get-tuple-element.66), channel_id=1, source_target_pairs={{0,2},{2,0},{4,6},{6,4},{8,10},{10,8},{12,14},{14,12},{16,18},{18,... | collective-permute-start | bytes 405512 | tf_op jit(solution)/shard_map/ppermute | solution.py:531
  28.2 0.8 %collective-permute-start.5 = (f32[264,128]{1,0:T(8,128)S(1)}, f32[264,128]{1,0:T(8,128)S(1)}, u32[]{:S(2)}, u32[]{:S(2)}) collective-permute-start(f32[264,128]{1,0:T(8,128)S(1)} %get-tuple-element.67), channel_id=1, source_target_pairs={{0,4},{2,6},{4,0},{6,2},{8,12},{10,14},{12,8},{14,10},{16,20},{18,... | collective-permute-start | bytes 405512 | tf_op jit(solution)/shard_map/ppermute | solution.py:531
  29.0 1.4 %collective-permute-start.6 = (f32[264,128]{1,0:T(8,128)S(1)}, f32[264,128]{1,0:T(8,128)S(1)}, u32[]{:S(2)}, u32[]{:S(2)}) collective-permute-start(f32[264,128]{1,0:T(8,128)S(1)} %get-tuple-element.68), channel_id=1, source_target_pairs={{0,6},{2,4},{4,2},{6,0},{8,14},{10,12},{12,10},{14,8},{16,22},{18,... | collective-permute-start | bytes 405512 | tf_op jit(solution)/shard_map/ppermute | solution.py:531
  30.5 2.7 %nearby.1.near_ref = f32[128,2048]{1,0:T(8,128)S(1)} custom-call(f32[128,128]{1,0:T(8,128)S(1)} %copy-done.5, f32[16,128]{1,0:T(8,128)S(1)} %copy-done.6, bf16[128,2048]{1,0:T(8,128)(2,1)S(1)} %copy-done, bf16[128,2048]{1,0:T(8,128)(2,1)S(1)} %copy-done.1, bf16[128,2048]{1,0:T(8,128)(2,1)S(1)} %copy-done.2), custom_call_target="tpu_custom_call" | custom-call | flops 201326592 | bytes 2621440 | tf_op jit(solution)/shard_map/nearby/pallas_call | solution.py:123
  33.9 1.0 %collective-permute-done.5.refs_2_.refs_14_ = f32[264,128]{1,0:T(8,128)S(1)} collective-permute-done((f32[264,128]{1,0:T(8,128)S(1)}, f32[264,128]{1,0:T(8,128)S(1)}, u32[]{:S(2)}, u32[]{:S(2)}) %collective-permute-start.5) | collective-permute-done | bytes 135200 | tf_op jit(solution)/shard_map/ppermute | solution.py:531
  34.9 1.4 %collective-permute-done.6.refs_3_.refs_15_ = f32[264,128]{1,0:T(8,128)S(1)} collective-permute-done((f32[264,128]{1,0:T(8,128)S(1)}, f32[264,128]{1,0:T(8,128)S(1)}, u32[]{:S(2)}, u32[]{:S(2)}) %collective-permute-start.6) | collective-permute-done | bytes 135200 | tf_op jit(solution)/shard_map/ppermute | solution.py:531
  36.3 0.5 attended.3
  36.9 1.2 %collective-permute-done.14.refs_1_ = f32[8,128]{1,0:T(8,128)S(1)} collective-permute-done((f32[8,128]{1,0:T(8,128)S(1)}, f32[8,128]{1,0:T(8,128)S(1)}, u32[]{:S(2)}, u32[]{:S(2)}) %collective-permute-start.14) | collective-permute-done | bytes 4128 | tf_op jit(solution)/shard_map/ppermute | solution.py:604
  38.0 0.6 back.4
  38.6 1.3 %collective-permute-start.15 = (f32[264,128]{1,0:T(8,128)S(1)}, f32[264,128]{1,0:T(8,128)S(1)}, u32[]{:S(2)}, u32[]{:S(2)}) collective-permute-start(f32[264,128]{1,0:T(8,128)S(1)} %get-tuple-element.94), channel_id=1, source_target_pairs={{0,2},{2,0},{4,6},{6,4},{8,10},{10,8},{12,14},{14,12},{16,18},{18,... | collective-permute-start | bytes 405512 | tf_op jit(solution)/shard_map/ppermute | solution.py:531
  39.9 1.3 %collective-permute-start.16 = (f32[264,128]{1,0:T(8,128)S(1)}, f32[264,128]{1,0:T(8,128)S(1)}, u32[]{:S(2)}, u32[]{:S(2)}) collective-permute-start(f32[264,128]{1,0:T(8,128)S(1)} %get-tuple-element.95), channel_id=1, source_target_pairs={{0,4},{2,6},{4,0},{6,2},{8,12},{10,14},{12,8},{14,10},{16,20},{18,... | collective-permute-start | bytes 405512 | tf_op jit(solution)/shard_map/ppermute | solution.py:531
  41.3 0.9 %collective-permute-start.17 = (f32[264,128]{1,0:T(8,128)S(1)}, f32[264,128]{1,0:T(8,128)S(1)}, u32[]{:S(2)}, u32[]{:S(2)}) collective-permute-start(f32[264,128]{1,0:T(8,128)S(1)} %get-tuple-element.96), channel_id=1, source_target_pairs={{0,6},{2,4},{4,2},{6,0},{8,14},{10,12},{12,10},{14,8},{16,22},{18,... | collective-permute-start | bytes 405512 | tf_op jit(solution)/shard_map/ppermute | solution.py:531
  42.2 0.5 back.5
  42.6 1.3 %collective-permute-start.22 = (f32[264,128]{1,0:T(8,128)S(1)}, f32[264,128]{1,0:T(8,128)S(1)}, u32[]{:S(2)}, u32[]{:S(2)}) collective-permute-start(f32[264,128]{1,0:T(8,128)S(1)} %get-tuple-element.103), channel_id=1, source_target_pairs={{0,2},{2,0},{4,6},{6,4},{8,10},{10,8},{12,14},{14,12},{16,18},{18,... | collective-permute-start | bytes 405512 | tf_op jit(solution)/shard_map/ppermute | solution.py:531
  43.9 1.3 %collective-permute-start.23 = (f32[264,128]{1,0:T(8,128)S(1)}, f32[264,128]{1,0:T(8,128)S(1)}, u32[]{:S(2)}, u32[]{:S(2)}) collective-permute-start(f32[264,128]{1,0:T(8,128)S(1)} %get-tuple-element.104), channel_id=1, source_target_pairs={{0,4},{2,6},{4,0},{6,2},{8,12},{10,14},{12,8},{14,10},{16,20},{18,... | collective-permute-start | bytes 405512 | tf_op jit(solution)/shard_map/ppermute | solution.py:531
  45.3 1.8 %collective-permute-start.24 = (f32[264,128]{1,0:T(8,128)S(1)}, f32[264,128]{1,0:T(8,128)S(1)}, u32[]{:S(2)}, u32[]{:S(2)}) collective-permute-start(f32[264,128]{1,0:T(8,128)S(1)} %get-tuple-element.105), channel_id=1, source_target_pairs={{0,6},{2,4},{4,2},{6,0},{8,14},{10,12},{12,10},{14,8},{16,22},{18,... | collective-permute-start | bytes 405512 | tf_op jit(solution)/shard_map/ppermute | solution.py:531
  47.1 0.4 back.3
  47.5 0.9 %collective-permute-done.16.refs_2_ = f32[264,128]{1,0:T(8,128)S(1)} collective-permute-done((f32[264,128]{1,0:T(8,128)S(1)}, f32[264,128]{1,0:T(8,128)S(1)}, u32[]{:S(2)}, u32[]{:S(2)}) %collective-permute-start.16) | collective-permute-done | bytes 135200 | tf_op jit(solution)/shard_map/ppermute | solution.py:531
  48.8 2.0 %collective-permute-start.18 = (f32[264,128]{1,0:T(8,128)S(1)}, f32[264,128]{1,0:T(8,128)S(1)}, u32[]{:S(2)}, u32[]{:S(2)}) collective-permute-start(f32[264,128]{1,0:T(8,128)S(1)} %get-tuple-element.97), channel_id=1, source_target_pairs={{0,24},{2,26},{4,28},{6,30},{8,0},{10,2},{12,4},{14,6},{16,8},{18,... | collective-permute-start | bytes 405512 | tf_op jit(solution)/shard_map/ppermute | solution.py:546
  50.8 0.8 %collective-permute-start.25 = (f32[8,128]{1,0:T(8,128)S(1)}, f32[8,128]{1,0:T(8,128)S(1)}, u32[]{:S(2)}, u32[]{:S(2)}) collective-permute-start(f32[8,128]{1,0:T(8,128)S(1)} %get-tuple-element.106.refs_4_), channel_id=1, source_target_pairs={{0,16},{2,18},{4,20},{6,22},{8,24},{10,26},{12,28},{14,30},{16,0},... | collective-permute-start | bytes 12296 | tf_op jit(solution)/shard_map/ppermute | solution.py:546
  51.6 2.4 %collective-permute-done.23.refs_2_ = f32[264,128]{1,0:T(8,128)S(1)} collective-permute-done((f32[264,128]{1,0:T(8,128)S(1)}, f32[264,128]{1,0:T(8,128)S(1)}, u32[]{:S(2)}, u32[]{:S(2)}) %collective-permute-start.23) | collective-permute-done | bytes 135200 | tf_op jit(solution)/shard_map/ppermute | solution.py:531
  54.0 1.3 %collective-permute-done.25.refs_5_ = f32[8,128]{1,0:T(8,128)S(1)} collective-permute-done((f32[8,128]{1,0:T(8,128)S(1)}, f32[8,128]{1,0:T(8,128)S(1)}, u32[]{:S(2)}, u32[]{:S(2)}) %collective-permute-start.25) | collective-permute-done | bytes 4128 | tf_op jit(solution)/shard_map/ppermute | solution.py:546
  55.4 2.4 %collective-permute-start.26 = (f32[264,128]{1,0:T(8,128)S(1)}, f32[264,128]{1,0:T(8,128)S(1)}, u32[]{:S(2)}, u32[]{:S(2)}) collective-permute-start(f32[264,128]{1,0:T(8,128)S(1)} %total.7.refs_5_), channel_id=1, source_target_pairs={{0,24},{2,26},{4,28},{6,30},{8,0},{10,2},{12,4},{14,6},{16,8},{18,... | collective-permute-start | bytes 405512 | tf_op jit(solution)/shard_map/ppermute | solution.py:546
  58.0 0.9 %collective-permute-start.19 = (f32[264,128]{1,0:T(8,128)S(1)}, f32[264,128]{1,0:T(8,128)S(1)}, u32[]{:S(2)}, u32[]{:S(2)}) collective-permute-start(f32[264,128]{1,0:T(8,128)S(1)} %get-tuple-element.99), channel_id=1, source_target_pairs={{0,2},{2,0},{4,6},{6,4},{8,10},{10,8},{12,14},{14,12},{16,18},{18,... | collective-permute-start | bytes 405512 | tf_op jit(solution)/shard_map/ppermute | solution.py:531
  58.9 1.3 %collective-permute-start.20 = (f32[264,128]{1,0:T(8,128)S(1)}, f32[264,128]{1,0:T(8,128)S(1)}, u32[]{:S(2)}, u32[]{:S(2)}) collective-permute-start(f32[264,128]{1,0:T(8,128)S(1)} %get-tuple-element.100), channel_id=1, source_target_pairs={{0,4},{2,6},{4,0},{6,2},{8,12},{10,14},{12,8},{14,10},{16,20},{18,... | collective-permute-start | bytes 405512 | tf_op jit(solution)/shard_map/ppermute | solution.py:531
  60.2 1.4 %collective-permute-start.21 = (f32[264,128]{1,0:T(8,128)S(1)}, f32[264,128]{1,0:T(8,128)S(1)}, u32[]{:S(2)}, u32[]{:S(2)}) collective-permute-start(f32[264,128]{1,0:T(8,128)S(1)} %get-tuple-element.101), channel_id=1, source_target_pairs={{0,6},{2,4},{4,2},{6,0},{8,14},{10,12},{12,10},{14,8},{16,22},{18,... | collective-permute-start | bytes 405512 | tf_op jit(solution)/shard_map/ppermute | solution.py:531
  61.8 1.6 %collective-permute-start.27 = (f32[264,128]{1,0:T(8,128)S(1)}, f32[264,128]{1,0:T(8,128)S(1)}, u32[]{:S(2)}, u32[]{:S(2)}) collective-permute-start(f32[264,128]{1,0:T(8,128)S(1)} %get-tuple-element.107), channel_id=1, source_target_pairs={{0,6},{2,4},{4,2},{6,0},{8,14},{10,12},{12,10},{14,8},{16,22},{18,... | collective-permute-start | bytes 405512 | tf_op jit(solution)/shard_map/ppermute | solution.py:531
  63.4 0.7 %collective-permute-start.28 = (f32[264,128]{1,0:T(8,128)S(1)}, f32[264,128]{1,0:T(8,128)S(1)}, u32[]{:S(2)}, u32[]{:S(2)}) collective-permute-start(f32[264,128]{1,0:T(8,128)S(1)} %get-tuple-element.108), channel_id=1, source_target_pairs={{0,4},{2,6},{4,0},{6,2},{8,12},{10,14},{12,8},{14,10},{16,20},{18,... | collective-permute-start | bytes 405512 | tf_op jit(solution)/shard_map/ppermute | solution.py:531
  64.4 1.0 %collective-permute-start.29 = (f32[264,128]{1,0:T(8,128)S(1)}, f32[264,128]{1,0:T(8,128)S(1)}, u32[]{:S(2)}, u32[]{:S(2)}) collective-permute-start(f32[264,128]{1,0:T(8,128)S(1)} %get-tuple-element.109), channel_id=1, source_target_pairs={{0,2},{2,0},{4,6},{6,4},{8,10},{10,8},{12,14},{14,12},{16,18},{18,... | collective-permute-start | bytes 405512 | tf_op jit(solution)/shard_map/ppermute | solution.py:531
  65.3 5.1 %gradients.1 = (bf16[128,2048]{1,0:T(8,128)(2,1)}, f32[128,2048]{1,0:T(8,128)S(1)}, f32[128,2048]{1,0:T(8,128)S(1)}) custom-call(f32[128,128]{1,0:T(8,128)S(1)} %copy-done.5, f32[16,128]{1,0:T(8,128)S(1)} %copy-done.6, bf16[128,2048]{1,0:T(8,128)(2,1)S(1)} %copy-done, bf16[128,2048]{1,0:T(8,128)(2,1)S(1)} %copy-done.1, bf16[128,2048]{1,0:T(8,128)(2,1)S(1)} %copy-done.2, ...), custom_call_target="tpu_custom_call" | custom-call | flops 872415232 | bytes 6291456 | tf_op jit(solution)/shard_map/gradients/pallas_call | solution.py:123
  70.6 1.5 %final.1 = (bf16[128,2048]{1,0:T(8,128)(2,1)}, bf16[128,2048]{1,0:T(8,128)(2,1)}, f32[1,2048]{1,0:T(1,128)}) custom-call(f32[128,128]{1,0:T(8,128)S(1)} %copy-done.5, f32[16,128]{1,0:T(8,128)S(1)} %copy-done.6, bf16[128,2048]{1,0:T(8,128)(2,1)S(1)} %copy-done.1, bf16[128,2048]{1,0:T(8,128)(2,1)S(1)} %copy-done.2, ...), custom_call_target="tpu_custom_call" | custom-call | flops 268435456 | bytes 6291456 | tf_op jit(solution)/shard_map/final/pallas_call | solution.py:123
  (46 shorter events, 3.1 us)
Async XLA Ops:
  0.6 6.8 %copy-start.1 = (bf16[128,2048]{1,0:T(8,128)(2,1)S(1)}, bf16[128,2048]{1,0:T(8,128)(2,1)}, u32[]{:S(2)}) copy-start(bf16[128,2048]{1,0:T(8,128)(2,1)} %key_ref.7) | copy-start | bytes 1572868
  0.6 6.7 %copy-start.2 = (bf16[128,2048]{1,0:T(8,128)(2,1)S(1)}, bf16[128,2048]{1,0:T(8,128)(2,1)}, u32[]{:S(2)}) copy-start(bf16[128,2048]{1,0:T(8,128)(2,1)} %value_ref.7) | copy-start | bytes 1572868
  2.8 4.6 %copy-start.6 = (f32[16,128]{1,0:T(8,128)S(1)}, f32[16,128]{1,0:T(8,128)}, u32[]{:S(2)}) copy-start(f32[16,128]{1,0:T(8,128)} %get-tuple-element.60.rates_ref) | copy-start | bytes 24580
  2.8 9.3 %collective-permute-start.7 = (f32[264,128]{1,0:T(8,128)}, f32[264,128]{1,0:T(8,128)S(1)}, u32[]{:S(2)}, u32[]{:S(2)}) collective-permute-start(f32[264,128]{1,0:T(8,128)} %get-tuple-element.70), channel_id=1, source_target_pairs={{0,2},{2,0},{4,6},{6,4},{8,10},{10,8},{12,14},{14,12},{16,18},{18,... | collective-permute-start | bytes 405512 | tf_op jit(solution)/shard_map/ppermute | solution.py:531
  5.8 8.7 %collective-permute-start.8 = (f32[264,128]{1,0:T(8,128)}, f32[264,128]{1,0:T(8,128)S(1)}, u32[]{:S(2)}, u32[]{:S(2)}) collective-permute-start(f32[264,128]{1,0:T(8,128)} %get-tuple-element.71), channel_id=1, source_target_pairs={{0,4},{2,6},{4,0},{6,2},{8,12},{10,14},{12,8},{14,10},{16,20},{18,... | collective-permute-start | bytes 405512 | tf_op jit(solution)/shard_map/ppermute | solution.py:531
  7.4 7.7 %collective-permute-start.9 = (f32[264,128]{1,0:T(8,128)}, f32[264,128]{1,0:T(8,128)S(1)}, u32[]{:S(2)}, u32[]{:S(2)}) collective-permute-start(f32[264,128]{1,0:T(8,128)} %get-tuple-element.72), channel_id=1, source_target_pairs={{0,6},{2,4},{4,2},{6,0},{8,14},{10,12},{12,10},{14,8},{16,22},{18,... | collective-permute-start | bytes 405512 | tf_op jit(solution)/shard_map/ppermute | solution.py:531
  7.4 0.8 %copy-start.4 = (f32[128,128]{1,0:T(8,128)S(1)}, f32[128,128]{1,0:T(8,128)}, u32[]{:S(2)}) copy-start(f32[128,128]{1,0:T(8,128)} %get-tuple-element.59.mark_ref) | copy-start | bytes 196612
  8.6 8.3 %collective-permute-start = (f32[264,128]{1,0:T(8,128)S(1)}, f32[264,128]{1,0:T(8,128)S(1)}, u32[]{:S(2)}, u32[]{:S(2)}) collective-permute-start(f32[264,128]{1,0:T(8,128)S(1)} %get-tuple-element.62), channel_id=1, source_target_pairs={{0,2},{2,0},{4,6},{6,4},{8,10},{10,8},{12,14},{14,12},{16,18},{18,... | collective-permute-start | bytes 405512 | tf_op jit(solution)/shard_map/ppermute | solution.py:531
  10.7 9.1 %collective-permute-start.1 = (f32[264,128]{1,0:T(8,128)S(1)}, f32[264,128]{1,0:T(8,128)S(1)}, u32[]{:S(2)}, u32[]{:S(2)}) collective-permute-start(f32[264,128]{1,0:T(8,128)S(1)} %get-tuple-element.63), channel_id=1, source_target_pairs={{0,4},{2,6},{4,0},{6,2},{8,12},{10,14},{12,8},{14,10},{16,20},{18,... | collective-permute-start | bytes 405512 | tf_op jit(solution)/shard_map/ppermute | solution.py:531
  12.2 7.6 %collective-permute-start.2 = (f32[264,128]{1,0:T(8,128)S(1)}, f32[264,128]{1,0:T(8,128)S(1)}, u32[]{:S(2)}, u32[]{:S(2)}) collective-permute-start(f32[264,128]{1,0:T(8,128)S(1)} %get-tuple-element.64), channel_id=1, source_target_pairs={{0,6},{2,4},{4,2},{6,0},{8,14},{10,12},{12,10},{14,8},{16,22},{18,... | collective-permute-start | bytes 405512 | tf_op jit(solution)/shard_map/ppermute | solution.py:531
  15.1 6.9 %collective-permute-start.10 = (f32[264,128]{1,0:T(8,128)S(1)}, f32[264,128]{1,0:T(8,128)S(1)}, u32[]{:S(2)}, u32[]{:S(2)}) collective-permute-start(f32[264,128]{1,0:T(8,128)S(1)} %total.5), channel_id=1, source_target_pairs={{0,8},{2,10},{4,12},{6,14},{8,16},{10,18},{12,20},{14,22},{16,24},... | collective-permute-start | bytes 405512 | tf_op jit(solution)/shard_map/ppermute | solution.py:546
  19.9 10.6 %copy-start = (bf16[128,2048]{1,0:T(8,128)(2,1)S(1)}, bf16[128,2048]{1,0:T(8,128)(2,1)}, u32[]{:S(2)}) copy-start(bf16[128,2048]{1,0:T(8,128)(2,1)} %query_ref.13) | copy-start | bytes 1572868
  19.9 6.9 %collective-permute-start.3 = (f32[264,128]{1,0:T(8,128)S(1)}, f32[264,128]{1,0:T(8,128)S(1)}, u32[]{:S(2)}, u32[]{:S(2)}) collective-permute-start(f32[264,128]{1,0:T(8,128)S(1)} %total.4), channel_id=1, source_target_pairs={{0,8},{2,10},{4,12},{6,14},{8,16},{10,18},{12,20},{14,22},{16,24},... | collective-permute-start | bytes 405512 | tf_op jit(solution)/shard_map/ppermute | solution.py:546
  22.2 6.9 %collective-permute-start.11 = (f32[264,128]{1,0:T(8,128)S(1)}, f32[264,128]{1,0:T(8,128)S(1)}, u32[]{:S(2)}, u32[]{:S(2)}) collective-permute-start(f32[264,128]{1,0:T(8,128)S(1)} %get-tuple-element.74), channel_id=1, source_target_pairs={{0,2},{2,0},{4,6},{6,4},{8,10},{10,8},{12,14},{14,12},{16,18},{18,... | collective-permute-start | bytes 405512 | tf_op jit(solution)/shard_map/ppermute | solution.py:531
  23.6 9.6 %collective-permute-start.12 = (f32[264,128]{1,0:T(8,128)S(1)}, f32[264,128]{1,0:T(8,128)S(1)}, u32[]{:S(2)}, u32[]{:S(2)}) collective-permute-start(f32[264,128]{1,0:T(8,128)S(1)} %get-tuple-element.75), channel_id=1, source_target_pairs={{0,4},{2,6},{4,0},{6,2},{8,12},{10,14},{12,8},{14,10},{16,20},{18,... | collective-permute-start | bytes 405512 | tf_op jit(solution)/shard_map/ppermute | solution.py:531
  24.7 5.8 %copy-start.5 = (f32[128,128]{1,0:T(8,128)S(1)}, f32[128,128]{1,0:T(8,128)}, u32[]{:S(2)}) copy-start(f32[128,128]{1,0:T(8,128)} %get-tuple-element.59.mark_ref) | copy-start | bytes 196612
  24.7 8.4 %collective-permute-start.13 = (f32[264,128]{1,0:T(8,128)S(1)}, f32[264,128]{1,0:T(8,128)S(1)}, u32[]{:S(2)}, u32[]{:S(2)}) collective-permute-start(f32[264,128]{1,0:T(8,128)S(1)} %get-tuple-element.76), channel_id=1, source_target_pairs={{0,6},{2,4},{4,2},{6,0},{8,14},{10,12},{12,10},{14,8},{16,22},{18,... | collective-permute-start | bytes 405512 | tf_op jit(solution)/shard_map/ppermute | solution.py:531
  26.9 7.0 %collective-permute-start.4 = (f32[264,128]{1,0:T(8,128)S(1)}, f32[264,128]{1,0:T(8,128)S(1)}, u32[]{:S(2)}, u32[]{:S(2)}) collective-permute-start(f32[264,128]{1,0:T(8,128)S(1)} %get-tuple-element.66), channel_id=1, source_target_pairs={{0,2},{2,0},{4,6},{6,4},{8,10},{10,8},{12,14},{14,12},{16,18},{18,... | collective-permute-start | bytes 405512 | tf_op jit(solution)/shard_map/ppermute | solution.py:531
  28.2 6.7 %collective-permute-start.5 = (f32[264,128]{1,0:T(8,128)S(1)}, f32[264,128]{1,0:T(8,128)S(1)}, u32[]{:S(2)}, u32[]{:S(2)}) collective-permute-start(f32[264,128]{1,0:T(8,128)S(1)} %get-tuple-element.67), channel_id=1, source_target_pairs={{0,4},{2,6},{4,0},{6,2},{8,12},{10,14},{12,8},{14,10},{16,20},{18,... | collective-permute-start | bytes 405512 | tf_op jit(solution)/shard_map/ppermute | solution.py:531
  29.0 4.1 %copy-start.3 = (bf16[128,2048]{1,0:T(8,128)(2,1)S(1)}, bf16[128,2048]{1,0:T(8,128)(2,1)}, u32[]{:S(2)}) copy-start(bf16[128,2048]{1,0:T(8,128)(2,1)} %grad_ref.9) | copy-start | bytes 1572868
  29.0 7.3 %collective-permute-start.6 = (f32[264,128]{1,0:T(8,128)S(1)}, f32[264,128]{1,0:T(8,128)S(1)}, u32[]{:S(2)}, u32[]{:S(2)}) collective-permute-start(f32[264,128]{1,0:T(8,128)S(1)} %get-tuple-element.68), channel_id=1, source_target_pairs={{0,6},{2,4},{4,2},{6,0},{8,14},{10,12},{12,10},{14,8},{16,22},{18,... | collective-permute-start | bytes 405512 | tf_op jit(solution)/shard_map/ppermute | solution.py:531
  30.5 2.7 %copy-start.7 = (f32[2048]{0:T(1024)S(1)}, f32[2048]{0:T(1024)}, u32[]{:S(2)}) copy-start(f32[2048]{0:T(1024)} %param.12) | copy-start | bytes 24580
  36.8 1.2 %collective-permute-start.14 = (f32[8,128]{1,0:T(8,128)S(1)}, f32[8,128]{1,0:T(8,128)S(1)}, u32[]{:S(2)}, u32[]{:S(2)}) collective-permute-start(f32[8,128]{1,0:T(8,128)S(1)} %get-tuple-element.81.refs_0_), channel_id=1, source_target_pairs={{0,1},{1,0},{2,3},{3,2},{4,5},{5,4},{6,7},{7,6},{8,9},{9,8},{10,11... | collective-permute-start | bytes 12296 | tf_op jit(solution)/shard_map/ppermute | solution.py:604
  38.6 6.7 %collective-permute-start.15 = (f32[264,128]{1,0:T(8,128)S(1)}, f32[264,128]{1,0:T(8,128)S(1)}, u32[]{:S(2)}, u32[]{:S(2)}) collective-permute-start(f32[264,128]{1,0:T(8,128)S(1)} %get-tuple-element.94), channel_id=1, source_target_pairs={{0,2},{2,0},{4,6},{6,4},{8,10},{10,8},{12,14},{14,12},{16,18},{18,... | collective-permute-start | bytes 405512 | tf_op jit(solution)/shard_map/ppermute | solution.py:531
  39.9 8.5 %collective-permute-start.16 = (f32[264,128]{1,0:T(8,128)S(1)}, f32[264,128]{1,0:T(8,128)S(1)}, u32[]{:S(2)}, u32[]{:S(2)}) collective-permute-start(f32[264,128]{1,0:T(8,128)S(1)} %get-tuple-element.95), channel_id=1, source_target_pairs={{0,4},{2,6},{4,0},{6,2},{8,12},{10,14},{12,8},{14,10},{16,20},{18,... | collective-permute-start | bytes 405512 | tf_op jit(solution)/shard_map/ppermute | solution.py:531
  41.3 7.5 %collective-permute-start.17 = (f32[264,128]{1,0:T(8,128)S(1)}, f32[264,128]{1,0:T(8,128)S(1)}, u32[]{:S(2)}, u32[]{:S(2)}) collective-permute-start(f32[264,128]{1,0:T(8,128)S(1)} %get-tuple-element.96), channel_id=1, source_target_pairs={{0,6},{2,4},{4,2},{6,0},{8,14},{10,12},{12,10},{14,8},{16,22},{18,... | collective-permute-start | bytes 405512 | tf_op jit(solution)/shard_map/ppermute | solution.py:531
  42.6 9.0 %collective-permute-start.22 = (f32[264,128]{1,0:T(8,128)S(1)}, f32[264,128]{1,0:T(8,128)S(1)}, u32[]{:S(2)}, u32[]{:S(2)}) collective-permute-start(f32[264,128]{1,0:T(8,128)S(1)} %get-tuple-element.103), channel_id=1, source_target_pairs={{0,2},{2,0},{4,6},{6,4},{8,10},{10,8},{12,14},{14,12},{16,18},{18,... | collective-permute-start | bytes 405512 | tf_op jit(solution)/shard_map/ppermute | solution.py:531
  43.9 10.0 %collective-permute-start.23 = (f32[264,128]{1,0:T(8,128)S(1)}, f32[264,128]{1,0:T(8,128)S(1)}, u32[]{:S(2)}, u32[]{:S(2)}) collective-permute-start(f32[264,128]{1,0:T(8,128)S(1)} %get-tuple-element.104), channel_id=1, source_target_pairs={{0,4},{2,6},{4,0},{6,2},{8,12},{10,14},{12,8},{14,10},{16,20},{18,... | collective-permute-start | bytes 405512 | tf_op jit(solution)/shard_map/ppermute | solution.py:531
  45.3 8.7 %collective-permute-start.24 = (f32[264,128]{1,0:T(8,128)S(1)}, f32[264,128]{1,0:T(8,128)S(1)}, u32[]{:S(2)}, u32[]{:S(2)}) collective-permute-start(f32[264,128]{1,0:T(8,128)S(1)} %get-tuple-element.105), channel_id=1, source_target_pairs={{0,6},{2,4},{4,2},{6,0},{8,14},{10,12},{12,10},{14,8},{16,22},{18,... | collective-permute-start | bytes 405512 | tf_op jit(solution)/shard_map/ppermute | solution.py:531
  48.8 9.0 %collective-permute-start.18 = (f32[264,128]{1,0:T(8,128)S(1)}, f32[264,128]{1,0:T(8,128)S(1)}, u32[]{:S(2)}, u32[]{:S(2)}) collective-permute-start(f32[264,128]{1,0:T(8,128)S(1)} %get-tuple-element.97), channel_id=1, source_target_pairs={{0,24},{2,26},{4,28},{6,30},{8,0},{10,2},{12,4},{14,6},{16,8},{18,... | collective-permute-start | bytes 405512 | tf_op jit(solution)/shard_map/ppermute | solution.py:546
  50.8 4.5 %collective-permute-start.25 = (f32[8,128]{1,0:T(8,128)S(1)}, f32[8,128]{1,0:T(8,128)S(1)}, u32[]{:S(2)}, u32[]{:S(2)}) collective-permute-start(f32[8,128]{1,0:T(8,128)S(1)} %get-tuple-element.106.refs_4_), channel_id=1, source_target_pairs={{0,16},{2,18},{4,20},{6,22},{8,24},{10,26},{12,28},{14,30},{16,0},... | collective-permute-start | bytes 12296 | tf_op jit(solution)/shard_map/ppermute | solution.py:546
  55.4 6.2 %collective-permute-start.26 = (f32[264,128]{1,0:T(8,128)S(1)}, f32[264,128]{1,0:T(8,128)S(1)}, u32[]{:S(2)}, u32[]{:S(2)}) collective-permute-start(f32[264,128]{1,0:T(8,128)S(1)} %total.7.refs_5_), channel_id=1, source_target_pairs={{0,24},{2,26},{4,28},{6,30},{8,0},{10,2},{12,4},{14,6},{16,8},{18,... | collective-permute-start | bytes 405512 | tf_op jit(solution)/shard_map/ppermute | solution.py:546
  58.0 6.4 %collective-permute-start.19 = (f32[264,128]{1,0:T(8,128)S(1)}, f32[264,128]{1,0:T(8,128)S(1)}, u32[]{:S(2)}, u32[]{:S(2)}) collective-permute-start(f32[264,128]{1,0:T(8,128)S(1)} %get-tuple-element.99), channel_id=1, source_target_pairs={{0,2},{2,0},{4,6},{6,4},{8,10},{10,8},{12,14},{14,12},{16,18},{18,... | collective-permute-start | bytes 405512 | tf_op jit(solution)/shard_map/ppermute | solution.py:531
  58.9 11.6 %collective-permute-start.20 = (f32[264,128]{1,0:T(8,128)S(1)}, f32[264,128]{1,0:T(8,128)S(1)}, u32[]{:S(2)}, u32[]{:S(2)}) collective-permute-start(f32[264,128]{1,0:T(8,128)S(1)} %get-tuple-element.100), channel_id=1, source_target_pairs={{0,4},{2,6},{4,0},{6,2},{8,12},{10,14},{12,8},{14,10},{16,20},{18,... | collective-permute-start | bytes 405512 | tf_op jit(solution)/shard_map/ppermute | solution.py:531
  60.2 10.3 %collective-permute-start.21 = (f32[264,128]{1,0:T(8,128)S(1)}, f32[264,128]{1,0:T(8,128)S(1)}, u32[]{:S(2)}, u32[]{:S(2)}) collective-permute-start(f32[264,128]{1,0:T(8,128)S(1)} %get-tuple-element.101), channel_id=1, source_target_pairs={{0,6},{2,4},{4,2},{6,0},{8,14},{10,12},{12,10},{14,8},{16,22},{18,... | collective-permute-start | bytes 405512 | tf_op jit(solution)/shard_map/ppermute | solution.py:531
  61.8 8.7 %collective-permute-start.27 = (f32[264,128]{1,0:T(8,128)S(1)}, f32[264,128]{1,0:T(8,128)S(1)}, u32[]{:S(2)}, u32[]{:S(2)}) collective-permute-start(f32[264,128]{1,0:T(8,128)S(1)} %get-tuple-element.107), channel_id=1, source_target_pairs={{0,6},{2,4},{4,2},{6,0},{8,14},{10,12},{12,10},{14,8},{16,22},{18,... | collective-permute-start | bytes 405512 | tf_op jit(solution)/shard_map/ppermute | solution.py:531
  63.4 7.2 %collective-permute-start.28 = (f32[264,128]{1,0:T(8,128)S(1)}, f32[264,128]{1,0:T(8,128)S(1)}, u32[]{:S(2)}, u32[]{:S(2)}) collective-permute-start(f32[264,128]{1,0:T(8,128)S(1)} %get-tuple-element.108), channel_id=1, source_target_pairs={{0,4},{2,6},{4,0},{6,2},{8,12},{10,14},{12,8},{14,10},{16,20},{18,... | collective-permute-start | bytes 405512 | tf_op jit(solution)/shard_map/ppermute | solution.py:531
  64.4 6.2 %collective-permute-start.29 = (f32[264,128]{1,0:T(8,128)S(1)}, f32[264,128]{1,0:T(8,128)S(1)}, u32[]{:S(2)}, u32[]{:S(2)}) collective-permute-start(f32[264,128]{1,0:T(8,128)S(1)} %get-tuple-element.109), channel_id=1, source_target_pairs={{0,2},{2,0},{4,6},{6,4},{8,10},{10,8},{12,14},{14,12},{16,18},{18,... | collective-permute-start | bytes 405512 | tf_op jit(solution)/shard_map/ppermute | solution.py:531

commit v8 on v7

--- a/solution.py
+++ b/solution.py
@@ -42,6 +42,7 @@
         self.state = self.each * self.dim
         self.payload = jax.ShapeDtypeStruct((self.state + self.info, self.dim), f32)
         self.block = jax.ShapeDtypeStruct((self.rows, self.features), f32)
+        self.bare = jax.ShapeDtypeStruct((self.state, self.dim), f32)
         self.rows_of_gain = jax.ShapeDtypeStruct((self.info, self.dim), f32)
 
 
@@ -119,7 +120,7 @@
     return rate[:, :1] if size.rows != size.dim else rate
 
 
-def call(body, name, inputs, outputs, flops, moved, scratch=(), in_specs=None, out_specs=None, vmem=16, aliases=None):
+def call(body, name, inputs, outputs, flops, moved, scratch=(), in_specs=None, out_specs=None, vmem=8, aliases=None):
     return pl.pallas_call(
         body,
         out_shape=outputs,
@@ -299,7 +300,8 @@
                     now = jnp.where(place[k] < place[to], jnp.minimum(now, marks[k]), now)
                 else:
                     now = jnp.where(place[k] < place[to], jnp.maximum(now, marks[k]), now)
-            put_rows(outs[to], size.state, with_marks(size, now, now, gains))
+            if to == 0 or backward:
+                put_rows(outs[to], size.state, with_marks(size, now, now, gains))
             far = (place[to] * size.rows).astype(f32)
             steps.append([steps_if(jnp.logical_and(outer == now, jnp.logical_not(first)), far)])
             for k in range(GROUP):
@@ -316,7 +318,7 @@
                 outs[to][cols, :] = total
 
     return call(
-        body, "prefixes", (rates, *parts, entering, *riders, *own), [size.payload] * GROUP,
+        body, "prefixes", (rates, *parts, entering, *riders, *own), [size.payload] + [size.payload if backward else size.bare] * (GROUP - 1),
         size.state * size.dim * 40, size.state * size.dim * 36,
     )
 

time: 72.5 us -> 72.2 us (level)
  no operation moved by 1% of the time
where the time goes in v8:
time: 72.2 us; the launch traced here: 72 us
  starting transfers between devices  40.2 us (56%)
  Pallas kernels  15.1 us (21%)
  waiting for transfers between devices  14.8 us (20%)
  between operations  1.02 us (1%)
  local copies, waits for them, and re-layouts  0.87 us (1%)
    ppermute x24, starting transfers between devices, swap(): lax.ppermute(array, 'seq', [(i, i ^ distance) for i in range(members)])  31.7 us
    pallas_call x18, Pallas kernels, call(): pl.pallas_call(body, out_shape=outputs, in_specs=in_specs if in_specs is...  15.1 us
    ppermute x24, waiting for transfers between devices, swap(): lax.ppermute(array, 'seq', [(i, i ^ distance) for i in range(members)])  11.2 us
    ppermute x5, starting transfers between devices, cyclic(): lax.ppermute(array, 'seq', [(i, (i + by) % members) for i in range(member...  8.46 us
    ppermute x5, waiting for transfers between devices, cyclic(): lax.ppermute(array, 'seq', [(i, (i + by) % members) for i in range(member...  2.43 us
  transfers between devices with their start and end apart: 30, of which 16 were waited for; matrix products, arithmetic and copies ran while one was open for 0% of the time, Pallas kernels for 14%

profile of v8, /device:TPU:0, one launch (start us, length us, event | category | flops | bytes accessed | tf_op | source)
XLA Modules:
  0.0 72.0 jit_solution(14478326987764913936)
XLA Ops:
  0.7 2.2 %states.2 = (f32[264,128]{1,0:T(8,128)}, f32[264,128]{1,0:T(8,128)}, f32[264,128]{1,0:T(8,128)}, f32[128,128]{1,0:T(8,128)}, f32[16,128]{1,0:T(8,128)}) custom-call(s32[1,128]{1,0:T(1,128)} %bitcast.9, f32[1,16]{1,0:T(1,128)} %bitcast.10, bf16[128,2048]{1,0:T(8,128)(2,1)} %key_ref.7, bf16[128,2048]{1,0:T(8,128)(2,1)} %value_ref.7), custom_call_target="tpu_custom_call" | custom-call | flops 50331648 | bytes 786432 | tf_op jit(solution)/shard_map/states/pallas_call | solution.py:124
  2.8 3.0 %collective-permute-start.7 = (f32[264,128]{1,0:T(8,128)}, f32[264,128]{1,0:T(8,128)S(1)}, u32[]{:S(2)}, u32[]{:S(2)}) collective-permute-start(f32[264,128]{1,0:T(8,128)} %get-tuple-element.70), channel_id=1, source_target_pairs={{0,2},{2,0},{4,6},{6,4},{8,10},{10,8},{12,14},{14,12},{16,18},{18,... | collective-permute-start | bytes 405512 | tf_op jit(solution)/shard_map/ppermute | solution.py:533
  5.8 1.5 %collective-permute-start.8 = (f32[264,128]{1,0:T(8,128)}, f32[264,128]{1,0:T(8,128)S(1)}, u32[]{:S(2)}, u32[]{:S(2)}) collective-permute-start(f32[264,128]{1,0:T(8,128)} %get-tuple-element.71), channel_id=1, source_target_pairs={{0,4},{2,6},{4,0},{6,2},{8,12},{10,14},{12,8},{14,10},{16,20},{18,... | collective-permute-start | bytes 405512 | tf_op jit(solution)/shard_map/ppermute | solution.py:533
  7.4 0.8 %copy-done.4 = f32[128,128]{1,0:T(8,128)S(1)} copy-done((f32[128,128]{1,0:T(8,128)S(1)}, f32[128,128]{1,0:T(8,128)}, u32[]{:S(2)}) %copy-start.4) | copy-done | bytes 65560
  8.6 2.0 %collective-permute-start = (f32[264,128]{1,0:T(8,128)S(1)}, f32[264,128]{1,0:T(8,128)S(1)}, u32[]{:S(2)}, u32[]{:S(2)}) collective-permute-start(f32[264,128]{1,0:T(8,128)S(1)} %get-tuple-element.62), channel_id=1, source_target_pairs={{0,2},{2,0},{4,6},{6,4},{8,10},{10,8},{12,14},{14,12},{16,18},{18,... | collective-permute-start | bytes 405512 | tf_op jit(solution)/shard_map/ppermute | solution.py:533
  10.7 1.5 %collective-permute-start.1 = (f32[264,128]{1,0:T(8,128)S(1)}, f32[264,128]{1,0:T(8,128)S(1)}, u32[]{:S(2)}, u32[]{:S(2)}) collective-permute-start(f32[264,128]{1,0:T(8,128)S(1)} %get-tuple-element.63), channel_id=1, source_target_pairs={{0,4},{2,6},{4,0},{6,2},{8,12},{10,14},{12,8},{14,10},{16,20},{18,... | collective-permute-start | bytes 405512 | tf_op jit(solution)/shard_map/ppermute | solution.py:533
  12.2 1.3 %collective-permute-start.2 = (f32[264,128]{1,0:T(8,128)S(1)}, f32[264,128]{1,0:T(8,128)S(1)}, u32[]{:S(2)}, u32[]{:S(2)}) collective-permute-start(f32[264,128]{1,0:T(8,128)S(1)} %get-tuple-element.64), channel_id=1, source_target_pairs={{0,6},{2,4},{4,2},{6,0},{8,14},{10,12},{12,10},{14,8},{16,22},{18,... | collective-permute-start | bytes 405512 | tf_op jit(solution)/shard_map/ppermute | solution.py:533
  13.5 1.1 %collective-permute-done.8.refs_2_ = f32[264,128]{1,0:T(8,128)S(1)} collective-permute-done((f32[264,128]{1,0:T(8,128)}, f32[264,128]{1,0:T(8,128)S(1)}, u32[]{:S(2)}, u32[]{:S(2)}) %collective-permute-start.8) | collective-permute-done | bytes 135200 | tf_op jit(solution)/shard_map/ppermute | solution.py:533
  14.6 0.5 collective-permute-done.9.refs_3_
  15.1 1.6 %collective-permute-start.10 = (f32[264,128]{1,0:T(8,128)S(1)}, f32[264,128]{1,0:T(8,128)S(1)}, u32[]{:S(2)}, u32[]{:S(2)}) collective-permute-start(f32[264,128]{1,0:T(8,128)S(1)} %total.5), channel_id=1, source_target_pairs={{0,8},{2,10},{4,12},{6,14},{8,16},{10,18},{12,20},{14,22},{16,24},... | collective-permute-start | bytes 405512 | tf_op jit(solution)/shard_map/ppermute | solution.py:548
  16.9 2.9 %collective-permute-done.1.refs_2_ = f32[264,128]{1,0:T(8,128)S(1)} collective-permute-done((f32[264,128]{1,0:T(8,128)S(1)}, f32[264,128]{1,0:T(8,128)S(1)}, u32[]{:S(2)}, u32[]{:S(2)}) %collective-permute-start.1) | collective-permute-done | bytes 135200 | tf_op jit(solution)/shard_map/ppermute | solution.py:533
  19.9 1.6 %collective-permute-start.3 = (f32[264,128]{1,0:T(8,128)S(1)}, f32[264,128]{1,0:T(8,128)S(1)}, u32[]{:S(2)}, u32[]{:S(2)}) collective-permute-start(f32[264,128]{1,0:T(8,128)S(1)} %total.4), channel_id=1, source_target_pairs={{0,8},{2,10},{4,12},{6,14},{8,16},{10,18},{12,20},{14,22},{16,24},... | collective-permute-start | bytes 405512 | tf_op jit(solution)/shard_map/ppermute | solution.py:548
  21.5 0.5 collective-permute-done.10.refs_4_
  22.2 1.4 %collective-permute-start.11 = (f32[256,128]{1,0:T(8,128)S(1)}, f32[256,128]{1,0:T(8,128)S(1)}, u32[]{:S(2)}, u32[]{:S(2)}) collective-permute-start(f32[256,128]{1,0:T(8,128)S(1)} %get-tuple-element.74), channel_id=1, source_target_pairs={{0,2},{2,0},{4,6},{6,4},{8,10},{10,8},{12,14},{14,12},{16,18},{18,... | collective-permute-start | bytes 393224 | tf_op jit(solution)/shard_map/ppermute | solution.py:533
  23.6 1.2 %collective-permute-start.12 = (f32[256,128]{1,0:T(8,128)S(1)}, f32[256,128]{1,0:T(8,128)S(1)}, u32[]{:S(2)}, u32[]{:S(2)}) collective-permute-start(f32[256,128]{1,0:T(8,128)S(1)} %get-tuple-element.75), channel_id=1, source_target_pairs={{0,4},{2,6},{4,0},{6,2},{8,12},{10,14},{12,8},{14,10},{16,20},{18,... | collective-permute-start | bytes 393224 | tf_op jit(solution)/shard_map/ppermute | solution.py:533
  24.7 1.4 %collective-permute-start.13 = (f32[256,128]{1,0:T(8,128)S(1)}, f32[256,128]{1,0:T(8,128)S(1)}, u32[]{:S(2)}, u32[]{:S(2)}) collective-permute-start(f32[256,128]{1,0:T(8,128)S(1)} %get-tuple-element.76), channel_id=1, source_target_pairs={{0,6},{2,4},{4,2},{6,0},{8,14},{10,12},{12,10},{14,8},{16,22},{18,... | collective-permute-start | bytes 393224 | tf_op jit(solution)/shard_map/ppermute | solution.py:533
  26.1 0.6 collective-permute-done.3.refs_4_
  26.9 1.3 %collective-permute-start.4 = (f32[256,128]{1,0:T(8,128)S(1)}, f32[256,128]{1,0:T(8,128)S(1)}, u32[]{:S(2)}, u32[]{:S(2)}) collective-permute-start(f32[256,128]{1,0:T(8,128)S(1)} %get-tuple-element.66), channel_id=1, source_target_pairs={{0,2},{2,0},{4,6},{6,4},{8,10},{10,8},{12,14},{14,12},{16,18},{18,... | collective-permute-start | bytes 393224 | tf_op jit(solution)/shard_map/ppermute | solution.py:533
  28.2 0.8 %collective-permute-start.5 = (f32[256,128]{1,0:T(8,128)S(1)}, f32[256,128]{1,0:T(8,128)S(1)}, u32[]{:S(2)}, u32[]{:S(2)}) collective-permute-start(f32[256,128]{1,0:T(8,128)S(1)} %get-tuple-element.67), channel_id=1, source_target_pairs={{0,4},{2,6},{4,0},{6,2},{8,12},{10,14},{12,8},{14,10},{16,20},{18,... | collective-permute-start | bytes 393224 | tf_op jit(solution)/shard_map/ppermute | solution.py:533
  29.1 1.4 %collective-permute-start.6 = (f32[256,128]{1,0:T(8,128)S(1)}, f32[256,128]{1,0:T(8,128)S(1)}, u32[]{:S(2)}, u32[]{:S(2)}) collective-permute-start(f32[256,128]{1,0:T(8,128)S(1)} %get-tuple-element.68), channel_id=1, source_target_pairs={{0,6},{2,4},{4,2},{6,0},{8,14},{10,12},{12,10},{14,8},{16,22},{18,... | collective-permute-start | bytes 393224 | tf_op jit(solution)/shard_map/ppermute | solution.py:533
  30.5 2.7 %nearby.1.near_ref = f32[128,2048]{1,0:T(8,128)S(1)} custom-call(f32[128,128]{1,0:T(8,128)S(1)} %copy-done.5, f32[16,128]{1,0:T(8,128)S(1)} %copy-done.6, bf16[128,2048]{1,0:T(8,128)(2,1)S(1)} %copy-done, bf16[128,2048]{1,0:T(8,128)(2,1)S(1)} %copy-done.2, bf16[128,2048]{1,0:T(8,128)(2,1)S(1)} %copy-done.3), custom_call_target="tpu_custom_call" | custom-call | flops 201326592 | bytes 2621440 | tf_op jit(solution)/shard_map/nearby/pallas_call | solution.py:124
  33.6 1.0 %collective-permute-done.5.refs_2_.refs_14_ = f32[256,128]{1,0:T(8,128)S(1)} collective-permute-done((f32[256,128]{1,0:T(8,128)S(1)}, f32[256,128]{1,0:T(8,128)S(1)}, u32[]{:S(2)}, u32[]{:S(2)}) %collective-permute-start.5) | collective-permute-done | bytes 131104 | tf_op jit(solution)/shard_map/ppermute | solution.py:533
  34.7 1.4 %collective-permute-done.6.refs_3_.refs_15_ = f32[256,128]{1,0:T(8,128)S(1)} collective-permute-done((f32[256,128]{1,0:T(8,128)S(1)}, f32[256,128]{1,0:T(8,128)S(1)}, u32[]{:S(2)}, u32[]{:S(2)}) %collective-permute-start.6) | collective-permute-done | bytes 131104 | tf_op jit(solution)/shard_map/ppermute | solution.py:533
  36.1 0.5 attended.3
  36.6 1.2 %collective-permute-done.14.refs_1_ = f32[8,128]{1,0:T(8,128)S(1)} collective-permute-done((f32[8,128]{1,0:T(8,128)S(1)}, f32[8,128]{1,0:T(8,128)S(1)}, u32[]{:S(2)}, u32[]{:S(2)}) %collective-permute-start.14) | collective-permute-done | bytes 4128 | tf_op jit(solution)/shard_map/ppermute | solution.py:606
  37.8 0.6 back.4
  38.4 1.3 %collective-permute-start.15 = (f32[264,128]{1,0:T(8,128)S(1)}, f32[264,128]{1,0:T(8,128)S(1)}, u32[]{:S(2)}, u32[]{:S(2)}) collective-permute-start(f32[264,128]{1,0:T(8,128)S(1)} %get-tuple-element.94), channel_id=1, source_target_pairs={{0,2},{2,0},{4,6},{6,4},{8,10},{10,8},{12,14},{14,12},{16,18},{18,... | collective-permute-start | bytes 405512 | tf_op jit(solution)/shard_map/ppermute | solution.py:533
  39.6 1.4 %collective-permute-start.16 = (f32[264,128]{1,0:T(8,128)S(1)}, f32[264,128]{1,0:T(8,128)S(1)}, u32[]{:S(2)}, u32[]{:S(2)}) collective-permute-start(f32[264,128]{1,0:T(8,128)S(1)} %get-tuple-element.95), channel_id=1, source_target_pairs={{0,4},{2,6},{4,0},{6,2},{8,12},{10,14},{12,8},{14,10},{16,20},{18,... | collective-permute-start | bytes 405512 | tf_op jit(solution)/shard_map/ppermute | solution.py:533
  41.0 0.9 %collective-permute-start.17 = (f32[264,128]{1,0:T(8,128)S(1)}, f32[264,128]{1,0:T(8,128)S(1)}, u32[]{:S(2)}, u32[]{:S(2)}) collective-permute-start(f32[264,128]{1,0:T(8,128)S(1)} %get-tuple-element.96), channel_id=1, source_target_pairs={{0,6},{2,4},{4,2},{6,0},{8,14},{10,12},{12,10},{14,8},{16,22},{18,... | collective-permute-start | bytes 405512 | tf_op jit(solution)/shard_map/ppermute | solution.py:533
  41.9 0.5 back.5
  42.4 1.3 %collective-permute-start.22 = (f32[264,128]{1,0:T(8,128)S(1)}, f32[264,128]{1,0:T(8,128)S(1)}, u32[]{:S(2)}, u32[]{:S(2)}) collective-permute-start(f32[264,128]{1,0:T(8,128)S(1)} %get-tuple-element.103), channel_id=1, source_target_pairs={{0,2},{2,0},{4,6},{6,4},{8,10},{10,8},{12,14},{14,12},{16,18},{18,... | collective-permute-start | bytes 405512 | tf_op jit(solution)/shard_map/ppermute | solution.py:533
  43.6 1.4 %collective-permute-start.23 = (f32[264,128]{1,0:T(8,128)S(1)}, f32[264,128]{1,0:T(8,128)S(1)}, u32[]{:S(2)}, u32[]{:S(2)}) collective-permute-start(f32[264,128]{1,0:T(8,128)S(1)} %get-tuple-element.104), channel_id=1, source_target_pairs={{0,4},{2,6},{4,0},{6,2},{8,12},{10,14},{12,8},{14,10},{16,20},{18,... | collective-permute-start | bytes 405512 | tf_op jit(solution)/shard_map/ppermute | solution.py:533
  45.0 1.8 %collective-permute-start.24 = (f32[264,128]{1,0:T(8,128)S(1)}, f32[264,128]{1,0:T(8,128)S(1)}, u32[]{:S(2)}, u32[]{:S(2)}) collective-permute-start(f32[264,128]{1,0:T(8,128)S(1)} %get-tuple-element.105), channel_id=1, source_target_pairs={{0,6},{2,4},{4,2},{6,0},{8,14},{10,12},{12,10},{14,8},{16,22},{18,... | collective-permute-start | bytes 405512 | tf_op jit(solution)/shard_map/ppermute | solution.py:533
  46.9 0.4 back.3
  47.3 0.8 %collective-permute-done.16.refs_2_ = f32[264,128]{1,0:T(8,128)S(1)} collective-permute-done((f32[264,128]{1,0:T(8,128)S(1)}, f32[264,128]{1,0:T(8,128)S(1)}, u32[]{:S(2)}, u32[]{:S(2)}) %collective-permute-start.16) | collective-permute-done | bytes 135200 | tf_op jit(solution)/shard_map/ppermute | solution.py:533
  48.5 2.0 %collective-permute-start.18 = (f32[264,128]{1,0:T(8,128)S(1)}, f32[264,128]{1,0:T(8,128)S(1)}, u32[]{:S(2)}, u32[]{:S(2)}) collective-permute-start(f32[264,128]{1,0:T(8,128)S(1)} %get-tuple-element.97), channel_id=1, source_target_pairs={{0,24},{2,26},{4,28},{6,30},{8,0},{10,2},{12,4},{14,6},{16,8},{18,... | collective-permute-start | bytes 405512 | tf_op jit(solution)/shard_map/ppermute | solution.py:548
  50.5 0.8 %collective-permute-start.25 = (f32[8,128]{1,0:T(8,128)S(1)}, f32[8,128]{1,0:T(8,128)S(1)}, u32[]{:S(2)}, u32[]{:S(2)}) collective-permute-start(f32[8,128]{1,0:T(8,128)S(1)} %get-tuple-element.106.refs_4_), channel_id=1, source_target_pairs={{0,16},{2,18},{4,20},{6,22},{8,24},{10,26},{12,28},{14,30},{16,0},... | collective-permute-start | bytes 12296 | tf_op jit(solution)/shard_map/ppermute | solution.py:548
  51.3 2.4 %collective-permute-done.23.refs_2_ = f32[264,128]{1,0:T(8,128)S(1)} collective-permute-done((f32[264,128]{1,0:T(8,128)S(1)}, f32[264,128]{1,0:T(8,128)S(1)}, u32[]{:S(2)}, u32[]{:S(2)}) %collective-permute-start.23) | collective-permute-done | bytes 135200 | tf_op jit(solution)/shard_map/ppermute | solution.py:533
  53.7 1.3 %collective-permute-done.25.refs_5_ = f32[8,128]{1,0:T(8,128)S(1)} collective-permute-done((f32[8,128]{1,0:T(8,128)S(1)}, f32[8,128]{1,0:T(8,128)S(1)}, u32[]{:S(2)}, u32[]{:S(2)}) %collective-permute-start.25) | collective-permute-done | bytes 4128 | tf_op jit(solution)/shard_map/ppermute | solution.py:548
  55.1 2.4 %collective-permute-start.26 = (f32[264,128]{1,0:T(8,128)S(1)}, f32[264,128]{1,0:T(8,128)S(1)}, u32[]{:S(2)}, u32[]{:S(2)}) collective-permute-start(f32[264,128]{1,0:T(8,128)S(1)} %total.7.refs_5_), channel_id=1, source_target_pairs={{0,24},{2,26},{4,28},{6,30},{8,0},{10,2},{12,4},{14,6},{16,8},{18,... | collective-permute-start | bytes 405512 | tf_op jit(solution)/shard_map/ppermute | solution.py:548
  57.7 0.8 %collective-permute-start.19 = (f32[264,128]{1,0:T(8,128)S(1)}, f32[264,128]{1,0:T(8,128)S(1)}, u32[]{:S(2)}, u32[]{:S(2)}) collective-permute-start(f32[264,128]{1,0:T(8,128)S(1)} %get-tuple-element.99), channel_id=1, source_target_pairs={{0,2},{2,0},{4,6},{6,4},{8,10},{10,8},{12,14},{14,12},{16,18},{18,... | collective-permute-start | bytes 405512 | tf_op jit(solution)/shard_map/ppermute | solution.py:533
  58.5 1.4 %collective-permute-start.20 = (f32[264,128]{1,0:T(8,128)S(1)}, f32[264,128]{1,0:T(8,128)S(1)}, u32[]{:S(2)}, u32[]{:S(2)}) collective-permute-start(f32[264,128]{1,0:T(8,128)S(1)} %get-tuple-element.100), channel_id=1, source_target_pairs={{0,4},{2,6},{4,0},{6,2},{8,12},{10,14},{12,8},{14,10},{16,20},{18,... | collective-permute-start | bytes 405512 | tf_op jit(solution)/shard_map/ppermute | solution.py:533
  59.9 1.4 %collective-permute-start.21 = (f32[264,128]{1,0:T(8,128)S(1)}, f32[264,128]{1,0:T(8,128)S(1)}, u32[]{:S(2)}, u32[]{:S(2)}) collective-permute-start(f32[264,128]{1,0:T(8,128)S(1)} %get-tuple-element.101), channel_id=1, source_target_pairs={{0,6},{2,4},{4,2},{6,0},{8,14},{10,12},{12,10},{14,8},{16,22},{18,... | collective-permute-start | bytes 405512 | tf_op jit(solution)/shard_map/ppermute | solution.py:533
  61.5 1.6 %collective-permute-start.27 = (f32[264,128]{1,0:T(8,128)S(1)}, f32[264,128]{1,0:T(8,128)S(1)}, u32[]{:S(2)}, u32[]{:S(2)}) collective-permute-start(f32[264,128]{1,0:T(8,128)S(1)} %get-tuple-element.107), channel_id=1, source_target_pairs={{0,6},{2,4},{4,2},{6,0},{8,14},{10,12},{12,10},{14,8},{16,22},{18,... | collective-permute-start | bytes 405512 | tf_op jit(solution)/shard_map/ppermute | solution.py:533
  63.1 0.7 collective-permute-start.28
  64.1 0.9 %collective-permute-start.29 = (f32[264,128]{1,0:T(8,128)S(1)}, f32[264,128]{1,0:T(8,128)S(1)}, u32[]{:S(2)}, u32[]{:S(2)}) collective-permute-start(f32[264,128]{1,0:T(8,128)S(1)} %get-tuple-element.109), channel_id=1, source_target_pairs={{0,2},{2,0},{4,6},{6,4},{8,10},{10,8},{12,14},{14,12},{16,18},{18,... | collective-permute-start | bytes 405512 | tf_op jit(solution)/shard_map/ppermute | solution.py:533
  65.0 5.1 %gradients.1 = (bf16[128,2048]{1,0:T(8,128)(2,1)}, f32[128,2048]{1,0:T(8,128)S(1)}, f32[128,2048]{1,0:T(8,128)S(1)}) custom-call(f32[128,128]{1,0:T(8,128)S(1)} %copy-done.5, f32[16,128]{1,0:T(8,128)S(1)} %copy-done.6, bf16[128,2048]{1,0:T(8,128)(2,1)S(1)} %copy-done, bf16[128,2048]{1,0:T(8,128)(2,1)S(1)} %copy-done.2, bf16[128,2048]{1,0:T(8,128)(2,1)S(1)} %copy-done.3, ...), custom_call_target="tpu_custom_call" | custom-call | flops 872415232 | bytes 6291456 | tf_op jit(solution)/shard_map/gradients/pallas_call | solution.py:124
  70.3 1.5 %final.1 = (bf16[128,2048]{1,0:T(8,128)(2,1)}, bf16[128,2048]{1,0:T(8,128)(2,1)}, f32[1,2048]{1,0:T(1,128)}) custom-call(f32[128,128]{1,0:T(8,128)S(1)} %copy-done.5, f32[16,128]{1,0:T(8,128)S(1)} %copy-done.6, bf16[128,2048]{1,0:T(8,128)(2,1)S(1)} %copy-done.2, bf16[128,2048]{1,0:T(8,128)(2,1)S(1)} %copy-done.3, ...), custom_call_target="tpu_custom_call" | custom-call | flops 268435456 | bytes 6291456 | tf_op jit(solution)/shard_map/final/pallas_call | solution.py:124
  (46 shorter events, 3.0 us)
Async XLA Ops:
  0.6 6.8 %copy-start.2 = (bf16[128,2048]{1,0:T(8,128)(2,1)S(1)}, bf16[128,2048]{1,0:T(8,128)(2,1)}, u32[]{:S(2)}) copy-start(bf16[128,2048]{1,0:T(8,128)(2,1)} %key_ref.7) | copy-start | bytes 1572868
  0.6 6.7 %copy-start.3 = (bf16[128,2048]{1,0:T(8,128)(2,1)S(1)}, bf16[128,2048]{1,0:T(8,128)(2,1)}, u32[]{:S(2)}) copy-start(bf16[128,2048]{1,0:T(8,128)(2,1)} %value_ref.7) | copy-start | bytes 1572868
  2.8 4.6 %copy-start.6 = (f32[16,128]{1,0:T(8,128)S(1)}, f32[16,128]{1,0:T(8,128)}, u32[]{:S(2)}) copy-start(f32[16,128]{1,0:T(8,128)} %get-tuple-element.60.rates_ref) | copy-start | bytes 24580
  2.8 9.3 %collective-permute-start.7 = (f32[264,128]{1,0:T(8,128)}, f32[264,128]{1,0:T(8,128)S(1)}, u32[]{:S(2)}, u32[]{:S(2)}) collective-permute-start(f32[264,128]{1,0:T(8,128)} %get-tuple-element.70), channel_id=1, source_target_pairs={{0,2},{2,0},{4,6},{6,4},{8,10},{10,8},{12,14},{14,12},{16,18},{18,... | collective-permute-start | bytes 405512 | tf_op jit(solution)/shard_map/ppermute | solution.py:533
  5.8 8.7 %collective-permute-start.8 = (f32[264,128]{1,0:T(8,128)}, f32[264,128]{1,0:T(8,128)S(1)}, u32[]{:S(2)}, u32[]{:S(2)}) collective-permute-start(f32[264,128]{1,0:T(8,128)} %get-tuple-element.71), channel_id=1, source_target_pairs={{0,4},{2,6},{4,0},{6,2},{8,12},{10,14},{12,8},{14,10},{16,20},{18,... | collective-permute-start | bytes 405512 | tf_op jit(solution)/shard_map/ppermute | solution.py:533
  7.4 7.7 %collective-permute-start.9 = (f32[264,128]{1,0:T(8,128)}, f32[264,128]{1,0:T(8,128)S(1)}, u32[]{:S(2)}, u32[]{:S(2)}) collective-permute-start(f32[264,128]{1,0:T(8,128)} %get-tuple-element.72), channel_id=1, source_target_pairs={{0,6},{2,4},{4,2},{6,0},{8,14},{10,12},{12,10},{14,8},{16,22},{18,... | collective-permute-start | bytes 405512 | tf_op jit(solution)/shard_map/ppermute | solution.py:533
  7.4 0.8 %copy-start.4 = (f32[128,128]{1,0:T(8,128)S(1)}, f32[128,128]{1,0:T(8,128)}, u32[]{:S(2)}) copy-start(f32[128,128]{1,0:T(8,128)} %get-tuple-element.59.mark_ref) | copy-start | bytes 196612
  8.6 8.3 %collective-permute-start = (f32[264,128]{1,0:T(8,128)S(1)}, f32[264,128]{1,0:T(8,128)S(1)}, u32[]{:S(2)}, u32[]{:S(2)}) collective-permute-start(f32[264,128]{1,0:T(8,128)S(1)} %get-tuple-element.62), channel_id=1, source_target_pairs={{0,2},{2,0},{4,6},{6,4},{8,10},{10,8},{12,14},{14,12},{16,18},{18,... | collective-permute-start | bytes 405512 | tf_op jit(solution)/shard_map/ppermute | solution.py:533
  10.7 9.1 %collective-permute-start.1 = (f32[264,128]{1,0:T(8,128)S(1)}, f32[264,128]{1,0:T(8,128)S(1)}, u32[]{:S(2)}, u32[]{:S(2)}) collective-permute-start(f32[264,128]{1,0:T(8,128)S(1)} %get-tuple-element.63), channel_id=1, source_target_pairs={{0,4},{2,6},{4,0},{6,2},{8,12},{10,14},{12,8},{14,10},{16,20},{18,... | collective-permute-start | bytes 405512 | tf_op jit(solution)/shard_map/ppermute | solution.py:533
  12.2 7.6 %collective-permute-start.2 = (f32[264,128]{1,0:T(8,128)S(1)}, f32[264,128]{1,0:T(8,128)S(1)}, u32[]{:S(2)}, u32[]{:S(2)}) collective-permute-start(f32[264,128]{1,0:T(8,128)S(1)} %get-tuple-element.64), channel_id=1, source_target_pairs={{0,6},{2,4},{4,2},{6,0},{8,14},{10,12},{12,10},{14,8},{16,22},{18,... | collective-permute-start | bytes 405512 | tf_op jit(solution)/shard_map/ppermute | solution.py:533
  15.1 6.9 %collective-permute-start.10 = (f32[264,128]{1,0:T(8,128)S(1)}, f32[264,128]{1,0:T(8,128)S(1)}, u32[]{:S(2)}, u32[]{:S(2)}) collective-permute-start(f32[264,128]{1,0:T(8,128)S(1)} %total.5), channel_id=1, source_target_pairs={{0,8},{2,10},{4,12},{6,14},{8,16},{10,18},{12,20},{14,22},{16,24},... | collective-permute-start | bytes 405512 | tf_op jit(solution)/shard_map/ppermute | solution.py:548
  19.9 10.6 %copy-start = (bf16[128,2048]{1,0:T(8,128)(2,1)S(1)}, bf16[128,2048]{1,0:T(8,128)(2,1)}, u32[]{:S(2)}) copy-start(bf16[128,2048]{1,0:T(8,128)(2,1)} %query_ref.13) | copy-start | bytes 1572868
  19.9 6.9 %collective-permute-start.3 = (f32[264,128]{1,0:T(8,128)S(1)}, f32[264,128]{1,0:T(8,128)S(1)}, u32[]{:S(2)}, u32[]{:S(2)}) collective-permute-start(f32[264,128]{1,0:T(8,128)S(1)} %total.4), channel_id=1, source_target_pairs={{0,8},{2,10},{4,12},{6,14},{8,16},{10,18},{12,20},{14,22},{16,24},... | collective-permute-start | bytes 405512 | tf_op jit(solution)/shard_map/ppermute | solution.py:548
  22.2 6.9 %collective-permute-start.11 = (f32[256,128]{1,0:T(8,128)S(1)}, f32[256,128]{1,0:T(8,128)S(1)}, u32[]{:S(2)}, u32[]{:S(2)}) collective-permute-start(f32[256,128]{1,0:T(8,128)S(1)} %get-tuple-element.74), channel_id=1, source_target_pairs={{0,2},{2,0},{4,6},{6,4},{8,10},{10,8},{12,14},{14,12},{16,18},{18,... | collective-permute-start | bytes 393224 | tf_op jit(solution)/shard_map/ppermute | solution.py:533
  23.6 9.6 %collective-permute-start.12 = (f32[256,128]{1,0:T(8,128)S(1)}, f32[256,128]{1,0:T(8,128)S(1)}, u32[]{:S(2)}, u32[]{:S(2)}) collective-permute-start(f32[256,128]{1,0:T(8,128)S(1)} %get-tuple-element.75), channel_id=1, source_target_pairs={{0,4},{2,6},{4,0},{6,2},{8,12},{10,14},{12,8},{14,10},{16,20},{18,... | collective-permute-start | bytes 393224 | tf_op jit(solution)/shard_map/ppermute | solution.py:533
  24.7 5.8 %copy-start.5 = (f32[128,128]{1,0:T(8,128)S(1)}, f32[128,128]{1,0:T(8,128)}, u32[]{:S(2)}) copy-start(f32[128,128]{1,0:T(8,128)} %get-tuple-element.59.mark_ref) | copy-start | bytes 196612
  24.7 8.5 %collective-permute-start.13 = (f32[256,128]{1,0:T(8,128)S(1)}, f32[256,128]{1,0:T(8,128)S(1)}, u32[]{:S(2)}, u32[]{:S(2)}) collective-permute-start(f32[256,128]{1,0:T(8,128)S(1)} %get-tuple-element.76), channel_id=1, source_target_pairs={{0,6},{2,4},{4,2},{6,0},{8,14},{10,12},{12,10},{14,8},{16,22},{18,... | collective-permute-start | bytes 393224 | tf_op jit(solution)/shard_map/ppermute | solution.py:533
  26.9 6.7 %collective-permute-start.4 = (f32[256,128]{1,0:T(8,128)S(1)}, f32[256,128]{1,0:T(8,128)S(1)}, u32[]{:S(2)}, u32[]{:S(2)}) collective-permute-start(f32[256,128]{1,0:T(8,128)S(1)} %get-tuple-element.66), channel_id=1, source_target_pairs={{0,2},{2,0},{4,6},{6,4},{8,10},{10,8},{12,14},{14,12},{16,18},{18,... | collective-permute-start | bytes 393224 | tf_op jit(solution)/shard_map/ppermute | solution.py:533
  28.2 6.4 %collective-permute-start.5 = (f32[256,128]{1,0:T(8,128)S(1)}, f32[256,128]{1,0:T(8,128)S(1)}, u32[]{:S(2)}, u32[]{:S(2)}) collective-permute-start(f32[256,128]{1,0:T(8,128)S(1)} %get-tuple-element.67), channel_id=1, source_target_pairs={{0,4},{2,6},{4,0},{6,2},{8,12},{10,14},{12,8},{14,10},{16,20},{18,... | collective-permute-start | bytes 393224 | tf_op jit(solution)/shard_map/ppermute | solution.py:533
  29.1 4.1 %copy-start.1 = (bf16[128,2048]{1,0:T(8,128)(2,1)S(1)}, bf16[128,2048]{1,0:T(8,128)(2,1)}, u32[]{:S(2)}) copy-start(bf16[128,2048]{1,0:T(8,128)(2,1)} %grad_ref.9) | copy-start | bytes 1572868
  29.1 7.0 %collective-permute-start.6 = (f32[256,128]{1,0:T(8,128)S(1)}, f32[256,128]{1,0:T(8,128)S(1)}, u32[]{:S(2)}, u32[]{:S(2)}) collective-permute-start(f32[256,128]{1,0:T(8,128)S(1)} %get-tuple-element.68), channel_id=1, source_target_pairs={{0,6},{2,4},{4,2},{6,0},{8,14},{10,12},{12,10},{14,8},{16,22},{18,... | collective-permute-start | bytes 393224 | tf_op jit(solution)/shard_map/ppermute | solution.py:533
  30.5 2.7 %copy-start.7 = (f32[2048]{0:T(1024)S(1)}, f32[2048]{0:T(1024)}, u32[]{:S(2)}) copy-start(f32[2048]{0:T(1024)} %param.12) | copy-start | bytes 24580
  36.5 1.2 %collective-permute-start.14 = (f32[8,128]{1,0:T(8,128)S(1)}, f32[8,128]{1,0:T(8,128)S(1)}, u32[]{:S(2)}, u32[]{:S(2)}) collective-permute-start(f32[8,128]{1,0:T(8,128)S(1)} %get-tuple-element.81.refs_0_), channel_id=1, source_target_pairs={{0,1},{1,0},{2,3},{3,2},{4,5},{5,4},{6,7},{7,6},{8,9},{9,8},{10,11... | collective-permute-start | bytes 12296 | tf_op jit(solution)/shard_map/ppermute | solution.py:606
  38.4 6.7 %collective-permute-start.15 = (f32[264,128]{1,0:T(8,128)S(1)}, f32[264,128]{1,0:T(8,128)S(1)}, u32[]{:S(2)}, u32[]{:S(2)}) collective-permute-start(f32[264,128]{1,0:T(8,128)S(1)} %get-tuple-element.94), channel_id=1, source_target_pairs={{0,2},{2,0},{4,6},{6,4},{8,10},{10,8},{12,14},{14,12},{16,18},{18,... | collective-permute-start | bytes 405512 | tf_op jit(solution)/shard_map/ppermute | solution.py:533
  39.6 8.5 %collective-permute-start.16 = (f32[264,128]{1,0:T(8,128)S(1)}, f32[264,128]{1,0:T(8,128)S(1)}, u32[]{:S(2)}, u32[]{:S(2)}) collective-permute-start(f32[264,128]{1,0:T(8,128)S(1)} %get-tuple-element.95), channel_id=1, source_target_pairs={{0,4},{2,6},{4,0},{6,2},{8,12},{10,14},{12,8},{14,10},{16,20},{18,... | collective-permute-start | bytes 405512 | tf_op jit(solution)/shard_map/ppermute | solution.py:533
  41.0 7.4 %collective-permute-start.17 = (f32[264,128]{1,0:T(8,128)S(1)}, f32[264,128]{1,0:T(8,128)S(1)}, u32[]{:S(2)}, u32[]{:S(2)}) collective-permute-start(f32[264,128]{1,0:T(8,128)S(1)} %get-tuple-element.96), channel_id=1, source_target_pairs={{0,6},{2,4},{4,2},{6,0},{8,14},{10,12},{12,10},{14,8},{16,22},{18,... | collective-permute-start | bytes 405512 | tf_op jit(solution)/shard_map/ppermute | solution.py:533
  42.4 8.9 %collective-permute-start.22 = (f32[264,128]{1,0:T(8,128)S(1)}, f32[264,128]{1,0:T(8,128)S(1)}, u32[]{:S(2)}, u32[]{:S(2)}) collective-permute-start(f32[264,128]{1,0:T(8,128)S(1)} %get-tuple-element.103), channel_id=1, source_target_pairs={{0,2},{2,0},{4,6},{6,4},{8,10},{10,8},{12,14},{14,12},{16,18},{18,... | collective-permute-start | bytes 405512 | tf_op jit(solution)/shard_map/ppermute | solution.py:533
  43.6 10.1 %collective-permute-start.23 = (f32[264,128]{1,0:T(8,128)S(1)}, f32[264,128]{1,0:T(8,128)S(1)}, u32[]{:S(2)}, u32[]{:S(2)}) collective-permute-start(f32[264,128]{1,0:T(8,128)S(1)} %get-tuple-element.104), channel_id=1, source_target_pairs={{0,4},{2,6},{4,0},{6,2},{8,12},{10,14},{12,8},{14,10},{16,20},{18,... | collective-permute-start | bytes 405512 | tf_op jit(solution)/shard_map/ppermute | solution.py:533
  45.0 8.7 %collective-permute-start.24 = (f32[264,128]{1,0:T(8,128)S(1)}, f32[264,128]{1,0:T(8,128)S(1)}, u32[]{:S(2)}, u32[]{:S(2)}) collective-permute-start(f32[264,128]{1,0:T(8,128)S(1)} %get-tuple-element.105), channel_id=1, source_target_pairs={{0,6},{2,4},{4,2},{6,0},{8,14},{10,12},{12,10},{14,8},{16,22},{18,... | collective-permute-start | bytes 405512 | tf_op jit(solution)/shard_map/ppermute | solution.py:533
  48.5 9.0 %collective-permute-start.18 = (f32[264,128]{1,0:T(8,128)S(1)}, f32[264,128]{1,0:T(8,128)S(1)}, u32[]{:S(2)}, u32[]{:S(2)}) collective-permute-start(f32[264,128]{1,0:T(8,128)S(1)} %get-tuple-element.97), channel_id=1, source_target_pairs={{0,24},{2,26},{4,28},{6,30},{8,0},{10,2},{12,4},{14,6},{16,8},{18,... | collective-permute-start | bytes 405512 | tf_op jit(solution)/shard_map/ppermute | solution.py:548
  50.5 4.5 %collective-permute-start.25 = (f32[8,128]{1,0:T(8,128)S(1)}, f32[8,128]{1,0:T(8,128)S(1)}, u32[]{:S(2)}, u32[]{:S(2)}) collective-permute-start(f32[8,128]{1,0:T(8,128)S(1)} %get-tuple-element.106.refs_4_), channel_id=1, source_target_pairs={{0,16},{2,18},{4,20},{6,22},{8,24},{10,26},{12,28},{14,30},{16,0},... | collective-permute-start | bytes 12296 | tf_op jit(solution)/shard_map/ppermute | solution.py:548
  55.1 6.2 %collective-permute-start.26 = (f32[264,128]{1,0:T(8,128)S(1)}, f32[264,128]{1,0:T(8,128)S(1)}, u32[]{:S(2)}, u32[]{:S(2)}) collective-permute-start(f32[264,128]{1,0:T(8,128)S(1)} %total.7.refs_5_), channel_id=1, source_target_pairs={{0,24},{2,26},{4,28},{6,30},{8,0},{10,2},{12,4},{14,6},{16,8},{18,... | collective-permute-start | bytes 405512 | tf_op jit(solution)/shard_map/ppermute | solution.py:548
  57.7 6.4 %collective-permute-start.19 = (f32[264,128]{1,0:T(8,128)S(1)}, f32[264,128]{1,0:T(8,128)S(1)}, u32[]{:S(2)}, u32[]{:S(2)}) collective-permute-start(f32[264,128]{1,0:T(8,128)S(1)} %get-tuple-element.99), channel_id=1, source_target_pairs={{0,2},{2,0},{4,6},{6,4},{8,10},{10,8},{12,14},{14,12},{16,18},{18,... | collective-permute-start | bytes 405512 | tf_op jit(solution)/shard_map/ppermute | solution.py:533
  58.5 11.6 %collective-permute-start.20 = (f32[264,128]{1,0:T(8,128)S(1)}, f32[264,128]{1,0:T(8,128)S(1)}, u32[]{:S(2)}, u32[]{:S(2)}) collective-permute-start(f32[264,128]{1,0:T(8,128)S(1)} %get-tuple-element.100), channel_id=1, source_target_pairs={{0,4},{2,6},{4,0},{6,2},{8,12},{10,14},{12,8},{14,10},{16,20},{18,... | collective-permute-start | bytes 405512 | tf_op jit(solution)/shard_map/ppermute | solution.py:533
  59.9 10.3 %collective-permute-start.21 = (f32[264,128]{1,0:T(8,128)S(1)}, f32[264,128]{1,0:T(8,128)S(1)}, u32[]{:S(2)}, u32[]{:S(2)}) collective-permute-start(f32[264,128]{1,0:T(8,128)S(1)} %get-tuple-element.101), channel_id=1, source_target_pairs={{0,6},{2,4},{4,2},{6,0},{8,14},{10,12},{12,10},{14,8},{16,22},{18,... | collective-permute-start | bytes 405512 | tf_op jit(solution)/shard_map/ppermute | solution.py:533
  61.5 8.7 %collective-permute-start.27 = (f32[264,128]{1,0:T(8,128)S(1)}, f32[264,128]{1,0:T(8,128)S(1)}, u32[]{:S(2)}, u32[]{:S(2)}) collective-permute-start(f32[264,128]{1,0:T(8,128)S(1)} %get-tuple-element.107), channel_id=1, source_target_pairs={{0,6},{2,4},{4,2},{6,0},{8,14},{10,12},{12,10},{14,8},{16,22},{18,... | collective-permute-start | bytes 405512 | tf_op jit(solution)/shard_map/ppermute | solution.py:533
  63.1 7.2 %collective-permute-start.28 = (f32[264,128]{1,0:T(8,128)S(1)}, f32[264,128]{1,0:T(8,128)S(1)}, u32[]{:S(2)}, u32[]{:S(2)}) collective-permute-start(f32[264,128]{1,0:T(8,128)S(1)} %get-tuple-element.108), channel_id=1, source_target_pairs={{0,4},{2,6},{4,0},{6,2},{8,12},{10,14},{12,8},{14,10},{16,20},{18,... | collective-permute-start | bytes 405512 | tf_op jit(solution)/shard_map/ppermute | solution.py:533
  64.1 6.2 %collective-permute-start.29 = (f32[264,128]{1,0:T(8,128)S(1)}, f32[264,128]{1,0:T(8,128)S(1)}, u32[]{:S(2)}, u32[]{:S(2)}) collective-permute-start(f32[264,128]{1,0:T(8,128)S(1)} %get-tuple-element.109), channel_id=1, source_target_pairs={{0,2},{2,0},{4,6},{6,4},{8,10},{10,8},{12,14},{14,12},{16,18},{18,... | collective-permute-start | bytes 405512 | tf_op jit(solution)/shard_map/ppermute | solution.py:533

commit v9 on v8

--- a/solution.py
+++ b/solution.py
@@ -331,6 +331,11 @@
         group = partners()
         mark = mark_ref[...]
         behind = steps_if(mark == states[0][size.state : size.state + 1, :], position(size) + 1.0)
+        if before:
+            for c in range(GROUP):
+                for h in range(wave * size.each):
+                    here = columns(size, group[c], h)
+                    outs[0][:, here] = earlier[0][:, here]
         square = earlier[1][...] if before else jnp.zeros((size.rows, size.dim), f32)
         cross = earlier[2][...] if before else jnp.zeros((size.rows, size.dim), f32)
         for c in range(GROUP):

time: 72.2 us -> 72.3 us (level)
  no operation moved by 1% of the time
where the time goes in v9:
time: 72.3 us; the launch traced here: 72.1 us
  starting transfers between devices  40.2 us (56%)
  Pallas kernels  15.2 us (21%)
  waiting for transfers between devices  14.8 us (20%)
  between operations  1.02 us (1%)
  local copies, waits for them, and re-layouts  0.87 us (1%)
    ppermute x24, starting transfers between devices, swap(): lax.ppermute(array, 'seq', [(i, i ^ distance) for i in range(members)])  31.7 us
    pallas_call x18, Pallas kernels, call(): pl.pallas_call(body, out_shape=outputs, in_specs=in_specs if in_specs is...  15.2 us
    ppermute x24, waiting for transfers between devices, swap(): lax.ppermute(array, 'seq', [(i, i ^ distance) for i in range(members)])  11.2 us
    ppermute x5, starting transfers between devices, cyclic(): lax.ppermute(array, 'seq', [(i, (i + by) % members) for i in range(member...  8.45 us
    ppermute x5, waiting for transfers between devices, cyclic(): lax.ppermute(array, 'seq', [(i, (i + by) % members) for i in range(member...  2.43 us
  transfers between devices with their start and end apart: 30, of which 16 were waited for; matrix products, arithmetic and copies ran while one was open for 0% of the time, Pallas kernels for 14%

profile of v9, /device:TPU:0, one launch (start us, length us, event | category | flops | bytes accessed | tf_op | source)
XLA Modules:
  0.0 72.1 jit_solution(2790997213700840522)
XLA Ops:
  0.7 2.2 %states.2 = (f32[264,128]{1,0:T(8,128)}, f32[264,128]{1,0:T(8,128)}, f32[264,128]{1,0:T(8,128)}, f32[128,128]{1,0:T(8,128)}, f32[16,128]{1,0:T(8,128)}) custom-call(s32[1,128]{1,0:T(1,128)} %bitcast.9, f32[1,16]{1,0:T(1,128)} %bitcast.10, bf16[128,2048]{1,0:T(8,128)(2,1)} %key_ref.7, bf16[128,2048]{1,0:T(8,128)(2,1)} %value_ref.7), custom_call_target="tpu_custom_call" | custom-call | flops 50331648 | bytes 786432 | tf_op jit(solution)/shard_map/states/pallas_call | solution.py:124
  2.8 3.0 %collective-permute-start.7 = (f32[264,128]{1,0:T(8,128)}, f32[264,128]{1,0:T(8,128)S(1)}, u32[]{:S(2)}, u32[]{:S(2)}) collective-permute-start(f32[264,128]{1,0:T(8,128)} %get-tuple-element.70), channel_id=1, source_target_pairs={{0,2},{2,0},{4,6},{6,4},{8,10},{10,8},{12,14},{14,12},{16,18},{18,... | collective-permute-start | bytes 405512 | tf_op jit(solution)/shard_map/ppermute | solution.py:538
  5.8 1.5 %collective-permute-start.8 = (f32[264,128]{1,0:T(8,128)}, f32[264,128]{1,0:T(8,128)S(1)}, u32[]{:S(2)}, u32[]{:S(2)}) collective-permute-start(f32[264,128]{1,0:T(8,128)} %get-tuple-element.71), channel_id=1, source_target_pairs={{0,4},{2,6},{4,0},{6,2},{8,12},{10,14},{12,8},{14,10},{16,20},{18,... | collective-permute-start | bytes 405512 | tf_op jit(solution)/shard_map/ppermute | solution.py:538
  7.4 0.8 %copy-done.4 = f32[128,128]{1,0:T(8,128)S(1)} copy-done((f32[128,128]{1,0:T(8,128)S(1)}, f32[128,128]{1,0:T(8,128)}, u32[]{:S(2)}) %copy-start.4) | copy-done | bytes 65560
  8.6 2.0 %collective-permute-start = (f32[264,128]{1,0:T(8,128)S(1)}, f32[264,128]{1,0:T(8,128)S(1)}, u32[]{:S(2)}, u32[]{:S(2)}) collective-permute-start(f32[264,128]{1,0:T(8,128)S(1)} %get-tuple-element.62), channel_id=1, source_target_pairs={{0,2},{2,0},{4,6},{6,4},{8,10},{10,8},{12,14},{14,12},{16,18},{18,... | collective-permute-start | bytes 405512 | tf_op jit(solution)/shard_map/ppermute | solution.py:538
  10.7 1.5 %collective-permute-start.1 = (f32[264,128]{1,0:T(8,128)S(1)}, f32[264,128]{1,0:T(8,128)S(1)}, u32[]{:S(2)}, u32[]{:S(2)}) collective-permute-start(f32[264,128]{1,0:T(8,128)S(1)} %get-tuple-element.63), channel_id=1, source_target_pairs={{0,4},{2,6},{4,0},{6,2},{8,12},{10,14},{12,8},{14,10},{16,20},{18,... | collective-permute-start | bytes 405512 | tf_op jit(solution)/shard_map/ppermute | solution.py:538
  12.2 1.3 %collective-permute-start.2 = (f32[264,128]{1,0:T(8,128)S(1)}, f32[264,128]{1,0:T(8,128)S(1)}, u32[]{:S(2)}, u32[]{:S(2)}) collective-permute-start(f32[264,128]{1,0:T(8,128)S(1)} %get-tuple-element.64), channel_id=1, source_target_pairs={{0,6},{2,4},{4,2},{6,0},{8,14},{10,12},{12,10},{14,8},{16,22},{18,... | collective-permute-start | bytes 405512 | tf_op jit(solution)/shard_map/ppermute | solution.py:538
  13.5 1.1 %collective-permute-done.8.refs_2_ = f32[264,128]{1,0:T(8,128)S(1)} collective-permute-done((f32[264,128]{1,0:T(8,128)}, f32[264,128]{1,0:T(8,128)S(1)}, u32[]{:S(2)}, u32[]{:S(2)}) %collective-permute-start.8) | collective-permute-done | bytes 135200 | tf_op jit(solution)/shard_map/ppermute | solution.py:538
  14.6 0.5 collective-permute-done.9.refs_3_
  15.1 1.6 %collective-permute-start.10 = (f32[264,128]{1,0:T(8,128)S(1)}, f32[264,128]{1,0:T(8,128)S(1)}, u32[]{:S(2)}, u32[]{:S(2)}) collective-permute-start(f32[264,128]{1,0:T(8,128)S(1)} %total.5), channel_id=1, source_target_pairs={{0,8},{2,10},{4,12},{6,14},{8,16},{10,18},{12,20},{14,22},{16,24},... | collective-permute-start | bytes 405512 | tf_op jit(solution)/shard_map/ppermute | solution.py:553
  16.9 2.9 %collective-permute-done.1.refs_2_ = f32[264,128]{1,0:T(8,128)S(1)} collective-permute-done((f32[264,128]{1,0:T(8,128)S(1)}, f32[264,128]{1,0:T(8,128)S(1)}, u32[]{:S(2)}, u32[]{:S(2)}) %collective-permute-start.1) | collective-permute-done | bytes 135200 | tf_op jit(solution)/shard_map/ppermute | solution.py:538
  19.9 1.6 %collective-permute-start.3 = (f32[264,128]{1,0:T(8,128)S(1)}, f32[264,128]{1,0:T(8,128)S(1)}, u32[]{:S(2)}, u32[]{:S(2)}) collective-permute-start(f32[264,128]{1,0:T(8,128)S(1)} %total.4), channel_id=1, source_target_pairs={{0,8},{2,10},{4,12},{6,14},{8,16},{10,18},{12,20},{14,22},{16,24},... | collective-permute-start | bytes 405512 | tf_op jit(solution)/shard_map/ppermute | solution.py:553
  21.5 0.5 collective-permute-done.10.refs_4_
  22.2 1.4 %collective-permute-start.11 = (f32[256,128]{1,0:T(8,128)S(1)}, f32[256,128]{1,0:T(8,128)S(1)}, u32[]{:S(2)}, u32[]{:S(2)}) collective-permute-start(f32[256,128]{1,0:T(8,128)S(1)} %get-tuple-element.74), channel_id=1, source_target_pairs={{0,2},{2,0},{4,6},{6,4},{8,10},{10,8},{12,14},{14,12},{16,18},{18,... | collective-permute-start | bytes 393224 | tf_op jit(solution)/shard_map/ppermute | solution.py:538
  23.6 1.2 %collective-permute-start.12 = (f32[256,128]{1,0:T(8,128)S(1)}, f32[256,128]{1,0:T(8,128)S(1)}, u32[]{:S(2)}, u32[]{:S(2)}) collective-permute-start(f32[256,128]{1,0:T(8,128)S(1)} %get-tuple-element.75), channel_id=1, source_target_pairs={{0,4},{2,6},{4,0},{6,2},{8,12},{10,14},{12,8},{14,10},{16,20},{18,... | collective-permute-start | bytes 393224 | tf_op jit(solution)/shard_map/ppermute | solution.py:538
  24.7 1.4 %collective-permute-start.13 = (f32[256,128]{1,0:T(8,128)S(1)}, f32[256,128]{1,0:T(8,128)S(1)}, u32[]{:S(2)}, u32[]{:S(2)}) collective-permute-start(f32[256,128]{1,0:T(8,128)S(1)} %get-tuple-element.76), channel_id=1, source_target_pairs={{0,6},{2,4},{4,2},{6,0},{8,14},{10,12},{12,10},{14,8},{16,22},{18,... | collective-permute-start | bytes 393224 | tf_op jit(solution)/shard_map/ppermute | solution.py:538
  26.1 0.6 collective-permute-done.3.refs_4_
  26.9 1.3 %collective-permute-start.4 = (f32[256,128]{1,0:T(8,128)S(1)}, f32[256,128]{1,0:T(8,128)S(1)}, u32[]{:S(2)}, u32[]{:S(2)}) collective-permute-start(f32[256,128]{1,0:T(8,128)S(1)} %get-tuple-element.66), channel_id=1, source_target_pairs={{0,2},{2,0},{4,6},{6,4},{8,10},{10,8},{12,14},{14,12},{16,18},{18,... | collective-permute-start | bytes 393224 | tf_op jit(solution)/shard_map/ppermute | solution.py:538
  28.2 0.8 %collective-permute-start.5 = (f32[256,128]{1,0:T(8,128)S(1)}, f32[256,128]{1,0:T(8,128)S(1)}, u32[]{:S(2)}, u32[]{:S(2)}) collective-permute-start(f32[256,128]{1,0:T(8,128)S(1)} %get-tuple-element.67), channel_id=1, source_target_pairs={{0,4},{2,6},{4,0},{6,2},{8,12},{10,14},{12,8},{14,10},{16,20},{18,... | collective-permute-start | bytes 393224 | tf_op jit(solution)/shard_map/ppermute | solution.py:538
  29.1 1.4 %collective-permute-start.6 = (f32[256,128]{1,0:T(8,128)S(1)}, f32[256,128]{1,0:T(8,128)S(1)}, u32[]{:S(2)}, u32[]{:S(2)}) collective-permute-start(f32[256,128]{1,0:T(8,128)S(1)} %get-tuple-element.68), channel_id=1, source_target_pairs={{0,6},{2,4},{4,2},{6,0},{8,14},{10,12},{12,10},{14,8},{16,22},{18,... | collective-permute-start | bytes 393224 | tf_op jit(solution)/shard_map/ppermute | solution.py:538
  30.5 2.7 %nearby.1.near_ref = f32[128,2048]{1,0:T(8,128)S(1)} custom-call(f32[128,128]{1,0:T(8,128)S(1)} %copy-done.5, f32[16,128]{1,0:T(8,128)S(1)} %copy-done.6, bf16[128,2048]{1,0:T(8,128)(2,1)S(1)} %copy-done, bf16[128,2048]{1,0:T(8,128)(2,1)S(1)} %copy-done.2, bf16[128,2048]{1,0:T(8,128)(2,1)S(1)} %copy-done.3), custom_call_target="tpu_custom_call" | custom-call | flops 201326592 | bytes 2621440 | tf_op jit(solution)/shard_map/nearby/pallas_call | solution.py:124
  33.6 1.0 %collective-permute-done.5.refs_2_.refs_14_ = f32[256,128]{1,0:T(8,128)S(1)} collective-permute-done((f32[256,128]{1,0:T(8,128)S(1)}, f32[256,128]{1,0:T(8,128)S(1)}, u32[]{:S(2)}, u32[]{:S(2)}) %collective-permute-start.5) | collective-permute-done | bytes 131104 | tf_op jit(solution)/shard_map/ppermute | solution.py:538
  34.7 1.4 %collective-permute-done.6.refs_3_.refs_15_ = f32[256,128]{1,0:T(8,128)S(1)} collective-permute-done((f32[256,128]{1,0:T(8,128)S(1)}, f32[256,128]{1,0:T(8,128)S(1)}, u32[]{:S(2)}, u32[]{:S(2)}) %collective-permute-start.6) | collective-permute-done | bytes 131104 | tf_op jit(solution)/shard_map/ppermute | solution.py:538
  36.1 0.6 attended.3
  36.7 1.2 %collective-permute-done.14.refs_1_ = f32[8,128]{1,0:T(8,128)S(1)} collective-permute-done((f32[8,128]{1,0:T(8,128)S(1)}, f32[8,128]{1,0:T(8,128)S(1)}, u32[]{:S(2)}, u32[]{:S(2)}) %collective-permute-start.14) | collective-permute-done | bytes 4128 | tf_op jit(solution)/shard_map/ppermute | solution.py:611
  37.9 0.6 back.4
  38.4 1.3 %collective-permute-start.15 = (f32[264,128]{1,0:T(8,128)S(1)}, f32[264,128]{1,0:T(8,128)S(1)}, u32[]{:S(2)}, u32[]{:S(2)}) collective-permute-start(f32[264,128]{1,0:T(8,128)S(1)} %get-tuple-element.94), channel_id=1, source_target_pairs={{0,2},{2,0},{4,6},{6,4},{8,10},{10,8},{12,14},{14,12},{16,18},{18,... | collective-permute-start | bytes 405512 | tf_op jit(solution)/shard_map/ppermute | solution.py:538
  39.7 1.4 %collective-permute-start.16 = (f32[264,128]{1,0:T(8,128)S(1)}, f32[264,128]{1,0:T(8,128)S(1)}, u32[]{:S(2)}, u32[]{:S(2)}) collective-permute-start(f32[264,128]{1,0:T(8,128)S(1)} %get-tuple-element.95), channel_id=1, source_target_pairs={{0,4},{2,6},{4,0},{6,2},{8,12},{10,14},{12,8},{14,10},{16,20},{18,... | collective-permute-start | bytes 405512 | tf_op jit(solution)/shard_map/ppermute | solution.py:538
  41.1 0.9 %collective-permute-start.17 = (f32[264,128]{1,0:T(8,128)S(1)}, f32[264,128]{1,0:T(8,128)S(1)}, u32[]{:S(2)}, u32[]{:S(2)}) collective-permute-start(f32[264,128]{1,0:T(8,128)S(1)} %get-tuple-element.96), channel_id=1, source_target_pairs={{0,6},{2,4},{4,2},{6,0},{8,14},{10,12},{12,10},{14,8},{16,22},{18,... | collective-permute-start | bytes 405512 | tf_op jit(solution)/shard_map/ppermute | solution.py:538
  42.0 0.5 back.5
  42.5 1.3 %collective-permute-start.22 = (f32[264,128]{1,0:T(8,128)S(1)}, f32[264,128]{1,0:T(8,128)S(1)}, u32[]{:S(2)}, u32[]{:S(2)}) collective-permute-start(f32[264,128]{1,0:T(8,128)S(1)} %get-tuple-element.103), channel_id=1, source_target_pairs={{0,2},{2,0},{4,6},{6,4},{8,10},{10,8},{12,14},{14,12},{16,18},{18,... | collective-permute-start | bytes 405512 | tf_op jit(solution)/shard_map/ppermute | solution.py:538
  43.7 1.4 %collective-permute-start.23 = (f32[264,128]{1,0:T(8,128)S(1)}, f32[264,128]{1,0:T(8,128)S(1)}, u32[]{:S(2)}, u32[]{:S(2)}) collective-permute-start(f32[264,128]{1,0:T(8,128)S(1)} %get-tuple-element.104), channel_id=1, source_target_pairs={{0,4},{2,6},{4,0},{6,2},{8,12},{10,14},{12,8},{14,10},{16,20},{18,... | collective-permute-start | bytes 405512 | tf_op jit(solution)/shard_map/ppermute | solution.py:538
  45.1 1.8 %collective-permute-start.24 = (f32[264,128]{1,0:T(8,128)S(1)}, f32[264,128]{1,0:T(8,128)S(1)}, u32[]{:S(2)}, u32[]{:S(2)}) collective-permute-start(f32[264,128]{1,0:T(8,128)S(1)} %get-tuple-element.105), channel_id=1, source_target_pairs={{0,6},{2,4},{4,2},{6,0},{8,14},{10,12},{12,10},{14,8},{16,22},{18,... | collective-permute-start | bytes 405512 | tf_op jit(solution)/shard_map/ppermute | solution.py:538
  47.0 0.4 back.3
  47.4 0.8 %collective-permute-done.16.refs_2_ = f32[264,128]{1,0:T(8,128)S(1)} collective-permute-done((f32[264,128]{1,0:T(8,128)S(1)}, f32[264,128]{1,0:T(8,128)S(1)}, u32[]{:S(2)}, u32[]{:S(2)}) %collective-permute-start.16) | collective-permute-done | bytes 135200 | tf_op jit(solution)/shard_map/ppermute | solution.py:538
  48.6 2.0 %collective-permute-start.18 = (f32[264,128]{1,0:T(8,128)S(1)}, f32[264,128]{1,0:T(8,128)S(1)}, u32[]{:S(2)}, u32[]{:S(2)}) collective-permute-start(f32[264,128]{1,0:T(8,128)S(1)} %get-tuple-element.97), channel_id=1, source_target_pairs={{0,24},{2,26},{4,28},{6,30},{8,0},{10,2},{12,4},{14,6},{16,8},{18,... | collective-permute-start | bytes 405512 | tf_op jit(solution)/shard_map/ppermute | solution.py:553
  50.6 0.8 %collective-permute-start.25 = (f32[8,128]{1,0:T(8,128)S(1)}, f32[8,128]{1,0:T(8,128)S(1)}, u32[]{:S(2)}, u32[]{:S(2)}) collective-permute-start(f32[8,128]{1,0:T(8,128)S(1)} %get-tuple-element.106.refs_4_), channel_id=1, source_target_pairs={{0,16},{2,18},{4,20},{6,22},{8,24},{10,26},{12,28},{14,30},{16,0},... | collective-permute-start | bytes 12296 | tf_op jit(solution)/shard_map/ppermute | solution.py:553
  51.4 2.4 %collective-permute-done.23.refs_2_ = f32[264,128]{1,0:T(8,128)S(1)} collective-permute-done((f32[264,128]{1,0:T(8,128)S(1)}, f32[264,128]{1,0:T(8,128)S(1)}, u32[]{:S(2)}, u32[]{:S(2)}) %collective-permute-start.23) | collective-permute-done | bytes 135200 | tf_op jit(solution)/shard_map/ppermute | solution.py:538
  53.8 1.3 %collective-permute-done.25.refs_5_ = f32[8,128]{1,0:T(8,128)S(1)} collective-permute-done((f32[8,128]{1,0:T(8,128)S(1)}, f32[8,128]{1,0:T(8,128)S(1)}, u32[]{:S(2)}, u32[]{:S(2)}) %collective-permute-start.25) | collective-permute-done | bytes 4128 | tf_op jit(solution)/shard_map/ppermute | solution.py:553
  55.2 2.4 %collective-permute-start.26 = (f32[264,128]{1,0:T(8,128)S(1)}, f32[264,128]{1,0:T(8,128)S(1)}, u32[]{:S(2)}, u32[]{:S(2)}) collective-permute-start(f32[264,128]{1,0:T(8,128)S(1)} %total.7.refs_5_), channel_id=1, source_target_pairs={{0,24},{2,26},{4,28},{6,30},{8,0},{10,2},{12,4},{14,6},{16,8},{18,... | collective-permute-start | bytes 405512 | tf_op jit(solution)/shard_map/ppermute | solution.py:553
  57.8 0.8 %collective-permute-start.19 = (f32[264,128]{1,0:T(8,128)S(1)}, f32[264,128]{1,0:T(8,128)S(1)}, u32[]{:S(2)}, u32[]{:S(2)}) collective-permute-start(f32[264,128]{1,0:T(8,128)S(1)} %get-tuple-element.99), channel_id=1, source_target_pairs={{0,2},{2,0},{4,6},{6,4},{8,10},{10,8},{12,14},{14,12},{16,18},{18,... | collective-permute-start | bytes 405512 | tf_op jit(solution)/shard_map/ppermute | solution.py:538
  58.6 1.4 %collective-permute-start.20 = (f32[264,128]{1,0:T(8,128)S(1)}, f32[264,128]{1,0:T(8,128)S(1)}, u32[]{:S(2)}, u32[]{:S(2)}) collective-permute-start(f32[264,128]{1,0:T(8,128)S(1)} %get-tuple-element.100), channel_id=1, source_target_pairs={{0,4},{2,6},{4,0},{6,2},{8,12},{10,14},{12,8},{14,10},{16,20},{18,... | collective-permute-start | bytes 405512 | tf_op jit(solution)/shard_map/ppermute | solution.py:538
  60.0 1.4 %collective-permute-start.21 = (f32[264,128]{1,0:T(8,128)S(1)}, f32[264,128]{1,0:T(8,128)S(1)}, u32[]{:S(2)}, u32[]{:S(2)}) collective-permute-start(f32[264,128]{1,0:T(8,128)S(1)} %get-tuple-element.101), channel_id=1, source_target_pairs={{0,6},{2,4},{4,2},{6,0},{8,14},{10,12},{12,10},{14,8},{16,22},{18,... | collective-permute-start | bytes 405512 | tf_op jit(solution)/shard_map/ppermute | solution.py:538
  61.6 1.6 %collective-permute-start.27 = (f32[264,128]{1,0:T(8,128)S(1)}, f32[264,128]{1,0:T(8,128)S(1)}, u32[]{:S(2)}, u32[]{:S(2)}) collective-permute-start(f32[264,128]{1,0:T(8,128)S(1)} %get-tuple-element.107), channel_id=1, source_target_pairs={{0,6},{2,4},{4,2},{6,0},{8,14},{10,12},{12,10},{14,8},{16,22},{18,... | collective-permute-start | bytes 405512 | tf_op jit(solution)/shard_map/ppermute | solution.py:538
  63.2 0.7 collective-permute-start.28
  64.2 0.9 %collective-permute-start.29 = (f32[264,128]{1,0:T(8,128)S(1)}, f32[264,128]{1,0:T(8,128)S(1)}, u32[]{:S(2)}, u32[]{:S(2)}) collective-permute-start(f32[264,128]{1,0:T(8,128)S(1)} %get-tuple-element.109), channel_id=1, source_target_pairs={{0,2},{2,0},{4,6},{6,4},{8,10},{10,8},{12,14},{14,12},{16,18},{18,... | collective-permute-start | bytes 405512 | tf_op jit(solution)/shard_map/ppermute | solution.py:538
  65.1 5.1 %gradients.1 = (bf16[128,2048]{1,0:T(8,128)(2,1)}, f32[128,2048]{1,0:T(8,128)S(1)}, f32[128,2048]{1,0:T(8,128)S(1)}) custom-call(f32[128,128]{1,0:T(8,128)S(1)} %copy-done.5, f32[16,128]{1,0:T(8,128)S(1)} %copy-done.6, bf16[128,2048]{1,0:T(8,128)(2,1)S(1)} %copy-done, bf16[128,2048]{1,0:T(8,128)(2,1)S(1)} %copy-done.2, bf16[128,2048]{1,0:T(8,128)(2,1)S(1)} %copy-done.3, ...), custom_call_target="tpu_custom_call" | custom-call | flops 872415232 | bytes 6291456 | tf_op jit(solution)/shard_map/gradients/pallas_call | solution.py:124
  70.4 1.5 %final.1 = (bf16[128,2048]{1,0:T(8,128)(2,1)}, bf16[128,2048]{1,0:T(8,128)(2,1)}, f32[1,2048]{1,0:T(1,128)}) custom-call(f32[128,128]{1,0:T(8,128)S(1)} %copy-done.5, f32[16,128]{1,0:T(8,128)S(1)} %copy-done.6, bf16[128,2048]{1,0:T(8,128)(2,1)S(1)} %copy-done.2, bf16[128,2048]{1,0:T(8,128)(2,1)S(1)} %copy-done.3, ...), custom_call_target="tpu_custom_call" | custom-call | flops 268435456 | bytes 6291456 | tf_op jit(solution)/shard_map/final/pallas_call | solution.py:124
  (46 shorter events, 3.1 us)
Async XLA Ops:
  0.6 6.8 %copy-start.2 = (bf16[128,2048]{1,0:T(8,128)(2,1)S(1)}, bf16[128,2048]{1,0:T(8,128)(2,1)}, u32[]{:S(2)}) copy-start(bf16[128,2048]{1,0:T(8,128)(2,1)} %key_ref.7) | copy-start | bytes 1572868
  0.6 6.7 %copy-start.3 = (bf16[128,2048]{1,0:T(8,128)(2,1)S(1)}, bf16[128,2048]{1,0:T(8,128)(2,1)}, u32[]{:S(2)}) copy-start(bf16[128,2048]{1,0:T(8,128)(2,1)} %value_ref.7) | copy-start | bytes 1572868
  2.8 4.6 %copy-start.6 = (f32[16,128]{1,0:T(8,128)S(1)}, f32[16,128]{1,0:T(8,128)}, u32[]{:S(2)}) copy-start(f32[16,128]{1,0:T(8,128)} %get-tuple-element.60.rates_ref) | copy-start | bytes 24580
  2.8 9.3 %collective-permute-start.7 = (f32[264,128]{1,0:T(8,128)}, f32[264,128]{1,0:T(8,128)S(1)}, u32[]{:S(2)}, u32[]{:S(2)}) collective-permute-start(f32[264,128]{1,0:T(8,128)} %get-tuple-element.70), channel_id=1, source_target_pairs={{0,2},{2,0},{4,6},{6,4},{8,10},{10,8},{12,14},{14,12},{16,18},{18,... | collective-permute-start | bytes 405512 | tf_op jit(solution)/shard_map/ppermute | solution.py:538
  5.8 8.7 %collective-permute-start.8 = (f32[264,128]{1,0:T(8,128)}, f32[264,128]{1,0:T(8,128)S(1)}, u32[]{:S(2)}, u32[]{:S(2)}) collective-permute-start(f32[264,128]{1,0:T(8,128)} %get-tuple-element.71), channel_id=1, source_target_pairs={{0,4},{2,6},{4,0},{6,2},{8,12},{10,14},{12,8},{14,10},{16,20},{18,... | collective-permute-start | bytes 405512 | tf_op jit(solution)/shard_map/ppermute | solution.py:538
  7.4 7.7 %collective-permute-start.9 = (f32[264,128]{1,0:T(8,128)}, f32[264,128]{1,0:T(8,128)S(1)}, u32[]{:S(2)}, u32[]{:S(2)}) collective-permute-start(f32[264,128]{1,0:T(8,128)} %get-tuple-element.72), channel_id=1, source_target_pairs={{0,6},{2,4},{4,2},{6,0},{8,14},{10,12},{12,10},{14,8},{16,22},{18,... | collective-permute-start | bytes 405512 | tf_op jit(solution)/shard_map/ppermute | solution.py:538
  7.4 0.8 %copy-start.4 = (f32[128,128]{1,0:T(8,128)S(1)}, f32[128,128]{1,0:T(8,128)}, u32[]{:S(2)}) copy-start(f32[128,128]{1,0:T(8,128)} %get-tuple-element.59.mark_ref) | copy-start | bytes 196612
  8.6 8.3 %collective-permute-start = (f32[264,128]{1,0:T(8,128)S(1)}, f32[264,128]{1,0:T(8,128)S(1)}, u32[]{:S(2)}, u32[]{:S(2)}) collective-permute-start(f32[264,128]{1,0:T(8,128)S(1)} %get-tuple-element.62), channel_id=1, source_target_pairs={{0,2},{2,0},{4,6},{6,4},{8,10},{10,8},{12,14},{14,12},{16,18},{18,... | collective-permute-start | bytes 405512 | tf_op jit(solution)/shard_map/ppermute | solution.py:538
  10.7 9.1 %collective-permute-start.1 = (f32[264,128]{1,0:T(8,128)S(1)}, f32[264,128]{1,0:T(8,128)S(1)}, u32[]{:S(2)}, u32[]{:S(2)}) collective-permute-start(f32[264,128]{1,0:T(8,128)S(1)} %get-tuple-element.63), channel_id=1, source_target_pairs={{0,4},{2,6},{4,0},{6,2},{8,12},{10,14},{12,8},{14,10},{16,20},{18,... | collective-permute-start | bytes 405512 | tf_op jit(solution)/shard_map/ppermute | solution.py:538
  12.2 7.6 %collective-permute-start.2 = (f32[264,128]{1,0:T(8,128)S(1)}, f32[264,128]{1,0:T(8,128)S(1)}, u32[]{:S(2)}, u32[]{:S(2)}) collective-permute-start(f32[264,128]{1,0:T(8,128)S(1)} %get-tuple-element.64), channel_id=1, source_target_pairs={{0,6},{2,4},{4,2},{6,0},{8,14},{10,12},{12,10},{14,8},{16,22},{18,... | collective-permute-start | bytes 405512 | tf_op jit(solution)/shard_map/ppermute | solution.py:538
  15.1 6.9 %collective-permute-start.10 = (f32[264,128]{1,0:T(8,128)S(1)}, f32[264,128]{1,0:T(8,128)S(1)}, u32[]{:S(2)}, u32[]{:S(2)}) collective-permute-start(f32[264,128]{1,0:T(8,128)S(1)} %total.5), channel_id=1, source_target_pairs={{0,8},{2,10},{4,12},{6,14},{8,16},{10,18},{12,20},{14,22},{16,24},... | collective-permute-start | bytes 405512 | tf_op jit(solution)/shard_map/ppermute | solution.py:553
  19.9 10.6 %copy-start = (bf16[128,2048]{1,0:T(8,128)(2,1)S(1)}, bf16[128,2048]{1,0:T(8,128)(2,1)}, u32[]{:S(2)}) copy-start(bf16[128,2048]{1,0:T(8,128)(2,1)} %query_ref.13) | copy-start | bytes 1572868
  19.9 6.9 %collective-permute-start.3 = (f32[264,128]{1,0:T(8,128)S(1)}, f32[264,128]{1,0:T(8,128)S(1)}, u32[]{:S(2)}, u32[]{:S(2)}) collective-permute-start(f32[264,128]{1,0:T(8,128)S(1)} %total.4), channel_id=1, source_target_pairs={{0,8},{2,10},{4,12},{6,14},{8,16},{10,18},{12,20},{14,22},{16,24},... | collective-permute-start | bytes 405512 | tf_op jit(solution)/shard_map/ppermute | solution.py:553
  22.2 6.9 %collective-permute-start.11 = (f32[256,128]{1,0:T(8,128)S(1)}, f32[256,128]{1,0:T(8,128)S(1)}, u32[]{:S(2)}, u32[]{:S(2)}) collective-permute-start(f32[256,128]{1,0:T(8,128)S(1)} %get-tuple-element.74), channel_id=1, source_target_pairs={{0,2},{2,0},{4,6},{6,4},{8,10},{10,8},{12,14},{14,12},{16,18},{18,... | collective-permute-start | bytes 393224 | tf_op jit(solution)/shard_map/ppermute | solution.py:538
  23.6 9.6 %collective-permute-start.12 = (f32[256,128]{1,0:T(8,128)S(1)}, f32[256,128]{1,0:T(8,128)S(1)}, u32[]{:S(2)}, u32[]{:S(2)}) collective-permute-start(f32[256,128]{1,0:T(8,128)S(1)} %get-tuple-element.75), channel_id=1, source_target_pairs={{0,4},{2,6},{4,0},{6,2},{8,12},{10,14},{12,8},{14,10},{16,20},{18,... | collective-permute-start | bytes 393224 | tf_op jit(solution)/shard_map/ppermute | solution.py:538
  24.7 5.8 %copy-start.5 = (f32[128,128]{1,0:T(8,128)S(1)}, f32[128,128]{1,0:T(8,128)}, u32[]{:S(2)}) copy-start(f32[128,128]{1,0:T(8,128)} %get-tuple-element.59.mark_ref) | copy-start | bytes 196612
  24.7 8.5 %collective-permute-start.13 = (f32[256,128]{1,0:T(8,128)S(1)}, f32[256,128]{1,0:T(8,128)S(1)}, u32[]{:S(2)}, u32[]{:S(2)}) collective-permute-start(f32[256,128]{1,0:T(8,128)S(1)} %get-tuple-element.76), channel_id=1, source_target_pairs={{0,6},{2,4},{4,2},{6,0},{8,14},{10,12},{12,10},{14,8},{16,22},{18,... | collective-permute-start | bytes 393224 | tf_op jit(solution)/shard_map/ppermute | solution.py:538
  26.9 6.7 %collective-permute-start.4 = (f32[256,128]{1,0:T(8,128)S(1)}, f32[256,128]{1,0:T(8,128)S(1)}, u32[]{:S(2)}, u32[]{:S(2)}) collective-permute-start(f32[256,128]{1,0:T(8,128)S(1)} %get-tuple-element.66), channel_id=1, source_target_pairs={{0,2},{2,0},{4,6},{6,4},{8,10},{10,8},{12,14},{14,12},{16,18},{18,... | collective-permute-start | bytes 393224 | tf_op jit(solution)/shard_map/ppermute | solution.py:538
  28.2 6.4 %collective-permute-start.5 = (f32[256,128]{1,0:T(8,128)S(1)}, f32[256,128]{1,0:T(8,128)S(1)}, u32[]{:S(2)}, u32[]{:S(2)}) collective-permute-start(f32[256,128]{1,0:T(8,128)S(1)} %get-tuple-element.67), channel_id=1, source_target_pairs={{0,4},{2,6},{4,0},{6,2},{8,12},{10,14},{12,8},{14,10},{16,20},{18,... | collective-permute-start | bytes 393224 | tf_op jit(solution)/shard_map/ppermute | solution.py:538
  29.1 4.1 %copy-start.1 = (bf16[128,2048]{1,0:T(8,128)(2,1)S(1)}, bf16[128,2048]{1,0:T(8,128)(2,1)}, u32[]{:S(2)}) copy-start(bf16[128,2048]{1,0:T(8,128)(2,1)} %grad_ref.9) | copy-start | bytes 1572868
  29.1 7.0 %collective-permute-start.6 = (f32[256,128]{1,0:T(8,128)S(1)}, f32[256,128]{1,0:T(8,128)S(1)}, u32[]{:S(2)}, u32[]{:S(2)}) collective-permute-start(f32[256,128]{1,0:T(8,128)S(1)} %get-tuple-element.68), channel_id=1, source_target_pairs={{0,6},{2,4},{4,2},{6,0},{8,14},{10,12},{12,10},{14,8},{16,22},{18,... | collective-permute-start | bytes 393224 | tf_op jit(solution)/shard_map/ppermute | solution.py:538
  30.5 2.7 %copy-start.7 = (f32[2048]{0:T(1024)S(1)}, f32[2048]{0:T(1024)}, u32[]{:S(2)}) copy-start(f32[2048]{0:T(1024)} %param.12) | copy-start | bytes 24580
  36.6 1.2 %collective-permute-start.14 = (f32[8,128]{1,0:T(8,128)S(1)}, f32[8,128]{1,0:T(8,128)S(1)}, u32[]{:S(2)}, u32[]{:S(2)}) collective-permute-start(f32[8,128]{1,0:T(8,128)S(1)} %get-tuple-element.81.refs_0_), channel_id=1, source_target_pairs={{0,1},{1,0},{2,3},{3,2},{4,5},{5,4},{6,7},{7,6},{8,9},{9,8},{10,11... | collective-permute-start | bytes 12296 | tf_op jit(solution)/shard_map/ppermute | solution.py:611
  38.4 6.7 %collective-permute-start.15 = (f32[264,128]{1,0:T(8,128)S(1)}, f32[264,128]{1,0:T(8,128)S(1)}, u32[]{:S(2)}, u32[]{:S(2)}) collective-permute-start(f32[264,128]{1,0:T(8,128)S(1)} %get-tuple-element.94), channel_id=1, source_target_pairs={{0,2},{2,0},{4,6},{6,4},{8,10},{10,8},{12,14},{14,12},{16,18},{18,... | collective-permute-start | bytes 405512 | tf_op jit(solution)/shard_map/ppermute | solution.py:538
  39.7 8.5 %collective-permute-start.16 = (f32[264,128]{1,0:T(8,128)S(1)}, f32[264,128]{1,0:T(8,128)S(1)}, u32[]{:S(2)}, u32[]{:S(2)}) collective-permute-start(f32[264,128]{1,0:T(8,128)S(1)} %get-tuple-element.95), channel_id=1, source_target_pairs={{0,4},{2,6},{4,0},{6,2},{8,12},{10,14},{12,8},{14,10},{16,20},{18,... | collective-permute-start | bytes 405512 | tf_op jit(solution)/shard_map/ppermute | solution.py:538
  41.1 7.5 %collective-permute-start.17 = (f32[264,128]{1,0:T(8,128)S(1)}, f32[264,128]{1,0:T(8,128)S(1)}, u32[]{:S(2)}, u32[]{:S(2)}) collective-permute-start(f32[264,128]{1,0:T(8,128)S(1)} %get-tuple-element.96), channel_id=1, source_target_pairs={{0,6},{2,4},{4,2},{6,0},{8,14},{10,12},{12,10},{14,8},{16,22},{18,... | collective-permute-start | bytes 405512 | tf_op jit(solution)/shard_map/ppermute | solution.py:538
  42.5 8.9 %collective-permute-start.22 = (f32[264,128]{1,0:T(8,128)S(1)}, f32[264,128]{1,0:T(8,128)S(1)}, u32[]{:S(2)}, u32[]{:S(2)}) collective-permute-start(f32[264,128]{1,0:T(8,128)S(1)} %get-tuple-element.103), channel_id=1, source_target_pairs={{0,2},{2,0},{4,6},{6,4},{8,10},{10,8},{12,14},{14,12},{16,18},{18,... | collective-permute-start | bytes 405512 | tf_op jit(solution)/shard_map/ppermute | solution.py:538
  43.7 10.1 %collective-permute-start.23 = (f32[264,128]{1,0:T(8,128)S(1)}, f32[264,128]{1,0:T(8,128)S(1)}, u32[]{:S(2)}, u32[]{:S(2)}) collective-permute-start(f32[264,128]{1,0:T(8,128)S(1)} %get-tuple-element.104), channel_id=1, source_target_pairs={{0,4},{2,6},{4,0},{6,2},{8,12},{10,14},{12,8},{14,10},{16,20},{18,... | collective-permute-start | bytes 405512 | tf_op jit(solution)/shard_map/ppermute | solution.py:538
  45.1 8.7 %collective-permute-start.24 = (f32[264,128]{1,0:T(8,128)S(1)}, f32[264,128]{1,0:T(8,128)S(1)}, u32[]{:S(2)}, u32[]{:S(2)}) collective-permute-start(f32[264,128]{1,0:T(8,128)S(1)} %get-tuple-element.105), channel_id=1, source_target_pairs={{0,6},{2,4},{4,2},{6,0},{8,14},{10,12},{12,10},{14,8},{16,22},{18,... | collective-permute-start | bytes 405512 | tf_op jit(solution)/shard_map/ppermute | solution.py:538
  48.6 9.0 %collective-permute-start.18 = (f32[264,128]{1,0:T(8,128)S(1)}, f32[264,128]{1,0:T(8,128)S(1)}, u32[]{:S(2)}, u32[]{:S(2)}) collective-permute-start(f32[264,128]{1,0:T(8,128)S(1)} %get-tuple-element.97), channel_id=1, source_target_pairs={{0,24},{2,26},{4,28},{6,30},{8,0},{10,2},{12,4},{14,6},{16,8},{18,... | collective-permute-start | bytes 405512 | tf_op jit(solution)/shard_map/ppermute | solution.py:553
  50.6 4.5 %collective-permute-start.25 = (f32[8,128]{1,0:T(8,128)S(1)}, f32[8,128]{1,0:T(8,128)S(1)}, u32[]{:S(2)}, u32[]{:S(2)}) collective-permute-start(f32[8,128]{1,0:T(8,128)S(1)} %get-tuple-element.106.refs_4_), channel_id=1, source_target_pairs={{0,16},{2,18},{4,20},{6,22},{8,24},{10,26},{12,28},{14,30},{16,0},... | collective-permute-start | bytes 12296 | tf_op jit(solution)/shard_map/ppermute | solution.py:553
  55.2 6.2 %collective-permute-start.26 = (f32[264,128]{1,0:T(8,128)S(1)}, f32[264,128]{1,0:T(8,128)S(1)}, u32[]{:S(2)}, u32[]{:S(2)}) collective-permute-start(f32[264,128]{1,0:T(8,128)S(1)} %total.7.refs_5_), channel_id=1, source_target_pairs={{0,24},{2,26},{4,28},{6,30},{8,0},{10,2},{12,4},{14,6},{16,8},{18,... | collective-permute-start | bytes 405512 | tf_op jit(solution)/shard_map/ppermute | solution.py:553
  57.8 6.4 %collective-permute-start.19 = (f32[264,128]{1,0:T(8,128)S(1)}, f32[264,128]{1,0:T(8,128)S(1)}, u32[]{:S(2)}, u32[]{:S(2)}) collective-permute-start(f32[264,128]{1,0:T(8,128)S(1)} %get-tuple-element.99), channel_id=1, source_target_pairs={{0,2},{2,0},{4,6},{6,4},{8,10},{10,8},{12,14},{14,12},{16,18},{18,... | collective-permute-start | bytes 405512 | tf_op jit(solution)/shard_map/ppermute | solution.py:538
  58.6 11.6 %collective-permute-start.20 = (f32[264,128]{1,0:T(8,128)S(1)}, f32[264,128]{1,0:T(8,128)S(1)}, u32[]{:S(2)}, u32[]{:S(2)}) collective-permute-start(f32[264,128]{1,0:T(8,128)S(1)} %get-tuple-element.100), channel_id=1, source_target_pairs={{0,4},{2,6},{4,0},{6,2},{8,12},{10,14},{12,8},{14,10},{16,20},{18,... | collective-permute-start | bytes 405512 | tf_op jit(solution)/shard_map/ppermute | solution.py:538
  60.0 10.3 %collective-permute-start.21 = (f32[264,128]{1,0:T(8,128)S(1)}, f32[264,128]{1,0:T(8,128)S(1)}, u32[]{:S(2)}, u32[]{:S(2)}) collective-permute-start(f32[264,128]{1,0:T(8,128)S(1)} %get-tuple-element.101), channel_id=1, source_target_pairs={{0,6},{2,4},{4,2},{6,0},{8,14},{10,12},{12,10},{14,8},{16,22},{18,... | collective-permute-start | bytes 405512 | tf_op jit(solution)/shard_map/ppermute | solution.py:538
  61.6 8.7 %collective-permute-start.27 = (f32[264,128]{1,0:T(8,128)S(1)}, f32[264,128]{1,0:T(8,128)S(1)}, u32[]{:S(2)}, u32[]{:S(2)}) collective-permute-start(f32[264,128]{1,0:T(8,128)S(1)} %get-tuple-element.107), channel_id=1, source_target_pairs={{0,6},{2,4},{4,2},{6,0},{8,14},{10,12},{12,10},{14,8},{16,22},{18,... | collective-permute-start | bytes 405512 | tf_op jit(solution)/shard_map/ppermute | solution.py:538
  63.2 7.3 %collective-permute-start.28 = (f32[264,128]{1,0:T(8,128)S(1)}, f32[264,128]{1,0:T(8,128)S(1)}, u32[]{:S(2)}, u32[]{:S(2)}) collective-permute-start(f32[264,128]{1,0:T(8,128)S(1)} %get-tuple-element.108), channel_id=1, source_target_pairs={{0,4},{2,6},{4,0},{6,2},{8,12},{10,14},{12,8},{14,10},{16,20},{18,... | collective-permute-start | bytes 405512 | tf_op jit(solution)/shard_map/ppermute | solution.py:538
  64.2 6.2 %collective-permute-start.29 = (f32[264,128]{1,0:T(8,128)S(1)}, f32[264,128]{1,0:T(8,128)S(1)}, u32[]{:S(2)}, u32[]{:S(2)}) collective-permute-start(f32[264,128]{1,0:T(8,128)S(1)} %get-tuple-element.109), channel_id=1, source_target_pairs={{0,2},{2,0},{4,6},{6,4},{8,10},{10,8},{12,14},{14,12},{16,18},{18,... | collective-permute-start | bytes 405512 | tf_op jit(solution)/shard_map/ppermute | solution.py:538

commit v10 on v9

--- a/solution.py
+++ b/solution.py
@@ -328,6 +328,7 @@
 
     def body(mark_ref, rates_ref, query_ref, grad_ref, gain_ref, near_ref, *refs):
         states, earlier, outs = refs[:GROUP], refs[GROUP : GROUP + len(before)], refs[GROUP + len(before) :]
+        states = states[::-1] if last else states
         group = partners()
         mark = mark_ref[...]
         behind = steps_if(mark == states[0][size.state : size.state + 1, :], position(size) + 1.0)
@@ -361,7 +362,8 @@
         sums = [jax.ShapeDtypeStruct((8, size.rows), f32)]
     else:
         sums = [jax.ShapeDtypeStruct((size.rows, size.dim), f32)] * 2
-    inputs = (mark, rates, queries, out_grad, gain, near, *entering, *before)
+    farthest_first = entering[::-1] if last else entering
+    inputs = (mark, rates, queries, out_grad, gain, near, *farthest_first, *before)
     return call(
         body, "attended", inputs, [size.block] + sums,
         GROUP * size.each * 4 * size.rows * size.dim * size.dim, GROUP * size.state * size.rows * 16,

time: 72.3 us -> 72.3 us (level)
  no operation moved by 1% of the time
where the time goes in v10:
time: 72.3 us; the launch traced here: 72.1 us
  starting transfers between devices  40.6 us (56%)
  Pallas kernels  15.2 us (21%)
  waiting for transfers between devices  14.4 us (20%)
  between operations  1.02 us (1%)
  local copies, waits for them, and re-layouts  0.87 us (1%)
    ppermute x24, starting transfers between devices, swap(): lax.ppermute(array, 'seq', [(i, i ^ distance) for i in range(members)])  32.1 us
    pallas_call x18, Pallas kernels, call(): pl.pallas_call(body, out_shape=outputs, in_specs=in_specs if in_specs is...  15.2 us
    ppermute x24, waiting for transfers between devices, swap(): lax.ppermute(array, 'seq', [(i, i ^ distance) for i in range(members)])  10.8 us
    ppermute x5, starting transfers between devices, cyclic(): lax.ppermute(array, 'seq', [(i, (i + by) % members) for i in range(member...  8.48 us
    ppermute x5, waiting for transfers between devices, cyclic(): lax.ppermute(array, 'seq', [(i, (i + by) % members) for i in range(member...  2.43 us
  transfers between devices with their start and end apart: 30, of which 16 were waited for; matrix products, arithmetic and copies ran while one was open for 0% of the time, Pallas kernels for 14%

profile of v10, /device:TPU:0, one launch (start us, length us, event | category | flops | bytes accessed | tf_op | source)
XLA Modules:
  0.0 72.1 jit_solution(18320642304842594824)
XLA Ops:
  0.7 2.2 %states.2 = (f32[264,128]{1,0:T(8,128)}, f32[264,128]{1,0:T(8,128)}, f32[264,128]{1,0:T(8,128)}, f32[128,128]{1,0:T(8,128)}, f32[16,128]{1,0:T(8,128)}) custom-call(s32[1,128]{1,0:T(1,128)} %bitcast.9, f32[1,16]{1,0:T(1,128)} %bitcast.10, bf16[128,2048]{1,0:T(8,128)(2,1)} %key_ref.7, bf16[128,2048]{1,0:T(8,128)(2,1)} %value_ref.7), custom_call_target="tpu_custom_call" | custom-call | flops 50331648 | bytes 786432 | tf_op jit(solution)/shard_map/states/pallas_call | solution.py:124
  2.8 3.0 %collective-permute-start.7 = (f32[264,128]{1,0:T(8,128)}, f32[264,128]{1,0:T(8,128)S(1)}, u32[]{:S(2)}, u32[]{:S(2)}) collective-permute-start(f32[264,128]{1,0:T(8,128)} %get-tuple-element.70), channel_id=1, source_target_pairs={{0,2},{2,0},{4,6},{6,4},{8,10},{10,8},{12,14},{14,12},{16,18},{18,... | collective-permute-start | bytes 405512 | tf_op jit(solution)/shard_map/ppermute | solution.py:540
  5.8 1.5 %collective-permute-start.8 = (f32[264,128]{1,0:T(8,128)}, f32[264,128]{1,0:T(8,128)S(1)}, u32[]{:S(2)}, u32[]{:S(2)}) collective-permute-start(f32[264,128]{1,0:T(8,128)} %get-tuple-element.71), channel_id=1, source_target_pairs={{0,4},{2,6},{4,0},{6,2},{8,12},{10,14},{12,8},{14,10},{16,20},{18,... | collective-permute-start | bytes 405512 | tf_op jit(solution)/shard_map/ppermute | solution.py:540
  7.4 0.8 %copy-done.4 = f32[128,128]{1,0:T(8,128)S(1)} copy-done((f32[128,128]{1,0:T(8,128)S(1)}, f32[128,128]{1,0:T(8,128)}, u32[]{:S(2)}) %copy-start.4) | copy-done | bytes 65560
  8.6 2.0 %collective-permute-start = (f32[264,128]{1,0:T(8,128)S(1)}, f32[264,128]{1,0:T(8,128)S(1)}, u32[]{:S(2)}, u32[]{:S(2)}) collective-permute-start(f32[264,128]{1,0:T(8,128)S(1)} %get-tuple-element.62), channel_id=1, source_target_pairs={{0,2},{2,0},{4,6},{6,4},{8,10},{10,8},{12,14},{14,12},{16,18},{18,... | collective-permute-start | bytes 405512 | tf_op jit(solution)/shard_map/ppermute | solution.py:540
  10.7 1.5 %collective-permute-start.1 = (f32[264,128]{1,0:T(8,128)S(1)}, f32[264,128]{1,0:T(8,128)S(1)}, u32[]{:S(2)}, u32[]{:S(2)}) collective-permute-start(f32[264,128]{1,0:T(8,128)S(1)} %get-tuple-element.63), channel_id=1, source_target_pairs={{0,4},{2,6},{4,0},{6,2},{8,12},{10,14},{12,8},{14,10},{16,20},{18,... | collective-permute-start | bytes 405512 | tf_op jit(solution)/shard_map/ppermute | solution.py:540
  12.2 1.3 %collective-permute-start.2 = (f32[264,128]{1,0:T(8,128)S(1)}, f32[264,128]{1,0:T(8,128)S(1)}, u32[]{:S(2)}, u32[]{:S(2)}) collective-permute-start(f32[264,128]{1,0:T(8,128)S(1)} %get-tuple-element.64), channel_id=1, source_target_pairs={{0,6},{2,4},{4,2},{6,0},{8,14},{10,12},{12,10},{14,8},{16,22},{18,... | collective-permute-start | bytes 405512 | tf_op jit(solution)/shard_map/ppermute | solution.py:540
  13.5 1.1 %collective-permute-done.8.refs_2_ = f32[264,128]{1,0:T(8,128)S(1)} collective-permute-done((f32[264,128]{1,0:T(8,128)}, f32[264,128]{1,0:T(8,128)S(1)}, u32[]{:S(2)}, u32[]{:S(2)}) %collective-permute-start.8) | collective-permute-done | bytes 135200 | tf_op jit(solution)/shard_map/ppermute | solution.py:540
  14.6 0.5 collective-permute-done.9.refs_3_
  15.1 1.6 %collective-permute-start.10 = (f32[264,128]{1,0:T(8,128)S(1)}, f32[264,128]{1,0:T(8,128)S(1)}, u32[]{:S(2)}, u32[]{:S(2)}) collective-permute-start(f32[264,128]{1,0:T(8,128)S(1)} %total.5), channel_id=1, source_target_pairs={{0,8},{2,10},{4,12},{6,14},{8,16},{10,18},{12,20},{14,22},{16,24},... | collective-permute-start | bytes 405512 | tf_op jit(solution)/shard_map/ppermute | solution.py:555
  16.9 2.9 %collective-permute-done.1.refs_2_ = f32[264,128]{1,0:T(8,128)S(1)} collective-permute-done((f32[264,128]{1,0:T(8,128)S(1)}, f32[264,128]{1,0:T(8,128)S(1)}, u32[]{:S(2)}, u32[]{:S(2)}) %collective-permute-start.1) | collective-permute-done | bytes 135200 | tf_op jit(solution)/shard_map/ppermute | solution.py:540
  19.9 1.6 %collective-permute-start.3 = (f32[264,128]{1,0:T(8,128)S(1)}, f32[264,128]{1,0:T(8,128)S(1)}, u32[]{:S(2)}, u32[]{:S(2)}) collective-permute-start(f32[264,128]{1,0:T(8,128)S(1)} %total.4), channel_id=1, source_target_pairs={{0,8},{2,10},{4,12},{6,14},{8,16},{10,18},{12,20},{14,22},{16,24},... | collective-permute-start | bytes 405512 | tf_op jit(solution)/shard_map/ppermute | solution.py:555
  21.5 0.5 collective-permute-done.10.refs_4_
  22.2 1.4 %collective-permute-start.11 = (f32[256,128]{1,0:T(8,128)S(1)}, f32[256,128]{1,0:T(8,128)S(1)}, u32[]{:S(2)}, u32[]{:S(2)}) collective-permute-start(f32[256,128]{1,0:T(8,128)S(1)} %get-tuple-element.74), channel_id=1, source_target_pairs={{0,2},{2,0},{4,6},{6,4},{8,10},{10,8},{12,14},{14,12},{16,18},{18,... | collective-permute-start | bytes 393224 | tf_op jit(solution)/shard_map/ppermute | solution.py:540
  23.6 1.2 %collective-permute-start.12 = (f32[256,128]{1,0:T(8,128)S(1)}, f32[256,128]{1,0:T(8,128)S(1)}, u32[]{:S(2)}, u32[]{:S(2)}) collective-permute-start(f32[256,128]{1,0:T(8,128)S(1)} %get-tuple-element.75), channel_id=1, source_target_pairs={{0,4},{2,6},{4,0},{6,2},{8,12},{10,14},{12,8},{14,10},{16,20},{18,... | collective-permute-start | bytes 393224 | tf_op jit(solution)/shard_map/ppermute | solution.py:540
  24.7 1.4 %collective-permute-start.13 = (f32[256,128]{1,0:T(8,128)S(1)}, f32[256,128]{1,0:T(8,128)S(1)}, u32[]{:S(2)}, u32[]{:S(2)}) collective-permute-start(f32[256,128]{1,0:T(8,128)S(1)} %get-tuple-element.76), channel_id=1, source_target_pairs={{0,6},{2,4},{4,2},{6,0},{8,14},{10,12},{12,10},{14,8},{16,22},{18,... | collective-permute-start | bytes 393224 | tf_op jit(solution)/shard_map/ppermute | solution.py:540
  26.1 0.6 collective-permute-done.3.refs_4_
  26.9 1.6 %collective-permute-start.4 = (f32[256,128]{1,0:T(8,128)S(1)}, f32[256,128]{1,0:T(8,128)S(1)}, u32[]{:S(2)}, u32[]{:S(2)}) collective-permute-start(f32[256,128]{1,0:T(8,128)S(1)} %get-tuple-element.65), channel_id=1, source_target_pairs={{0,6},{2,4},{4,2},{6,0},{8,14},{10,12},{12,10},{14,8},{16,22},{18,... | collective-permute-start | bytes 393224 | tf_op jit(solution)/shard_map/ppermute | solution.py:540
  28.5 1.2 %collective-permute-start.5 = (f32[256,128]{1,0:T(8,128)S(1)}, f32[256,128]{1,0:T(8,128)S(1)}, u32[]{:S(2)}, u32[]{:S(2)}) collective-permute-start(f32[256,128]{1,0:T(8,128)S(1)} %get-tuple-element.66), channel_id=1, source_target_pairs={{0,4},{2,6},{4,0},{6,2},{8,12},{10,14},{12,8},{14,10},{16,20},{18,... | collective-permute-start | bytes 393224 | tf_op jit(solution)/shard_map/ppermute | solution.py:540
  29.7 0.8 %collective-permute-start.6 = (f32[256,128]{1,0:T(8,128)S(1)}, f32[256,128]{1,0:T(8,128)S(1)}, u32[]{:S(2)}, u32[]{:S(2)}) collective-permute-start(f32[256,128]{1,0:T(8,128)S(1)} %get-tuple-element.67), channel_id=1, source_target_pairs={{0,2},{2,0},{4,6},{6,4},{8,10},{10,8},{12,14},{14,12},{16,18},{18,... | collective-permute-start | bytes 393224 | tf_op jit(solution)/shard_map/ppermute | solution.py:540
  30.5 2.7 %nearby.1.near_ref = f32[128,2048]{1,0:T(8,128)S(1)} custom-call(f32[128,128]{1,0:T(8,128)S(1)} %copy-done.5, f32[16,128]{1,0:T(8,128)S(1)} %copy-done.6, bf16[128,2048]{1,0:T(8,128)(2,1)S(1)} %copy-done, bf16[128,2048]{1,0:T(8,128)(2,1)S(1)} %copy-done.2, bf16[128,2048]{1,0:T(8,128)(2,1)S(1)} %copy-done.3), custom_call_target="tpu_custom_call" | custom-call | flops 201326592 | bytes 2621440 | tf_op jit(solution)/shard_map/nearby/pallas_call | solution.py:124
  33.6 1.1 %collective-permute-done.4.refs_0_.refs_15_ = f32[256,128]{1,0:T(8,128)S(1)} collective-permute-done((f32[256,128]{1,0:T(8,128)S(1)}, f32[256,128]{1,0:T(8,128)S(1)}, u32[]{:S(2)}, u32[]{:S(2)}) %collective-permute-start.4) | collective-permute-done | bytes 131104 | tf_op jit(solution)/shard_map/ppermute | solution.py:540
  34.7 0.8 %collective-permute-done.5.refs_1_.refs_14_ = f32[256,128]{1,0:T(8,128)S(1)} collective-permute-done((f32[256,128]{1,0:T(8,128)S(1)}, f32[256,128]{1,0:T(8,128)S(1)}, u32[]{:S(2)}, u32[]{:S(2)}) %collective-permute-start.5) | collective-permute-done | bytes 131104 | tf_op jit(solution)/shard_map/ppermute | solution.py:540
  35.7 0.5 attended.3
  36.3 1.2 %collective-permute-done.14.refs_1_ = f32[8,128]{1,0:T(8,128)S(1)} collective-permute-done((f32[8,128]{1,0:T(8,128)S(1)}, f32[8,128]{1,0:T(8,128)S(1)}, u32[]{:S(2)}, u32[]{:S(2)}) %collective-permute-start.14) | collective-permute-done | bytes 4128 | tf_op jit(solution)/shard_map/ppermute | solution.py:613
  37.4 0.6 back.4
  38.0 1.7 %collective-permute-start.15 = (f32[264,128]{1,0:T(8,128)S(1)}, f32[264,128]{1,0:T(8,128)S(1)}, u32[]{:S(2)}, u32[]{:S(2)}) collective-permute-start(f32[264,128]{1,0:T(8,128)S(1)} %get-tuple-element.94), channel_id=1, source_target_pairs={{0,2},{2,0},{4,6},{6,4},{8,10},{10,8},{12,14},{14,12},{16,18},{18,... | collective-permute-start | bytes 405512 | tf_op jit(solution)/shard_map/ppermute | solution.py:540
  39.7 1.3 %collective-permute-start.16 = (f32[264,128]{1,0:T(8,128)S(1)}, f32[264,128]{1,0:T(8,128)S(1)}, u32[]{:S(2)}, u32[]{:S(2)}) collective-permute-start(f32[264,128]{1,0:T(8,128)S(1)} %get-tuple-element.95), channel_id=1, source_target_pairs={{0,4},{2,6},{4,0},{6,2},{8,12},{10,14},{12,8},{14,10},{16,20},{18,... | collective-permute-start | bytes 405512 | tf_op jit(solution)/shard_map/ppermute | solution.py:540
  41.1 0.5 collective-permute-start.17
  41.6 0.5 back.5
  42.0 1.7 %collective-permute-start.22 = (f32[264,128]{1,0:T(8,128)S(1)}, f32[264,128]{1,0:T(8,128)S(1)}, u32[]{:S(2)}, u32[]{:S(2)}) collective-permute-start(f32[264,128]{1,0:T(8,128)S(1)} %get-tuple-element.103), channel_id=1, source_target_pairs={{0,2},{2,0},{4,6},{6,4},{8,10},{10,8},{12,14},{14,12},{16,18},{18,... | collective-permute-start | bytes 405512 | tf_op jit(solution)/shard_map/ppermute | solution.py:540
  43.7 1.3 %collective-permute-start.23 = (f32[264,128]{1,0:T(8,128)S(1)}, f32[264,128]{1,0:T(8,128)S(1)}, u32[]{:S(2)}, u32[]{:S(2)}) collective-permute-start(f32[264,128]{1,0:T(8,128)S(1)} %get-tuple-element.104), channel_id=1, source_target_pairs={{0,4},{2,6},{4,0},{6,2},{8,12},{10,14},{12,8},{14,10},{16,20},{18,... | collective-permute-start | bytes 405512 | tf_op jit(solution)/shard_map/ppermute | solution.py:540
  45.1 1.8 %collective-permute-start.24 = (f32[264,128]{1,0:T(8,128)S(1)}, f32[264,128]{1,0:T(8,128)S(1)}, u32[]{:S(2)}, u32[]{:S(2)}) collective-permute-start(f32[264,128]{1,0:T(8,128)S(1)} %get-tuple-element.105), channel_id=1, source_target_pairs={{0,6},{2,4},{4,2},{6,0},{8,14},{10,12},{12,10},{14,8},{16,22},{18,... | collective-permute-start | bytes 405512 | tf_op jit(solution)/shard_map/ppermute | solution.py:540
  46.9 0.4 back.3
  47.4 0.9 %collective-permute-done.16.refs_2_ = f32[264,128]{1,0:T(8,128)S(1)} collective-permute-done((f32[264,128]{1,0:T(8,128)S(1)}, f32[264,128]{1,0:T(8,128)S(1)}, u32[]{:S(2)}, u32[]{:S(2)}) %collective-permute-start.16) | collective-permute-done | bytes 135200 | tf_op jit(solution)/shard_map/ppermute | solution.py:540
  48.6 2.0 %collective-permute-start.18 = (f32[264,128]{1,0:T(8,128)S(1)}, f32[264,128]{1,0:T(8,128)S(1)}, u32[]{:S(2)}, u32[]{:S(2)}) collective-permute-start(f32[264,128]{1,0:T(8,128)S(1)} %get-tuple-element.97), channel_id=1, source_target_pairs={{0,24},{2,26},{4,28},{6,30},{8,0},{10,2},{12,4},{14,6},{16,8},{18,... | collective-permute-start | bytes 405512 | tf_op jit(solution)/shard_map/ppermute | solution.py:555
  50.6 0.8 %collective-permute-start.25 = (f32[8,128]{1,0:T(8,128)S(1)}, f32[8,128]{1,0:T(8,128)S(1)}, u32[]{:S(2)}, u32[]{:S(2)}) collective-permute-start(f32[8,128]{1,0:T(8,128)S(1)} %get-tuple-element.106.refs_4_), channel_id=1, source_target_pairs={{0,16},{2,18},{4,20},{6,22},{8,24},{10,26},{12,28},{14,30},{16,0},... | collective-permute-start | bytes 12296 | tf_op jit(solution)/shard_map/ppermute | solution.py:555
  51.4 2.4 %collective-permute-done.23.refs_2_ = f32[264,128]{1,0:T(8,128)S(1)} collective-permute-done((f32[264,128]{1,0:T(8,128)S(1)}, f32[264,128]{1,0:T(8,128)S(1)}, u32[]{:S(2)}, u32[]{:S(2)}) %collective-permute-start.23) | collective-permute-done | bytes 135200 | tf_op jit(solution)/shard_map/ppermute | solution.py:540
  53.8 1.3 %collective-permute-done.25.refs_5_ = f32[8,128]{1,0:T(8,128)S(1)} collective-permute-done((f32[8,128]{1,0:T(8,128)S(1)}, f32[8,128]{1,0:T(8,128)S(1)}, u32[]{:S(2)}, u32[]{:S(2)}) %collective-permute-start.25) | collective-permute-done | bytes 4128 | tf_op jit(solution)/shard_map/ppermute | solution.py:555
  55.2 2.4 %collective-permute-start.26 = (f32[264,128]{1,0:T(8,128)S(1)}, f32[264,128]{1,0:T(8,128)S(1)}, u32[]{:S(2)}, u32[]{:S(2)}) collective-permute-start(f32[264,128]{1,0:T(8,128)S(1)} %total.7.refs_5_), channel_id=1, source_target_pairs={{0,24},{2,26},{4,28},{6,30},{8,0},{10,2},{12,4},{14,6},{16,8},{18,... | collective-permute-start | bytes 405512 | tf_op jit(solution)/shard_map/ppermute | solution.py:555
  57.8 0.8 %collective-permute-start.19 = (f32[264,128]{1,0:T(8,128)S(1)}, f32[264,128]{1,0:T(8,128)S(1)}, u32[]{:S(2)}, u32[]{:S(2)}) collective-permute-start(f32[264,128]{1,0:T(8,128)S(1)} %get-tuple-element.99), channel_id=1, source_target_pairs={{0,2},{2,0},{4,6},{6,4},{8,10},{10,8},{12,14},{14,12},{16,18},{18,... | collective-permute-start | bytes 405512 | tf_op jit(solution)/shard_map/ppermute | solution.py:540
  58.6 1.3 %collective-permute-start.20 = (f32[264,128]{1,0:T(8,128)S(1)}, f32[264,128]{1,0:T(8,128)S(1)}, u32[]{:S(2)}, u32[]{:S(2)}) collective-permute-start(f32[264,128]{1,0:T(8,128)S(1)} %get-tuple-element.100), channel_id=1, source_target_pairs={{0,4},{2,6},{4,0},{6,2},{8,12},{10,14},{12,8},{14,10},{16,20},{18,... | collective-permute-start | bytes 405512 | tf_op jit(solution)/shard_map/ppermute | solution.py:540
  60.0 1.4 %collective-permute-start.21 = (f32[264,128]{1,0:T(8,128)S(1)}, f32[264,128]{1,0:T(8,128)S(1)}, u32[]{:S(2)}, u32[]{:S(2)}) collective-permute-start(f32[264,128]{1,0:T(8,128)S(1)} %get-tuple-element.101), channel_id=1, source_target_pairs={{0,6},{2,4},{4,2},{6,0},{8,14},{10,12},{12,10},{14,8},{16,22},{18,... | collective-permute-start | bytes 405512 | tf_op jit(solution)/shard_map/ppermute | solution.py:540
  61.6 1.6 %collective-permute-start.27 = (f32[264,128]{1,0:T(8,128)S(1)}, f32[264,128]{1,0:T(8,128)S(1)}, u32[]{:S(2)}, u32[]{:S(2)}) collective-permute-start(f32[264,128]{1,0:T(8,128)S(1)} %get-tuple-element.107), channel_id=1, source_target_pairs={{0,6},{2,4},{4,2},{6,0},{8,14},{10,12},{12,10},{14,8},{16,22},{18,... | collective-permute-start | bytes 405512 | tf_op jit(solution)/shard_map/ppermute | solution.py:540
  63.2 0.7 collective-permute-start.28
  64.2 0.9 %collective-permute-start.29 = (f32[264,128]{1,0:T(8,128)S(1)}, f32[264,128]{1,0:T(8,128)S(1)}, u32[]{:S(2)}, u32[]{:S(2)}) collective-permute-start(f32[264,128]{1,0:T(8,128)S(1)} %get-tuple-element.109), channel_id=1, source_target_pairs={{0,2},{2,0},{4,6},{6,4},{8,10},{10,8},{12,14},{14,12},{16,18},{18,... | collective-permute-start | bytes 405512 | tf_op jit(solution)/shard_map/ppermute | solution.py:540
  65.1 5.1 %gradients.1 = (bf16[128,2048]{1,0:T(8,128)(2,1)}, f32[128,2048]{1,0:T(8,128)S(1)}, f32[128,2048]{1,0:T(8,128)S(1)}) custom-call(f32[128,128]{1,0:T(8,128)S(1)} %copy-done.5, f32[16,128]{1,0:T(8,128)S(1)} %copy-done.6, bf16[128,2048]{1,0:T(8,128)(2,1)S(1)} %copy-done, bf16[128,2048]{1,0:T(8,128)(2,1)S(1)} %copy-done.2, bf16[128,2048]{1,0:T(8,128)(2,1)S(1)} %copy-done.3, ...), custom_call_target="tpu_custom_call" | custom-call | flops 872415232 | bytes 6291456 | tf_op jit(solution)/shard_map/gradients/pallas_call | solution.py:124
  70.4 1.5 %final.1 = (bf16[128,2048]{1,0:T(8,128)(2,1)}, bf16[128,2048]{1,0:T(8,128)(2,1)}, f32[1,2048]{1,0:T(1,128)}) custom-call(f32[128,128]{1,0:T(8,128)S(1)} %copy-done.5, f32[16,128]{1,0:T(8,128)S(1)} %copy-done.6, bf16[128,2048]{1,0:T(8,128)(2,1)S(1)} %copy-done.2, bf16[128,2048]{1,0:T(8,128)(2,1)S(1)} %copy-done.3, ...), custom_call_target="tpu_custom_call" | custom-call | flops 268435456 | bytes 6291456 | tf_op jit(solution)/shard_map/final/pallas_call | solution.py:124
  (46 shorter events, 3.0 us)
Async XLA Ops:
  0.6 6.8 %copy-start.2 = (bf16[128,2048]{1,0:T(8,128)(2,1)S(1)}, bf16[128,2048]{1,0:T(8,128)(2,1)}, u32[]{:S(2)}) copy-start(bf16[128,2048]{1,0:T(8,128)(2,1)} %key_ref.7) | copy-start | bytes 1572868
  0.6 6.7 %copy-start.3 = (bf16[128,2048]{1,0:T(8,128)(2,1)S(1)}, bf16[128,2048]{1,0:T(8,128)(2,1)}, u32[]{:S(2)}) copy-start(bf16[128,2048]{1,0:T(8,128)(2,1)} %value_ref.7) | copy-start | bytes 1572868
  2.8 4.6 %copy-start.6 = (f32[16,128]{1,0:T(8,128)S(1)}, f32[16,128]{1,0:T(8,128)}, u32[]{:S(2)}) copy-start(f32[16,128]{1,0:T(8,128)} %get-tuple-element.60.rates_ref) | copy-start | bytes 24580
  2.8 9.3 %collective-permute-start.7 = (f32[264,128]{1,0:T(8,128)}, f32[264,128]{1,0:T(8,128)S(1)}, u32[]{:S(2)}, u32[]{:S(2)}) collective-permute-start(f32[264,128]{1,0:T(8,128)} %get-tuple-element.70), channel_id=1, source_target_pairs={{0,2},{2,0},{4,6},{6,4},{8,10},{10,8},{12,14},{14,12},{16,18},{18,... | collective-permute-start | bytes 405512 | tf_op jit(solution)/shard_map/ppermute | solution.py:540
  5.8 8.7 %collective-permute-start.8 = (f32[264,128]{1,0:T(8,128)}, f32[264,128]{1,0:T(8,128)S(1)}, u32[]{:S(2)}, u32[]{:S(2)}) collective-permute-start(f32[264,128]{1,0:T(8,128)} %get-tuple-element.71), channel_id=1, source_target_pairs={{0,4},{2,6},{4,0},{6,2},{8,12},{10,14},{12,8},{14,10},{16,20},{18,... | collective-permute-start | bytes 405512 | tf_op jit(solution)/shard_map/ppermute | solution.py:540
  7.4 7.7 %collective-permute-start.9 = (f32[264,128]{1,0:T(8,128)}, f32[264,128]{1,0:T(8,128)S(1)}, u32[]{:S(2)}, u32[]{:S(2)}) collective-permute-start(f32[264,128]{1,0:T(8,128)} %get-tuple-element.72), channel_id=1, source_target_pairs={{0,6},{2,4},{4,2},{6,0},{8,14},{10,12},{12,10},{14,8},{16,22},{18,... | collective-permute-start | bytes 405512 | tf_op jit(solution)/shard_map/ppermute | solution.py:540
  7.4 0.8 %copy-start.4 = (f32[128,128]{1,0:T(8,128)S(1)}, f32[128,128]{1,0:T(8,128)}, u32[]{:S(2)}) copy-start(f32[128,128]{1,0:T(8,128)} %get-tuple-element.59.mark_ref) | copy-start | bytes 196612
  8.6 8.3 %collective-permute-start = (f32[264,128]{1,0:T(8,128)S(1)}, f32[264,128]{1,0:T(8,128)S(1)}, u32[]{:S(2)}, u32[]{:S(2)}) collective-permute-start(f32[264,128]{1,0:T(8,128)S(1)} %get-tuple-element.62), channel_id=1, source_target_pairs={{0,2},{2,0},{4,6},{6,4},{8,10},{10,8},{12,14},{14,12},{16,18},{18,... | collective-permute-start | bytes 405512 | tf_op jit(solution)/shard_map/ppermute | solution.py:540
  10.7 9.1 %collective-permute-start.1 = (f32[264,128]{1,0:T(8,128)S(1)}, f32[264,128]{1,0:T(8,128)S(1)}, u32[]{:S(2)}, u32[]{:S(2)}) collective-permute-start(f32[264,128]{1,0:T(8,128)S(1)} %get-tuple-element.63), channel_id=1, source_target_pairs={{0,4},{2,6},{4,0},{6,2},{8,12},{10,14},{12,8},{14,10},{16,20},{18,... | collective-permute-start | bytes 405512 | tf_op jit(solution)/shard_map/ppermute | solution.py:540
  12.2 7.6 %collective-permute-start.2 = (f32[264,128]{1,0:T(8,128)S(1)}, f32[264,128]{1,0:T(8,128)S(1)}, u32[]{:S(2)}, u32[]{:S(2)}) collective-permute-start(f32[264,128]{1,0:T(8,128)S(1)} %get-tuple-element.64), channel_id=1, source_target_pairs={{0,6},{2,4},{4,2},{6,0},{8,14},{10,12},{12,10},{14,8},{16,22},{18,... | collective-permute-start | bytes 405512 | tf_op jit(solution)/shard_map/ppermute | solution.py:540
  15.1 6.9 %collective-permute-start.10 = (f32[264,128]{1,0:T(8,128)S(1)}, f32[264,128]{1,0:T(8,128)S(1)}, u32[]{:S(2)}, u32[]{:S(2)}) collective-permute-start(f32[264,128]{1,0:T(8,128)S(1)} %total.5), channel_id=1, source_target_pairs={{0,8},{2,10},{4,12},{6,14},{8,16},{10,18},{12,20},{14,22},{16,24},... | collective-permute-start | bytes 405512 | tf_op jit(solution)/shard_map/ppermute | solution.py:555
  19.9 10.6 %copy-start = (bf16[128,2048]{1,0:T(8,128)(2,1)S(1)}, bf16[128,2048]{1,0:T(8,128)(2,1)}, u32[]{:S(2)}) copy-start(bf16[128,2048]{1,0:T(8,128)(2,1)} %query_ref.13) | copy-start | bytes 1572868
  19.9 6.9 %collective-permute-start.3 = (f32[264,128]{1,0:T(8,128)S(1)}, f32[264,128]{1,0:T(8,128)S(1)}, u32[]{:S(2)}, u32[]{:S(2)}) collective-permute-start(f32[264,128]{1,0:T(8,128)S(1)} %total.4), channel_id=1, source_target_pairs={{0,8},{2,10},{4,12},{6,14},{8,16},{10,18},{12,20},{14,22},{16,24},... | collective-permute-start | bytes 405512 | tf_op jit(solution)/shard_map/ppermute | solution.py:555
  22.2 7.5 %collective-permute-start.11 = (f32[256,128]{1,0:T(8,128)S(1)}, f32[256,128]{1,0:T(8,128)S(1)}, u32[]{:S(2)}, u32[]{:S(2)}) collective-permute-start(f32[256,128]{1,0:T(8,128)S(1)} %get-tuple-element.74), channel_id=1, source_target_pairs={{0,2},{2,0},{4,6},{6,4},{8,10},{10,8},{12,14},{14,12},{16,18},{18,... | collective-permute-start | bytes 393224 | tf_op jit(solution)/shard_map/ppermute | solution.py:540
  23.6 9.6 %collective-permute-start.12 = (f32[256,128]{1,0:T(8,128)S(1)}, f32[256,128]{1,0:T(8,128)S(1)}, u32[]{:S(2)}, u32[]{:S(2)}) collective-permute-start(f32[256,128]{1,0:T(8,128)S(1)} %get-tuple-element.75), channel_id=1, source_target_pairs={{0,4},{2,6},{4,0},{6,2},{8,12},{10,14},{12,8},{14,10},{16,20},{18,... | collective-permute-start | bytes 393224 | tf_op jit(solution)/shard_map/ppermute | solution.py:540
  24.7 5.8 %copy-start.5 = (f32[128,128]{1,0:T(8,128)S(1)}, f32[128,128]{1,0:T(8,128)}, u32[]{:S(2)}) copy-start(f32[128,128]{1,0:T(8,128)} %get-tuple-element.59.mark_ref) | copy-start | bytes 196612
  24.7 8.5 %collective-permute-start.13 = (f32[256,128]{1,0:T(8,128)S(1)}, f32[256,128]{1,0:T(8,128)S(1)}, u32[]{:S(2)}, u32[]{:S(2)}) collective-permute-start(f32[256,128]{1,0:T(8,128)S(1)} %get-tuple-element.76), channel_id=1, source_target_pairs={{0,6},{2,4},{4,2},{6,0},{8,14},{10,12},{12,10},{14,8},{16,22},{18,... | collective-permute-start | bytes 393224 | tf_op jit(solution)/shard_map/ppermute | solution.py:540
  26.9 7.8 %collective-permute-start.4 = (f32[256,128]{1,0:T(8,128)S(1)}, f32[256,128]{1,0:T(8,128)S(1)}, u32[]{:S(2)}, u32[]{:S(2)}) collective-permute-start(f32[256,128]{1,0:T(8,128)S(1)} %get-tuple-element.65), channel_id=1, source_target_pairs={{0,6},{2,4},{4,2},{6,0},{8,14},{10,12},{12,10},{14,8},{16,22},{18,... | collective-permute-start | bytes 393224 | tf_op jit(solution)/shard_map/ppermute | solution.py:540
  28.5 7.1 %collective-permute-start.5 = (f32[256,128]{1,0:T(8,128)S(1)}, f32[256,128]{1,0:T(8,128)S(1)}, u32[]{:S(2)}, u32[]{:S(2)}) collective-permute-start(f32[256,128]{1,0:T(8,128)S(1)} %get-tuple-element.66), channel_id=1, source_target_pairs={{0,4},{2,6},{4,0},{6,2},{8,12},{10,14},{12,8},{14,10},{16,20},{18,... | collective-permute-start | bytes 393224 | tf_op jit(solution)/shard_map/ppermute | solution.py:540
  29.7 3.5 %copy-start.1 = (bf16[128,2048]{1,0:T(8,128)(2,1)S(1)}, bf16[128,2048]{1,0:T(8,128)(2,1)}, u32[]{:S(2)}) copy-start(bf16[128,2048]{1,0:T(8,128)(2,1)} %grad_ref.9) | copy-start | bytes 1572868
  29.7 6.0 %collective-permute-start.6 = (f32[256,128]{1,0:T(8,128)S(1)}, f32[256,128]{1,0:T(8,128)S(1)}, u32[]{:S(2)}, u32[]{:S(2)}) collective-permute-start(f32[256,128]{1,0:T(8,128)S(1)} %get-tuple-element.67), channel_id=1, source_target_pairs={{0,2},{2,0},{4,6},{6,4},{8,10},{10,8},{12,14},{14,12},{16,18},{18,... | collective-permute-start | bytes 393224 | tf_op jit(solution)/shard_map/ppermute | solution.py:540
  30.5 2.7 %copy-start.7 = (f32[2048]{0:T(1024)S(1)}, f32[2048]{0:T(1024)}, u32[]{:S(2)}) copy-start(f32[2048]{0:T(1024)} %param.12) | copy-start | bytes 24580
  36.2 1.2 %collective-permute-start.14 = (f32[8,128]{1,0:T(8,128)S(1)}, f32[8,128]{1,0:T(8,128)S(1)}, u32[]{:S(2)}, u32[]{:S(2)}) collective-permute-start(f32[8,128]{1,0:T(8,128)S(1)} %get-tuple-element.81.refs_0_), channel_id=1, source_target_pairs={{0,1},{1,0},{2,3},{3,2},{4,5},{5,4},{6,7},{7,6},{8,9},{9,8},{10,11... | collective-permute-start | bytes 12296 | tf_op jit(solution)/shard_map/ppermute | solution.py:613
  38.0 7.1 %collective-permute-start.15 = (f32[264,128]{1,0:T(8,128)S(1)}, f32[264,128]{1,0:T(8,128)S(1)}, u32[]{:S(2)}, u32[]{:S(2)}) collective-permute-start(f32[264,128]{1,0:T(8,128)S(1)} %get-tuple-element.94), channel_id=1, source_target_pairs={{0,2},{2,0},{4,6},{6,4},{8,10},{10,8},{12,14},{14,12},{16,18},{18,... | collective-permute-start | bytes 405512 | tf_op jit(solution)/shard_map/ppermute | solution.py:540
  39.7 8.5 %collective-permute-start.16 = (f32[264,128]{1,0:T(8,128)S(1)}, f32[264,128]{1,0:T(8,128)S(1)}, u32[]{:S(2)}, u32[]{:S(2)}) collective-permute-start(f32[264,128]{1,0:T(8,128)S(1)} %get-tuple-element.95), channel_id=1, source_target_pairs={{0,4},{2,6},{4,0},{6,2},{8,12},{10,14},{12,8},{14,10},{16,20},{18,... | collective-permute-start | bytes 405512 | tf_op jit(solution)/shard_map/ppermute | solution.py:540
  41.1 7.5 %collective-permute-start.17 = (f32[264,128]{1,0:T(8,128)S(1)}, f32[264,128]{1,0:T(8,128)S(1)}, u32[]{:S(2)}, u32[]{:S(2)}) collective-permute-start(f32[264,128]{1,0:T(8,128)S(1)} %get-tuple-element.96), channel_id=1, source_target_pairs={{0,6},{2,4},{4,2},{6,0},{8,14},{10,12},{12,10},{14,8},{16,22},{18,... | collective-permute-start | bytes 405512 | tf_op jit(solution)/shard_map/ppermute | solution.py:540
  42.0 9.4 %collective-permute-start.22 = (f32[264,128]{1,0:T(8,128)S(1)}, f32[264,128]{1,0:T(8,128)S(1)}, u32[]{:S(2)}, u32[]{:S(2)}) collective-permute-start(f32[264,128]{1,0:T(8,128)S(1)} %get-tuple-element.103), channel_id=1, source_target_pairs={{0,2},{2,0},{4,6},{6,4},{8,10},{10,8},{12,14},{14,12},{16,18},{18,... | collective-permute-start | bytes 405512 | tf_op jit(solution)/shard_map/ppermute | solution.py:540
  43.7 10.0 %collective-permute-start.23 = (f32[264,128]{1,0:T(8,128)S(1)}, f32[264,128]{1,0:T(8,128)S(1)}, u32[]{:S(2)}, u32[]{:S(2)}) collective-permute-start(f32[264,128]{1,0:T(8,128)S(1)} %get-tuple-element.104), channel_id=1, source_target_pairs={{0,4},{2,6},{4,0},{6,2},{8,12},{10,14},{12,8},{14,10},{16,20},{18,... | collective-permute-start | bytes 405512 | tf_op jit(solution)/shard_map/ppermute | solution.py:540
  45.1 8.7 %collective-permute-start.24 = (f32[264,128]{1,0:T(8,128)S(1)}, f32[264,128]{1,0:T(8,128)S(1)}, u32[]{:S(2)}, u32[]{:S(2)}) collective-permute-start(f32[264,128]{1,0:T(8,128)S(1)} %get-tuple-element.105), channel_id=1, source_target_pairs={{0,6},{2,4},{4,2},{6,0},{8,14},{10,12},{12,10},{14,8},{16,22},{18,... | collective-permute-start | bytes 405512 | tf_op jit(solution)/shard_map/ppermute | solution.py:540
  48.6 9.0 %collective-permute-start.18 = (f32[264,128]{1,0:T(8,128)S(1)}, f32[264,128]{1,0:T(8,128)S(1)}, u32[]{:S(2)}, u32[]{:S(2)}) collective-permute-start(f32[264,128]{1,0:T(8,128)S(1)} %get-tuple-element.97), channel_id=1, source_target_pairs={{0,24},{2,26},{4,28},{6,30},{8,0},{10,2},{12,4},{14,6},{16,8},{18,... | collective-permute-start | bytes 405512 | tf_op jit(solution)/shard_map/ppermute | solution.py:555
  50.6 4.5 %collective-permute-start.25 = (f32[8,128]{1,0:T(8,128)S(1)}, f32[8,128]{1,0:T(8,128)S(1)}, u32[]{:S(2)}, u32[]{:S(2)}) collective-permute-start(f32[8,128]{1,0:T(8,128)S(1)} %get-tuple-element.106.refs_4_), channel_id=1, source_target_pairs={{0,16},{2,18},{4,20},{6,22},{8,24},{10,26},{12,28},{14,30},{16,0},... | collective-permute-start | bytes 12296 | tf_op jit(solution)/shard_map/ppermute | solution.py:555
  55.2 6.2 %collective-permute-start.26 = (f32[264,128]{1,0:T(8,128)S(1)}, f32[264,128]{1,0:T(8,128)S(1)}, u32[]{:S(2)}, u32[]{:S(2)}) collective-permute-start(f32[264,128]{1,0:T(8,128)S(1)} %total.7.refs_5_), channel_id=1, source_target_pairs={{0,24},{2,26},{4,28},{6,30},{8,0},{10,2},{12,4},{14,6},{16,8},{18,... | collective-permute-start | bytes 405512 | tf_op jit(solution)/shard_map/ppermute | solution.py:555
  57.8 6.4 %collective-permute-start.19 = (f32[264,128]{1,0:T(8,128)S(1)}, f32[264,128]{1,0:T(8,128)S(1)}, u32[]{:S(2)}, u32[]{:S(2)}) collective-permute-start(f32[264,128]{1,0:T(8,128)S(1)} %get-tuple-element.99), channel_id=1, source_target_pairs={{0,2},{2,0},{4,6},{6,4},{8,10},{10,8},{12,14},{14,12},{16,18},{18,... | collective-permute-start | bytes 405512 | tf_op jit(solution)/shard_map/ppermute | solution.py:540
  58.6 11.6 %collective-permute-start.20 = (f32[264,128]{1,0:T(8,128)S(1)}, f32[264,128]{1,0:T(8,128)S(1)}, u32[]{:S(2)}, u32[]{:S(2)}) collective-permute-start(f32[264,128]{1,0:T(8,128)S(1)} %get-tuple-element.100), channel_id=1, source_target_pairs={{0,4},{2,6},{4,0},{6,2},{8,12},{10,14},{12,8},{14,10},{16,20},{18,... | collective-permute-start | bytes 405512 | tf_op jit(solution)/shard_map/ppermute | solution.py:540
  60.0 10.3 %collective-permute-start.21 = (f32[264,128]{1,0:T(8,128)S(1)}, f32[264,128]{1,0:T(8,128)S(1)}, u32[]{:S(2)}, u32[]{:S(2)}) collective-permute-start(f32[264,128]{1,0:T(8,128)S(1)} %get-tuple-element.101), channel_id=1, source_target_pairs={{0,6},{2,4},{4,2},{6,0},{8,14},{10,12},{12,10},{14,8},{16,22},{18,... | collective-permute-start | bytes 405512 | tf_op jit(solution)/shard_map/ppermute | solution.py:540
  61.6 8.7 %collective-permute-start.27 = (f32[264,128]{1,0:T(8,128)S(1)}, f32[264,128]{1,0:T(8,128)S(1)}, u32[]{:S(2)}, u32[]{:S(2)}) collective-permute-start(f32[264,128]{1,0:T(8,128)S(1)} %get-tuple-element.107), channel_id=1, source_target_pairs={{0,6},{2,4},{4,2},{6,0},{8,14},{10,12},{12,10},{14,8},{16,22},{18,... | collective-permute-start | bytes 405512 | tf_op jit(solution)/shard_map/ppermute | solution.py:540
  63.2 7.3 %collective-permute-start.28 = (f32[264,128]{1,0:T(8,128)S(1)}, f32[264,128]{1,0:T(8,128)S(1)}, u32[]{:S(2)}, u32[]{:S(2)}) collective-permute-start(f32[264,128]{1,0:T(8,128)S(1)} %get-tuple-element.108), channel_id=1, source_target_pairs={{0,4},{2,6},{4,0},{6,2},{8,12},{10,14},{12,8},{14,10},{16,20},{18,... | collective-permute-start | bytes 405512 | tf_op jit(solution)/shard_map/ppermute | solution.py:540
  64.2 6.2 %collective-permute-start.29 = (f32[264,128]{1,0:T(8,128)S(1)}, f32[264,128]{1,0:T(8,128)S(1)}, u32[]{:S(2)}, u32[]{:S(2)}) collective-permute-start(f32[264,128]{1,0:T(8,128)S(1)} %get-tuple-element.109), channel_id=1, source_target_pairs={{0,2},{2,0},{4,6},{6,4},{8,10},{10,8},{12,14},{14,12},{16,18},{18,... | collective-permute-start | bytes 405512 | tf_op jit(solution)/shard_map/ppermute | solution.py:540
